TPU v7x, 32 devices: a whole 2x2x4 slice. The times are simulated.
32 devices in a mesh: dp: 8 (over z, x), group: 4 (over y, core).
Axes of the slice: x: 2, y: 2, z: 4, core: 2. Of those that a mesh axis runs over, the one named last changes fastest.
Arguments:
- image_emb: bfloat16 [8192, 1152], P(('dp', 'group')), may hold values from -0.17675781 to 0.17675781
- text_emb: float32 [8192, 1152], P(('dp', 'group')), may hold values from -0.17677669 to 0.17677669
- text_accum: float32 [8192, 1152], P(('dp', 'group')), may hold values from -6 to 6
- pair_ids: int32 [8192], P(('dp', 'group')), may hold values from 0 to 127
- log_scale: float32 [1], replicated, may hold values from 1 to 2
- bias: float32 [1], replicated, may hold values from -3 to 0
Outputs:
- row_loss: float32 [8192], P(('dp', 'group'))
- image_grad: bfloat16 [8192, 1152], P(('dp', 'group'))
- text_grad: float32 [8192, 1152], P(('dp', 'group'))
Inputs may be any that keep to these rules, and one draw needn't show every extreme that they name: `pair_ids`: two examples form a positive pair exactly where their ids are equal.
All inputs are finite; a program needn't handle non-finite values.
Results may differ from a plain program's by a relative error of at most 0.0059.
Values may be sent and summed in bfloat16 or wider, within the bound.
No kernel may reach another device: no remote copies, remote signals or barrier semaphores. Data moves between devices by JAX's collectives and lax.ppermute only.
A program may use at most 64 MiB of HBM per device.

v0:
```python
import jax
import jax.numpy as jnp
from jax import lax
from jax.sharding import PartitionSpec as P

SHIFTS = 2


def from_behind(block, axis, distance):
    devices = range(lax.axis_size(axis))
    route = [((i - distance) % len(devices), i) for i in devices]
    return lax.ppermute(block, axis, route)


def block_terms(image_block, text_block, image_ids, text_ids, scale, shift):
    logits = (
        scale
        * lax.dot_general(
            image_block, text_block, (((1,), (1,)), ((), ())), preferred_element_type=jnp.float32
        )
        + shift
    )
    signs = jnp.where(image_ids[:, None] == text_ids[None, :], 1.0, -1.0).astype(jnp.float32)
    loss = jnp.sum(jax.nn.softplus(-signs * logits), axis=1)
    coef = (-signs * jax.nn.sigmoid(-signs * logits) * scale).astype(jnp.bfloat16)
    image_part = jnp.dot(coef, text_block, preferred_element_type=jnp.float32)
    text_part = lax.dot_general(
        coef, image_block, (((0,), (0,)), ((), ())), preferred_element_type=jnp.float32
    )
    return (loss, image_part, text_part)


def body(image_emb, text_emb, text_accum, pair_ids, log_scale, bias):
    scale = jnp.exp(log_scale[0])
    shift = bias[0]
    texts = text_emb.astype(jnp.bfloat16)
    loss, image_sum, text_part = block_terms(image_emb, texts, pair_ids, pair_ids, scale, shift)
    text_ids = pair_ids
    carried = text_accum + text_part
    for step in range(SHIFTS):
        texts = from_behind(texts, ("dp", "group"), 1)
        text_ids, carried = from_behind((text_ids, carried), ("dp", "group"), 1)
        part_loss, image_part, text_part = block_terms(
            image_emb, texts, pair_ids, text_ids, scale, shift
        )
        loss = loss + part_loss
        image_sum = image_sum + image_part
        carried = carried + text_part
    row_loss = loss / ((SHIFTS + 1) * image_emb.shape[0])
    return (row_loss, image_sum.astype(jnp.bfloat16), carried)


def solution(mesh):
    in_specs = (
        P(("dp", "group"), None),
        P(("dp", "group"), None),
        P(("dp", "group"), None),
        P(("dp", "group")),
        P(),
        P(),
    )
    out_specs = (P(("dp", "group")), P(("dp", "group"), None), P(("dp", "group"), None))
    return jax.shard_map(body, mesh=mesh, in_specs=in_specs, out_specs=out_specs, check_vma=False)
```

profile of v0, /device:TPU:0, one launch (start us, length us, event | category | flops | bytes accessed | tf_op | source)
XLA Modules:
  0.0 61.1 jit_solution(4088010473387304953)
XLA Ops:
  0.6 0.0 copy-start
  0.6 0.0 copy-start.2
  2.0 1.3 %convert_element_type.15 = bf16[256,1152]{1,0:T(8,128)(2,1)S(1)} convert(f32[256,1152]{1,0:T(8,128)} %param.7) | non-fusion elementwise | flops 294912 | bytes 1769472 | tf_op jit(solution)/shard_map/convert_element_type | solution.py:36
  3.4 0.0 copy-start.1
  3.4 0.0 copy-done
  3.4 0.0 copy-done.2
  3.4 0.5 fusion.7
  4.0 0.7 %copy-done.1 = f32[256,1152]{1,0:T(8,128)S(1)} copy-done((f32[256,1152]{1,0:T(8,128)S(1)}, f32[256,1152]{1,0:T(8,128)}, u32[]{:S(2)}) %copy-start.1) | copy-done | bytes 1179672
  4.7 0.4 convolution_add_fusion.1
  5.1 0.5 collective-permute-start.4
  5.6 2.6 %collective-permute-start.1 = (bf16[256,1152]{1,0:T(8,128)(2,1)S(1)}, bf16[256,1152]{1,0:T(8,128)(2,1)S(1)}, u32[]{:S(2)}, u32[]{:S(2)}) collective-permute-start(bf16[256,1152]{1,0:T(8,128)(2,1)S(1)} %convert_element_type.15), channel_id=1, source_target_pairs={{31,0},{0,1},{1,2},{2,3},{3,4},{4,5},{5,6},{6,7},{7,8},{8,9},{9,10... | collective-permute-start | bytes 1769480 | tf_op jit(solution)/shard_map/ppermute | solution.py:12
  8.2 0.1 collective-permute-start
  8.3 23.4 %collective-permute-done.1 = bf16[256,1152]{1,0:T(8,128)(2,1)S(1)} collective-permute-done((bf16[256,1152]{1,0:T(8,128)(2,1)S(1)}, bf16[256,1152]{1,0:T(8,128)(2,1)S(1)}, u32[]{:S(2)}, u32[]{:S(2)}) %collective-permute-start.1) | collective-permute-done | bytes 589856 | tf_op jit(solution)/shard_map/ppermute | solution.py:12
  31.7 0.0 collective-permute-start.3
  31.7 0.0 collective-permute-done
  31.7 0.5 fusion.8
  32.3 0.0 collective-permute-done.4
  32.3 0.4 convolution_add_fusion
  32.7 0.1 collective-permute-start.5
  32.8 0.5 fusion.10
  33.2 0.1 collective-permute-start.2
  33.3 0.5 convolution_add_fusion.3
  33.8 23.5 %collective-permute-done.2 = s32[256]{0:T(256)S(1)} collective-permute-done((s32[256]{0:T(256)S(1)}, s32[256]{0:T(256)S(1)}, u32[]{:S(2)}, u32[]{:S(2)}) %collective-permute-start.2) | collective-permute-done | bytes 1056 | tf_op jit(solution)/shard_map/ppermute | solution.py:12
  57.3 0.0 collective-permute-done.3
  57.3 0.5 fusion.9
  57.8 0.6 add_multiply_fusion
  58.4 1.3 %fusion = bf16[256,1152]{1,0:T(8,128)(2,1)} fusion(f32[256,1152]{1,0:T(8,128)S(1)} %convolution_add_fusion.3, bf16[256,1152]{1,0:T(8,128)(2,1)S(1)} %collective-permute-done.3, f32[256,256]{0,1:T(8,128)S(1)} %get-tuple-element.4, f32[]{:T(128)} %bitcast, s32[256]{0:T(256)S(1)} %copy-done.2, s32[256]{0:T(256)S(1)} %collective-permute-done.2), kind=kOutput, calls=%fused_computation.4 | convolution fusion | flops 152174592 | bytes 2623492 | tf_op jit(solution)/shard_map/dot_general | solution.py:26
  59.7 0.0 collective-permute-done.5
  59.7 1.4 %fusion.12 = f32[256,1152]{1,0:T(8,128)} fusion(f32[256,1152]{1,0:T(8,128)S(1)} %collective-permute-done.5, bf16[256,1152]{1,0:T(8,128)(2,1)S(1)} %copy-done, f32[256,256]{0,1:T(8,128)S(1)} %get-tuple-element.4, f32[]{:T(128)} %bitcast, s32[256]{0:T(256)S(1)} %copy-done.2, s32[256]{0:T(256)S(1)} %collective-permute-done.2), kind=kOutput, calls=%fused_computation.29 | convolution fusion | flops 151879680 | bytes 3213316 | tf_op jit(solution)/shard_map/dot_general | solution.py:27
Async XLA Ops:
  0.6 2.8 %copy-start = (bf16[256,1152]{1,0:T(8,128)(2,1)S(1)}, bf16[256,1152]{1,0:T(8,128)(2,1)}, u32[]{:S(2)}) copy-start(bf16[256,1152]{1,0:T(8,128)(2,1)} %param.6) | copy-start | bytes 1769476
  0.6 2.8 %copy-start.2 = (s32[256]{0:T(256)S(1)}, s32[256]{0:T(256)}, u32[]{:S(2)}) copy-start(s32[256]{0:T(256)} %param.9) | copy-start | bytes 3076
  3.4 1.3 %copy-start.1 = (f32[256,1152]{1,0:T(8,128)S(1)}, f32[256,1152]{1,0:T(8,128)}, u32[]{:S(2)}) copy-start(f32[256,1152]{1,0:T(8,128)} %param.8) | copy-start | bytes 3538948
  5.1 27.2 %collective-permute-start.4 = (f32[256,1152]{1,0:T(8,128)S(1)}, f32[256,1152]{1,0:T(8,128)S(1)}, u32[]{:S(2)}, u32[]{:S(2)}) collective-permute-start(f32[256,1152]{1,0:T(8,128)S(1)} %convolution_add_fusion.1), channel_id=1, source_target_pairs={{31,0},{0,1},{1,2},{2,3},{3,4},{4,5},{5,6},{6,7},{7,8},{8,9},{9,10... | collective-permute-start | bytes 3538952 | tf_op jit(solution)/shard_map/ppermute | solution.py:12
  5.6 26.1 %collective-permute-start.1 = (bf16[256,1152]{1,0:T(8,128)(2,1)S(1)}, bf16[256,1152]{1,0:T(8,128)(2,1)S(1)}, u32[]{:S(2)}, u32[]{:S(2)}) collective-permute-start(bf16[256,1152]{1,0:T(8,128)(2,1)S(1)} %convert_element_type.15), channel_id=1, source_target_pairs={{31,0},{0,1},{1,2},{2,3},{3,4},{4,5},{5,6},{6,7},{7,8},{8,9},{9,10... | collective-permute-start | bytes 1769480 | tf_op jit(solution)/shard_map/ppermute | solution.py:12
  8.2 23.5 %collective-permute-start = (s32[256]{0:T(256)S(1)}, s32[256]{0:T(256)S(1)}, u32[]{:S(2)}, u32[]{:S(2)}) collective-permute-start(s32[256]{0:T(256)S(1)} %copy-done.2), channel_id=1, source_target_pairs={{31,0},{0,1},{1,2},{2,3},{3,4},{4,5},{5,6},{6,7},{7,8},{8,9},{9,10... | collective-permute-start | bytes 3080 | tf_op jit(solution)/shard_map/ppermute | solution.py:12
  31.7 25.6 %collective-permute-start.3 = (bf16[256,1152]{1,0:T(8,128)(2,1)S(1)}, bf16[256,1152]{1,0:T(8,128)(2,1)S(1)}, u32[]{:S(2)}, u32[]{:S(2)}) collective-permute-start(bf16[256,1152]{1,0:T(8,128)(2,1)S(1)} %collective-permute-done.1), channel_id=1, source_target_pairs={{31,0},{0,1},{1,2},{2,3},{3,4},{4,5},{5,6},{6,7},{7,8},{8,9},{9,10... | collective-permute-start | bytes 1769480 | tf_op jit(solution)/shard_map/ppermute | solution.py:12
  32.7 27.0 %collective-permute-start.5 = (f32[256,1152]{1,0:T(8,128)S(1)}, f32[256,1152]{1,0:T(8,128)S(1)}, u32[]{:S(2)}, u32[]{:S(2)}) collective-permute-start(f32[256,1152]{1,0:T(8,128)S(1)} %convolution_add_fusion), channel_id=1, source_target_pairs={{31,0},{0,1},{1,2},{2,3},{3,4},{4,5},{5,6},{6,7},{7,8},{8,9},{9,10... | collective-permute-start | bytes 3538952 | tf_op jit(solution)/shard_map/ppermute | solution.py:12
  33.2 24.1 %collective-permute-start.2 = (s32[256]{0:T(256)S(1)}, s32[256]{0:T(256)S(1)}, u32[]{:S(2)}, u32[]{:S(2)}) collective-permute-start(s32[256]{0:T(256)S(1)} %collective-permute-done), channel_id=1, source_target_pairs={{31,0},{0,1},{1,2},{2,3},{3,4},{4,5},{5,6},{6,7},{7,8},{8,9},{9,10... | collective-permute-start | bytes 3080 | tf_op jit(solution)/shard_map/ppermute | solution.py:12
where the time goes:
time: 61.3 us; the launch traced here: 61.1 us
  waiting for transfers between devices  47 us (77%)
  matrix products  6.02 us (10%)
  starting transfers between devices  3.32 us (5%)
  between operations  2.12 us (3%)
  other arithmetic  1.91 us (3%)
  local copies, waits for them, and re-layouts  0.72 us (1%)
    ppermute x6, waiting for transfers between devices, from_behind(): return lax.ppermute(block, axis, route)  47 us
    ppermute x6, starting transfers between devices, from_behind(): return lax.ppermute(block, axis, route)  3.32 us
    dot_general x3, matrix products, block_terms(): image_part = jnp.dot(coef, text_block, preferred_element_type=jnp.float32)  2.22 us
    dot_general x3, matrix products, block_terms(): lax.dot_general(coef, image_block, (((0,), (0,)), ((), ())), preferred_el...  2.22 us
    dot_general x3, matrix products, block_terms(): lax.dot_general(image_block, text_block, (((1,), (1,)), ((), ())), prefer...  1.58 us
    convert_element_type x1, other arithmetic, body(): texts = text_emb.astype(jnp.bfloat16)  1.33 us
  transfers between devices with their start and end apart: 6, of which 2 were waited for; matrix products, arithmetic and copies ran while one was open for 7% of the time, Pallas kernels for 0%

commit v1 on v0

v1 whole, which is shorter than its diff:
```python
import jax
import jax.numpy as jnp
from jax import lax
from jax.sharding import PartitionSpec as P

SHIFTS = 2
AXES = ("dp", "group")


def rows_of(a, b):
    return lax.dot_general(a, b, (((1,), (1,)), ((), ())), preferred_element_type=jnp.float32)


def back(coef, images):
    return lax.dot_general(coef, images, (((0,), (0,)), ((), ())), preferred_element_type=jnp.float32)


def pair(images, texts, image_ids, text_ids, scale, shift):
    logits = scale * rows_of(images, texts) + shift
    signs = jnp.where(image_ids[:, None] == text_ids[None, :], 1.0, -1.0).astype(jnp.float32)
    margin = -signs * logits
    coef = (-signs * jax.nn.sigmoid(margin) * scale).astype(jnp.bfloat16)
    return margin, coef


def body(image_emb, text_emb, text_accum, pair_ids, log_scale, bias):
    count = lax.axis_size(AXES)
    rows = image_emb.shape[0]
    even = lax.axis_index("group") % 2 == 0
    scale = jnp.exp(log_scale[0])
    shift = bias[0]

    def send(value, route):
        return lax.ppermute(value, AXES, route)

    skip = [(i, (i + 2) % count) for i in range(count)]
    swap = [(i, i ^ 1) for i in range(count)]
    to_odd = [(i, i + 1) for i in range(0, count, 2)]
    to_even = [(i + 1, i) for i in range(0, count, 2)]

    texts = text_emb.astype(jnp.bfloat16)
    mate_ids = send(pair_ids, swap)
    texts_2 = send(texts, skip)
    mate_images = send(image_emb, swap)
    texts_in = send(texts, to_odd)
    both_ids = send(jnp.concatenate([pair_ids, mate_ids]), skip)
    ids_2 = both_ids[:rows]
    ids_1 = jnp.where(even, both_ids[rows:], mate_ids)

    margin_0, coef_0 = pair(image_emb, texts, pair_ids, pair_ids, scale, shift)
    _, mate_coef = pair(mate_images, texts, mate_ids, pair_ids, scale, shift)
    mate_coef = jnp.where(even, mate_coef, jnp.zeros_like(mate_coef))
    outgoing = text_accum + back(coef_0, image_emb) + back(mate_coef, mate_images)
    arrived = send(outgoing.astype(jnp.bfloat16), skip)

    margin_2, coef_2 = pair(image_emb, texts_2, pair_ids, ids_2, scale, shift)
    _, mate_coef = pair(mate_images, texts_2, mate_ids, ids_2, scale, shift)
    mate_coef = jnp.where(even, jnp.zeros_like(mate_coef), mate_coef)
    late = back(coef_2, image_emb) + back(mate_coef, mate_images)

    texts_1 = jnp.where(even, send(texts_2, to_even), texts_in)
    margin_1, coef_1 = pair(image_emb, texts_1, pair_ids, ids_1, scale, shift)

    loss = sum(jnp.sum(jax.nn.softplus(m), axis=1) for m in (margin_0, margin_1, margin_2))
    image_grad = (
        jnp.dot(coef_0, texts, preferred_element_type=jnp.float32)
        + jnp.dot(coef_1, texts_1, preferred_element_type=jnp.float32)
        + jnp.dot(coef_2, texts_2, preferred_element_type=jnp.float32)
    )
    text_grad = arrived.astype(jnp.float32) + late
    return (loss / ((SHIFTS + 1) * rows), image_grad.astype(jnp.bfloat16), text_grad)


def solution(mesh):
    in_specs = (P(AXES, None), P(AXES, None), P(AXES, None), P(AXES), P(), P())
    out_specs = (P(AXES), P(AXES, None), P(AXES, None))
    return jax.shard_map(body, mesh=mesh, in_specs=in_specs, out_specs=out_specs, check_vma=False)
```

time: 61.3 us -> 49.3 us (0.80)
  waiting for transfers between devices: 47 us -> 19.8 us
  matrix products: 6.02 us -> 15.4 us
  starting transfers between devices: 3.32 us -> 8.52 us
  other arithmetic: 1.91 us -> 2.79 us
  local copies, waits for them, and re-layouts: 0.72 us -> 0.02 us
    ppermute x6 -> x7, waiting for transfers between devices: 47 us -> 19.8 us  [send(): return lax.ppermute(value, AXES, route)]
    dot_general x9 -> x10, matrix products: 6.02 us -> 15.4 us  [the longest x4 5.64 us: back(): lax.dot_general(coef, images, (((0,), (0,)), ((), ())), preferred_element...]
    ppermute x6 -> x7, starting transfers between devices: 3.32 us -> 8.52 us  [send(): return lax.ppermute(value, AXES, route)]
    convert_element_type x1, other arithmetic: 1.33 us -> 2.21 us  [body(): texts = text_emb.astype(jnp.bfloat16)]
    unnamed x6 -> x10, local copies, waits for them, and re-layouts: 0.72 us -> 0.02 us
  transfers between devices with their start and end apart: 6 -> 7, of which waited for: 2 -> 2; matrix products, arithmetic and copies ran while one was open for 7% -> 29% of each run, Pallas kernels for 0% -> 0%
where the time goes in v1:
time: 49.3 us; the launch traced here: 48.6 us
  waiting for transfers between devices  19.8 us (40%)
  matrix products  15.4 us (31%)
  starting transfers between devices  8.52 us (17%)
  other arithmetic  2.79 us (6%)
  between operations  2.09 us (4%)
    ppermute x7, waiting for transfers between devices, send(): return lax.ppermute(value, AXES, route)  19.8 us
    ppermute x7, starting transfers between devices, send(): return lax.ppermute(value, AXES, route)  8.52 us
    dot_general x4, matrix products, back(): lax.dot_general(coef, images, (((0,), (0,)), ((), ())), preferred_element...  5.64 us
    dot_general x3, matrix products, rows_of(): lax.dot_general(a, b, (((1,), (1,)), ((), ())), preferred_element_type=jn...  4.39 us
    dot_general x1, matrix products, body(): jnp.dot(coef_0, texts, preferred_element_type=jnp.float32)  2.54 us
    convert_element_type x1, other arithmetic, body(): texts = text_emb.astype(jnp.bfloat16)  2.21 us
    dot_general x1, matrix products, body(): jnp.dot(coef_1, texts_1, preferred_element_type=jnp.float32)  1.54 us
    dot_general x1, matrix products, body(): jnp.dot(coef_2, texts_2, preferred_element_type=jnp.float32)  1.29 us
  transfers between devices with their start and end apart: 7, of which 2 were waited for; matrix products, arithmetic and copies ran while one was open for 29% of the time, Pallas kernels for 0%

profile of v1, /device:TPU:0, one launch (start us, length us, event | category | flops | bytes accessed | tf_op | source)
XLA Modules:
  0.0 48.6 jit_solution(7758713512793724517)
XLA Ops:
  0.6 0.0 copy-start.3
  0.6 0.0 copy-start
  0.7 2.2 %convert_element_type.27 = bf16[256,1152]{1,0:T(8,128)(2,1)} convert(f32[256,1152]{1,0:T(8,128)} %param.7) | non-fusion elementwise | flops 294912 | bytes 1769472 | tf_op jit(solution)/shard_map/convert_element_type | solution.py:41
  2.9 0.0 copy-start.1
  2.9 3.0 %collective-permute-start.2 = (bf16[256,1152]{1,0:T(8,128)(2,1)}, bf16[256,1152]{1,0:T(8,128)(2,1)S(1)}, u32[]{:S(2)}, u32[]{:S(2)}) collective-permute-start(bf16[256,1152]{1,0:T(8,128)(2,1)} %convert_element_type.27), channel_id=1, source_target_pairs={{0,2},{1,3},{2,4},{3,5},{4,6},{5,7},{6,8},{7,9},{8,10},{9,11},{10,... | collective-permute-start | bytes 1769480 | tf_op jit(solution)/shard_map/ppermute | solution.py:34
  5.8 2.3 %collective-permute-start.4 = (bf16[256,1152]{1,0:T(8,128)(2,1)}, bf16[256,1152]{1,0:T(8,128)(2,1)}, u32[]{:S(2)}, u32[]{:S(2)}) collective-permute-start(bf16[256,1152]{1,0:T(8,128)(2,1)} %convert_element_type.27), channel_id=1, source_target_pairs={{0,1},{2,3},{4,5},{6,7},{8,9},{10,11},{12,13},{14,15},{16,17},{18,... | collective-permute-start | bytes 1769480 | tf_op jit(solution)/shard_map/ppermute | solution.py:34
  8.1 0.0 copy-done.3
  8.1 0.0 collective-permute-start
  8.1 0.0 copy-done
  8.1 0.5 %collective-permute-start.5 = (bf16[256,1152]{1,0:T(8,128)(2,1)S(1)}, bf16[256,1152]{1,0:T(8,128)(2,1)S(1)}, u32[]{:S(2)}, u32[]{:S(2)}) collective-permute-start(bf16[256,1152]{1,0:T(8,128)(2,1)S(1)} %copy-done), channel_id=1, source_target_pairs={{0,1},{1,0},{2,3},{3,2},{4,5},{5,4},{6,7},{7,6},{8,9},{9,8},{10,11... | collective-permute-start | bytes 1769480 | tf_op jit(solution)/shard_map/ppermute | solution.py:34
  10.0 2.2 %fusion.29 = (f32[256]{0:T(256)}, f32[256,256]{0,1:T(8,128)S(1)}) fusion(f32[]{:T(128)} %bitcast.21, bf16[256,1152]{1,0:T(8,128)(2,1)S(1)} %copy-done, bf16[256,1152]{1,0:T(8,128)(2,1)} %convert_element_type.27, f32[]{:T(128)} %bitcast, s32[256]{0:T(256)S(1)} %copy-done.3), kind=kOutput, calls=%fused_computation.44 | convolution fusion | flops 151846656 | bytes 1443848 | tf_op jit(solution)/shard_map/dot_general | solution.py:11
  12.1 0.0 copy-done.1
  12.1 0.4 convolution_add_fusion.2
  12.5 0.0 collective-permute-done
  12.5 1.5 %collective-permute-start.1 = (s32[512]{0:T(512)S(1)}, s32[512]{0:T(512)S(1)}, u32[]{:S(2)}, u32[]{:S(2)}) collective-permute-start(s32[512]{0:T(512)S(1)} %pad_add_fusion), channel_id=1, source_target_pairs={{0,2},{1,3},{2,4},{3,5},{4,6},{5,7},{6,8},{7,9},{8,10},{9,11},{10,... | collective-permute-start | bytes 6152 | tf_op jit(solution)/shard_map/ppermute | solution.py:34
  14.0 2.5 %fusion.67 = f32[256,1152]{1,0:T(8,128)} fusion(bf16[256,1152]{1,0:T(8,128)(2,1)} %convert_element_type.27, f32[256,256]{0,1:T(8,128)S(1)} %get-tuple-element.8, f32[]{:T(128)} %bitcast, s32[256]{0:T(256)S(1)} %copy-done.3), kind=kOutput, calls=%fused_computation.91 | convolution fusion | flops 151584768 | bytes 2032644 | tf_op jit(solution)/shard_map/dot_general | solution.py:66
  16.6 6.8 %collective-permute-done.1 = s32[512]{0:T(512)S(1)} collective-permute-done((s32[512]{0:T(512)S(1)}, s32[512]{0:T(512)S(1)}, u32[]{:S(2)}, u32[]{:S(2)}) %collective-permute-start.1) | collective-permute-done | bytes 2080 | tf_op jit(solution)/shard_map/ppermute | solution.py:34
  23.4 0.0 collective-permute-done.2
  23.4 1.3 %collective-permute-start.3 = (bf16[256,1152]{1,0:T(8,128)(2,1)S(1)}, bf16[256,1152]{1,0:T(8,128)(2,1)}, u32[]{:S(2)}, u32[]{:S(2)}) collective-permute-start(bf16[256,1152]{1,0:T(8,128)(2,1)S(1)} %collective-permute-done.2), channel_id=1, source_target_pairs={{1,0},{3,2},{5,4},{7,6},{9,8},{11,10},{13,12},{15,14},{17,16},{19,... | collective-permute-start | bytes 1769480 | tf_op jit(solution)/shard_map/ppermute | solution.py:34
  24.7 0.0 collective-permute-done.5
  24.7 2.9 %fusion.1 = bf16[256,1152]{1,0:T(8,128)(2,1)} fusion(f32[256,1152]{1,0:T(8,128)S(1)} %convolution_add_fusion.2, bf16[256,1152]{1,0:T(8,128)(2,1)S(1)} %collective-permute-done.5, bf16[256,1152]{1,0:T(8,128)(2,1)} %convert_element_type.27, s32[256]{0:T(256)S(1)} %collective-permute-done, f32[]{:T(128)} %bitcast.23, f32[]{:T(128)} %bitcast, ...), kind=kOutput, calls=%fused_computation.6 | convolution fusion | flops 303431680 | bytes 2951177 | tf_op jit(solution)/shard_map/dot_general | solution.py:15
  27.6 0.0 collective-permute-start.6
  27.6 0.5 %fusion.31 = (f32[256]{0:T(256)S(1)}, f32[256,256]{0,1:T(8,128)S(1)}) fusion(f32[]{:T(128)} %bitcast.24, bf16[256,1152]{1,0:T(8,128)(2,1)S(1)} %copy-done, bf16[256,1152]{1,0:T(8,128)(2,1)S(1)} %collective-permute-done.2, f32[]{:T(128)} %bitcast, s32[256]{0:T(256)S(1)} %get-tuple-element.4, s32[256]{0:T(256)S(1)} %copy-done.3), kind=kOutput, calls=%fused_computation.46 | convolution fusion | flops 151846656 | bytes 1444872 | tf_op jit(solution)/shard_map/dot_general | solution.py:11
  28.1 0.4 fusion.68
  28.5 0.0 collective-permute-done.4
  28.5 0.0 collective-permute-done.3
  28.5 0.0 copy-start.4
  28.5 0.0 copy-start.2
  28.5 1.7 %fusion.30 = (f32[256]{0:T(256)S(1)}, f32[256,256]{0,1:T(8,128)S(1)}) fusion(f32[]{:T(128)} %bitcast.22, bf16[256,1152]{1,0:T(8,128)(2,1)S(1)} %copy-done, bf16[256,1152]{1,0:T(8,128)(2,1)} %collective-permute-done.3, bf16[256,1152]{1,0:T(8,128)(2,1)} %collective-permute-done.4, pred[]{:T(512)S(6)} %eq.27, f32[]{:T(128)} %bitcast, ...), kind=kOutput, calls=%fused_computation.45 | convolution fusion | flops 152141568 | bytes 2034697 | tf_op jit(solution)/shard_map/dot_general | solution.py:11
  30.3 0.0 copy-done.4
  30.3 0.6 %add_multiply_fusion = f32[256]{0:T(256)} fusion(f32[256]{0:T(256)S(1)} %get-tuple-element.5, f32[256]{0:T(256)S(1)} %copy-done.4, f32[256]{0:T(256)S(1)} %get-tuple-element.9), kind=kLoop, calls=%fused_computation.81 | loop fusion | flops 768 | bytes 4096 | tf_op jit(solution)/shard_map/div | solution.py:71
  30.8 0.0 copy-done.2
  30.8 1.5 %convolution_add_fusion.4 = f32[256,1152]{1,0:T(8,128)S(1)} fusion(f32[256,1152]{1,0:T(8,128)S(1)} %copy-done.2, bf16[256,1152]{1,0:T(8,128)(2,1)} %collective-permute-done.3, bf16[256,1152]{1,0:T(8,128)(2,1)} %collective-permute-done.4, pred[]{:T(512)S(6)} %eq.27, f32[256,256]{0,1:T(8,128)S(1)} %get-tuple-element.10, f32[]{:T(128)} %bitcast, ...), kind=kOutput, calls=%fused_computation.4 | convolution fusion | flops 152174592 | bytes 3803141 | tf_op jit(solution)/shard_map/dot_general | solution.py:67
  32.4 1.3 %fusion = bf16[256,1152]{1,0:T(8,128)(2,1)} fusion(f32[256,1152]{1,0:T(8,128)S(1)} %convolution_add_fusion.4, bf16[256,1152]{1,0:T(8,128)(2,1)S(1)} %collective-permute-done.2, f32[256,256]{0,1:T(8,128)S(1)} %get-tuple-element.6, f32[]{:T(128)} %bitcast, s32[256]{0:T(256)S(1)} %copy-done.3, s32[256]{0:T(256)S(1)} %get-tuple-element.4), kind=kOutput, calls=%fused_computation.5 | convolution fusion | flops 152174592 | bytes 2623492 | tf_op jit(solution)/shard_map/dot_general | solution.py:68
  33.7 12.9 %collective-permute-done.6 = bf16[256,1152]{1,0:T(8,128)(2,1)S(1)} collective-permute-done((bf16[256,1152]{1,0:T(8,128)(2,1)}, bf16[256,1152]{1,0:T(8,128)(2,1)S(1)}, u32[]{:S(2)}, u32[]{:S(2)}) %collective-permute-start.6) | collective-permute-done | bytes 589856 | tf_op jit(solution)/shard_map/ppermute | solution.py:34
  46.6 2.0 %convert_add_fusion = f32[256,1152]{1,0:T(8,128)} fusion(bf16[256,1152]{1,0:T(8,128)(2,1)S(1)} %collective-permute-done.6, f32[256,1152]{1,0:T(8,128)S(1)} %fusion.68, bf16[256,1152]{1,0:T(8,128)(2,1)S(1)} %collective-permute-done.5, bf16[256,1152]{1,0:T(8,128)(2,1)S(1)} %collective-permute-done.2, s32[256]{0:T(256)S(1)} %collective-permute-done, ...), kind=kOutput, calls=%fused_computation.7 | convolution fusion | flops 303726592 | bytes 4130825 | tf_op jit(solution)/shard_map/dot_general | solution.py:15
  (2 shorter events, 0.0 us)
Async XLA Ops:
  0.6 7.5 %copy-start.3 = (s32[256]{0:T(256)S(1)}, s32[256]{0:T(256)}, u32[]{:S(2)}) copy-start(s32[256]{0:T(256)} %param.9) | copy-start | bytes 3076
  0.6 7.5 %copy-start = (bf16[256,1152]{1,0:T(8,128)(2,1)S(1)}, bf16[256,1152]{1,0:T(8,128)(2,1)}, u32[]{:S(2)}) copy-start(bf16[256,1152]{1,0:T(8,128)(2,1)} %param.6) | copy-start | bytes 1769476
  2.9 9.3 %copy-start.1 = (f32[256,1152]{1,0:T(8,128)S(1)}, f32[256,1152]{1,0:T(8,128)}, u32[]{:S(2)}) copy-start(f32[256,1152]{1,0:T(8,128)} %param.8) | copy-start | bytes 3538948
  2.9 20.5 %collective-permute-start.2 = (bf16[256,1152]{1,0:T(8,128)(2,1)}, bf16[256,1152]{1,0:T(8,128)(2,1)S(1)}, u32[]{:S(2)}, u32[]{:S(2)}) collective-permute-start(bf16[256,1152]{1,0:T(8,128)(2,1)} %convert_element_type.27), channel_id=1, source_target_pairs={{0,2},{1,3},{2,4},{3,5},{4,6},{5,7},{6,8},{7,9},{8,10},{9,11},{10,... | collective-permute-start | bytes 1769480 | tf_op jit(solution)/shard_map/ppermute | solution.py:34
  5.8 22.7 %collective-permute-start.4 = (bf16[256,1152]{1,0:T(8,128)(2,1)}, bf16[256,1152]{1,0:T(8,128)(2,1)}, u32[]{:S(2)}, u32[]{:S(2)}) collective-permute-start(bf16[256,1152]{1,0:T(8,128)(2,1)} %convert_element_type.27), channel_id=1, source_target_pairs={{0,1},{2,3},{4,5},{6,7},{8,9},{10,11},{12,13},{14,15},{16,17},{18,... | collective-permute-start | bytes 1769480 | tf_op jit(solution)/shard_map/ppermute | solution.py:34
  8.1 4.4 %collective-permute-start = (s32[256]{0:T(256)S(1)}, s32[256]{0:T(256)S(1)}, u32[]{:S(2)}, u32[]{:S(2)}) collective-permute-start(s32[256]{0:T(256)S(1)} %copy-done.3), channel_id=1, source_target_pairs={{0,1},{1,0},{2,3},{3,2},{4,5},{5,4},{6,7},{7,6},{8,9},{9,8},{10,11... | collective-permute-start | bytes 3080 | tf_op jit(solution)/shard_map/ppermute | solution.py:34
  8.1 16.6 %collective-permute-start.5 = (bf16[256,1152]{1,0:T(8,128)(2,1)S(1)}, bf16[256,1152]{1,0:T(8,128)(2,1)S(1)}, u32[]{:S(2)}, u32[]{:S(2)}) collective-permute-start(bf16[256,1152]{1,0:T(8,128)(2,1)S(1)} %copy-done), channel_id=1, source_target_pairs={{0,1},{1,0},{2,3},{3,2},{4,5},{5,4},{6,7},{7,6},{8,9},{9,8},{10,11... | collective-permute-start | bytes 1769480 | tf_op jit(solution)/shard_map/ppermute | solution.py:34
  12.5 10.8 %collective-permute-start.1 = (s32[512]{0:T(512)S(1)}, s32[512]{0:T(512)S(1)}, u32[]{:S(2)}, u32[]{:S(2)}) collective-permute-start(s32[512]{0:T(512)S(1)} %pad_add_fusion), channel_id=1, source_target_pairs={{0,2},{1,3},{2,4},{3,5},{4,6},{5,7},{6,8},{7,9},{8,10},{9,11},{10,... | collective-permute-start | bytes 6152 | tf_op jit(solution)/shard_map/ppermute | solution.py:34
  23.4 5.1 %collective-permute-start.3 = (bf16[256,1152]{1,0:T(8,128)(2,1)S(1)}, bf16[256,1152]{1,0:T(8,128)(2,1)}, u32[]{:S(2)}, u32[]{:S(2)}) collective-permute-start(bf16[256,1152]{1,0:T(8,128)(2,1)S(1)} %collective-permute-done.2), channel_id=1, source_target_pairs={{1,0},{3,2},{5,4},{7,6},{9,8},{11,10},{13,12},{15,14},{17,16},{19,... | collective-permute-start | bytes 1769480 | tf_op jit(solution)/shard_map/ppermute | solution.py:34
  27.6 19.0 %collective-permute-start.6 = (bf16[256,1152]{1,0:T(8,128)(2,1)}, bf16[256,1152]{1,0:T(8,128)(2,1)S(1)}, u32[]{:S(2)}, u32[]{:S(2)}) collective-permute-start(bf16[256,1152]{1,0:T(8,128)(2,1)} %fusion.1), channel_id=1, source_target_pairs={{0,2},{1,3},{2,4},{3,5},{4,6},{5,7},{6,8},{7,9},{8,10},{9,11},{10,... | collective-permute-start | bytes 1769480 | tf_op jit(solution)/shard_map/ppermute | solution.py:34
  28.5 1.7 %copy-start.4 = (f32[256]{0:T(256)S(1)}, f32[256]{0:T(256)}, u32[]{:S(2)}) copy-start(f32[256]{0:T(256)} %get-tuple-element.7) | copy-start | bytes 3076
  28.5 2.3 %copy-start.2 = (f32[256,1152]{1,0:T(8,128)S(1)}, f32[256,1152]{1,0:T(8,128)}, u32[]{:S(2)}) copy-start(f32[256,1152]{1,0:T(8,128)} %fusion.67) | copy-start | bytes 3538948

commit v2 on v1

v2 whole, which is shorter than its diff:
```python
import jax
import jax.numpy as jnp
from jax import lax
from jax.experimental import pallas as pl
from jax.experimental.pallas import tpu as pltpu
from jax.sharding import PartitionSpec as P

SHIFTS = 2
AXES = ("dp", "group")
PAD = 16
CHUNKS = 4
VMEM = pl.BlockSpec(memory_space=pltpu.VMEM)
SMEM = pl.BlockSpec(memory_space=pltpu.SMEM)
HBM = pl.BlockSpec(memory_space=pltpu.HBM)


def dot(a, b, contract):
    return lax.dot_general(a, b, ((contract[:1], contract[1:]), ((), ())), preferred_element_type=jnp.float32)


def ids_of(text, at, rows):
    parts = text[at:, :rows].astype(jnp.float32).astype(jnp.int32)
    return parts[0:1] + parts[1:2] * 256 + parts[2:3] * 65536 + parts[3:4] * 16777216


def pair(images, texts, image_ids, text_ids, params):
    raw = dot(images, texts, (1, 1))
    rows = raw.shape[0]
    scale = jnp.exp(jnp.full((1, rows), params[0], jnp.float32))
    logits = scale * raw + params[1]
    same = jnp.broadcast_to(image_ids, (rows, rows)).T == text_ids
    margin = jnp.where(same, -logits, logits)
    tail = jnp.exp(-jnp.abs(margin))
    loss = jnp.maximum(margin, 0.0) + jnp.log1p(tail)
    sigmoid = jnp.where(margin >= 0, 1.0, tail) / (1.0 + tail)
    coef = jnp.where(same, -sigmoid, sigmoid) * scale
    return jnp.sum(loss.T, axis=0, keepdims=True), coef


def low(coef):
    return coef.astype(jnp.bfloat16)


def cast_kernel(ids, text, out, staged, sems):
    rows, width = text.shape
    step = rows // CHUNKS
    copies = [
        pltpu.make_async_copy(text.at[pl.ds(k * step, step)], staged.at[pl.ds(k * step, step)], sems.at[k])
        for k in range(CHUNKS)
    ]
    for copy in copies:
        copy.start()
    row = lax.broadcasted_iota(jnp.int32, (PAD, rows), 0)
    spread = jnp.broadcast_to(ids[...], (PAD, rows))
    parts = jnp.zeros((PAD, rows), jnp.int32)
    for k in range(4):
        parts = jnp.where(row == k, (spread >> (8 * k)) & 255, parts)
    out[rows:, :] = jnp.zeros((PAD, width), out.dtype)
    out[rows:, :rows] = parts.astype(jnp.float32).astype(out.dtype)
    for k, copy in enumerate(copies):
        copy.wait()
        out[k * step:(k + 1) * step, :] = staged[k * step:(k + 1) * step, :].astype(out.dtype)


def own_kernel(flags, params, ids, mate_ids, image, mate_a, mate_b, text, accum, out, image_sum, loss):
    rows = image.shape[0]
    own_loss, coef = pair(image[...], text[:rows, :], ids[...], ids[...], params)
    loss[...] = own_loss
    total = accum[...] + dot(low(coef.T), image[...], (1, 0))

    @pl.when(flags[0] == 0)
    def _():
        mate = jnp.concatenate([mate_a[...], mate_b[...]], axis=0)
        _, mate_coef = pair(mate, text[:rows, :], mate_ids[...], ids[...], params)
        out[...] = (total + dot(low(mate_coef.T), mate, (1, 0))).astype(out.dtype)

    @pl.when(flags[0] == 1)
    def _():
        out[...] = total.astype(out.dtype)

    image_sum[...] = dot(low(coef), text[:rows, :], (1, 0))


def relay_kernel(flags, token, text, far, out_a, out_b):
    cut = out_a.shape[0]

    def fill(source):
        out_a[...] = source[:cut, :]
        out_b[...] = source[cut:, :]

    pl.when(flags[0] == 0)(lambda: fill(text))
    pl.when(flags[0] == 1)(lambda: fill(far))


def far_kernel(flags, params, ids, mate_ids, image, mate_a, mate_b, far, image_in, loss_in, late, image_sum, loss):
    rows = image.shape[0]
    far_ids = ids_of(far, rows, rows)
    more, coef = pair(image[...], far[:rows, :], ids[...], far_ids, params)
    loss[...] = loss_in[...] + more
    image_sum[...] = image_in[...] + dot(low(coef), far[:rows, :], (1, 0))
    part = dot(low(coef.T), image[...], (1, 0))

    @pl.when(flags[0] == 0)
    def _():
        late[...] = part

    @pl.when(flags[0] == 1)
    def _():
        mate = jnp.concatenate([mate_a[...], mate_b[...]], axis=0)
        _, mate_coef = pair(mate, far[:rows, :], mate_ids[...], far_ids, params)
        late[...] = part + dot(low(mate_coef.T), mate, (1, 0))


def near_kernel(params, ids, image, near_a, near_b, image_in, loss_in, image_grad, loss):
    rows = image.shape[0]
    rest = rows - near_a.shape[0]
    near = jnp.concatenate([near_a[...], near_b[:rest, :]], axis=0)
    more, coef = pair(image[...], near, ids[...], ids_of(near_b, rest, rows), params)
    loss[...] = (loss_in[...] + more) * (1.0 / ((SHIFTS + 1) * rows))
    image_grad[...] = (image_in[...] + dot(low(coef), near, (1, 0))).astype(image_grad.dtype)


def call(kernel, name, outs, scalars, *operands):
    return pl.pallas_call(
        kernel,
        out_shape=[jax.ShapeDtypeStruct(s, d) for s, d in outs],
        in_specs=[SMEM] * len(scalars) + [VMEM] * len(operands),
        out_specs=[VMEM] * len(outs),
        compiler_params=pltpu.CompilerParams(vmem_limit_bytes=32 * 1024 * 1024),
        cost_estimate=pl.CostEstimate(flops=0, bytes_accessed=0, transcendentals=0),
        name=name,
    )(*scalars, *operands)


def body(image_emb, text_emb, text_accum, pair_ids, log_scale, bias):
    count = lax.axis_size(AXES)
    rows, width = image_emb.shape
    half = rows // 2
    f32, bf16 = jnp.float32, jnp.bfloat16
    flags = (lax.axis_index("group") % 2).astype(jnp.int32).reshape(1)
    params = jnp.concatenate([log_scale, bias])
    ids = pair_ids.reshape(1, rows)

    skip = [(i, (i + 2) % count) for i in range(count)]
    swap = [(i, i ^ 1) for i in range(count)]

    def ahead(value):
        return lax.ppermute(value, AXES, skip)

    def across(value):
        return lax.ppermute(value, AXES, swap)

    text = pl.pallas_call(
        cast_kernel,
        out_shape=jax.ShapeDtypeStruct((rows + PAD, width), bf16),
        in_specs=[VMEM, HBM],
        out_specs=VMEM,
        scratch_shapes=[pltpu.VMEM((rows, width), f32), pltpu.SemaphoreType.DMA((CHUNKS,))],
        cost_estimate=pl.CostEstimate(flops=0, bytes_accessed=0, transcendentals=0),
        name="cast",
    )(ids, text_emb)
    far = ahead(text)

    image, text = lax.optimization_barrier((image_emb, text))
    mate_a, mate_b = across(image[:half]), across(image[half:])
    mate_ids = across(ids)

    outgoing, image_sum, loss = call(
        own_kernel, "own", [((rows, width), bf16), ((rows, width), f32), ((1, rows), f32)],
        (flags, params), ids, mate_ids, image_emb, mate_a, mate_b, text, text_accum,
    )
    arrived = ahead(outgoing)

    passed_a, passed_b = call(
        relay_kernel, "relay", [((half, width), bf16), ((rows + PAD - half, width), bf16)],
        (flags,), loss, text, far,
    )
    near_a, near_b = across(passed_a), across(passed_b)
    late, image_sum, loss = call(
        far_kernel, "far", [((rows, width), f32), ((rows, width), f32), ((1, rows), f32)],
        (flags, params), ids, mate_ids, image_emb, mate_a, mate_b, far, image_sum, loss,
    )
    image_grad, loss = call(
        near_kernel, "near", [((rows, width), bf16), ((1, rows), f32)],
        (params,), ids, image_emb, near_a, near_b, image_sum, loss,
    )
    late, image_grad = lax.optimization_barrier((late, image_grad))
    text_grad = arrived.astype(f32) + late
    return (loss.reshape(rows), image_grad, text_grad)


def solution(mesh):
    in_specs = (P(AXES, None), P(AXES, None), P(AXES, None), P(AXES), P(), P())
    out_specs = (P(AXES), P(AXES, None), P(AXES, None))
    return jax.shard_map(body, mesh=mesh, in_specs=in_specs, out_specs=out_specs, check_vma=False)
```

time: 49.3 us -> 38.8 us (0.79); the launches traced: 48.6 us -> 38.6 us
  matrix products: 15.4 us -> 0 us
  Pallas kernels: 0 us -> 10.3 us
  starting transfers between devices: 8.52 us -> 5.72 us
  waiting for transfers between devices: 19.8 us -> 18.1 us
  other arithmetic: 2.79 us -> 1.22 us
  local copies, waits for them, and re-layouts: 0.02 us -> 1.33 us
    dot_general x10 -> x0, matrix products: 15.4 us -> none  [the longest x4 5.64 us: back(): lax.dot_general(coef, images, (((0,), (0,)), ((), ())), preferred_element...]
    pallas_call x0 -> x5, Pallas kernels: none -> 10.3 us  [the longest x4 7.42 us: call(): pl.pallas_call(kernel, out_shape=[jax.ShapeDtypeStruct(s, d) for s, d in...]
    ppermute x7, starting transfers between devices: 8.52 us -> 5.72 us  [the longest x2 4.51 us: ahead(): return lax.ppermute(value, AXES, skip)]
    convert_element_type x1 -> x0, other arithmetic: 2.21 us -> none  [body(): texts = text_emb.astype(jnp.bfloat16)]
    ppermute x7, waiting for transfers between devices: 19.8 us -> 18.1 us  [the longest x2 18 us: ahead(): return lax.ppermute(value, AXES, skip)]
    unnamed x10 -> x8, local copies, waits for them, and re-layouts: 0.02 us -> 1.28 us
    add x0 -> x1, other arithmetic: none -> 1.15 us  [body(): text_grad = arrived.astype(f32) + late]
    div x1 -> x0, other arithmetic: 0.57 us -> none  [body(): loss / ((SHIFTS + 1) * rows)]
  transfers between devices with their start and end apart: 7 -> 7, of which waited for: 2 -> 2; matrix products, arithmetic and copies ran while one was open for 29% -> 0% of each run, Pallas kernels for 0% -> 19%
where the time goes in v2:
time: 38.8 us; the launch traced here: 38.6 us
  waiting for transfers between devices  18.1 us (47%)
  Pallas kernels  10.3 us (27%)
  starting transfers between devices  5.72 us (15%)
  between operations  2.04 us (5%)
  local copies, waits for them, and re-layouts  1.33 us (3%)
  other arithmetic  1.22 us (3%)
    ppermute x2, waiting for transfers between devices, ahead(): return lax.ppermute(value, AXES, skip)  18 us
    pallas_call x4, Pallas kernels, call(): pl.pallas_call(kernel, out_shape=[jax.ShapeDtypeStruct(s, d) for s, d in...  7.42 us
    ppermute x2, starting transfers between devices, ahead(): return lax.ppermute(value, AXES, skip)  4.51 us
    pallas_call x1, Pallas kernels, body(): pl.pallas_call(cast_kernel, out_shape=jax.ShapeDtypeStruct((rows + PAD, w...  2.85 us
    unnamed x8, local copies, waits for them, and re-layouts  1.28 us
    ppermute x5, starting transfers between devices, across(): return lax.ppermute(value, AXES, swap)  1.21 us
    add x1, other arithmetic, body(): text_grad = arrived.astype(f32) + late  1.15 us
  transfers between devices with their start and end apart: 7, of which 2 were waited for; matrix products, arithmetic and copies ran while one was open for 0% of the time, Pallas kernels for 19%

profile of v2, /device:TPU:0, one launch (start us, length us, event | category | flops | bytes accessed | tf_op | source)
XLA Modules:
  0.0 38.6 jit_solution(10210199679986715466)
XLA Ops:
  0.6 0.0 copy-start
  0.6 0.0 copy-start.3
  0.7 2.8 %cast.1.text = bf16[272,1152]{1,0:T(8,128)(2,1)} custom-call(s32[1,256]{1,0:T(1,128)} %bitcast.3, f32[256,1152]{1,0:T(8,128)} %text.1), custom_call_target="tpu_custom_call" | custom-call | tf_op jit(solution)/shard_map/cast/pallas_call | solution.py:153
  3.5 0.0 copy-start.1
  3.5 3.0 %collective-permute-start.3 = (bf16[272,1152]{1,0:T(8,128)(2,1)}, bf16[272,1152]{1,0:T(8,128)(2,1)S(1)}, u32[]{:S(2)}, u32[]{:S(2)}) collective-permute-start(bf16[272,1152]{1,0:T(8,128)(2,1)} %cast.1.text), channel_id=1, source_target_pairs={{0,2},{1,3},{2,4},{3,5},{4,6},{5,7},{6,8},{7,9},{8,10},{9,11},{10,... | collective-permute-start | bytes 1880072 | tf_op jit(solution)/shard_map/ppermute | solution.py:148
  6.5 0.0 copy-done
  6.6 0.1 collective-permute-start.2
  6.7 0.5 %collective-permute-start.1 = (bf16[128,1152]{1,0:T(8,128)(2,1)S(1)}, bf16[128,1152]{1,0:T(8,128)(2,1)S(1)}, u32[]{:S(2)}, u32[]{:S(2)}) collective-permute-start(bf16[128,1152]{1,0:T(8,128)(2,1)S(1)} %get-tuple-element.32), channel_id=1, source_target_pairs={{0,1},{1,0},{2,3},{3,2},{4,5},{5,4},{6,7},{7,6},{8,9},{9,8},{10,11... | collective-permute-start | bytes 884744 | tf_op jit(solution)/shard_map/ppermute | solution.py:151
  7.2 0.0 copy-done.3
  7.2 0.1 collective-permute-start
  8.5 0.1 pad_maximum_fusion.params
  8.6 0.0 collective-permute-done.mate_ids
  8.7 0.0 collective-permute-done.2.mate_b
  8.7 0.0 collective-permute-done.1.mate_a
  8.7 0.0 copy-done.1
  8.7 0.0 copy-start.2
  8.7 1.3 %copy-done.2 = f32[256,1152]{1,0:T(8,128)S(1)} copy-done((f32[256,1152]{1,0:T(8,128)S(1)}, f32[256,1152]{1,0:T(8,128)}, u32[]{:S(2)}) %copy-start.2) | copy-done | bytes 1179672
  9.9 3.1 %own.1 = (bf16[256,1152]{1,0:T(8,128)(2,1)S(1)}, f32[256,1152]{1,0:T(8,128)S(1)}, f32[1,256]{1,0:T(1,128)S(1)}) custom-call(s32[1]{0:T(128)} %bitcast.1.flags, f32[2]{0:T(128)S(1)} %pad_maximum_fusion.params, s32[1,256]{1,0:T(1,128)S(1)} %bitcast.5, s32[1,256]{1,0:T(1,128)S(1)} %collective-permute-done.mate_ids, bf16[256,1152]{1,0:T(8,128)(2,1)S(1)} %copy-done, ...), custom_call_target="tpu_custom_call" | custom-call | tf_op jit(solution)/shard_map/own/pallas_call | solution.py:124
  13.1 1.5 %collective-permute-start.6 = (bf16[256,1152]{1,0:T(8,128)(2,1)S(1)}, bf16[256,1152]{1,0:T(8,128)(2,1)S(1)}, u32[]{:S(2)}, u32[]{:S(2)}) collective-permute-start(bf16[256,1152]{1,0:T(8,128)(2,1)S(1)} %get-tuple-element.29), channel_id=1, source_target_pairs={{0,2},{1,3},{2,4},{3,5},{4,6},{5,7},{6,8},{7,9},{8,10},{9,11},{10,... | collective-permute-start | bytes 1769480 | tf_op jit(solution)/shard_map/ppermute | solution.py:148
  14.6 11.1 %collective-permute-done.3.far = bf16[272,1152]{1,0:T(8,128)(2,1)S(1)} collective-permute-done((bf16[272,1152]{1,0:T(8,128)(2,1)}, bf16[272,1152]{1,0:T(8,128)(2,1)S(1)}, u32[]{:S(2)}, u32[]{:S(2)}) %collective-permute-start.3) | collective-permute-done | bytes 626720 | tf_op jit(solution)/shard_map/ppermute | solution.py:148
  25.7 0.1 relay.1
  25.7 0.1 collective-permute-start.5
  25.8 0.5 %collective-permute-start.4 = (bf16[128,1152]{1,0:T(8,128)(2,1)S(1)}, bf16[128,1152]{1,0:T(8,128)(2,1)S(1)}, u32[]{:S(2)}, u32[]{:S(2)}) collective-permute-start(bf16[128,1152]{1,0:T(8,128)(2,1)S(1)} %get-tuple-element.20), channel_id=1, source_target_pairs={{0,1},{1,0},{2,3},{3,2},{4,5},{5,4},{6,7},{7,6},{8,9},{9,8},{10,11... | collective-permute-start | bytes 884744 | tf_op jit(solution)/shard_map/ppermute | solution.py:151
  26.3 1.8 %far.1 = (f32[256,1152]{1,0:T(8,128)S(1)}, f32[256,1152]{1,0:T(8,128)S(1)}, f32[1,256]{1,0:T(1,128)S(1)}) custom-call(s32[1]{0:T(128)} %bitcast.1.flags, f32[2]{0:T(128)S(1)} %pad_maximum_fusion.params, s32[1,256]{1,0:T(1,128)S(1)} %bitcast.6, s32[1,256]{1,0:T(1,128)S(1)} %collective-permute-done.mate_ids, bf16[256,1152]{1,0:T(8,128)(2,1)S(1)} %copy-done, ...), custom_call_target="tpu_custom_call" | custom-call | tf_op jit(solution)/shard_map/far/pallas_call | solution.py:124
  28.1 0.0 collective-permute-done.4.near_a
  28.2 0.0 collective-permute-done.5.near_b
  28.2 2.4 %near.1 = (bf16[256,1152]{1,0:T(8,128)(2,1)}, f32[1,256]{1,0:T(1,128)}) custom-call(f32[2]{0:T(128)S(1)} %pad_maximum_fusion.params, s32[1,256]{1,0:T(1,128)S(1)} %bitcast.7, bf16[256,1152]{1,0:T(8,128)(2,1)S(1)} %copy-done, bf16[128,1152]{1,0:T(8,128)(2,1)S(1)} %collective-permute-done.4.near_a, bf16[144,1152]{1,0:T(8,128)(2,1)S(1)} %collective-permute-done.5.near_b, ...), custom_call_target="tpu_custom_call" | custom-call | tf_op jit(solution)/shard_map/near/pallas_call | solution.py:124
  30.6 6.9 %collective-permute-done.6 = bf16[256,1152]{1,0:T(8,128)(2,1)S(1)} collective-permute-done((bf16[256,1152]{1,0:T(8,128)(2,1)S(1)}, bf16[256,1152]{1,0:T(8,128)(2,1)S(1)}, u32[]{:S(2)}, u32[]{:S(2)}) %collective-permute-start.6) | collective-permute-done | bytes 589856 | tf_op jit(solution)/shard_map/ppermute | solution.py:148
  37.5 1.1 %convert_add_fusion = f32[256,1152]{1,0:T(8,128)} fusion(f32[256,1152]{1,0:T(8,128)S(1)} %get-tuple-element.30, bf16[256,1152]{1,0:T(8,128)(2,1)S(1)} %collective-permute-done.6), kind=kLoop, calls=%fused_computation | loop fusion | flops 589824 | bytes 2949120 | tf_op jit(solution)/shard_map/add | solution.py:188
  (1 shorter events, 0.0 us)
Async XLA Ops:
  0.6 5.9 %copy-start = (bf16[256,1152]{1,0:T(8,128)(2,1)S(1)}, bf16[256,1152]{1,0:T(8,128)(2,1)}, u32[]{:S(2)}) copy-start(bf16[256,1152]{1,0:T(8,128)(2,1)} %image.5) | copy-start | bytes 1769476
  0.6 6.5 %copy-start.3 = (s32[256]{0:T(256)S(1)}, s32[256]{0:T(256)}, u32[]{:S(2)}) copy-start(s32[256]{0:T(256)} %param.9) | copy-start | bytes 3076
  3.5 5.2 %copy-start.1 = (bf16[272,1152]{1,0:T(8,128)(2,1)S(1)}, bf16[272,1152]{1,0:T(8,128)(2,1)}, u32[]{:S(2)}) copy-start(bf16[272,1152]{1,0:T(8,128)(2,1)} %cast.1.text) | copy-start | bytes 1880068
  3.5 22.1 %collective-permute-start.3 = (bf16[272,1152]{1,0:T(8,128)(2,1)}, bf16[272,1152]{1,0:T(8,128)(2,1)S(1)}, u32[]{:S(2)}, u32[]{:S(2)}) collective-permute-start(bf16[272,1152]{1,0:T(8,128)(2,1)} %cast.1.text), channel_id=1, source_target_pairs={{0,2},{1,3},{2,4},{3,5},{4,6},{5,7},{6,8},{7,9},{8,10},{9,11},{10,... | collective-permute-start | bytes 1880072 | tf_op jit(solution)/shard_map/ppermute | solution.py:148
  6.6 2.1 %collective-permute-start.2 = (bf16[128,1152]{1,0:T(8,128)(2,1)S(1)}, bf16[128,1152]{1,0:T(8,128)(2,1)S(1)}, u32[]{:S(2)}, u32[]{:S(2)}) collective-permute-start(bf16[128,1152]{1,0:T(8,128)(2,1)S(1)} %get-tuple-element.31), channel_id=1, source_target_pairs={{0,1},{1,0},{2,3},{3,2},{4,5},{5,4},{6,7},{7,6},{8,9},{9,8},{10,11... | collective-permute-start | bytes 884744 | tf_op jit(solution)/shard_map/ppermute | solution.py:151
  6.7 2.0 %collective-permute-start.1 = (bf16[128,1152]{1,0:T(8,128)(2,1)S(1)}, bf16[128,1152]{1,0:T(8,128)(2,1)S(1)}, u32[]{:S(2)}, u32[]{:S(2)}) collective-permute-start(bf16[128,1152]{1,0:T(8,128)(2,1)S(1)} %get-tuple-element.32), channel_id=1, source_target_pairs={{0,1},{1,0},{2,3},{3,2},{4,5},{5,4},{6,7},{7,6},{8,9},{9,8},{10,11... | collective-permute-start | bytes 884744 | tf_op jit(solution)/shard_map/ppermute | solution.py:151
  7.2 1.5 %collective-permute-start = (s32[1,256]{1,0:T(1,128)S(1)}, s32[1,256]{1,0:T(1,128)S(1)}, u32[]{:S(2)}, u32[]{:S(2)}) collective-permute-start(s32[1,256]{1,0:T(1,128)S(1)} %bitcast.4), channel_id=1, source_target_pairs={{0,1},{1,0},{2,3},{3,2},{4,5},{5,4},{6,7},{7,6},{8,9},{9,8},{10,11... | collective-permute-start | bytes 3080 | tf_op jit(solution)/shard_map/ppermute | solution.py:151
  8.7 1.3 %copy-start.2 = (f32[256,1152]{1,0:T(8,128)S(1)}, f32[256,1152]{1,0:T(8,128)}, u32[]{:S(2)}) copy-start(f32[256,1152]{1,0:T(8,128)} %accum.1) | copy-start | bytes 3538948
  13.1 24.4 %collective-permute-start.6 = (bf16[256,1152]{1,0:T(8,128)(2,1)S(1)}, bf16[256,1152]{1,0:T(8,128)(2,1)S(1)}, u32[]{:S(2)}, u32[]{:S(2)}) collective-permute-start(bf16[256,1152]{1,0:T(8,128)(2,1)S(1)} %get-tuple-element.29), channel_id=1, source_target_pairs={{0,2},{1,3},{2,4},{3,5},{4,6},{5,7},{6,8},{7,9},{8,10},{9,11},{10,... | collective-permute-start | bytes 1769480 | tf_op jit(solution)/shard_map/ppermute | solution.py:148
  25.7 2.4 %collective-permute-start.5 = (bf16[144,1152]{1,0:T(8,128)(2,1)S(1)}, bf16[144,1152]{1,0:T(8,128)(2,1)S(1)}, u32[]{:S(2)}, u32[]{:S(2)}) collective-permute-start(bf16[144,1152]{1,0:T(8,128)(2,1)S(1)} %get-tuple-element.21), channel_id=1, source_target_pairs={{0,1},{1,0},{2,3},{3,2},{4,5},{5,4},{6,7},{7,6},{8,9},{9,8},{10,11... | collective-permute-start | bytes 995336 | tf_op jit(solution)/shard_map/ppermute | solution.py:151
  25.8 2.3 %collective-permute-start.4 = (bf16[128,1152]{1,0:T(8,128)(2,1)S(1)}, bf16[128,1152]{1,0:T(8,128)(2,1)S(1)}, u32[]{:S(2)}, u32[]{:S(2)}) collective-permute-start(bf16[128,1152]{1,0:T(8,128)(2,1)S(1)} %get-tuple-element.20), channel_id=1, source_target_pairs={{0,1},{1,0},{2,3},{3,2},{4,5},{5,4},{6,7},{7,6},{8,9},{9,8},{10,11... | collective-permute-start | bytes 884744 | tf_op jit(solution)/shard_map/ppermute | solution.py:151

commit v3 on v2

--- a/solution.py
+++ b/solution.py
@@ -41,25 +41,41 @@
     return coef.astype(jnp.bfloat16)
 
 
-def cast_kernel(ids, text, out, staged, sems):
+def cast_kernel(ids, text, out, staged, ids_in, sems, ids_sem):
     rows, width = text.shape
     step = rows // CHUNKS
+    ids_copy = pltpu.make_async_copy(ids, ids_in, ids_sem)
     copies = [
         pltpu.make_async_copy(text.at[pl.ds(k * step, step)], staged.at[pl.ds(k * step, step)], sems.at[k])
         for k in range(CHUNKS)
     ]
     for copy in copies:
         copy.start()
+    ids_copy.start()
+    out[rows:, :] = jnp.zeros((PAD, width), out.dtype)
+    for k, copy in enumerate(copies):
+        copy.wait()
+        out[k * step:(k + 1) * step, :] = staged[k * step:(k + 1) * step, :].astype(out.dtype)
+    ids_copy.wait()
     row = lax.broadcasted_iota(jnp.int32, (PAD, rows), 0)
-    spread = jnp.broadcast_to(ids[...], (PAD, rows))
+    spread = jnp.broadcast_to(ids_in[...], (PAD, rows))
     parts = jnp.zeros((PAD, rows), jnp.int32)
     for k in range(4):
         parts = jnp.where(row == k, (spread >> (8 * k)) & 255, parts)
-    out[rows:, :] = jnp.zeros((PAD, width), out.dtype)
     out[rows:, :rows] = parts.astype(jnp.float32).astype(out.dtype)
-    for k, copy in enumerate(copies):
+
+
+def add_kernel(arrived, late, out, staged, sems):
+    rows = arrived.shape[0]
+    step = rows // CHUNKS
+    copies = []
+    for k in range(CHUNKS):
+        part = pl.ds(k * step, step)
+        staged[part, :] = arrived[part, :].astype(staged.dtype) + late[part, :]
+        copies.append(pltpu.make_async_copy(staged.at[part], out.at[part], sems.at[k]))
+        copies[-1].start()
+    for copy in copies:
         copy.wait()
-        out[k * step:(k + 1) * step, :] = staged[k * step:(k + 1) * step, :].astype(out.dtype)
 
 
 def own_kernel(flags, params, ids, mate_ids, image, mate_a, mate_b, text, accum, out, image_sum, loss):
@@ -126,7 +142,7 @@
         out_shape=[jax.ShapeDtypeStruct(s, d) for s, d in outs],
         in_specs=[SMEM] * len(scalars) + [VMEM] * len(operands),
         out_specs=[VMEM] * len(outs),
-        compiler_params=pltpu.CompilerParams(vmem_limit_bytes=32 * 1024 * 1024),
+        compiler_params=pltpu.CompilerParams(vmem_limit_bytes=16 * 1024 * 1024),
         cost_estimate=pl.CostEstimate(flops=0, bytes_accessed=0, transcendentals=0),
         name=name,
     )(*scalars, *operands)
@@ -153,9 +169,15 @@
     text = pl.pallas_call(
         cast_kernel,
         out_shape=jax.ShapeDtypeStruct((rows + PAD, width), bf16),
-        in_specs=[VMEM, HBM],
+        in_specs=[HBM, HBM],
         out_specs=VMEM,
-        scratch_shapes=[pltpu.VMEM((rows, width), f32), pltpu.SemaphoreType.DMA((CHUNKS,))],
+        scratch_shapes=[
+            pltpu.VMEM((rows, width), f32),
+            pltpu.VMEM((1, rows), jnp.int32),
+            pltpu.SemaphoreType.DMA((CHUNKS,)),
+            pltpu.SemaphoreType.DMA,
+        ],
+        compiler_params=pltpu.CompilerParams(vmem_limit_bytes=16 * 1024 * 1024),
         cost_estimate=pl.CostEstimate(flops=0, bytes_accessed=0, transcendentals=0),
         name="cast",
     )(ids, text_emb)
@@ -185,7 +207,16 @@
         (params,), ids, image_emb, near_a, near_b, image_sum, loss,
     )
     late, image_grad = lax.optimization_barrier((late, image_grad))
-    text_grad = arrived.astype(f32) + late
+    text_grad = pl.pallas_call(
+        add_kernel,
+        out_shape=jax.ShapeDtypeStruct((rows, width), f32),
+        in_specs=[VMEM, VMEM],
+        out_specs=HBM,
+        scratch_shapes=[pltpu.VMEM((rows, width), f32), pltpu.SemaphoreType.DMA((CHUNKS,))],
+        compiler_params=pltpu.CompilerParams(vmem_limit_bytes=16 * 1024 * 1024),
+        cost_estimate=pl.CostEstimate(flops=0, bytes_accessed=0, transcendentals=0),
+        name="add",
+    )(arrived, late)
     return (loss.reshape(rows), image_grad, text_grad)
 
 

time: 38.8 us -> 38 us (0.979)
  local copies, waits for them, and re-layouts: 1.33 us -> 2.64 us
  other arithmetic: 1.22 us -> 0.08 us
  waiting for transfers between devices: 18.1 us -> 17.4 us
  Pallas kernels: 10.3 us -> 9.91 us
    pallas_call x1, Pallas kernels: 2.85 us -> 0.96 us  [body(): pl.pallas_call(cast_kernel, out_shape=jax.ShapeDtypeStruct((rows + PAD, w...]
    unnamed x8 -> x6, local copies, waits for them, and re-layouts: 1.28 us -> 2.6 us
    add x1 -> x0, other arithmetic: 1.15 us -> none  [body(): text_grad = arrived.astype(f32) + late]
    pallas_call x0 -> x1, Pallas kernels: none -> 1.06 us  [body(): pl.pallas_call(add_kernel, out_shape=jax.ShapeDtypeStruct((rows, width),...]
    ppermute x2, waiting for transfers between devices: 18 us -> 17.1 us  [ahead(): return lax.ppermute(value, AXES, skip)]
    pallas_call x4, Pallas kernels: 7.42 us -> 7.88 us  [call(): pl.pallas_call(kernel, out_shape=[jax.ShapeDtypeStruct(s, d) for s, d in...]
  transfers between devices with their start and end apart: 7 -> 7, of which waited for: 2 -> 3; matrix products, arithmetic and copies ran while one was open for 0% -> 0% of each run, Pallas kernels for 19% -> 21%
where the time goes in v3:
time: 38 us; the launch traced here: 37.8 us
  waiting for transfers between devices  17.4 us (46%)
  Pallas kernels  9.91 us (26%)
  starting transfers between devices  5.72 us (15%)
  local copies, waits for them, and re-layouts  2.64 us (7%)
  between operations  2.02 us (5%)
    ppermute x2, waiting for transfers between devices, ahead(): return lax.ppermute(value, AXES, skip)  17.1 us
    pallas_call x4, Pallas kernels, call(): pl.pallas_call(kernel, out_shape=[jax.ShapeDtypeStruct(s, d) for s, d in...  7.88 us
    ppermute x2, starting transfers between devices, ahead(): return lax.ppermute(value, AXES, skip)  4.51 us
    unnamed x6, local copies, waits for them, and re-layouts  2.6 us
    ppermute x5, starting transfers between devices, across(): return lax.ppermute(value, AXES, swap)  1.21 us
    pallas_call x1, Pallas kernels, body(): pl.pallas_call(add_kernel, out_shape=jax.ShapeDtypeStruct((rows, width),...  1.06 us
    pallas_call x1, Pallas kernels, body(): pl.pallas_call(cast_kernel, out_shape=jax.ShapeDtypeStruct((rows + PAD, w...  0.96 us
  transfers between devices with their start and end apart: 7, of which 3 were waited for; matrix products, arithmetic and copies ran while one was open for 0% of the time, Pallas kernels for 21%

profile of v3, /device:TPU:0, one launch (start us, length us, event | category | flops | bytes accessed | tf_op | source)
XLA Modules:
  0.0 37.8 jit_solution(17185036151093787869)
XLA Ops:
  0.6 0.0 copy-start
  0.6 0.0 copy-start.1
  0.6 1.3 %copy-done.1 = f32[256,1152]{1,0:T(8,128)S(1)} copy-done((f32[256,1152]{1,0:T(8,128)S(1)}, f32[256,1152]{1,0:T(8,128)}, u32[]{:S(2)}) %copy-start.1) | copy-done | bytes 1179672
  2.0 1.0 %cast.1.text = bf16[272,1152]{1,0:T(8,128)(2,1)S(1)} custom-call(s32[1,256]{1,0:T(1,128)} %bitcast.ids, f32[256,1152]{1,0:T(8,128)S(1)} %copy-done.1), custom_call_target="tpu_custom_call" | custom-call | tf_op jit(solution)/shard_map/cast/pallas_call | solution.py:169
  2.9 3.0 %collective-permute-start.3 = (bf16[272,1152]{1,0:T(8,128)(2,1)S(1)}, bf16[272,1152]{1,0:T(8,128)(2,1)S(1)}, u32[]{:S(2)}, u32[]{:S(2)}) collective-permute-start(bf16[272,1152]{1,0:T(8,128)(2,1)S(1)} %cast.1.text), channel_id=1, source_target_pairs={{0,2},{1,3},{2,4},{3,5},{4,6},{5,7},{6,8},{7,9},{8,10},{9,11},{10,... | collective-permute-start | bytes 1880072 | tf_op jit(solution)/shard_map/ppermute | solution.py:164
  6.0 0.0 copy-done
  6.0 0.1 collective-permute-start.2
  6.1 0.5 %collective-permute-start.1 = (bf16[128,1152]{1,0:T(8,128)(2,1)S(1)}, bf16[128,1152]{1,0:T(8,128)(2,1)S(1)}, u32[]{:S(2)}, u32[]{:S(2)}) collective-permute-start(bf16[128,1152]{1,0:T(8,128)(2,1)S(1)} %get-tuple-element.32), channel_id=1, source_target_pairs={{0,1},{1,0},{2,3},{3,2},{4,5},{5,4},{6,7},{7,6},{8,9},{9,8},{10,11... | collective-permute-start | bytes 884744 | tf_op jit(solution)/shard_map/ppermute | solution.py:167
  6.6 0.1 collective-permute-start
  8.0 0.1 pad_maximum_fusion.params
  8.0 0.2 collective-permute-done.mate_ids
  8.3 0.0 collective-permute-done.2.mate_b
  8.3 0.0 collective-permute-done.1.mate_a
  8.3 0.0 copy-start.2
  8.3 1.3 %copy-done.2 = f32[256,1152]{1,0:T(8,128)S(1)} copy-done((f32[256,1152]{1,0:T(8,128)S(1)}, f32[256,1152]{1,0:T(8,128)}, u32[]{:S(2)}) %copy-start.2) | copy-done | bytes 1179672
  9.6 3.3 %own.1 = (bf16[256,1152]{1,0:T(8,128)(2,1)S(1)}, f32[256,1152]{1,0:T(8,128)S(1)}, f32[1,256]{1,0:T(1,128)S(1)}) custom-call(s32[1]{0:T(128)} %bitcast.1.flags, f32[2]{0:T(128)S(1)} %pad_maximum_fusion.params, s32[1,256]{1,0:T(1,128)} %bitcast.ids, s32[1,256]{1,0:T(1,128)S(1)} %collective-permute-done.mate_ids, bf16[256,1152]{1,0:T(8,128)(2,1)S(1)} %copy-done, ...), custom_call_target="tpu_custom_call" | custom-call | tf_op jit(solution)/shard_map/own/pallas_call | solution.py:140
  12.8 1.5 %collective-permute-start.6 = (bf16[256,1152]{1,0:T(8,128)(2,1)S(1)}, bf16[256,1152]{1,0:T(8,128)(2,1)S(1)}, u32[]{:S(2)}, u32[]{:S(2)}) collective-permute-start(bf16[256,1152]{1,0:T(8,128)(2,1)S(1)} %get-tuple-element.29), channel_id=1, source_target_pairs={{0,2},{1,3},{2,4},{3,5},{4,6},{5,7},{6,8},{7,9},{8,10},{9,11},{10,... | collective-permute-start | bytes 1769480 | tf_op jit(solution)/shard_map/ppermute | solution.py:164
  14.3 10.6 %collective-permute-done.3.far = bf16[272,1152]{1,0:T(8,128)(2,1)S(1)} collective-permute-done((bf16[272,1152]{1,0:T(8,128)(2,1)S(1)}, bf16[272,1152]{1,0:T(8,128)(2,1)S(1)}, u32[]{:S(2)}, u32[]{:S(2)}) %collective-permute-start.3) | collective-permute-done | bytes 626720 | tf_op jit(solution)/shard_map/ppermute | solution.py:164
  24.9 0.1 relay.1
  24.9 0.1 collective-permute-start.5
  25.0 0.5 %collective-permute-start.4 = (bf16[128,1152]{1,0:T(8,128)(2,1)S(1)}, bf16[128,1152]{1,0:T(8,128)(2,1)S(1)}, u32[]{:S(2)}, u32[]{:S(2)}) collective-permute-start(bf16[128,1152]{1,0:T(8,128)(2,1)S(1)} %get-tuple-element.20), channel_id=1, source_target_pairs={{0,1},{1,0},{2,3},{3,2},{4,5},{5,4},{6,7},{7,6},{8,9},{9,8},{10,11... | collective-permute-start | bytes 884744 | tf_op jit(solution)/shard_map/ppermute | solution.py:167
  25.5 2.0 %far.1 = (f32[256,1152]{1,0:T(8,128)S(1)}, f32[256,1152]{1,0:T(8,128)S(1)}, f32[1,256]{1,0:T(1,128)S(1)}) custom-call(s32[1]{0:T(128)} %bitcast.1.flags, f32[2]{0:T(128)S(1)} %pad_maximum_fusion.params, s32[1,256]{1,0:T(1,128)} %bitcast.ids, s32[1,256]{1,0:T(1,128)S(1)} %collective-permute-done.mate_ids, bf16[256,1152]{1,0:T(8,128)(2,1)S(1)} %copy-done, ...), custom_call_target="tpu_custom_call" | custom-call | tf_op jit(solution)/shard_map/far/pallas_call | solution.py:140
  27.5 0.0 collective-permute-done.4.near_a
  27.5 0.0 collective-permute-done.5.near_b
  27.5 2.6 %near.1 = (bf16[256,1152]{1,0:T(8,128)(2,1)}, f32[1,256]{1,0:T(1,128)}) custom-call(f32[2]{0:T(128)S(1)} %pad_maximum_fusion.params, s32[1,256]{1,0:T(1,128)} %bitcast.ids, bf16[256,1152]{1,0:T(8,128)(2,1)S(1)} %copy-done, bf16[128,1152]{1,0:T(8,128)(2,1)S(1)} %collective-permute-done.4.near_a, bf16[144,1152]{1,0:T(8,128)(2,1)S(1)} %collective-permute-done.5.near_b, ...), custom_call_target="tpu_custom_call" | custom-call | tf_op jit(solution)/shard_map/near/pallas_call | solution.py:140
  30.1 6.6 %collective-permute-done.6.arrived = bf16[256,1152]{1,0:T(8,128)(2,1)S(1)} collective-permute-done((bf16[256,1152]{1,0:T(8,128)(2,1)S(1)}, bf16[256,1152]{1,0:T(8,128)(2,1)S(1)}, u32[]{:S(2)}, u32[]{:S(2)}) %collective-permute-start.6) | collective-permute-done | bytes 589856 | tf_op jit(solution)/shard_map/ppermute | solution.py:164
  36.7 1.1 %add.6 = f32[256,1152]{1,0:T(8,128)} custom-call(bf16[256,1152]{1,0:T(8,128)(2,1)S(1)} %collective-permute-done.6.arrived, f32[256,1152]{1,0:T(8,128)S(1)} %get-tuple-element.30.late), custom_call_target="tpu_custom_call" | custom-call | tf_op jit(solution)/shard_map/add/pallas_call | solution.py:210
  (1 shorter events, 0.0 us)
Async XLA Ops:
  0.6 5.3 %copy-start = (bf16[256,1152]{1,0:T(8,128)(2,1)S(1)}, bf16[256,1152]{1,0:T(8,128)(2,1)}, u32[]{:S(2)}) copy-start(bf16[256,1152]{1,0:T(8,128)(2,1)} %image.5) | copy-start | bytes 1769476
  0.6 1.3 %copy-start.1 = (f32[256,1152]{1,0:T(8,128)S(1)}, f32[256,1152]{1,0:T(8,128)}, u32[]{:S(2)}) copy-start(f32[256,1152]{1,0:T(8,128)} %text.1) | copy-start | bytes 3538948
  2.9 21.9 %collective-permute-start.3 = (bf16[272,1152]{1,0:T(8,128)(2,1)S(1)}, bf16[272,1152]{1,0:T(8,128)(2,1)S(1)}, u32[]{:S(2)}, u32[]{:S(2)}) collective-permute-start(bf16[272,1152]{1,0:T(8,128)(2,1)S(1)} %cast.1.text), channel_id=1, source_target_pairs={{0,2},{1,3},{2,4},{3,5},{4,6},{5,7},{6,8},{7,9},{8,10},{9,11},{10,... | collective-permute-start | bytes 1880072 | tf_op jit(solution)/shard_map/ppermute | solution.py:164
  6.0 2.3 %collective-permute-start.2 = (bf16[128,1152]{1,0:T(8,128)(2,1)S(1)}, bf16[128,1152]{1,0:T(8,128)(2,1)S(1)}, u32[]{:S(2)}, u32[]{:S(2)}) collective-permute-start(bf16[128,1152]{1,0:T(8,128)(2,1)S(1)} %get-tuple-element.31), channel_id=1, source_target_pairs={{0,1},{1,0},{2,3},{3,2},{4,5},{5,4},{6,7},{7,6},{8,9},{9,8},{10,11... | collective-permute-start | bytes 884744 | tf_op jit(solution)/shard_map/ppermute | solution.py:167
  6.1 2.2 %collective-permute-start.1 = (bf16[128,1152]{1,0:T(8,128)(2,1)S(1)}, bf16[128,1152]{1,0:T(8,128)(2,1)S(1)}, u32[]{:S(2)}, u32[]{:S(2)}) collective-permute-start(bf16[128,1152]{1,0:T(8,128)(2,1)S(1)} %get-tuple-element.32), channel_id=1, source_target_pairs={{0,1},{1,0},{2,3},{3,2},{4,5},{5,4},{6,7},{7,6},{8,9},{9,8},{10,11... | collective-permute-start | bytes 884744 | tf_op jit(solution)/shard_map/ppermute | solution.py:167
  6.6 1.7 %collective-permute-start = (s32[1,256]{1,0:T(1,128)}, s32[1,256]{1,0:T(1,128)S(1)}, u32[]{:S(2)}, u32[]{:S(2)}) collective-permute-start(s32[1,256]{1,0:T(1,128)} %bitcast.ids), channel_id=1, source_target_pairs={{0,1},{1,0},{2,3},{3,2},{4,5},{5,4},{6,7},{7,6},{8,9},{9,8},{10,11... | collective-permute-start | bytes 3080 | tf_op jit(solution)/shard_map/ppermute | solution.py:167
  8.3 1.3 %copy-start.2 = (f32[256,1152]{1,0:T(8,128)S(1)}, f32[256,1152]{1,0:T(8,128)}, u32[]{:S(2)}) copy-start(f32[256,1152]{1,0:T(8,128)} %accum.1) | copy-start | bytes 3538948
  12.8 23.8 %collective-permute-start.6 = (bf16[256,1152]{1,0:T(8,128)(2,1)S(1)}, bf16[256,1152]{1,0:T(8,128)(2,1)S(1)}, u32[]{:S(2)}, u32[]{:S(2)}) collective-permute-start(bf16[256,1152]{1,0:T(8,128)(2,1)S(1)} %get-tuple-element.29), channel_id=1, source_target_pairs={{0,2},{1,3},{2,4},{3,5},{4,6},{5,7},{6,8},{7,9},{8,10},{9,11},{10,... | collective-permute-start | bytes 1769480 | tf_op jit(solution)/shard_map/ppermute | solution.py:164
  24.9 2.6 %collective-permute-start.5 = (bf16[144,1152]{1,0:T(8,128)(2,1)S(1)}, bf16[144,1152]{1,0:T(8,128)(2,1)S(1)}, u32[]{:S(2)}, u32[]{:S(2)}) collective-permute-start(bf16[144,1152]{1,0:T(8,128)(2,1)S(1)} %get-tuple-element.21), channel_id=1, source_target_pairs={{0,1},{1,0},{2,3},{3,2},{4,5},{5,4},{6,7},{7,6},{8,9},{9,8},{10,11... | collective-permute-start | bytes 995336 | tf_op jit(solution)/shard_map/ppermute | solution.py:167
  25.0 2.5 %collective-permute-start.4 = (bf16[128,1152]{1,0:T(8,128)(2,1)S(1)}, bf16[128,1152]{1,0:T(8,128)(2,1)S(1)}, u32[]{:S(2)}, u32[]{:S(2)}) collective-permute-start(bf16[128,1152]{1,0:T(8,128)(2,1)S(1)} %get-tuple-element.20), channel_id=1, source_target_pairs={{0,1},{1,0},{2,3},{3,2},{4,5},{5,4},{6,7},{7,6},{8,9},{9,8},{10,11... | collective-permute-start | bytes 884744 | tf_op jit(solution)/shard_map/ppermute | solution.py:167

commit v4 on v3

--- a/solution.py
+++ b/solution.py
@@ -7,7 +7,7 @@
 
 SHIFTS = 2
 AXES = ("dp", "group")
-PAD = 16
+PAD = 8
 CHUNKS = 4
 VMEM = pl.BlockSpec(memory_space=pltpu.VMEM)
 SMEM = pl.BlockSpec(memory_space=pltpu.SMEM)
@@ -41,28 +41,11 @@
     return coef.astype(jnp.bfloat16)
 
 
-def cast_kernel(ids, text, out, staged, ids_in, sems, ids_sem):
+def cast_kernel(parts, text, out):
     rows, width = text.shape
-    step = rows // CHUNKS
-    ids_copy = pltpu.make_async_copy(ids, ids_in, ids_sem)
-    copies = [
-        pltpu.make_async_copy(text.at[pl.ds(k * step, step)], staged.at[pl.ds(k * step, step)], sems.at[k])
-        for k in range(CHUNKS)
-    ]
-    for copy in copies:
-        copy.start()
-    ids_copy.start()
+    out[:rows, :] = text[...].astype(out.dtype)
     out[rows:, :] = jnp.zeros((PAD, width), out.dtype)
-    for k, copy in enumerate(copies):
-        copy.wait()
-        out[k * step:(k + 1) * step, :] = staged[k * step:(k + 1) * step, :].astype(out.dtype)
-    ids_copy.wait()
-    row = lax.broadcasted_iota(jnp.int32, (PAD, rows), 0)
-    spread = jnp.broadcast_to(ids_in[...], (PAD, rows))
-    parts = jnp.zeros((PAD, rows), jnp.int32)
-    for k in range(4):
-        parts = jnp.where(row == k, (spread >> (8 * k)) & 255, parts)
-    out[rows:, :rows] = parts.astype(jnp.float32).astype(out.dtype)
+    out[rows:, :rows] = parts[...].astype(out.dtype)
 
 
 def add_kernel(arrived, late, out, staged, sems):
@@ -166,24 +149,13 @@
     def across(value):
         return lax.ppermute(value, AXES, swap)
 
-    text = pl.pallas_call(
-        cast_kernel,
-        out_shape=jax.ShapeDtypeStruct((rows + PAD, width), bf16),
-        in_specs=[HBM, HBM],
-        out_specs=VMEM,
-        scratch_shapes=[
-            pltpu.VMEM((rows, width), f32),
-            pltpu.VMEM((1, rows), jnp.int32),
-            pltpu.SemaphoreType.DMA((CHUNKS,)),
-            pltpu.SemaphoreType.DMA,
-        ],
-        compiler_params=pltpu.CompilerParams(vmem_limit_bytes=16 * 1024 * 1024),
-        cost_estimate=pl.CostEstimate(flops=0, bytes_accessed=0, transcendentals=0),
-        name="cast",
-    )(ids, text_emb)
+    shifts = jnp.minimum(8 * jnp.arange(PAD, dtype=jnp.int32), 24)[:, None]
+    parts = ((ids >> shifts) & 255).astype(f32)
+    (text,) = call(cast_kernel, "cast", [((rows + PAD, width), bf16)], (), parts, text_emb)
     far = ahead(text)
 
     image, text = lax.optimization_barrier((image_emb, text))
+    image_emb = image
     mate_a, mate_b = across(image[:half]), across(image[half:])
     mate_ids = across(ids)
 

time: 38 us -> 37.4 us (0.984)
  Pallas kernels: 9.91 us -> 8.56 us
  other arithmetic: 0.08 us -> 0.89 us
    pallas_call x1 -> x0, Pallas kernels: 0.96 us -> none  [body(): pl.pallas_call(cast_kernel, out_shape=jax.ShapeDtypeStruct((rows + PAD, w...]
    convert_element_type x0 -> x1, other arithmetic: none -> 0.81 us  [body(): parts = (ids >> shifts & 255).astype(f32)]
    pallas_call x4 -> x5, Pallas kernels: 7.88 us -> 7.5 us  [call(): pl.pallas_call(kernel, out_shape=[jax.ShapeDtypeStruct(s, d) for s, d in...]
    unnamed x6 -> x8, local copies, waits for them, and re-layouts: 2.6 us -> 2.55 us
  transfers between devices with their start and end apart: 7 -> 7, of which waited for: 3 -> 2; matrix products, arithmetic and copies ran while one was open for 0% -> 0% of each run, Pallas kernels for 21% -> 20%
where the time goes in v4:
time: 37.4 us; the launch traced here: 37.2 us
  waiting for transfers between devices  17.4 us (47%)
  Pallas kernels  8.56 us (23%)
  starting transfers between devices  5.72 us (15%)
  local copies, waits for them, and re-layouts  2.59 us (7%)
  between operations  2.02 us (5%)
  other arithmetic  0.89 us (2%)
    ppermute x2, waiting for transfers between devices, ahead(): return lax.ppermute(value, AXES, skip)  17.4 us
    pallas_call x5, Pallas kernels, call(): pl.pallas_call(kernel, out_shape=[jax.ShapeDtypeStruct(s, d) for s, d in...  7.5 us
    ppermute x2, starting transfers between devices, ahead(): return lax.ppermute(value, AXES, skip)  4.51 us
    unnamed x8, local copies, waits for them, and re-layouts  2.55 us
    ppermute x5, starting transfers between devices, across(): return lax.ppermute(value, AXES, swap)  1.21 us
    pallas_call x1, Pallas kernels, body(): pl.pallas_call(add_kernel, out_shape=jax.ShapeDtypeStruct((rows, width),...  1.06 us
    convert_element_type x1, other arithmetic, body(): parts = (ids >> shifts & 255).astype(f32)  0.81 us
  transfers between devices with their start and end apart: 7, of which 2 were waited for; matrix products, arithmetic and copies ran while one was open for 0% of the time, Pallas kernels for 20%

profile of v4, /device:TPU:0, one launch (start us, length us, event | category | flops | bytes accessed | tf_op | source)
XLA Modules:
  0.0 37.2 jit_solution(17998881000439043173)
XLA Ops:
  0.6 0.0 copy-start
  0.7 0.8 %and_convert_fusion.parts = f32[8,256]{1,0:T(8,128)S(1)} fusion(s32[8]{0:T(128)S(1)} %multiply_minimum_fusion, s32[256]{0:T(256)} %param.9), kind=kLoop, calls=%fused_computation | loop fusion | flops 6144 | bytes 9248 | tf_op jit(solution)/shard_map/convert_element_type | solution.py:153
  1.5 0.0 copy-start.1
  1.5 1.3 %copy-done.1 = f32[256,1152]{1,0:T(8,128)S(1)} copy-done((f32[256,1152]{1,0:T(8,128)S(1)}, f32[256,1152]{1,0:T(8,128)}, u32[]{:S(2)}) %copy-start.1) | copy-done | bytes 1179672
  2.7 0.0 copy-start.3
  2.7 0.1 cast.1.text
  2.8 3.0 %collective-permute-start.3 = (bf16[264,1152]{1,0:T(8,128)(2,1)S(1)}, bf16[264,1152]{1,0:T(8,128)(2,1)S(1)}, u32[]{:S(2)}, u32[]{:S(2)}) collective-permute-start(bf16[264,1152]{1,0:T(8,128)(2,1)S(1)} %cast.1.text), channel_id=1, source_target_pairs={{0,2},{1,3},{2,4},{3,5},{4,6},{5,7},{6,8},{7,9},{8,10},{9,11},{10,... | collective-permute-start | bytes 1824776 | tf_op jit(solution)/shard_map/ppermute | solution.py:147
  5.8 0.0 copy-done
  5.9 0.1 collective-permute-start.2
  6.0 0.5 %collective-permute-start.1 = (bf16[128,1152]{1,0:T(8,128)(2,1)S(1)}, bf16[128,1152]{1,0:T(8,128)(2,1)S(1)}, u32[]{:S(2)}, u32[]{:S(2)}) collective-permute-start(bf16[128,1152]{1,0:T(8,128)(2,1)S(1)} %get-tuple-element.32), channel_id=1, source_target_pairs={{0,1},{1,0},{2,3},{3,2},{4,5},{5,4},{6,7},{7,6},{8,9},{9,8},{10,11... | collective-permute-start | bytes 884744 | tf_op jit(solution)/shard_map/ppermute | solution.py:150
  6.4 0.0 copy-done.3
  6.5 0.1 collective-permute-start
  7.8 0.1 pad_maximum_fusion.params
  7.9 0.0 collective-permute-done.mate_ids
  7.9 0.0 collective-permute-done.2.mate_b
  7.9 0.0 collective-permute-done.1.mate_a
  7.9 0.0 copy-start.2
  8.0 1.3 %copy-done.2 = f32[256,1152]{1,0:T(8,128)S(1)} copy-done((f32[256,1152]{1,0:T(8,128)S(1)}, f32[256,1152]{1,0:T(8,128)}, u32[]{:S(2)}) %copy-start.2) | copy-done | bytes 1179672
  9.2 3.1 %own.1 = (bf16[256,1152]{1,0:T(8,128)(2,1)S(1)}, f32[256,1152]{1,0:T(8,128)S(1)}, f32[1,256]{1,0:T(1,128)S(1)}) custom-call(s32[1]{0:T(128)} %bitcast.1.flags, f32[2]{0:T(128)S(1)} %pad_maximum_fusion.params, s32[1,256]{1,0:T(1,128)S(1)} %bitcast.4, s32[1,256]{1,0:T(1,128)S(1)} %collective-permute-done.mate_ids, bf16[256,1152]{1,0:T(8,128)(2,1)S(1)} %copy-done, ...), custom_call_target="tpu_custom_call" | custom-call | tf_op jit(solution)/shard_map/own/pallas_call | solution.py:123
  12.4 1.5 %collective-permute-start.6 = (bf16[256,1152]{1,0:T(8,128)(2,1)S(1)}, bf16[256,1152]{1,0:T(8,128)(2,1)S(1)}, u32[]{:S(2)}, u32[]{:S(2)}) collective-permute-start(bf16[256,1152]{1,0:T(8,128)(2,1)S(1)} %get-tuple-element.29), channel_id=1, source_target_pairs={{0,2},{1,3},{2,4},{3,5},{4,6},{5,7},{6,8},{7,9},{8,10},{9,11},{10,... | collective-permute-start | bytes 1769480 | tf_op jit(solution)/shard_map/ppermute | solution.py:147
  13.8 10.5 %collective-permute-done.3.far = bf16[264,1152]{1,0:T(8,128)(2,1)S(1)} collective-permute-done((bf16[264,1152]{1,0:T(8,128)(2,1)S(1)}, bf16[264,1152]{1,0:T(8,128)(2,1)S(1)}, u32[]{:S(2)}, u32[]{:S(2)}) %collective-permute-start.3) | collective-permute-done | bytes 608288 | tf_op jit(solution)/shard_map/ppermute | solution.py:147
  24.4 0.1 collective-permute-start.5
  24.5 0.5 %collective-permute-start.4 = (bf16[128,1152]{1,0:T(8,128)(2,1)S(1)}, bf16[128,1152]{1,0:T(8,128)(2,1)S(1)}, u32[]{:S(2)}, u32[]{:S(2)}) collective-permute-start(bf16[128,1152]{1,0:T(8,128)(2,1)S(1)} %get-tuple-element.20), channel_id=1, source_target_pairs={{0,1},{1,0},{2,3},{3,2},{4,5},{5,4},{6,7},{7,6},{8,9},{9,8},{10,11... | collective-permute-start | bytes 884744 | tf_op jit(solution)/shard_map/ppermute | solution.py:150
  25.0 1.8 %far.1 = (f32[256,1152]{1,0:T(8,128)S(1)}, f32[256,1152]{1,0:T(8,128)S(1)}, f32[1,256]{1,0:T(1,128)S(1)}) custom-call(s32[1]{0:T(128)} %bitcast.1.flags, f32[2]{0:T(128)S(1)} %pad_maximum_fusion.params, s32[1,256]{1,0:T(1,128)S(1)} %bitcast.5, s32[1,256]{1,0:T(1,128)S(1)} %collective-permute-done.mate_ids, bf16[256,1152]{1,0:T(8,128)(2,1)S(1)} %copy-done, ...), custom_call_target="tpu_custom_call" | custom-call | tf_op jit(solution)/shard_map/far/pallas_call | solution.py:123
  26.8 0.0 collective-permute-done.4.near_a
  26.8 0.0 collective-permute-done.5.near_b
  26.8 2.4 %near.1 = (bf16[256,1152]{1,0:T(8,128)(2,1)}, f32[1,256]{1,0:T(1,128)}) custom-call(f32[2]{0:T(128)S(1)} %pad_maximum_fusion.params, s32[1,256]{1,0:T(1,128)S(1)} %bitcast.6, bf16[256,1152]{1,0:T(8,128)(2,1)S(1)} %copy-done, bf16[128,1152]{1,0:T(8,128)(2,1)S(1)} %collective-permute-done.4.near_a, bf16[136,1152]{1,0:T(8,128)(2,1)S(1)} %collective-permute-done.5.near_b, ...), custom_call_target="tpu_custom_call" | custom-call | tf_op jit(solution)/shard_map/near/pallas_call | solution.py:123
  29.3 6.9 %collective-permute-done.6.arrived = bf16[256,1152]{1,0:T(8,128)(2,1)S(1)} collective-permute-done((bf16[256,1152]{1,0:T(8,128)(2,1)S(1)}, bf16[256,1152]{1,0:T(8,128)(2,1)S(1)}, u32[]{:S(2)}, u32[]{:S(2)}) %collective-permute-start.6) | collective-permute-done | bytes 589856 | tf_op jit(solution)/shard_map/ppermute | solution.py:147
  36.1 1.1 %add.6 = f32[256,1152]{1,0:T(8,128)} custom-call(bf16[256,1152]{1,0:T(8,128)(2,1)S(1)} %collective-permute-done.6.arrived, f32[256,1152]{1,0:T(8,128)S(1)} %get-tuple-element.30.late), custom_call_target="tpu_custom_call" | custom-call | tf_op jit(solution)/shard_map/add/pallas_call | solution.py:182
  (3 shorter events, 0.1 us)
Async XLA Ops:
  0.6 5.2 %copy-start = (bf16[256,1152]{1,0:T(8,128)(2,1)S(1)}, bf16[256,1152]{1,0:T(8,128)(2,1)}, u32[]{:S(2)}) copy-start(bf16[256,1152]{1,0:T(8,128)(2,1)} %image.2) | copy-start | bytes 1769476
  1.5 1.3 %copy-start.1 = (f32[256,1152]{1,0:T(8,128)S(1)}, f32[256,1152]{1,0:T(8,128)}, u32[]{:S(2)}) copy-start(f32[256,1152]{1,0:T(8,128)} %text.1) | copy-start | bytes 3538948
  2.7 3.7 %copy-start.3 = (s32[256]{0:T(256)S(1)}, s32[256]{0:T(256)}, u32[]{:S(2)}) copy-start(s32[256]{0:T(256)} %param.9) | copy-start | bytes 3076
  2.8 21.5 %collective-permute-start.3 = (bf16[264,1152]{1,0:T(8,128)(2,1)S(1)}, bf16[264,1152]{1,0:T(8,128)(2,1)S(1)}, u32[]{:S(2)}, u32[]{:S(2)}) collective-permute-start(bf16[264,1152]{1,0:T(8,128)(2,1)S(1)} %cast.1.text), channel_id=1, source_target_pairs={{0,2},{1,3},{2,4},{3,5},{4,6},{5,7},{6,8},{7,9},{8,10},{9,11},{10,... | collective-permute-start | bytes 1824776 | tf_op jit(solution)/shard_map/ppermute | solution.py:147
  5.9 2.1 %collective-permute-start.2 = (bf16[128,1152]{1,0:T(8,128)(2,1)S(1)}, bf16[128,1152]{1,0:T(8,128)(2,1)S(1)}, u32[]{:S(2)}, u32[]{:S(2)}) collective-permute-start(bf16[128,1152]{1,0:T(8,128)(2,1)S(1)} %get-tuple-element.31), channel_id=1, source_target_pairs={{0,1},{1,0},{2,3},{3,2},{4,5},{5,4},{6,7},{7,6},{8,9},{9,8},{10,11... | collective-permute-start | bytes 884744 | tf_op jit(solution)/shard_map/ppermute | solution.py:150
  6.0 2.0 %collective-permute-start.1 = (bf16[128,1152]{1,0:T(8,128)(2,1)S(1)}, bf16[128,1152]{1,0:T(8,128)(2,1)S(1)}, u32[]{:S(2)}, u32[]{:S(2)}) collective-permute-start(bf16[128,1152]{1,0:T(8,128)(2,1)S(1)} %get-tuple-element.32), channel_id=1, source_target_pairs={{0,1},{1,0},{2,3},{3,2},{4,5},{5,4},{6,7},{7,6},{8,9},{9,8},{10,11... | collective-permute-start | bytes 884744 | tf_op jit(solution)/shard_map/ppermute | solution.py:150
  6.5 1.5 %collective-permute-start = (s32[1,256]{1,0:T(1,128)S(1)}, s32[1,256]{1,0:T(1,128)S(1)}, u32[]{:S(2)}, u32[]{:S(2)}) collective-permute-start(s32[1,256]{1,0:T(1,128)S(1)} %bitcast.3), channel_id=1, source_target_pairs={{0,1},{1,0},{2,3},{3,2},{4,5},{5,4},{6,7},{7,6},{8,9},{9,8},{10,11... | collective-permute-start | bytes 3080 | tf_op jit(solution)/shard_map/ppermute | solution.py:150
  7.9 1.3 %copy-start.2 = (f32[256,1152]{1,0:T(8,128)S(1)}, f32[256,1152]{1,0:T(8,128)}, u32[]{:S(2)}) copy-start(f32[256,1152]{1,0:T(8,128)} %accum.1) | copy-start | bytes 3538948
  12.4 23.8 %collective-permute-start.6 = (bf16[256,1152]{1,0:T(8,128)(2,1)S(1)}, bf16[256,1152]{1,0:T(8,128)(2,1)S(1)}, u32[]{:S(2)}, u32[]{:S(2)}) collective-permute-start(bf16[256,1152]{1,0:T(8,128)(2,1)S(1)} %get-tuple-element.29), channel_id=1, source_target_pairs={{0,2},{1,3},{2,4},{3,5},{4,6},{5,7},{6,8},{7,9},{8,10},{9,11},{10,... | collective-permute-start | bytes 1769480 | tf_op jit(solution)/shard_map/ppermute | solution.py:147
  24.4 2.4 %collective-permute-start.5 = (bf16[136,1152]{1,0:T(8,128)(2,1)S(1)}, bf16[136,1152]{1,0:T(8,128)(2,1)S(1)}, u32[]{:S(2)}, u32[]{:S(2)}) collective-permute-start(bf16[136,1152]{1,0:T(8,128)(2,1)S(1)} %get-tuple-element.21), channel_id=1, source_target_pairs={{0,1},{1,0},{2,3},{3,2},{4,5},{5,4},{6,7},{7,6},{8,9},{9,8},{10,11... | collective-permute-start | bytes 940040 | tf_op jit(solution)/shard_map/ppermute | solution.py:150
  24.5 2.3 %collective-permute-start.4 = (bf16[128,1152]{1,0:T(8,128)(2,1)S(1)}, bf16[128,1152]{1,0:T(8,128)(2,1)S(1)}, u32[]{:S(2)}, u32[]{:S(2)}) collective-permute-start(bf16[128,1152]{1,0:T(8,128)(2,1)S(1)} %get-tuple-element.20), channel_id=1, source_target_pairs={{0,1},{1,0},{2,3},{3,2},{4,5},{5,4},{6,7},{7,6},{8,9},{9,8},{10,11... | collective-permute-start | bytes 884744 | tf_op jit(solution)/shard_map/ppermute | solution.py:150

commit v5 on v4

--- a/solution.py
+++ b/solution.py
@@ -41,11 +41,23 @@
     return coef.astype(jnp.bfloat16)
 
 
-def cast_kernel(parts, text, out):
-    rows, width = text.shape
+def parts_kernel(ids, out):
+    row = lax.broadcasted_iota(jnp.int32, out.shape, 0)
+    spread = jnp.broadcast_to(ids[...], out.shape)
+    parts = jnp.zeros(out.shape, jnp.int32)
+    for k in range(4):
+        parts = jnp.where(row == k, (spread >> (8 * k)) & 255, parts)
+    out[...] = parts.astype(out.dtype)
+
+
+def cast_kernel(parts, text, out, main, rest):
+    rows, cut = text.shape[0], main.shape[0] - PAD
     out[:rows, :] = text[...].astype(out.dtype)
-    out[rows:, :] = jnp.zeros((PAD, width), out.dtype)
+    out[rows:, :] = jnp.zeros((PAD, text.shape[1]), out.dtype)
     out[rows:, :rows] = parts[...].astype(out.dtype)
+    main[:cut, :] = out[:cut, :]
+    main[cut:, :] = out[rows:, :]
+    rest[...] = out[cut:rows, :]
 
 
 def add_kernel(arrived, late, out, staged, sems):
@@ -80,12 +92,16 @@
     image_sum[...] = dot(low(coef), text[:rows, :], (1, 0))
 
 
-def relay_kernel(flags, token, text, far, out_a, out_b):
-    cut = out_a.shape[0]
+def relay_kernel(flags, token, text, far_most, far_main, far_turn, out_a, out_b, far):
+    half, rest = out_a.shape[0], far_turn.shape[0]
+    cut = far_main.shape[0] - PAD
+    far[:cut, :] = far_most[:cut, :] + far_main[:cut, :]
+    far[cut:cut + rest, :] = far_most[cut:cut + rest, :] + far_turn[...]
+    far[cut + rest:, :] = far_most[cut + rest:, :] + far_main[cut:, :]
 
     def fill(source):
-        out_a[...] = source[:cut, :]
-        out_b[...] = source[cut:, :]
+        out_a[...] = source[:half, :]
+        out_b[...] = source[half:, :]
 
     pl.when(flags[0] == 0)(lambda: fill(text))
     pl.when(flags[0] == 1)(lambda: fill(far))
@@ -119,14 +135,14 @@
     image_grad[...] = (image_in[...] + dot(low(coef), near, (1, 0))).astype(image_grad.dtype)
 
 
-def call(kernel, name, outs, scalars, *operands):
+def call(kernel, name, outs, scalars, *operands, cost=0):
     return pl.pallas_call(
         kernel,
         out_shape=[jax.ShapeDtypeStruct(s, d) for s, d in outs],
         in_specs=[SMEM] * len(scalars) + [VMEM] * len(operands),
         out_specs=[VMEM] * len(outs),
         compiler_params=pltpu.CompilerParams(vmem_limit_bytes=16 * 1024 * 1024),
-        cost_estimate=pl.CostEstimate(flops=0, bytes_accessed=0, transcendentals=0),
+        cost_estimate=pl.CostEstimate(flops=0, bytes_accessed=cost, transcendentals=0),
         name=name,
     )(*scalars, *operands)
 
@@ -149,13 +165,20 @@
     def across(value):
         return lax.ppermute(value, AXES, swap)
 
-    shifts = jnp.minimum(8 * jnp.arange(PAD, dtype=jnp.int32), 24)[:, None]
-    parts = ((ids >> shifts) & 255).astype(f32)
-    (text,) = call(cast_kernel, "cast", [((rows + PAD, width), bf16)], (), parts, text_emb)
-    far = ahead(text)
+    cut = rows - rows // 4
+    turn = lax.axis_size("group")
+    (parts,) = call(parts_kernel, "parts", [((PAD, rows), f32)], (), ids, cost=PAD << 20)
+    text, text_main, text_rest = call(
+        cast_kernel, "cast",
+        [((rows + PAD, width), bf16), ((cut + PAD, width), bf16), ((rows - cut, width), bf16)],
+        (), parts, text_emb,
+    )
+    far_most = lax.ppermute(text, AXES, skip[:-2])
+    far_main = lax.ppermute(text_main, AXES, skip[-2:])
+    to_turn = lax.ppermute(text_rest, AXES, [(count - 2, turn), (count - 1, turn + 1)])
+    far_turn = lax.ppermute(to_turn, AXES, [(turn, 0), (turn + 1, 1)])
 
     image, text = lax.optimization_barrier((image_emb, text))
-    image_emb = image
     mate_a, mate_b = across(image[:half]), across(image[half:])
     mate_ids = across(ids)
 
@@ -165,9 +188,10 @@
     )
     arrived = ahead(outgoing)
 
-    passed_a, passed_b = call(
-        relay_kernel, "relay", [((half, width), bf16), ((rows + PAD - half, width), bf16)],
-        (flags,), loss, text, far,
+    passed_a, passed_b, far = call(
+        relay_kernel, "relay",
+        [((half, width), bf16), ((rows + PAD - half, width), bf16), ((rows + PAD, width), bf16)],
+        (flags,), loss, text, far_most, far_main, far_turn,
     )
     near_a, near_b = across(passed_a), across(passed_b)
     late, image_sum, loss = call(

time: 37.4 us -> 48 us (1.28)
  the two profiles are of different devices: /device:TPU:0 before, /device:TPU:1 now
where the time goes in v5:
time: 48 us; the launch traced here: 47.7 us
  waiting for transfers between devices  18.5 us (39%)
  starting transfers between devices  13.7 us (29%)
  Pallas kernels  10.6 us (22%)
  local copies, waits for them, and re-layouts  2.88 us (6%)
  between operations  2.04 us (4%)
    ppermute x1, waiting for transfers between devices, body(): far_turn = lax.ppermute(to_turn, AXES, [(turn, 0), (turn + 1, 1)])  18.5 us
    pallas_call x6, Pallas kernels, call(): pl.pallas_call(kernel, out_shape=[jax.ShapeDtypeStruct(s, d) for s, d in...  9.49 us
    ppermute x5, starting transfers between devices, across(): return lax.ppermute(value, AXES, swap)  4.92 us
    ppermute x1, starting transfers between devices, body(): far_most = lax.ppermute(text, AXES, skip[:-2])  4.8 us
    unnamed x10, local copies, waits for them, and re-layouts  2.01 us
    ppermute x1, starting transfers between devices, body(): lax.ppermute(text_rest, AXES, [(count - 2, turn), (count - 1, turn + 1)])  1.33 us
    ppermute x1, starting transfers between devices, body(): far_turn = lax.ppermute(to_turn, AXES, [(turn, 0), (turn + 1, 1)])  1.29 us
    ppermute x1, starting transfers between devices, body(): far_main = lax.ppermute(text_main, AXES, skip[-2:])  1.28 us
  transfers between devices with their start and end apart: 10, of which 1 were waited for; matrix products, arithmetic and copies ran while one was open for 2% of the time, Pallas kernels for 18%

profile of v5, /device:TPU:1, one launch (start us, length us, event | category | flops | bytes accessed | tf_op | source)
XLA Modules:
  0.0 47.7 jit_solution(7974456378357020211)
XLA Ops:
  0.6 0.0 copy-start
  0.6 0.0 copy-start.3
  0.7 0.7 %copy-done.3 = s32[256]{0:T(256)S(1)} copy-done((s32[256]{0:T(256)S(1)}, s32[256]{0:T(256)}, u32[]{:S(2)}) %copy-start.3) | copy-done | bytes 1048
  1.4 0.0 copy-start.1
  1.4 1.3 %copy-done.1 = f32[256,1152]{1,0:T(8,128)S(1)} copy-done((f32[256,1152]{1,0:T(8,128)S(1)}, f32[256,1152]{1,0:T(8,128)}, u32[]{:S(2)}) %copy-start.1) | copy-done | bytes 1179672
  2.7 0.0 copy-start.4
  2.7 0.0 copy-start.2
  2.7 0.9 %cast.1 = (bf16[264,1152]{1,0:T(8,128)(2,1)S(1)}, bf16[200,1152]{1,0:T(8,128)(2,1)}, bf16[64,1152]{1,0:T(8,128)(2,1)}) custom-call(f32[8,256]{1,0:T(8,128)S(1)} %parts.1, f32[256,1152]{1,0:T(8,128)S(1)} %copy-done.1), custom_call_target="tpu_custom_call" | custom-call | tf_op jit(solution)/shard_map/cast/pallas_call | solution.py:139
  3.6 4.8 %collective-permute-start.3 = (bf16[264,1152]{1,0:T(8,128)(2,1)S(1)}, bf16[264,1152]{1,0:T(8,128)(2,1)}, u32[]{:S(2)}, u32[]{:S(2)}) collective-permute-start(bf16[264,1152]{1,0:T(8,128)(2,1)S(1)} %get-tuple-element.23.text), channel_id=1, source_target_pairs={{0,2},{1,3},{2,4},{3,5},{4,6},{5,7},{6,8},{7,9},{8,10},{9,11},{10,... | collective-permute-start | bytes 1824776 | tf_op jit(solution)/shard_map/ppermute | solution.py:176
  8.4 0.0 copy-done
  8.4 0.9 %fusion = (bf16[128,1152]{1,0:T(8,128)(2,1)}, bf16[128,1152]{1,0:T(8,128)(2,1)}) fusion(bf16[256,1152]{1,0:T(8,128)(2,1)S(1)} %copy-done), kind=kLoop, calls=%fused_computation.1 | loop fusion | bytes 1179648 | tf_op jit(solution)/shard_map/slice | solution.py:182
  9.2 1.0 %collective-permute-start.2 = (bf16[128,1152]{1,0:T(8,128)(2,1)}, bf16[128,1152]{1,0:T(8,128)(2,1)S(1)}, u32[]{:S(2)}, u32[]{:S(2)}) collective-permute-start(bf16[128,1152]{1,0:T(8,128)(2,1)} %get-tuple-element.39), channel_id=1, source_target_pairs={{0,1},{1,0},{2,3},{3,2},{4,5},{5,4},{6,7},{7,6},{8,9},{9,8},{10,11... | collective-permute-start | bytes 884744 | tf_op jit(solution)/shard_map/ppermute | solution.py:166
  10.2 0.0 collective-permute-start.1
  10.2 1.3 %collective-permute-start.4 = (bf16[200,1152]{1,0:T(8,128)(2,1)}, bf16[200,1152]{1,0:T(8,128)(2,1)S(1)}, u32[]{:S(2)}, u32[]{:S(2)}) collective-permute-start(bf16[200,1152]{1,0:T(8,128)(2,1)} %get-tuple-element.25), channel_id=1, source_target_pairs={{30,0},{31,1}} | collective-permute-start | bytes 1382408 | tf_op jit(solution)/shard_map/ppermute | solution.py:177
  11.5 0.0 copy-done.4
  11.5 0.6 %collective-permute-start = (s32[1,256]{1,0:T(1,128)S(1)}, s32[1,256]{1,0:T(1,128)S(1)}, u32[]{:S(2)}, u32[]{:S(2)}) collective-permute-start(s32[1,256]{1,0:T(1,128)S(1)} %bitcast.4), channel_id=1, source_target_pairs={{0,1},{1,0},{2,3},{3,2},{4,5},{5,4},{6,7},{7,6},{8,9},{9,8},{10,11... | collective-permute-start | bytes 3080 | tf_op jit(solution)/shard_map/ppermute | solution.py:166
  13.3 0.0 collective-permute-done.mate_ids
  13.4 1.3 %collective-permute-start.5 = (bf16[64,1152]{1,0:T(8,128)(2,1)}, bf16[64,1152]{1,0:T(8,128)(2,1)}, u32[]{:S(2)}, u32[]{:S(2)}) collective-permute-start(bf16[64,1152]{1,0:T(8,128)(2,1)} %get-tuple-element.26), channel_id=1, source_target_pairs={{30,4},{31,5}} | collective-permute-start | bytes 442376 | tf_op jit(solution)/shard_map/ppermute | solution.py:178
  14.7 0.1 pad_maximum_fusion.params
  14.8 0.0 collective-permute-done.2.mate_b
  14.8 0.0 collective-permute-done.1.mate_a
  14.8 0.0 copy-done.2
  14.8 2.1 %own.1 = (bf16[256,1152]{1,0:T(8,128)(2,1)S(1)}, f32[256,1152]{1,0:T(8,128)S(1)}, f32[1,256]{1,0:T(1,128)S(1)}) custom-call(s32[1]{0:T(128)} %bitcast.1.flags, f32[2]{0:T(128)S(1)} %pad_maximum_fusion.params, s32[1,256]{1,0:T(1,128)S(1)} %bitcast.5, s32[1,256]{1,0:T(1,128)S(1)} %collective-permute-done.mate_ids, bf16[256,1152]{1,0:T(8,128)(2,1)S(1)} %copy-done, ...), custom_call_target="tpu_custom_call" | custom-call | tf_op jit(solution)/shard_map/own/pallas_call | solution.py:139
  16.9 0.1 collective-permute-start.9
  16.9 0.0 collective-permute-done.5
  16.9 1.3 %collective-permute-start.6 = (bf16[64,1152]{1,0:T(8,128)(2,1)}, bf16[64,1152]{1,0:T(8,128)(2,1)S(1)}, u32[]{:S(2)}, u32[]{:S(2)}) collective-permute-start(bf16[64,1152]{1,0:T(8,128)(2,1)} %collective-permute-done.5), channel_id=1, source_target_pairs={{4,0},{5,1}} | collective-permute-start | bytes 442376 | tf_op jit(solution)/shard_map/ppermute | solution.py:179
  18.2 18.5 %collective-permute-done.6.far_turn = bf16[64,1152]{1,0:T(8,128)(2,1)S(1)} collective-permute-done((bf16[64,1152]{1,0:T(8,128)(2,1)}, bf16[64,1152]{1,0:T(8,128)(2,1)S(1)}, u32[]{:S(2)}, u32[]{:S(2)}) %collective-permute-start.6) | collective-permute-done | bytes 147488 | tf_op jit(solution)/shard_map/ppermute | solution.py:179
  36.7 0.0 collective-permute-done.4.far_main
  36.7 0.0 collective-permute-done.3.far_most
  36.7 1.2 %relay.1 = (bf16[128,1152]{1,0:T(8,128)(2,1)S(1)}, bf16[136,1152]{1,0:T(8,128)(2,1)S(1)}, bf16[264,1152]{1,0:T(8,128)(2,1)S(1)}) custom-call(s32[1]{0:T(128)} %bitcast.1.flags, f32[1,256]{1,0:T(1,128)S(1)} %get-tuple-element.24.token.loss_in, bf16[264,1152]{1,0:T(8,128)(2,1)S(1)} %get-tuple-element.23.text, ...), custom_call_target="tpu_custom_call" | custom-call | tf_op jit(solution)/shard_map/relay/pallas_call | solution.py:139
  37.9 3.3 %collective-permute-start.8 = (bf16[136,1152]{1,0:T(8,128)(2,1)S(1)}, bf16[136,1152]{1,0:T(8,128)(2,1)S(1)}, u32[]{:S(2)}, u32[]{:S(2)}) collective-permute-start(bf16[136,1152]{1,0:T(8,128)(2,1)S(1)} %get-tuple-element.28), channel_id=1, source_target_pairs={{0,1},{1,0},{2,3},{3,2},{4,5},{5,4},{6,7},{7,6},{8,9},{9,8},{10,11... | collective-permute-start | bytes 940040 | tf_op jit(solution)/shard_map/ppermute | solution.py:166
  41.2 0.1 collective-permute-start.7
  41.3 2.9 %far.1 = (f32[256,1152]{1,0:T(8,128)S(1)}, f32[256,1152]{1,0:T(8,128)S(1)}, f32[1,256]{1,0:T(1,128)S(1)}) custom-call(s32[1]{0:T(128)} %bitcast.1.flags, f32[2]{0:T(128)S(1)} %pad_maximum_fusion.params, s32[1,256]{1,0:T(1,128)S(1)} %bitcast.6, s32[1,256]{1,0:T(1,128)S(1)} %collective-permute-done.mate_ids, bf16[256,1152]{1,0:T(8,128)(2,1)S(1)} %copy-done, ...), custom_call_target="tpu_custom_call" | custom-call | tf_op jit(solution)/shard_map/far/pallas_call | solution.py:139
  44.2 0.0 collective-permute-done.7.near_a
  44.2 0.0 collective-permute-done.8.near_b
  44.2 2.4 %near.1 = (bf16[256,1152]{1,0:T(8,128)(2,1)}, f32[1,256]{1,0:T(1,128)}) custom-call(f32[2]{0:T(128)S(1)} %pad_maximum_fusion.params, s32[1,256]{1,0:T(1,128)S(1)} %bitcast.7, bf16[256,1152]{1,0:T(8,128)(2,1)S(1)} %copy-done, bf16[128,1152]{1,0:T(8,128)(2,1)S(1)} %collective-permute-done.7.near_a, bf16[136,1152]{1,0:T(8,128)(2,1)S(1)} %collective-permute-done.8.near_b, ...), custom_call_target="tpu_custom_call" | custom-call | tf_op jit(solution)/shard_map/near/pallas_call | solution.py:139
  46.6 0.0 collective-permute-done.9.arrived
  46.6 1.1 %add.6 = f32[256,1152]{1,0:T(8,128)} custom-call(bf16[256,1152]{1,0:T(8,128)(2,1)S(1)} %collective-permute-done.9.arrived, f32[256,1152]{1,0:T(8,128)S(1)} %get-tuple-element.38.late), custom_call_target="tpu_custom_call" | custom-call | tf_op jit(solution)/shard_map/add/pallas_call | solution.py:206
  (1 shorter events, 0.0 us)
Async XLA Ops:
  0.6 7.7 %copy-start = (bf16[256,1152]{1,0:T(8,128)(2,1)S(1)}, bf16[256,1152]{1,0:T(8,128)(2,1)}, u32[]{:S(2)}) copy-start(bf16[256,1152]{1,0:T(8,128)(2,1)} %image.5) | copy-start | bytes 1769476
  0.6 0.7 %copy-start.3 = (s32[256]{0:T(256)S(1)}, s32[256]{0:T(256)}, u32[]{:S(2)}) copy-start(s32[256]{0:T(256)} %param.9) | copy-start | bytes 3076
  1.4 1.3 %copy-start.1 = (f32[256,1152]{1,0:T(8,128)S(1)}, f32[256,1152]{1,0:T(8,128)}, u32[]{:S(2)}) copy-start(f32[256,1152]{1,0:T(8,128)} %text.1) | copy-start | bytes 3538948
  2.7 8.8 %copy-start.4 = (s32[256]{0:T(256)S(1)}, s32[256]{0:T(256)}, u32[]{:S(2)}) copy-start(s32[256]{0:T(256)} %param.9) | copy-start | bytes 3076
  2.7 12.1 %copy-start.2 = (f32[256,1152]{1,0:T(8,128)S(1)}, f32[256,1152]{1,0:T(8,128)}, u32[]{:S(2)}) copy-start(f32[256,1152]{1,0:T(8,128)} %accum.1) | copy-start | bytes 3538948
  3.6 33.1 %collective-permute-start.3 = (bf16[264,1152]{1,0:T(8,128)(2,1)S(1)}, bf16[264,1152]{1,0:T(8,128)(2,1)}, u32[]{:S(2)}, u32[]{:S(2)}) collective-permute-start(bf16[264,1152]{1,0:T(8,128)(2,1)S(1)} %get-tuple-element.23.text), channel_id=1, source_target_pairs={{0,2},{1,3},{2,4},{3,5},{4,6},{5,7},{6,8},{7,9},{8,10},{9,11},{10,... | collective-permute-start | bytes 1824776 | tf_op jit(solution)/shard_map/ppermute | solution.py:176
  9.2 5.5 %collective-permute-start.2 = (bf16[128,1152]{1,0:T(8,128)(2,1)}, bf16[128,1152]{1,0:T(8,128)(2,1)S(1)}, u32[]{:S(2)}, u32[]{:S(2)}) collective-permute-start(bf16[128,1152]{1,0:T(8,128)(2,1)} %get-tuple-element.39), channel_id=1, source_target_pairs={{0,1},{1,0},{2,3},{3,2},{4,5},{5,4},{6,7},{7,6},{8,9},{9,8},{10,11... | collective-permute-start | bytes 884744 | tf_op jit(solution)/shard_map/ppermute | solution.py:166
  10.2 4.6 %collective-permute-start.1 = (bf16[128,1152]{1,0:T(8,128)(2,1)}, bf16[128,1152]{1,0:T(8,128)(2,1)S(1)}, u32[]{:S(2)}, u32[]{:S(2)}) collective-permute-start(bf16[128,1152]{1,0:T(8,128)(2,1)} %get-tuple-element.40), channel_id=1, source_target_pairs={{0,1},{1,0},{2,3},{3,2},{4,5},{5,4},{6,7},{7,6},{8,9},{9,8},{10,11... | collective-permute-start | bytes 884744 | tf_op jit(solution)/shard_map/ppermute | solution.py:166
  10.2 26.5 %collective-permute-start.4 = (bf16[200,1152]{1,0:T(8,128)(2,1)}, bf16[200,1152]{1,0:T(8,128)(2,1)S(1)}, u32[]{:S(2)}, u32[]{:S(2)}) collective-permute-start(bf16[200,1152]{1,0:T(8,128)(2,1)} %get-tuple-element.25), channel_id=1, source_target_pairs={{30,0},{31,1}} | collective-permute-start | bytes 1382408 | tf_op jit(solution)/shard_map/ppermute | solution.py:177
  11.5 1.9 %collective-permute-start = (s32[1,256]{1,0:T(1,128)S(1)}, s32[1,256]{1,0:T(1,128)S(1)}, u32[]{:S(2)}, u32[]{:S(2)}) collective-permute-start(s32[1,256]{1,0:T(1,128)S(1)} %bitcast.4), channel_id=1, source_target_pairs={{0,1},{1,0},{2,3},{3,2},{4,5},{5,4},{6,7},{7,6},{8,9},{9,8},{10,11... | collective-permute-start | bytes 3080 | tf_op jit(solution)/shard_map/ppermute | solution.py:166
  13.4 3.6 %collective-permute-start.5 = (bf16[64,1152]{1,0:T(8,128)(2,1)}, bf16[64,1152]{1,0:T(8,128)(2,1)}, u32[]{:S(2)}, u32[]{:S(2)}) collective-permute-start(bf16[64,1152]{1,0:T(8,128)(2,1)} %get-tuple-element.26), channel_id=1, source_target_pairs={{30,4},{31,5}} | collective-permute-start | bytes 442376 | tf_op jit(solution)/shard_map/ppermute | solution.py:178
  16.9 29.8 %collective-permute-start.9 = (bf16[256,1152]{1,0:T(8,128)(2,1)S(1)}, bf16[256,1152]{1,0:T(8,128)(2,1)S(1)}, u32[]{:S(2)}, u32[]{:S(2)}) collective-permute-start(bf16[256,1152]{1,0:T(8,128)(2,1)S(1)} %get-tuple-element.37), channel_id=1, source_target_pairs={{0,2},{1,3},{2,4},{3,5},{4,6},{5,7},{6,8},{7,9},{8,10},{9,11},{10,... | collective-permute-start | bytes 1769480 | tf_op jit(solution)/shard_map/ppermute | solution.py:163
  16.9 19.8 %collective-permute-start.6 = (bf16[64,1152]{1,0:T(8,128)(2,1)}, bf16[64,1152]{1,0:T(8,128)(2,1)S(1)}, u32[]{:S(2)}, u32[]{:S(2)}) collective-permute-start(bf16[64,1152]{1,0:T(8,128)(2,1)} %collective-permute-done.5), channel_id=1, source_target_pairs={{4,0},{5,1}} | collective-permute-start | bytes 442376 | tf_op jit(solution)/shard_map/ppermute | solution.py:179
  37.9 6.3 %collective-permute-start.8 = (bf16[136,1152]{1,0:T(8,128)(2,1)S(1)}, bf16[136,1152]{1,0:T(8,128)(2,1)S(1)}, u32[]{:S(2)}, u32[]{:S(2)}) collective-permute-start(bf16[136,1152]{1,0:T(8,128)(2,1)S(1)} %get-tuple-element.28), channel_id=1, source_target_pairs={{0,1},{1,0},{2,3},{3,2},{4,5},{5,4},{6,7},{7,6},{8,9},{9,8},{10,11... | collective-permute-start | bytes 940040 | tf_op jit(solution)/shard_map/ppermute | solution.py:166
  41.2 3.0 %collective-permute-start.7 = (bf16[128,1152]{1,0:T(8,128)(2,1)S(1)}, bf16[128,1152]{1,0:T(8,128)(2,1)S(1)}, u32[]{:S(2)}, u32[]{:S(2)}) collective-permute-start(bf16[128,1152]{1,0:T(8,128)(2,1)S(1)} %get-tuple-element.27), channel_id=1, source_target_pairs={{0,1},{1,0},{2,3},{3,2},{4,5},{5,4},{6,7},{7,6},{8,9},{9,8},{10,11... | collective-permute-start | bytes 884744 | tf_op jit(solution)/shard_map/ppermute | solution.py:166

commit v6 on v3

--- a/solution.py
+++ b/solution.py
@@ -1,3 +1,5 @@
+import functools
+
 import jax
 import jax.numpy as jnp
 from jax import lax
@@ -7,7 +9,7 @@
 
 SHIFTS = 2
 AXES = ("dp", "group")
-PAD = 16
+PAD = 8
 CHUNKS = 4
 VMEM = pl.BlockSpec(memory_space=pltpu.VMEM)
 SMEM = pl.BlockSpec(memory_space=pltpu.SMEM)
@@ -65,34 +67,39 @@
     out[rows:, :rows] = parts.astype(jnp.float32).astype(out.dtype)
 
 
-def add_kernel(arrived, late, out, staged, sems):
-    rows = arrived.shape[0]
-    step = rows // CHUNKS
+def add_kernel(start, chunks, arrived, late, *refs):
+    out, staged, sems = refs[-3:]
+    step = arrived.shape[0] // chunks
     copies = []
-    for k in range(CHUNKS):
-        part = pl.ds(k * step, step)
-        staged[part, :] = arrived[part, :].astype(staged.dtype) + late[part, :]
-        copies.append(pltpu.make_async_copy(staged.at[part], out.at[part], sems.at[k]))
+    for k in range(chunks):
+        here, there = pl.ds(k * step, step), pl.ds(start + k * step, step)
+        staged[here, :] = arrived[here, :].astype(staged.dtype) + late[there, :]
+        copies.append(pltpu.make_async_copy(staged.at[here], out.at[there], sems.at[k]))
         copies[-1].start()
     for copy in copies:
         copy.wait()
 
 
-def own_kernel(flags, params, ids, mate_ids, image, mate_a, mate_b, text, accum, out, image_sum, loss):
+def own_kernel(flags, params, ids, mate_ids, image, mate_a, mate_b, text, accum, out_a, out_b, image_sum, loss):
     rows = image.shape[0]
     own_loss, coef = pair(image[...], text[:rows, :], ids[...], ids[...], params)
     loss[...] = own_loss
     total = accum[...] + dot(low(coef.T), image[...], (1, 0))
+    cut = out_a.shape[0]
+
+    def give(value):
+        out_a[...] = value[:cut, :].astype(out_a.dtype)
+        out_b[...] = value[cut:, :].astype(out_b.dtype)
 
     @pl.when(flags[0] == 0)
     def _():
         mate = jnp.concatenate([mate_a[...], mate_b[...]], axis=0)
         _, mate_coef = pair(mate, text[:rows, :], mate_ids[...], ids[...], params)
-        out[...] = (total + dot(low(mate_coef.T), mate, (1, 0))).astype(out.dtype)
+        give(total + dot(low(mate_coef.T), mate, (1, 0)))
 
     @pl.when(flags[0] == 1)
     def _():
-        out[...] = total.astype(out.dtype)
+        give(total)
 
     image_sum[...] = dot(low(coef), text[:rows, :], (1, 0))
 
@@ -146,6 +153,20 @@
         cost_estimate=pl.CostEstimate(flops=0, bytes_accessed=0, transcendentals=0),
         name=name,
     )(*scalars, *operands)
+
+
+def add_part(name, start, chunks, arrived, late, *before):
+    return pl.pallas_call(
+        functools.partial(add_kernel, start, chunks),
+        out_shape=jax.ShapeDtypeStruct(late.shape, late.dtype),
+        in_specs=[VMEM, VMEM] + [HBM] * len(before),
+        out_specs=HBM,
+        scratch_shapes=[pltpu.VMEM(arrived.shape, late.dtype), pltpu.SemaphoreType.DMA((chunks,))],
+        input_output_aliases={2: 0} if before else {},
+        compiler_params=pltpu.CompilerParams(vmem_limit_bytes=16 * 1024 * 1024),
+        cost_estimate=pl.CostEstimate(flops=0, bytes_accessed=0, transcendentals=0),
+        name=name,
+    )(arrived, late, *before)
 
 
 def body(image_emb, text_emb, text_accum, pair_ids, log_scale, bias):
@@ -177,21 +198,23 @@
             pltpu.SemaphoreType.DMA((CHUNKS,)),
             pltpu.SemaphoreType.DMA,
         ],
-        compiler_params=pltpu.CompilerParams(vmem_limit_bytes=16 * 1024 * 1024),
+        compiler_params=pltpu.CompilerParams(vmem_limit_bytes=63 * 1024 * 1024),
         cost_estimate=pl.CostEstimate(flops=0, bytes_accessed=0, transcendentals=0),
         name="cast",
     )(ids, text_emb)
     far = ahead(text)
 
     image, text = lax.optimization_barrier((image_emb, text))
+    image_emb = image
     mate_a, mate_b = across(image[:half]), across(image[half:])
     mate_ids = across(ids)
 
-    outgoing, image_sum, loss = call(
-        own_kernel, "own", [((rows, width), bf16), ((rows, width), f32), ((1, rows), f32)],
+    cut = rows - rows // 4
+    out_a, out_b, image_sum, loss = call(
+        own_kernel, "own", [((cut, width), bf16), ((rows - cut, width), bf16), ((rows, width), f32), ((1, rows), f32)],
         (flags, params), ids, mate_ids, image_emb, mate_a, mate_b, text, text_accum,
     )
-    arrived = ahead(outgoing)
+    arrived_a, arrived_b = ahead(out_a), ahead(out_b)
 
     passed_a, passed_b = call(
         relay_kernel, "relay", [((half, width), bf16), ((rows + PAD - half, width), bf16)],
@@ -207,16 +230,8 @@
         (params,), ids, image_emb, near_a, near_b, image_sum, loss,
     )
     late, image_grad = lax.optimization_barrier((late, image_grad))
-    text_grad = pl.pallas_call(
-        add_kernel,
-        out_shape=jax.ShapeDtypeStruct((rows, width), f32),
-        in_specs=[VMEM, VMEM],
-        out_specs=HBM,
-        scratch_shapes=[pltpu.VMEM((rows, width), f32), pltpu.SemaphoreType.DMA((CHUNKS,))],
-        compiler_params=pltpu.CompilerParams(vmem_limit_bytes=16 * 1024 * 1024),
-        cost_estimate=pl.CostEstimate(flops=0, bytes_accessed=0, transcendentals=0),
-        name="add",
-    )(arrived, late)
+    text_grad = add_part("add_a", 0, CHUNKS, arrived_a, late)
+    text_grad = add_part("add_b", cut, 2, arrived_b, late, text_grad)
     return (loss.reshape(rows), image_grad, text_grad)
 
 

time: 38 us -> 37.4 us (0.984)
  Pallas kernels: 9.91 us -> 11.3 us
  local copies, waits for them, and re-layouts: 2.64 us -> 1.33 us
  waiting for transfers between devices: 17.4 us -> 16.7 us
    unnamed x6 -> x8, local copies, waits for them, and re-layouts: 2.6 us -> 1.28 us
    pallas_call x1, Pallas kernels: 0.96 us -> 2.18 us  [body(): pl.pallas_call(cast_kernel, out_shape=jax.ShapeDtypeStruct((rows + PAD, w...]
    pallas_call x1 -> x2, Pallas kernels: 1.06 us -> 1.72 us  [add_part(): pl.pallas_call(functools.partial(add_kernel, start, chunks), out_shape=ja...]
    ppermute x2 -> x3, waiting for transfers between devices: 17.1 us -> 16.6 us  [ahead(): return lax.ppermute(value, AXES, skip)]
    pallas_call x4, Pallas kernels: 7.88 us -> 7.42 us  [call(): pl.pallas_call(kernel, out_shape=[jax.ShapeDtypeStruct(s, d) for s, d in...]
    ppermute x2 -> x3, starting transfers between devices: 4.51 us -> 4.51 us  [ahead(): return lax.ppermute(value, AXES, skip)]
  transfers between devices with their start and end apart: 7 -> 8, of which waited for: 3 -> 3; matrix products, arithmetic and copies ran while one was open for 0% -> 0% of each run, Pallas kernels for 21% -> 23%
where the time goes in v6:
time: 37.4 us; the launch traced here: 37.2 us
  waiting for transfers between devices  16.7 us (45%)
  Pallas kernels  11.3 us (30%)
  starting transfers between devices  5.72 us (15%)
  between operations  2.05 us (5%)
  local copies, waits for them, and re-layouts  1.33 us (4%)
    ppermute x3, waiting for transfers between devices, ahead(): return lax.ppermute(value, AXES, skip)  16.6 us
    pallas_call x4, Pallas kernels, call(): pl.pallas_call(kernel, out_shape=[jax.ShapeDtypeStruct(s, d) for s, d in...  7.42 us
    ppermute x3, starting transfers between devices, ahead(): return lax.ppermute(value, AXES, skip)  4.51 us
    pallas_call x1, Pallas kernels, body(): pl.pallas_call(cast_kernel, out_shape=jax.ShapeDtypeStruct((rows + PAD, w...  2.18 us
    pallas_call x2, Pallas kernels, add_part(): pl.pallas_call(functools.partial(add_kernel, start, chunks), out_shape=ja...  1.72 us
    unnamed x8, local copies, waits for them, and re-layouts  1.28 us
    ppermute x5, starting transfers between devices, across(): return lax.ppermute(value, AXES, swap)  1.21 us
  transfers between devices with their start and end apart: 8, of which 3 were waited for; matrix products, arithmetic and copies ran while one was open for 0% of the time, Pallas kernels for 23%

profile of v6, /device:TPU:0, one launch (start us, length us, event | category | flops | bytes accessed | tf_op | source)
XLA Modules:
  0.0 37.2 jit_solution(16041072970852119801)
XLA Ops:
  0.6 0.0 copy-start
  0.6 0.0 copy-start.3
  0.7 2.2 %cast.1.text = bf16[264,1152]{1,0:T(8,128)(2,1)} custom-call(s32[1,256]{1,0:T(1,128)} %bitcast.3, f32[256,1152]{1,0:T(8,128)} %text.1), custom_call_target="tpu_custom_call" | custom-call | tf_op jit(solution)/shard_map/cast/pallas_call | solution.py:190
  2.8 0.0 copy-start.1
  2.8 3.0 %collective-permute-start.3 = (bf16[264,1152]{1,0:T(8,128)(2,1)}, bf16[264,1152]{1,0:T(8,128)(2,1)S(1)}, u32[]{:S(2)}, u32[]{:S(2)}) collective-permute-start(bf16[264,1152]{1,0:T(8,128)(2,1)} %cast.1.text), channel_id=1, source_target_pairs={{0,2},{1,3},{2,4},{3,5},{4,6},{5,7},{6,8},{7,9},{8,10},{9,11},{10,... | collective-permute-start | bytes 1824776 | tf_op jit(solution)/shard_map/ppermute | solution.py:185
  5.9 0.0 copy-done
  5.9 0.1 collective-permute-start.2
  6.0 0.5 %collective-permute-start.1 = (bf16[128,1152]{1,0:T(8,128)(2,1)S(1)}, bf16[128,1152]{1,0:T(8,128)(2,1)S(1)}, u32[]{:S(2)}, u32[]{:S(2)}) collective-permute-start(bf16[128,1152]{1,0:T(8,128)(2,1)S(1)} %get-tuple-element.34), channel_id=1, source_target_pairs={{0,1},{1,0},{2,3},{3,2},{4,5},{5,4},{6,7},{7,6},{8,9},{9,8},{10,11... | collective-permute-start | bytes 884744 | tf_op jit(solution)/shard_map/ppermute | solution.py:188
  6.5 0.0 copy-done.3
  6.5 0.1 collective-permute-start
  7.9 0.1 pad_maximum_fusion.params
  7.9 0.0 collective-permute-done.mate_ids
  8.0 0.0 collective-permute-done.2.mate_b
  8.0 0.0 collective-permute-done.1.mate_a
  8.0 0.0 copy-done.1
  8.0 0.0 copy-start.2
  8.0 1.3 %copy-done.2 = f32[256,1152]{1,0:T(8,128)S(1)} copy-done((f32[256,1152]{1,0:T(8,128)S(1)}, f32[256,1152]{1,0:T(8,128)}, u32[]{:S(2)}) %copy-start.2) | copy-done | bytes 1179672
  9.3 3.1 %own.1 = (bf16[192,1152]{1,0:T(8,128)(2,1)S(1)}, bf16[64,1152]{1,0:T(8,128)(2,1)S(1)}, f32[256,1152]{1,0:T(8,128)S(1)}, f32[1,256]{1,0:T(1,128)S(1)}) custom-call(s32[1]{0:T(128)} %bitcast.1.flags, f32[2]{0:T(128)S(1)} %pad_maximum_fusion.params, s32[1,256]{1,0:T(1,128)S(1)} %bitcast.5, s32[1,256]{1,0:T(1,128)S(1)} %collective-permute-done.mate_ids, ...), custom_call_target="tpu_custom_call" | custom-call | tf_op jit(solution)/shard_map/own/pallas_call | solution.py:147
  12.4 1.5 %collective-permute-start.7 = (bf16[192,1152]{1,0:T(8,128)(2,1)S(1)}, bf16[192,1152]{1,0:T(8,128)(2,1)S(1)}, u32[]{:S(2)}, u32[]{:S(2)}) collective-permute-start(bf16[192,1152]{1,0:T(8,128)(2,1)S(1)} %get-tuple-element.32), channel_id=1, source_target_pairs={{0,2},{1,3},{2,4},{3,5},{4,6},{5,7},{6,8},{7,9},{8,10},{9,11},{10,... | collective-permute-start | bytes 1327112 | tf_op jit(solution)/shard_map/ppermute | solution.py:185
  13.9 10.7 %collective-permute-done.3.far = bf16[264,1152]{1,0:T(8,128)(2,1)S(1)} collective-permute-done((bf16[264,1152]{1,0:T(8,128)(2,1)}, bf16[264,1152]{1,0:T(8,128)(2,1)S(1)}, u32[]{:S(2)}, u32[]{:S(2)}) %collective-permute-start.3) | collective-permute-done | bytes 608288 | tf_op jit(solution)/shard_map/ppermute | solution.py:185
  24.7 0.1 collective-permute-start.5
  24.7 0.5 %collective-permute-start.4 = (bf16[128,1152]{1,0:T(8,128)(2,1)S(1)}, bf16[128,1152]{1,0:T(8,128)(2,1)S(1)}, u32[]{:S(2)}, u32[]{:S(2)}) collective-permute-start(bf16[128,1152]{1,0:T(8,128)(2,1)S(1)} %get-tuple-element.21), channel_id=1, source_target_pairs={{0,1},{1,0},{2,3},{3,2},{4,5},{5,4},{6,7},{7,6},{8,9},{9,8},{10,11... | collective-permute-start | bytes 884744 | tf_op jit(solution)/shard_map/ppermute | solution.py:188
  25.2 0.0 collective-permute-start.6
  25.2 1.8 %far.1 = (f32[256,1152]{1,0:T(8,128)S(1)}, f32[256,1152]{1,0:T(8,128)S(1)}, f32[1,256]{1,0:T(1,128)S(1)}) custom-call(s32[1]{0:T(128)} %bitcast.1.flags, f32[2]{0:T(128)S(1)} %pad_maximum_fusion.params, s32[1,256]{1,0:T(1,128)S(1)} %bitcast.6, s32[1,256]{1,0:T(1,128)S(1)} %collective-permute-done.mate_ids, bf16[256,1152]{1,0:T(8,128)(2,1)S(1)} %copy-done, ...), custom_call_target="tpu_custom_call" | custom-call | tf_op jit(solution)/shard_map/far/pallas_call | solution.py:147
  27.1 0.0 collective-permute-done.4.near_a
  27.1 0.0 collective-permute-done.5.near_b
  27.1 2.4 %near.1 = (bf16[256,1152]{1,0:T(8,128)(2,1)}, f32[1,256]{1,0:T(1,128)}) custom-call(f32[2]{0:T(128)S(1)} %pad_maximum_fusion.params, s32[1,256]{1,0:T(1,128)S(1)} %bitcast.7, bf16[256,1152]{1,0:T(8,128)(2,1)S(1)} %copy-done, bf16[128,1152]{1,0:T(8,128)(2,1)S(1)} %collective-permute-done.4.near_a, bf16[136,1152]{1,0:T(8,128)(2,1)S(1)} %collective-permute-done.5.near_b, ...), custom_call_target="tpu_custom_call" | custom-call | tf_op jit(solution)/shard_map/near/pallas_call | solution.py:147
  29.5 4.6 %collective-permute-done.7.arrived = bf16[192,1152]{1,0:T(8,128)(2,1)S(1)} collective-permute-done((bf16[192,1152]{1,0:T(8,128)(2,1)S(1)}, bf16[192,1152]{1,0:T(8,128)(2,1)S(1)}, u32[]{:S(2)}, u32[]{:S(2)}) %collective-permute-start.7) | collective-permute-done | bytes 442400 | tf_op jit(solution)/shard_map/ppermute | solution.py:185
  34.1 1.0 %add_a.1.refs_0_ = f32[256,1152]{1,0:T(8,128)} custom-call(bf16[192,1152]{1,0:T(8,128)(2,1)S(1)} %collective-permute-done.7.arrived, f32[256,1152]{1,0:T(8,128)S(1)} %get-tuple-element.31.late), custom_call_target="tpu_custom_call" | custom-call | tf_op jit(solution)/shard_map/add_a/pallas_call | solution.py:159
  35.1 1.4 %collective-permute-done.6.arrived = bf16[64,1152]{1,0:T(8,128)(2,1)S(1)} collective-permute-done((bf16[64,1152]{1,0:T(8,128)(2,1)S(1)}, bf16[64,1152]{1,0:T(8,128)(2,1)S(1)}, u32[]{:S(2)}, u32[]{:S(2)}) %collective-permute-start.6) | collective-permute-done | bytes 147488 | tf_op jit(solution)/shard_map/ppermute | solution.py:185
  36.4 0.7 %add_b.1 = f32[256,1152]{1,0:T(8,128)} custom-call(bf16[64,1152]{1,0:T(8,128)(2,1)S(1)} %collective-permute-done.6.arrived, f32[256,1152]{1,0:T(8,128)S(1)} %get-tuple-element.31.late, f32[256,1152]{1,0:T(8,128)} %add_a.1.refs_0_), custom_call_target="tpu_custom_call", output_to_operand_aliasing={{}: (2, {})} | custom-call | tf_op jit(solution)/shard_map/add_b/pallas_call | solution.py:159
  (2 shorter events, 0.1 us)
Async XLA Ops:
  0.6 5.2 %copy-start = (bf16[256,1152]{1,0:T(8,128)(2,1)S(1)}, bf16[256,1152]{1,0:T(8,128)(2,1)}, u32[]{:S(2)}) copy-start(bf16[256,1152]{1,0:T(8,128)(2,1)} %image.2) | copy-start | bytes 1769476
  0.6 5.9 %copy-start.3 = (s32[256]{0:T(256)S(1)}, s32[256]{0:T(256)}, u32[]{:S(2)}) copy-start(s32[256]{0:T(256)} %param.9) | copy-start | bytes 3076
  2.8 5.2 %copy-start.1 = (bf16[264,1152]{1,0:T(8,128)(2,1)S(1)}, bf16[264,1152]{1,0:T(8,128)(2,1)}, u32[]{:S(2)}) copy-start(bf16[264,1152]{1,0:T(8,128)(2,1)} %cast.1.text) | copy-start | bytes 1824772
  2.8 21.8 %collective-permute-start.3 = (bf16[264,1152]{1,0:T(8,128)(2,1)}, bf16[264,1152]{1,0:T(8,128)(2,1)S(1)}, u32[]{:S(2)}, u32[]{:S(2)}) collective-permute-start(bf16[264,1152]{1,0:T(8,128)(2,1)} %cast.1.text), channel_id=1, source_target_pairs={{0,2},{1,3},{2,4},{3,5},{4,6},{5,7},{6,8},{7,9},{8,10},{9,11},{10,... | collective-permute-start | bytes 1824776 | tf_op jit(solution)/shard_map/ppermute | solution.py:185
  5.9 2.1 %collective-permute-start.2 = (bf16[128,1152]{1,0:T(8,128)(2,1)S(1)}, bf16[128,1152]{1,0:T(8,128)(2,1)S(1)}, u32[]{:S(2)}, u32[]{:S(2)}) collective-permute-start(bf16[128,1152]{1,0:T(8,128)(2,1)S(1)} %get-tuple-element.33), channel_id=1, source_target_pairs={{0,1},{1,0},{2,3},{3,2},{4,5},{5,4},{6,7},{7,6},{8,9},{9,8},{10,11... | collective-permute-start | bytes 884744 | tf_op jit(solution)/shard_map/ppermute | solution.py:188
  6.0 2.0 %collective-permute-start.1 = (bf16[128,1152]{1,0:T(8,128)(2,1)S(1)}, bf16[128,1152]{1,0:T(8,128)(2,1)S(1)}, u32[]{:S(2)}, u32[]{:S(2)}) collective-permute-start(bf16[128,1152]{1,0:T(8,128)(2,1)S(1)} %get-tuple-element.34), channel_id=1, source_target_pairs={{0,1},{1,0},{2,3},{3,2},{4,5},{5,4},{6,7},{7,6},{8,9},{9,8},{10,11... | collective-permute-start | bytes 884744 | tf_op jit(solution)/shard_map/ppermute | solution.py:188
  6.5 1.5 %collective-permute-start = (s32[1,256]{1,0:T(1,128)S(1)}, s32[1,256]{1,0:T(1,128)S(1)}, u32[]{:S(2)}, u32[]{:S(2)}) collective-permute-start(s32[1,256]{1,0:T(1,128)S(1)} %bitcast.4), channel_id=1, source_target_pairs={{0,1},{1,0},{2,3},{3,2},{4,5},{5,4},{6,7},{7,6},{8,9},{9,8},{10,11... | collective-permute-start | bytes 3080 | tf_op jit(solution)/shard_map/ppermute | solution.py:188
  8.0 1.3 %copy-start.2 = (f32[256,1152]{1,0:T(8,128)S(1)}, f32[256,1152]{1,0:T(8,128)}, u32[]{:S(2)}) copy-start(f32[256,1152]{1,0:T(8,128)} %accum.1) | copy-start | bytes 3538948
  12.4 21.7 %collective-permute-start.7 = (bf16[192,1152]{1,0:T(8,128)(2,1)S(1)}, bf16[192,1152]{1,0:T(8,128)(2,1)S(1)}, u32[]{:S(2)}, u32[]{:S(2)}) collective-permute-start(bf16[192,1152]{1,0:T(8,128)(2,1)S(1)} %get-tuple-element.32), channel_id=1, source_target_pairs={{0,2},{1,3},{2,4},{3,5},{4,6},{5,7},{6,8},{7,9},{8,10},{9,11},{10,... | collective-permute-start | bytes 1327112 | tf_op jit(solution)/shard_map/ppermute | solution.py:185
  24.7 2.4 %collective-permute-start.5 = (bf16[136,1152]{1,0:T(8,128)(2,1)S(1)}, bf16[136,1152]{1,0:T(8,128)(2,1)S(1)}, u32[]{:S(2)}, u32[]{:S(2)}) collective-permute-start(bf16[136,1152]{1,0:T(8,128)(2,1)S(1)} %get-tuple-element.22), channel_id=1, source_target_pairs={{0,1},{1,0},{2,3},{3,2},{4,5},{5,4},{6,7},{7,6},{8,9},{9,8},{10,11... | collective-permute-start | bytes 940040 | tf_op jit(solution)/shard_map/ppermute | solution.py:188
  24.7 2.3 %collective-permute-start.4 = (bf16[128,1152]{1,0:T(8,128)(2,1)S(1)}, bf16[128,1152]{1,0:T(8,128)(2,1)S(1)}, u32[]{:S(2)}, u32[]{:S(2)}) collective-permute-start(bf16[128,1152]{1,0:T(8,128)(2,1)S(1)} %get-tuple-element.21), channel_id=1, source_target_pairs={{0,1},{1,0},{2,3},{3,2},{4,5},{5,4},{6,7},{7,6},{8,9},{9,8},{10,11... | collective-permute-start | bytes 884744 | tf_op jit(solution)/shard_map/ppermute | solution.py:188
  25.2 11.2 %collective-permute-start.6 = (bf16[64,1152]{1,0:T(8,128)(2,1)S(1)}, bf16[64,1152]{1,0:T(8,128)(2,1)S(1)}, u32[]{:S(2)}, u32[]{:S(2)}) collective-permute-start(bf16[64,1152]{1,0:T(8,128)(2,1)S(1)} %get-tuple-element.30), channel_id=1, source_target_pairs={{0,2},{1,3},{2,4},{3,5},{4,6},{5,7},{6,8},{7,9},{8,10},{9,11},{10,... | collective-permute-start | bytes 442376 | tf_op jit(solution)/shard_map/ppermute | solution.py:185

commit v7 on v6

--- a/solution.py
+++ b/solution.py
@@ -198,10 +198,10 @@
             pltpu.SemaphoreType.DMA((CHUNKS,)),
             pltpu.SemaphoreType.DMA,
         ],
-        compiler_params=pltpu.CompilerParams(vmem_limit_bytes=63 * 1024 * 1024),
+        compiler_params=pltpu.CompilerParams(vmem_limit_bytes=16 * 1024 * 1024),
         cost_estimate=pl.CostEstimate(flops=0, bytes_accessed=0, transcendentals=0),
         name="cast",
-    )(ids, text_emb)
+    )(*(pltpu.with_memory_space_constraint(value, pltpu.HBM) for value in (ids, text_emb)))
     far = ahead(text)
 
     image, text = lax.optimization_barrier((image_emb, text))

time: 37.4 us -> 36.3 us (0.971)
  Pallas kernels: 11.3 us -> 10.5 us
    pallas_call x1, Pallas kernels: 2.18 us -> 1.36 us  [body(): pl.pallas_call(cast_kernel, out_shape=jax.ShapeDtypeStruct((rows + PAD, w...]
    unnamed x8 -> x6, local copies, waits for them, and re-layouts: 1.28 us -> 1.28 us
where the time goes in v7:
time: 36.3 us; the launch traced here: 36.1 us
  waiting for transfers between devices  16.4 us (45%)
  Pallas kernels  10.5 us (29%)
  starting transfers between devices  5.72 us (16%)
  between operations  2.03 us (6%)
  local copies, waits for them, and re-layouts  1.32 us (4%)
    ppermute x3, waiting for transfers between devices, ahead(): return lax.ppermute(value, AXES, skip)  16.4 us
    pallas_call x4, Pallas kernels, call(): pl.pallas_call(kernel, out_shape=[jax.ShapeDtypeStruct(s, d) for s, d in...  7.44 us
    ppermute x3, starting transfers between devices, ahead(): return lax.ppermute(value, AXES, skip)  4.51 us
    pallas_call x2, Pallas kernels, add_part(): pl.pallas_call(functools.partial(add_kernel, start, chunks), out_shape=ja...  1.72 us
    pallas_call x1, Pallas kernels, body(): pl.pallas_call(cast_kernel, out_shape=jax.ShapeDtypeStruct((rows + PAD, w...  1.36 us
    unnamed x6, local copies, waits for them, and re-layouts  1.28 us
    ppermute x5, starting transfers between devices, across(): return lax.ppermute(value, AXES, swap)  1.21 us
  transfers between devices with their start and end apart: 8, of which 3 were waited for; matrix products, arithmetic and copies ran while one was open for 0% of the time, Pallas kernels for 23%

profile of v7, /device:TPU:0, one launch (start us, length us, event | category | flops | bytes accessed | tf_op | source)
XLA Modules:
  0.0 36.1 jit_solution(11786536490414666077)
XLA Ops:
  0.6 0.0 copy-start
  0.6 0.0 copy-start.2
  0.7 1.4 %cast.1.text = bf16[264,1152]{1,0:T(8,128)(2,1)S(1)} custom-call(s32[1,256]{1,0:T(1,128)} %bitcast.3, f32[256,1152]{1,0:T(8,128)} %text.1), custom_call_target="tpu_custom_call" | custom-call | tf_op jit(solution)/shard_map/cast/pallas_call | solution.py:190
  2.0 3.0 %collective-permute-start.3 = (bf16[264,1152]{1,0:T(8,128)(2,1)S(1)}, bf16[264,1152]{1,0:T(8,128)(2,1)S(1)}, u32[]{:S(2)}, u32[]{:S(2)}) collective-permute-start(bf16[264,1152]{1,0:T(8,128)(2,1)S(1)} %cast.1.text), channel_id=1, source_target_pairs={{0,2},{1,3},{2,4},{3,5},{4,6},{5,7},{6,8},{7,9},{8,10},{9,11},{10,... | collective-permute-start | bytes 1824776 | tf_op jit(solution)/shard_map/ppermute | solution.py:185
  5.0 0.0 copy-done
  5.1 0.1 collective-permute-start.2
  5.2 0.5 %collective-permute-start.1 = (bf16[128,1152]{1,0:T(8,128)(2,1)S(1)}, bf16[128,1152]{1,0:T(8,128)(2,1)S(1)}, u32[]{:S(2)}, u32[]{:S(2)}) collective-permute-start(bf16[128,1152]{1,0:T(8,128)(2,1)S(1)} %get-tuple-element.34), channel_id=1, source_target_pairs={{0,1},{1,0},{2,3},{3,2},{4,5},{5,4},{6,7},{7,6},{8,9},{9,8},{10,11... | collective-permute-start | bytes 884744 | tf_op jit(solution)/shard_map/ppermute | solution.py:188
  5.7 0.0 copy-done.2
  5.7 0.1 collective-permute-start
  7.0 0.1 pad_maximum_fusion.params
  7.1 0.0 collective-permute-done.mate_ids
  7.2 0.0 collective-permute-done.2.mate_b
  7.2 0.0 collective-permute-done.1.mate_a
  7.2 0.0 copy-start.1
  7.2 1.3 %copy-done.1 = f32[256,1152]{1,0:T(8,128)S(1)} copy-done((f32[256,1152]{1,0:T(8,128)S(1)}, f32[256,1152]{1,0:T(8,128)}, u32[]{:S(2)}) %copy-start.1) | copy-done | bytes 1179672
  8.4 3.1 %own.1 = (bf16[192,1152]{1,0:T(8,128)(2,1)S(1)}, bf16[64,1152]{1,0:T(8,128)(2,1)S(1)}, f32[256,1152]{1,0:T(8,128)S(1)}, f32[1,256]{1,0:T(1,128)S(1)}) custom-call(s32[1]{0:T(128)} %bitcast.1.flags, f32[2]{0:T(128)S(1)} %pad_maximum_fusion.params, s32[1,256]{1,0:T(1,128)S(1)} %bitcast.5, s32[1,256]{1,0:T(1,128)S(1)} %collective-permute-done.mate_ids, ...), custom_call_target="tpu_custom_call" | custom-call | tf_op jit(solution)/shard_map/own/pallas_call | solution.py:147
  11.6 1.5 %collective-permute-start.7 = (bf16[192,1152]{1,0:T(8,128)(2,1)S(1)}, bf16[192,1152]{1,0:T(8,128)(2,1)S(1)}, u32[]{:S(2)}, u32[]{:S(2)}) collective-permute-start(bf16[192,1152]{1,0:T(8,128)(2,1)S(1)} %get-tuple-element.32), channel_id=1, source_target_pairs={{0,2},{1,3},{2,4},{3,5},{4,6},{5,7},{6,8},{7,9},{8,10},{9,11},{10,... | collective-permute-start | bytes 1327112 | tf_op jit(solution)/shard_map/ppermute | solution.py:185
  13.1 10.5 %collective-permute-done.3.far = bf16[264,1152]{1,0:T(8,128)(2,1)S(1)} collective-permute-done((bf16[264,1152]{1,0:T(8,128)(2,1)S(1)}, bf16[264,1152]{1,0:T(8,128)(2,1)S(1)}, u32[]{:S(2)}, u32[]{:S(2)}) %collective-permute-start.3) | collective-permute-done | bytes 608288 | tf_op jit(solution)/shard_map/ppermute | solution.py:185
  23.6 0.1 collective-permute-start.5
  23.7 0.5 %collective-permute-start.4 = (bf16[128,1152]{1,0:T(8,128)(2,1)S(1)}, bf16[128,1152]{1,0:T(8,128)(2,1)S(1)}, u32[]{:S(2)}, u32[]{:S(2)}) collective-permute-start(bf16[128,1152]{1,0:T(8,128)(2,1)S(1)} %get-tuple-element.21), channel_id=1, source_target_pairs={{0,1},{1,0},{2,3},{3,2},{4,5},{5,4},{6,7},{7,6},{8,9},{9,8},{10,11... | collective-permute-start | bytes 884744 | tf_op jit(solution)/shard_map/ppermute | solution.py:188
  24.2 0.0 collective-permute-start.6
  24.2 1.8 %far.1 = (f32[256,1152]{1,0:T(8,128)S(1)}, f32[256,1152]{1,0:T(8,128)S(1)}, f32[1,256]{1,0:T(1,128)S(1)}) custom-call(s32[1]{0:T(128)} %bitcast.1.flags, f32[2]{0:T(128)S(1)} %pad_maximum_fusion.params, s32[1,256]{1,0:T(1,128)S(1)} %bitcast.6, s32[1,256]{1,0:T(1,128)S(1)} %collective-permute-done.mate_ids, bf16[256,1152]{1,0:T(8,128)(2,1)S(1)} %copy-done, ...), custom_call_target="tpu_custom_call" | custom-call | tf_op jit(solution)/shard_map/far/pallas_call | solution.py:147
  26.0 0.0 collective-permute-done.4.near_a
  26.0 0.0 collective-permute-done.5.near_b
  26.0 2.4 %near.1 = (bf16[256,1152]{1,0:T(8,128)(2,1)}, f32[1,256]{1,0:T(1,128)}) custom-call(f32[2]{0:T(128)S(1)} %pad_maximum_fusion.params, s32[1,256]{1,0:T(1,128)S(1)} %bitcast.7, bf16[256,1152]{1,0:T(8,128)(2,1)S(1)} %copy-done, bf16[128,1152]{1,0:T(8,128)(2,1)S(1)} %collective-permute-done.4.near_a, bf16[136,1152]{1,0:T(8,128)(2,1)S(1)} %collective-permute-done.5.near_b, ...), custom_call_target="tpu_custom_call" | custom-call | tf_op jit(solution)/shard_map/near/pallas_call | solution.py:147
  28.5 4.6 %collective-permute-done.7.arrived = bf16[192,1152]{1,0:T(8,128)(2,1)S(1)} collective-permute-done((bf16[192,1152]{1,0:T(8,128)(2,1)S(1)}, bf16[192,1152]{1,0:T(8,128)(2,1)S(1)}, u32[]{:S(2)}, u32[]{:S(2)}) %collective-permute-start.7) | collective-permute-done | bytes 442400 | tf_op jit(solution)/shard_map/ppermute | solution.py:185
  33.0 1.0 %add_a.1.refs_0_ = f32[256,1152]{1,0:T(8,128)} custom-call(bf16[192,1152]{1,0:T(8,128)(2,1)S(1)} %collective-permute-done.7.arrived, f32[256,1152]{1,0:T(8,128)S(1)} %get-tuple-element.31.late), custom_call_target="tpu_custom_call" | custom-call | tf_op jit(solution)/shard_map/add_a/pallas_call | solution.py:159
  34.0 1.4 %collective-permute-done.6.arrived = bf16[64,1152]{1,0:T(8,128)(2,1)S(1)} collective-permute-done((bf16[64,1152]{1,0:T(8,128)(2,1)S(1)}, bf16[64,1152]{1,0:T(8,128)(2,1)S(1)}, u32[]{:S(2)}, u32[]{:S(2)}) %collective-permute-start.6) | collective-permute-done | bytes 147488 | tf_op jit(solution)/shard_map/ppermute | solution.py:185
  35.4 0.7 %add_b.1 = f32[256,1152]{1,0:T(8,128)} custom-call(bf16[64,1152]{1,0:T(8,128)(2,1)S(1)} %collective-permute-done.6.arrived, f32[256,1152]{1,0:T(8,128)S(1)} %get-tuple-element.31.late, f32[256,1152]{1,0:T(8,128)} %add_a.1.refs_0_), custom_call_target="tpu_custom_call", output_to_operand_aliasing={{}: (2, {})} | custom-call | tf_op jit(solution)/shard_map/add_b/pallas_call | solution.py:159
  (2 shorter events, 0.1 us)
Async XLA Ops:
  0.6 4.4 %copy-start = (bf16[256,1152]{1,0:T(8,128)(2,1)S(1)}, bf16[256,1152]{1,0:T(8,128)(2,1)}, u32[]{:S(2)}) copy-start(bf16[256,1152]{1,0:T(8,128)(2,1)} %image.2) | copy-start | bytes 1769476
  0.6 5.0 %copy-start.2 = (s32[256]{0:T(256)S(1)}, s32[256]{0:T(256)}, u32[]{:S(2)}) copy-start(s32[256]{0:T(256)} %param.9) | copy-start | bytes 3076
  2.0 21.5 %collective-permute-start.3 = (bf16[264,1152]{1,0:T(8,128)(2,1)S(1)}, bf16[264,1152]{1,0:T(8,128)(2,1)S(1)}, u32[]{:S(2)}, u32[]{:S(2)}) collective-permute-start(bf16[264,1152]{1,0:T(8,128)(2,1)S(1)} %cast.1.text), channel_id=1, source_target_pairs={{0,2},{1,3},{2,4},{3,5},{4,6},{5,7},{6,8},{7,9},{8,10},{9,11},{10,... | collective-permute-start | bytes 1824776 | tf_op jit(solution)/shard_map/ppermute | solution.py:185
  5.1 2.1 %collective-permute-start.2 = (bf16[128,1152]{1,0:T(8,128)(2,1)S(1)}, bf16[128,1152]{1,0:T(8,128)(2,1)S(1)}, u32[]{:S(2)}, u32[]{:S(2)}) collective-permute-start(bf16[128,1152]{1,0:T(8,128)(2,1)S(1)} %get-tuple-element.33), channel_id=1, source_target_pairs={{0,1},{1,0},{2,3},{3,2},{4,5},{5,4},{6,7},{7,6},{8,9},{9,8},{10,11... | collective-permute-start | bytes 884744 | tf_op jit(solution)/shard_map/ppermute | solution.py:188
  5.2 2.0 %collective-permute-start.1 = (bf16[128,1152]{1,0:T(8,128)(2,1)S(1)}, bf16[128,1152]{1,0:T(8,128)(2,1)S(1)}, u32[]{:S(2)}, u32[]{:S(2)}) collective-permute-start(bf16[128,1152]{1,0:T(8,128)(2,1)S(1)} %get-tuple-element.34), channel_id=1, source_target_pairs={{0,1},{1,0},{2,3},{3,2},{4,5},{5,4},{6,7},{7,6},{8,9},{9,8},{10,11... | collective-permute-start | bytes 884744 | tf_op jit(solution)/shard_map/ppermute | solution.py:188
  5.7 1.5 %collective-permute-start = (s32[1,256]{1,0:T(1,128)S(1)}, s32[1,256]{1,0:T(1,128)S(1)}, u32[]{:S(2)}, u32[]{:S(2)}) collective-permute-start(s32[1,256]{1,0:T(1,128)S(1)} %bitcast.4), channel_id=1, source_target_pairs={{0,1},{1,0},{2,3},{3,2},{4,5},{5,4},{6,7},{7,6},{8,9},{9,8},{10,11... | collective-permute-start | bytes 3080 | tf_op jit(solution)/shard_map/ppermute | solution.py:188
  7.2 1.3 %copy-start.1 = (f32[256,1152]{1,0:T(8,128)S(1)}, f32[256,1152]{1,0:T(8,128)}, u32[]{:S(2)}) copy-start(f32[256,1152]{1,0:T(8,128)} %accum.1) | copy-start | bytes 3538948
  11.6 21.5 %collective-permute-start.7 = (bf16[192,1152]{1,0:T(8,128)(2,1)S(1)}, bf16[192,1152]{1,0:T(8,128)(2,1)S(1)}, u32[]{:S(2)}, u32[]{:S(2)}) collective-permute-start(bf16[192,1152]{1,0:T(8,128)(2,1)S(1)} %get-tuple-element.32), channel_id=1, source_target_pairs={{0,2},{1,3},{2,4},{3,5},{4,6},{5,7},{6,8},{7,9},{8,10},{9,11},{10,... | collective-permute-start | bytes 1327112 | tf_op jit(solution)/shard_map/ppermute | solution.py:185
  23.6 2.4 %collective-permute-start.5 = (bf16[136,1152]{1,0:T(8,128)(2,1)S(1)}, bf16[136,1152]{1,0:T(8,128)(2,1)S(1)}, u32[]{:S(2)}, u32[]{:S(2)}) collective-permute-start(bf16[136,1152]{1,0:T(8,128)(2,1)S(1)} %get-tuple-element.22), channel_id=1, source_target_pairs={{0,1},{1,0},{2,3},{3,2},{4,5},{5,4},{6,7},{7,6},{8,9},{9,8},{10,11... | collective-permute-start | bytes 940040 | tf_op jit(solution)/shard_map/ppermute | solution.py:188
  23.7 2.3 %collective-permute-start.4 = (bf16[128,1152]{1,0:T(8,128)(2,1)S(1)}, bf16[128,1152]{1,0:T(8,128)(2,1)S(1)}, u32[]{:S(2)}, u32[]{:S(2)}) collective-permute-start(bf16[128,1152]{1,0:T(8,128)(2,1)S(1)} %get-tuple-element.21), channel_id=1, source_target_pairs={{0,1},{1,0},{2,3},{3,2},{4,5},{5,4},{6,7},{7,6},{8,9},{9,8},{10,11... | collective-permute-start | bytes 884744 | tf_op jit(solution)/shard_map/ppermute | solution.py:188
  24.2 11.2 %collective-permute-start.6 = (bf16[64,1152]{1,0:T(8,128)(2,1)S(1)}, bf16[64,1152]{1,0:T(8,128)(2,1)S(1)}, u32[]{:S(2)}, u32[]{:S(2)}) collective-permute-start(bf16[64,1152]{1,0:T(8,128)(2,1)S(1)} %get-tuple-element.30), channel_id=1, source_target_pairs={{0,2},{1,3},{2,4},{3,5},{4,6},{5,7},{6,8},{7,9},{8,10},{9,11},{10,... | collective-permute-start | bytes 442376 | tf_op jit(solution)/shard_map/ppermute | solution.py:185

commit v8 on v7

--- a/solution.py
+++ b/solution.py
@@ -67,13 +67,13 @@
     out[rows:, :rows] = parts.astype(jnp.float32).astype(out.dtype)
 
 
-def add_kernel(start, chunks, arrived, late, *refs):
-    out, staged, sems = refs[-3:]
-    step = arrived.shape[0] // chunks
+def add_kernel(start, chunks, count, late, *refs):
+    arrived, (out, staged, sems) = refs[:count], refs[-3:]
+    step = staged.shape[0] // chunks
     copies = []
     for k in range(chunks):
         here, there = pl.ds(k * step, step), pl.ds(start + k * step, step)
-        staged[here, :] = arrived[here, :].astype(staged.dtype) + late[there, :]
+        staged[here, :] = sum((part[here, :].astype(staged.dtype) for part in arrived), late[there, :])
         copies.append(pltpu.make_async_copy(staged.at[here], out.at[there], sems.at[k]))
         copies[-1].start()
     for copy in copies:
@@ -155,18 +155,18 @@
     )(*scalars, *operands)
 
 
-def add_part(name, start, chunks, arrived, late, *before):
+def add_part(name, start, chunks, late, arrived, *before):
     return pl.pallas_call(
-        functools.partial(add_kernel, start, chunks),
+        functools.partial(add_kernel, start, chunks, len(arrived)),
         out_shape=jax.ShapeDtypeStruct(late.shape, late.dtype),
-        in_specs=[VMEM, VMEM] + [HBM] * len(before),
+        in_specs=[VMEM] * (1 + len(arrived)) + [HBM] * len(before),
         out_specs=HBM,
-        scratch_shapes=[pltpu.VMEM(arrived.shape, late.dtype), pltpu.SemaphoreType.DMA((chunks,))],
-        input_output_aliases={2: 0} if before else {},
+        scratch_shapes=[pltpu.VMEM(arrived[0].shape, late.dtype), pltpu.SemaphoreType.DMA((chunks,))],
+        input_output_aliases={1 + len(arrived): 0} if before else {},
         compiler_params=pltpu.CompilerParams(vmem_limit_bytes=16 * 1024 * 1024),
         cost_estimate=pl.CostEstimate(flops=0, bytes_accessed=0, transcendentals=0),
         name=name,
-    )(arrived, late, *before)
+    )(late, *arrived, *before)
 
 
 def body(image_emb, text_emb, text_accum, pair_ids, log_scale, bias):
@@ -209,16 +209,20 @@
     mate_a, mate_b = across(image[:half]), across(image[half:])
     mate_ids = across(ids)
 
-    cut = rows - rows // 4
+    cut = rows - rows * 3 // 16
     out_a, out_b, image_sum, loss = call(
         own_kernel, "own", [((cut, width), bf16), ((rows - cut, width), bf16), ((rows, width), f32), ((1, rows), f32)],
         (flags, params), ids, mate_ids, image_emb, mate_a, mate_b, text, text_accum,
     )
-    arrived_a, arrived_b = ahead(out_a), ahead(out_b)
+    turn = count - 4
+    arrived_a = ahead(out_a)
+    to_turn = lax.ppermute(out_b, AXES, [(count - 2, turn), (count - 1, turn + 1)])
+    turned = lax.ppermute(to_turn, AXES, [(turn, 0), (turn + 1, 1)])
+    arrived_b = lax.ppermute(out_b, AXES, skip[:-2])
 
     passed_a, passed_b = call(
         relay_kernel, "relay", [((half, width), bf16), ((rows + PAD - half, width), bf16)],
-        (flags,), loss, text, far,
+        (flags,), lax.optimization_barrier((loss, to_turn))[0], text, far,
     )
     near_a, near_b = across(passed_a), across(passed_b)
     late, image_sum, loss = call(
@@ -230,8 +234,8 @@
         (params,), ids, image_emb, near_a, near_b, image_sum, loss,
     )
     late, image_grad = lax.optimization_barrier((late, image_grad))
-    text_grad = add_part("add_a", 0, CHUNKS, arrived_a, late)
-    text_grad = add_part("add_b", cut, 2, arrived_b, late, text_grad)
+    text_grad = add_part("add_a", 0, 2, late, (arrived_a,))
+    text_grad = add_part("add_b", cut, 1, late, (arrived_b, turned), text_grad)
     return (loss.reshape(rows), image_grad, text_grad)
 
 

time: 36.3 us -> 45.1 us (1.24)
  waiting for transfers between devices: 16.4 us -> 22 us
  starting transfers between devices: 5.72 us -> 8.95 us
    ppermute x0 -> x3, waiting for transfers between devices: none -> 10.2 us  [the longest x1 10.2 us: body(): turned = lax.ppermute(to_turn, AXES, [(turn, 0), (turn + 1, 1)])]
    ppermute x3 -> x2, waiting for transfers between devices: 16.4 us -> 11.7 us  [ahead(): return lax.ppermute(value, AXES, skip)]
    ppermute x0 -> x3, starting transfers between devices: none -> 3.23 us  [the longest x1 1.29 us: body(): turned = lax.ppermute(to_turn, AXES, [(turn, 0), (turn + 1, 1)])]
    ppermute x3 -> x2, starting transfers between devices: 4.51 us -> 4.51 us  [ahead(): return lax.ppermute(value, AXES, skip)]
  transfers between devices with their start and end apart: 8 -> 10, of which waited for: 3 -> 3; matrix products, arithmetic and copies ran while one was open for 0% -> 0% of each run, Pallas kernels for 23% -> 19%
where the time goes in v8:
time: 45.1 us; the launch traced here: 44.9 us
  waiting for transfers between devices  22 us (49%)
  Pallas kernels  10.5 us (23%)
  starting transfers between devices  8.95 us (20%)
  between operations  2.07 us (5%)
  local copies, waits for them, and re-layouts  1.32 us (3%)
    ppermute x2, waiting for transfers between devices, ahead(): return lax.ppermute(value, AXES, skip)  11.7 us
    ppermute x1, waiting for transfers between devices, body(): turned = lax.ppermute(to_turn, AXES, [(turn, 0), (turn + 1, 1)])  10.2 us
    pallas_call x4, Pallas kernels, call(): pl.pallas_call(kernel, out_shape=[jax.ShapeDtypeStruct(s, d) for s, d in...  7.44 us
    ppermute x2, starting transfers between devices, ahead(): return lax.ppermute(value, AXES, skip)  4.51 us
    pallas_call x2, Pallas kernels, add_part(): pl.pallas_call(functools.partial(add_kernel, start, chunks, len(arrived))...  1.73 us
    pallas_call x1, Pallas kernels, body(): pl.pallas_call(cast_kernel, out_shape=jax.ShapeDtypeStruct((rows + PAD, w...  1.36 us
    ppermute x1, starting transfers between devices, body(): turned = lax.ppermute(to_turn, AXES, [(turn, 0), (turn + 1, 1)])  1.29 us
    ppermute x1, starting transfers between devices, body(): arrived_b = lax.ppermute(out_b, AXES, skip[:-2])  1.28 us
  transfers between devices with their start and end apart: 10, of which 3 were waited for; matrix products, arithmetic and copies ran while one was open for 0% of the time, Pallas kernels for 19%

profile of v8, /device:TPU:0, one launch (start us, length us, event | category | flops | bytes accessed | tf_op | source)
XLA Modules:
  0.0 44.9 jit_solution(13488098733090578670)
XLA Ops:
  0.6 0.0 copy-start
  0.6 0.0 copy-start.2
  0.7 1.4 %cast.1.text = bf16[264,1152]{1,0:T(8,128)(2,1)S(1)} custom-call(s32[1,256]{1,0:T(1,128)} %bitcast.3, f32[256,1152]{1,0:T(8,128)} %text.1), custom_call_target="tpu_custom_call" | custom-call | tf_op jit(solution)/shard_map/cast/pallas_call | solution.py:190
  2.0 3.0 %collective-permute-start.4 = (bf16[264,1152]{1,0:T(8,128)(2,1)S(1)}, bf16[264,1152]{1,0:T(8,128)(2,1)S(1)}, u32[]{:S(2)}, u32[]{:S(2)}) collective-permute-start(bf16[264,1152]{1,0:T(8,128)(2,1)S(1)} %cast.1.text), channel_id=1, source_target_pairs={{0,2},{1,3},{2,4},{3,5},{4,6},{5,7},{6,8},{7,9},{8,10},{9,11},{10,... | collective-permute-start | bytes 1824776 | tf_op jit(solution)/shard_map/ppermute | solution.py:185
  5.0 0.0 copy-done
  5.1 0.1 collective-permute-start.1
  5.2 0.5 %collective-permute-start.2 = (bf16[128,1152]{1,0:T(8,128)(2,1)S(1)}, bf16[128,1152]{1,0:T(8,128)(2,1)S(1)}, u32[]{:S(2)}, u32[]{:S(2)}) collective-permute-start(bf16[128,1152]{1,0:T(8,128)(2,1)S(1)} %get-tuple-element.35), channel_id=1, source_target_pairs={{0,1},{1,0},{2,3},{3,2},{4,5},{5,4},{6,7},{7,6},{8,9},{9,8},{10,11... | collective-permute-start | bytes 884744 | tf_op jit(solution)/shard_map/ppermute | solution.py:188
  5.7 0.0 copy-done.2
  5.7 0.1 collective-permute-start
  7.0 0.1 pad_maximum_fusion.params
  7.1 0.0 collective-permute-done.mate_ids
  7.2 0.0 collective-permute-done.1.mate_a
  7.2 0.0 collective-permute-done.2.mate_b
  7.2 0.0 copy-start.1
  7.2 1.3 %copy-done.1 = f32[256,1152]{1,0:T(8,128)S(1)} copy-done((f32[256,1152]{1,0:T(8,128)S(1)}, f32[256,1152]{1,0:T(8,128)}, u32[]{:S(2)}) %copy-start.1) | copy-done | bytes 1179672
  8.4 3.1 %own.1 = (bf16[208,1152]{1,0:T(8,128)(2,1)S(1)}, bf16[48,1152]{1,0:T(8,128)(2,1)S(1)}, f32[256,1152]{1,0:T(8,128)S(1)}, f32[1,256]{1,0:T(1,128)S(1)}) custom-call(s32[1]{0:T(128)} %bitcast.1.flags, f32[2]{0:T(128)S(1)} %pad_maximum_fusion.params, s32[1,256]{1,0:T(1,128)S(1)} %bitcast.5, s32[1,256]{1,0:T(1,128)S(1)} %collective-permute-done.mate_ids, ...), custom_call_target="tpu_custom_call" | custom-call | tf_op jit(solution)/shard_map/own/pallas_call | solution.py:147
  11.6 1.5 %collective-permute-start.9 = (bf16[208,1152]{1,0:T(8,128)(2,1)S(1)}, bf16[208,1152]{1,0:T(8,128)(2,1)S(1)}, u32[]{:S(2)}, u32[]{:S(2)}) collective-permute-start(bf16[208,1152]{1,0:T(8,128)(2,1)S(1)} %get-tuple-element.34), channel_id=1, source_target_pairs={{0,2},{1,3},{2,4},{3,5},{4,6},{5,7},{6,8},{7,9},{8,10},{9,11},{10,... | collective-permute-start | bytes 1437704 | tf_op jit(solution)/shard_map/ppermute | solution.py:185
  13.1 0.7 %collective-permute-start.3 = (bf16[48,1152]{1,0:T(8,128)(2,1)S(1)}, bf16[48,1152]{1,0:T(8,128)(2,1)S(1)}, u32[]{:S(2)}, u32[]{:S(2)}) collective-permute-start(bf16[48,1152]{1,0:T(8,128)(2,1)S(1)} %get-tuple-element.22), channel_id=1, source_target_pairs={{30,28},{31,29}} | collective-permute-start | bytes 331784 | tf_op jit(solution)/shard_map/ppermute | solution.py:219
  13.7 0.0 collective-permute-done.3
  13.7 9.8 %collective-permute-done.4.far = bf16[264,1152]{1,0:T(8,128)(2,1)S(1)} collective-permute-done((bf16[264,1152]{1,0:T(8,128)(2,1)S(1)}, bf16[264,1152]{1,0:T(8,128)(2,1)S(1)}, u32[]{:S(2)}, u32[]{:S(2)}) %collective-permute-start.4) | collective-permute-done | bytes 608288 | tf_op jit(solution)/shard_map/ppermute | solution.py:185
  23.6 0.1 collective-permute-start.6
  23.7 0.5 %collective-permute-start.5 = (bf16[128,1152]{1,0:T(8,128)(2,1)S(1)}, bf16[128,1152]{1,0:T(8,128)(2,1)S(1)}, u32[]{:S(2)}, u32[]{:S(2)}) collective-permute-start(bf16[128,1152]{1,0:T(8,128)(2,1)S(1)} %get-tuple-element.24), channel_id=1, source_target_pairs={{0,1},{1,0},{2,3},{3,2},{4,5},{5,4},{6,7},{7,6},{8,9},{9,8},{10,11... | collective-permute-start | bytes 884744 | tf_op jit(solution)/shard_map/ppermute | solution.py:188
  24.2 1.3 %collective-permute-start.7 = (bf16[48,1152]{1,0:T(8,128)(2,1)S(1)}, bf16[48,1152]{1,0:T(8,128)(2,1)S(1)}, u32[]{:S(2)}, u32[]{:S(2)}) collective-permute-start(bf16[48,1152]{1,0:T(8,128)(2,1)S(1)} %get-tuple-element.22), channel_id=1, source_target_pairs={{0,2},{1,3},{2,4},{3,5},{4,6},{5,7},{6,8},{7,9},{8,10},{9,11},{10,... | collective-permute-start | bytes 331784 | tf_op jit(solution)/shard_map/ppermute | solution.py:221
  25.5 1.3 %collective-permute-start.8 = (bf16[48,1152]{1,0:T(8,128)(2,1)S(1)}, bf16[48,1152]{1,0:T(8,128)(2,1)S(1)}, u32[]{:S(2)}, u32[]{:S(2)}) collective-permute-start(bf16[48,1152]{1,0:T(8,128)(2,1)S(1)} %collective-permute-done.3), channel_id=1, source_target_pairs={{28,0},{29,1}} | collective-permute-start | bytes 331784 | tf_op jit(solution)/shard_map/ppermute | solution.py:220
  26.8 1.8 %far.1 = (f32[256,1152]{1,0:T(8,128)S(1)}, f32[256,1152]{1,0:T(8,128)S(1)}, f32[1,256]{1,0:T(1,128)S(1)}) custom-call(s32[1]{0:T(128)} %bitcast.1.flags, f32[2]{0:T(128)S(1)} %pad_maximum_fusion.params, s32[1,256]{1,0:T(1,128)S(1)} %bitcast.6, s32[1,256]{1,0:T(1,128)S(1)} %collective-permute-done.mate_ids, bf16[256,1152]{1,0:T(8,128)(2,1)S(1)} %copy-done, ...), custom_call_target="tpu_custom_call" | custom-call | tf_op jit(solution)/shard_map/far/pallas_call | solution.py:147
  28.6 0.0 collective-permute-done.5.near_a
  28.6 0.0 collective-permute-done.6.near_b
  28.6 2.4 %near.1 = (bf16[256,1152]{1,0:T(8,128)(2,1)}, f32[1,256]{1,0:T(1,128)}) custom-call(f32[2]{0:T(128)S(1)} %pad_maximum_fusion.params, s32[1,256]{1,0:T(1,128)S(1)} %bitcast.7, bf16[256,1152]{1,0:T(8,128)(2,1)S(1)} %copy-done, bf16[128,1152]{1,0:T(8,128)(2,1)S(1)} %collective-permute-done.5.near_a, bf16[136,1152]{1,0:T(8,128)(2,1)S(1)} %collective-permute-done.6.near_b, ...), custom_call_target="tpu_custom_call" | custom-call | tf_op jit(solution)/shard_map/near/pallas_call | solution.py:147
  31.1 1.9 %collective-permute-done.9.refs_0_ = bf16[208,1152]{1,0:T(8,128)(2,1)S(1)} collective-permute-done((bf16[208,1152]{1,0:T(8,128)(2,1)S(1)}, bf16[208,1152]{1,0:T(8,128)(2,1)S(1)}, u32[]{:S(2)}, u32[]{:S(2)}) %collective-permute-start.9) | collective-permute-done | bytes 479264 | tf_op jit(solution)/shard_map/ppermute | solution.py:185
  33.0 1.0 %add_a.1.refs_2_ = f32[256,1152]{1,0:T(8,128)} custom-call(f32[256,1152]{1,0:T(8,128)S(1)} %get-tuple-element.33.late, bf16[208,1152]{1,0:T(8,128)(2,1)S(1)} %collective-permute-done.9.refs_0_), custom_call_target="tpu_custom_call" | custom-call | tf_op jit(solution)/shard_map/add_a/pallas_call | solution.py:159
  34.0 0.0 collective-permute-done.7.refs_0_
  34.0 10.2 %collective-permute-done.8.refs_1_ = bf16[48,1152]{1,0:T(8,128)(2,1)S(1)} collective-permute-done((bf16[48,1152]{1,0:T(8,128)(2,1)S(1)}, bf16[48,1152]{1,0:T(8,128)(2,1)S(1)}, u32[]{:S(2)}, u32[]{:S(2)}) %collective-permute-start.8) | collective-permute-done | bytes 110624 | tf_op jit(solution)/shard_map/ppermute | solution.py:220
  44.2 0.7 %add_b.1 = f32[256,1152]{1,0:T(8,128)} custom-call(f32[256,1152]{1,0:T(8,128)S(1)} %get-tuple-element.33.late, bf16[48,1152]{1,0:T(8,128)(2,1)S(1)} %collective-permute-done.7.refs_0_, bf16[48,1152]{1,0:T(8,128)(2,1)S(1)} %collective-permute-done.8.refs_1_, f32[256,1152]{1,0:T(8,128)} %add_a.1.refs_2_), custom_call_target="tpu_custom_call", output_to_operand_aliasing={{}: (3, {})} | custom-call | tf_op jit(solution)/shard_map/add_b/pallas_call | solution.py:159
  (2 shorter events, 0.1 us)
Async XLA Ops:
  0.6 4.4 %copy-start = (bf16[256,1152]{1,0:T(8,128)(2,1)S(1)}, bf16[256,1152]{1,0:T(8,128)(2,1)}, u32[]{:S(2)}) copy-start(bf16[256,1152]{1,0:T(8,128)(2,1)} %image.2) | copy-start | bytes 1769476
  0.6 5.0 %copy-start.2 = (s32[256]{0:T(256)S(1)}, s32[256]{0:T(256)}, u32[]{:S(2)}) copy-start(s32[256]{0:T(256)} %param.9) | copy-start | bytes 3076
  2.0 21.5 %collective-permute-start.4 = (bf16[264,1152]{1,0:T(8,128)(2,1)S(1)}, bf16[264,1152]{1,0:T(8,128)(2,1)S(1)}, u32[]{:S(2)}, u32[]{:S(2)}) collective-permute-start(bf16[264,1152]{1,0:T(8,128)(2,1)S(1)} %cast.1.text), channel_id=1, source_target_pairs={{0,2},{1,3},{2,4},{3,5},{4,6},{5,7},{6,8},{7,9},{8,10},{9,11},{10,... | collective-permute-start | bytes 1824776 | tf_op jit(solution)/shard_map/ppermute | solution.py:185
  5.1 2.1 %collective-permute-start.1 = (bf16[128,1152]{1,0:T(8,128)(2,1)S(1)}, bf16[128,1152]{1,0:T(8,128)(2,1)S(1)}, u32[]{:S(2)}, u32[]{:S(2)}) collective-permute-start(bf16[128,1152]{1,0:T(8,128)(2,1)S(1)} %get-tuple-element.36), channel_id=1, source_target_pairs={{0,1},{1,0},{2,3},{3,2},{4,5},{5,4},{6,7},{7,6},{8,9},{9,8},{10,11... | collective-permute-start | bytes 884744 | tf_op jit(solution)/shard_map/ppermute | solution.py:188
  5.2 2.0 %collective-permute-start.2 = (bf16[128,1152]{1,0:T(8,128)(2,1)S(1)}, bf16[128,1152]{1,0:T(8,128)(2,1)S(1)}, u32[]{:S(2)}, u32[]{:S(2)}) collective-permute-start(bf16[128,1152]{1,0:T(8,128)(2,1)S(1)} %get-tuple-element.35), channel_id=1, source_target_pairs={{0,1},{1,0},{2,3},{3,2},{4,5},{5,4},{6,7},{7,6},{8,9},{9,8},{10,11... | collective-permute-start | bytes 884744 | tf_op jit(solution)/shard_map/ppermute | solution.py:188
  5.7 1.5 %collective-permute-start = (s32[1,256]{1,0:T(1,128)S(1)}, s32[1,256]{1,0:T(1,128)S(1)}, u32[]{:S(2)}, u32[]{:S(2)}) collective-permute-start(s32[1,256]{1,0:T(1,128)S(1)} %bitcast.4), channel_id=1, source_target_pairs={{0,1},{1,0},{2,3},{3,2},{4,5},{5,4},{6,7},{7,6},{8,9},{9,8},{10,11... | collective-permute-start | bytes 3080 | tf_op jit(solution)/shard_map/ppermute | solution.py:188
  7.2 1.3 %copy-start.1 = (f32[256,1152]{1,0:T(8,128)S(1)}, f32[256,1152]{1,0:T(8,128)}, u32[]{:S(2)}) copy-start(f32[256,1152]{1,0:T(8,128)} %accum.1) | copy-start | bytes 3538948
  11.6 21.4 %collective-permute-start.9 = (bf16[208,1152]{1,0:T(8,128)(2,1)S(1)}, bf16[208,1152]{1,0:T(8,128)(2,1)S(1)}, u32[]{:S(2)}, u32[]{:S(2)}) collective-permute-start(bf16[208,1152]{1,0:T(8,128)(2,1)S(1)} %get-tuple-element.34), channel_id=1, source_target_pairs={{0,2},{1,3},{2,4},{3,5},{4,6},{5,7},{6,8},{7,9},{8,10},{9,11},{10,... | collective-permute-start | bytes 1437704 | tf_op jit(solution)/shard_map/ppermute | solution.py:185
  13.1 0.7 %collective-permute-start.3 = (bf16[48,1152]{1,0:T(8,128)(2,1)S(1)}, bf16[48,1152]{1,0:T(8,128)(2,1)S(1)}, u32[]{:S(2)}, u32[]{:S(2)}) collective-permute-start(bf16[48,1152]{1,0:T(8,128)(2,1)S(1)} %get-tuple-element.22), channel_id=1, source_target_pairs={{30,28},{31,29}} | collective-permute-start | bytes 331784 | tf_op jit(solution)/shard_map/ppermute | solution.py:219
  23.6 5.0 %collective-permute-start.6 = (bf16[136,1152]{1,0:T(8,128)(2,1)S(1)}, bf16[136,1152]{1,0:T(8,128)(2,1)S(1)}, u32[]{:S(2)}, u32[]{:S(2)}) collective-permute-start(bf16[136,1152]{1,0:T(8,128)(2,1)S(1)} %get-tuple-element.25), channel_id=1, source_target_pairs={{0,1},{1,0},{2,3},{3,2},{4,5},{5,4},{6,7},{7,6},{8,9},{9,8},{10,11... | collective-permute-start | bytes 940040 | tf_op jit(solution)/shard_map/ppermute | solution.py:188
  23.7 4.9 %collective-permute-start.5 = (bf16[128,1152]{1,0:T(8,128)(2,1)S(1)}, bf16[128,1152]{1,0:T(8,128)(2,1)S(1)}, u32[]{:S(2)}, u32[]{:S(2)}) collective-permute-start(bf16[128,1152]{1,0:T(8,128)(2,1)S(1)} %get-tuple-element.24), channel_id=1, source_target_pairs={{0,1},{1,0},{2,3},{3,2},{4,5},{5,4},{6,7},{7,6},{8,9},{9,8},{10,11... | collective-permute-start | bytes 884744 | tf_op jit(solution)/shard_map/ppermute | solution.py:188
  24.2 9.8 %collective-permute-start.7 = (bf16[48,1152]{1,0:T(8,128)(2,1)S(1)}, bf16[48,1152]{1,0:T(8,128)(2,1)S(1)}, u32[]{:S(2)}, u32[]{:S(2)}) collective-permute-start(bf16[48,1152]{1,0:T(8,128)(2,1)S(1)} %get-tuple-element.22), channel_id=1, source_target_pairs={{0,2},{1,3},{2,4},{3,5},{4,6},{5,7},{6,8},{7,9},{8,10},{9,11},{10,... | collective-permute-start | bytes 331784 | tf_op jit(solution)/shard_map/ppermute | solution.py:221
  25.5 18.7 %collective-permute-start.8 = (bf16[48,1152]{1,0:T(8,128)(2,1)S(1)}, bf16[48,1152]{1,0:T(8,128)(2,1)S(1)}, u32[]{:S(2)}, u32[]{:S(2)}) collective-permute-start(bf16[48,1152]{1,0:T(8,128)(2,1)S(1)} %collective-permute-done.3), channel_id=1, source_target_pairs={{28,0},{29,1}} | collective-permute-start | bytes 331784 | tf_op jit(solution)/shard_map/ppermute | solution.py:220

commit v9 on v8

--- a/solution.py
+++ b/solution.py
@@ -209,16 +209,16 @@
     mate_a, mate_b = across(image[:half]), across(image[half:])
     mate_ids = across(ids)
 
-    cut = rows - rows * 3 // 16
+    cut = rows - rows * 3 // 8
     out_a, out_b, image_sum, loss = call(
         own_kernel, "own", [((cut, width), bf16), ((rows - cut, width), bf16), ((rows, width), f32), ((1, rows), f32)],
         (flags, params), ids, mate_ids, image_emb, mate_a, mate_b, text, text_accum,
     )
     turn = count - 4
     arrived_a = ahead(out_a)
-    to_turn = lax.ppermute(out_b, AXES, [(count - 2, turn), (count - 1, turn + 1)])
-    turned = lax.ppermute(to_turn, AXES, [(turn, 0), (turn + 1, 1)])
-    arrived_b = lax.ppermute(out_b, AXES, skip[:-2])
+    to_turn = lax.ppermute(out_b, AXES, [(count - 2, turn)])
+    turned = lax.ppermute(to_turn, AXES, [(turn, 0)])
+    arrived_b = lax.ppermute(out_b, AXES, skip[:-2] + skip[-1:])
 
     passed_a, passed_b = call(
         relay_kernel, "relay", [((half, width), bf16), ((rows + PAD - half, width), bf16)],

time: 45.1 us -> 43.5 us (0.965)
  waiting for transfers between devices: 22 us -> 20.3 us
    ppermute x2, waiting for transfers between devices: 11.7 us -> 9.81 us  [ahead(): return lax.ppermute(value, AXES, skip)]
  transfers between devices with their start and end apart: 10 -> 10, of which waited for: 3 -> 2; matrix products, arithmetic and copies ran while one was open for 0% -> 0% of each run, Pallas kernels for 19% -> 19%
where the time goes in v9:
time: 43.5 us; the launch traced here: 43.3 us
  waiting for transfers between devices  20.3 us (47%)
  Pallas kernels  10.6 us (24%)
  starting transfers between devices  8.98 us (21%)
  between operations  2.06 us (5%)
  local copies, waits for them, and re-layouts  1.32 us (3%)
    ppermute x1, waiting for transfers between devices, body(): turned = lax.ppermute(to_turn, AXES, [(turn, 0)])  10.4 us
    ppermute x2, waiting for transfers between devices, ahead(): return lax.ppermute(value, AXES, skip)  9.81 us
    pallas_call x4, Pallas kernels, call(): pl.pallas_call(kernel, out_shape=[jax.ShapeDtypeStruct(s, d) for s, d in...  7.44 us
    ppermute x2, starting transfers between devices, ahead(): return lax.ppermute(value, AXES, skip)  4.51 us
    pallas_call x2, Pallas kernels, add_part(): pl.pallas_call(functools.partial(add_kernel, start, chunks, len(arrived))...  1.76 us
    pallas_call x1, Pallas kernels, body(): pl.pallas_call(cast_kernel, out_shape=jax.ShapeDtypeStruct((rows + PAD, w...  1.36 us
    ppermute x1, starting transfers between devices, body(): turned = lax.ppermute(to_turn, AXES, [(turn, 0)])  1.29 us
    ppermute x1, starting transfers between devices, body(): arrived_b = lax.ppermute(out_b, AXES, skip[:-2] + skip[-1:])  1.29 us
  transfers between devices with their start and end apart: 10, of which 2 were waited for; matrix products, arithmetic and copies ran while one was open for 0% of the time, Pallas kernels for 19%

profile of v9, /device:TPU:0, one launch (start us, length us, event | category | flops | bytes accessed | tf_op | source)
XLA Modules:
  0.0 43.3 jit_solution(1287027116017461573)
XLA Ops:
  0.6 0.0 copy-start
  0.6 0.0 copy-start.2
  0.7 1.4 %cast.1.text = bf16[264,1152]{1,0:T(8,128)(2,1)S(1)} custom-call(s32[1,256]{1,0:T(1,128)} %bitcast.3, f32[256,1152]{1,0:T(8,128)} %text.1), custom_call_target="tpu_custom_call" | custom-call | tf_op jit(solution)/shard_map/cast/pallas_call | solution.py:190
  2.0 3.0 %collective-permute-start.4 = (bf16[264,1152]{1,0:T(8,128)(2,1)S(1)}, bf16[264,1152]{1,0:T(8,128)(2,1)S(1)}, u32[]{:S(2)}, u32[]{:S(2)}) collective-permute-start(bf16[264,1152]{1,0:T(8,128)(2,1)S(1)} %cast.1.text), channel_id=1, source_target_pairs={{0,2},{1,3},{2,4},{3,5},{4,6},{5,7},{6,8},{7,9},{8,10},{9,11},{10,... | collective-permute-start | bytes 1824776 | tf_op jit(solution)/shard_map/ppermute | solution.py:185
  5.0 0.0 copy-done
  5.1 0.1 collective-permute-start.1
  5.2 0.5 %collective-permute-start.2 = (bf16[128,1152]{1,0:T(8,128)(2,1)S(1)}, bf16[128,1152]{1,0:T(8,128)(2,1)S(1)}, u32[]{:S(2)}, u32[]{:S(2)}) collective-permute-start(bf16[128,1152]{1,0:T(8,128)(2,1)S(1)} %get-tuple-element.35), channel_id=1, source_target_pairs={{0,1},{1,0},{2,3},{3,2},{4,5},{5,4},{6,7},{7,6},{8,9},{9,8},{10,11... | collective-permute-start | bytes 884744 | tf_op jit(solution)/shard_map/ppermute | solution.py:188
  5.7 0.0 copy-done.2
  5.7 0.1 collective-permute-start
  7.0 0.1 pad_maximum_fusion.params
  7.1 0.0 collective-permute-done.mate_ids
  7.2 0.0 collective-permute-done.1.mate_a
  7.2 0.0 collective-permute-done.2.mate_b
  7.2 0.0 copy-start.1
  7.2 1.3 %copy-done.1 = f32[256,1152]{1,0:T(8,128)S(1)} copy-done((f32[256,1152]{1,0:T(8,128)S(1)}, f32[256,1152]{1,0:T(8,128)}, u32[]{:S(2)}) %copy-start.1) | copy-done | bytes 1179672
  8.4 3.1 %own.1 = (bf16[160,1152]{1,0:T(8,128)(2,1)S(1)}, bf16[96,1152]{1,0:T(8,128)(2,1)S(1)}, f32[256,1152]{1,0:T(8,128)S(1)}, f32[1,256]{1,0:T(1,128)S(1)}) custom-call(s32[1]{0:T(128)} %bitcast.1.flags, f32[2]{0:T(128)S(1)} %pad_maximum_fusion.params, s32[1,256]{1,0:T(1,128)S(1)} %bitcast.5, s32[1,256]{1,0:T(1,128)S(1)} %collective-permute-done.mate_ids, ...), custom_call_target="tpu_custom_call" | custom-call | tf_op jit(solution)/shard_map/own/pallas_call | solution.py:147
  11.6 0.7 %collective-permute-start.3 = (bf16[96,1152]{1,0:T(8,128)(2,1)S(1)}, bf16[96,1152]{1,0:T(8,128)(2,1)S(1)}, u32[]{:S(2)}, u32[]{:S(2)}) collective-permute-start(bf16[96,1152]{1,0:T(8,128)(2,1)S(1)} %get-tuple-element.22), channel_id=1, source_target_pairs={{30,28}} | collective-permute-start | bytes 663560 | tf_op jit(solution)/shard_map/ppermute | solution.py:219
  12.3 1.5 %collective-permute-start.9 = (bf16[160,1152]{1,0:T(8,128)(2,1)S(1)}, bf16[160,1152]{1,0:T(8,128)(2,1)S(1)}, u32[]{:S(2)}, u32[]{:S(2)}) collective-permute-start(bf16[160,1152]{1,0:T(8,128)(2,1)S(1)} %get-tuple-element.34), channel_id=1, source_target_pairs={{0,2},{1,3},{2,4},{3,5},{4,6},{5,7},{6,8},{7,9},{8,10},{9,11},{10,... | collective-permute-start | bytes 1105928 | tf_op jit(solution)/shard_map/ppermute | solution.py:185
  13.7 0.0 collective-permute-done.3
  13.7 9.8 %collective-permute-done.4.far = bf16[264,1152]{1,0:T(8,128)(2,1)S(1)} collective-permute-done((bf16[264,1152]{1,0:T(8,128)(2,1)S(1)}, bf16[264,1152]{1,0:T(8,128)(2,1)S(1)}, u32[]{:S(2)}, u32[]{:S(2)}) %collective-permute-start.4) | collective-permute-done | bytes 608288 | tf_op jit(solution)/shard_map/ppermute | solution.py:185
  23.6 0.1 collective-permute-start.6
  23.7 0.5 %collective-permute-start.5 = (bf16[128,1152]{1,0:T(8,128)(2,1)S(1)}, bf16[128,1152]{1,0:T(8,128)(2,1)S(1)}, u32[]{:S(2)}, u32[]{:S(2)}) collective-permute-start(bf16[128,1152]{1,0:T(8,128)(2,1)S(1)} %get-tuple-element.24), channel_id=1, source_target_pairs={{0,1},{1,0},{2,3},{3,2},{4,5},{5,4},{6,7},{7,6},{8,9},{9,8},{10,11... | collective-permute-start | bytes 884744 | tf_op jit(solution)/shard_map/ppermute | solution.py:188
  24.2 1.3 %collective-permute-start.7 = (bf16[96,1152]{1,0:T(8,128)(2,1)S(1)}, bf16[96,1152]{1,0:T(8,128)(2,1)S(1)}, u32[]{:S(2)}, u32[]{:S(2)}) collective-permute-start(bf16[96,1152]{1,0:T(8,128)(2,1)S(1)} %get-tuple-element.22), channel_id=1, source_target_pairs={{0,2},{1,3},{2,4},{3,5},{4,6},{5,7},{6,8},{7,9},{8,10},{9,11},{10,... | collective-permute-start | bytes 663560 | tf_op jit(solution)/shard_map/ppermute | solution.py:221
  25.5 1.3 %collective-permute-start.8 = (bf16[96,1152]{1,0:T(8,128)(2,1)S(1)}, bf16[96,1152]{1,0:T(8,128)(2,1)S(1)}, u32[]{:S(2)}, u32[]{:S(2)}) collective-permute-start(bf16[96,1152]{1,0:T(8,128)(2,1)S(1)} %collective-permute-done.3), channel_id=1, source_target_pairs={{28,0}} | collective-permute-start | bytes 663560 | tf_op jit(solution)/shard_map/ppermute | solution.py:220
  26.8 1.8 %far.1 = (f32[256,1152]{1,0:T(8,128)S(1)}, f32[256,1152]{1,0:T(8,128)S(1)}, f32[1,256]{1,0:T(1,128)S(1)}) custom-call(s32[1]{0:T(128)} %bitcast.1.flags, f32[2]{0:T(128)S(1)} %pad_maximum_fusion.params, s32[1,256]{1,0:T(1,128)S(1)} %bitcast.6, s32[1,256]{1,0:T(1,128)S(1)} %collective-permute-done.mate_ids, bf16[256,1152]{1,0:T(8,128)(2,1)S(1)} %copy-done, ...), custom_call_target="tpu_custom_call" | custom-call | tf_op jit(solution)/shard_map/far/pallas_call | solution.py:147
  28.6 0.0 collective-permute-done.5.near_a
  28.6 0.0 collective-permute-done.6.near_b
  28.7 2.4 %near.1 = (bf16[256,1152]{1,0:T(8,128)(2,1)}, f32[1,256]{1,0:T(1,128)}) custom-call(f32[2]{0:T(128)S(1)} %pad_maximum_fusion.params, s32[1,256]{1,0:T(1,128)S(1)} %bitcast.7, bf16[256,1152]{1,0:T(8,128)(2,1)S(1)} %copy-done, bf16[128,1152]{1,0:T(8,128)(2,1)S(1)} %collective-permute-done.5.near_a, bf16[136,1152]{1,0:T(8,128)(2,1)S(1)} %collective-permute-done.6.near_b, ...), custom_call_target="tpu_custom_call" | custom-call | tf_op jit(solution)/shard_map/near/pallas_call | solution.py:147
  31.1 0.0 collective-permute-done.9.refs_0_
  31.1 0.9 %add_a.1.refs_2_ = f32[256,1152]{1,0:T(8,128)} custom-call(f32[256,1152]{1,0:T(8,128)S(1)} %get-tuple-element.33.late, bf16[160,1152]{1,0:T(8,128)(2,1)S(1)} %collective-permute-done.9.refs_0_), custom_call_target="tpu_custom_call" | custom-call | tf_op jit(solution)/shard_map/add_a/pallas_call | solution.py:159
  32.0 0.0 collective-permute-done.7.refs_0_
  32.0 10.4 %collective-permute-done.8.refs_1_ = bf16[96,1152]{1,0:T(8,128)(2,1)S(1)} collective-permute-done((bf16[96,1152]{1,0:T(8,128)(2,1)S(1)}, bf16[96,1152]{1,0:T(8,128)(2,1)S(1)}, u32[]{:S(2)}, u32[]{:S(2)}) %collective-permute-start.8) | collective-permute-done | bytes 221216 | tf_op jit(solution)/shard_map/ppermute | solution.py:220
  42.4 0.8 %add_b.1 = f32[256,1152]{1,0:T(8,128)} custom-call(f32[256,1152]{1,0:T(8,128)S(1)} %get-tuple-element.33.late, bf16[96,1152]{1,0:T(8,128)(2,1)S(1)} %collective-permute-done.7.refs_0_, bf16[96,1152]{1,0:T(8,128)(2,1)S(1)} %collective-permute-done.8.refs_1_, f32[256,1152]{1,0:T(8,128)} %add_a.1.refs_2_), custom_call_target="tpu_custom_call", output_to_operand_aliasing={{}: (3, {})} | custom-call | tf_op jit(solution)/shard_map/add_b/pallas_call | solution.py:159
  (2 shorter events, 0.1 us)
Async XLA Ops:
  0.6 4.4 %copy-start = (bf16[256,1152]{1,0:T(8,128)(2,1)S(1)}, bf16[256,1152]{1,0:T(8,128)(2,1)}, u32[]{:S(2)}) copy-start(bf16[256,1152]{1,0:T(8,128)(2,1)} %image.2) | copy-start | bytes 1769476
  0.6 5.0 %copy-start.2 = (s32[256]{0:T(256)S(1)}, s32[256]{0:T(256)}, u32[]{:S(2)}) copy-start(s32[256]{0:T(256)} %param.9) | copy-start | bytes 3076
  2.0 21.5 %collective-permute-start.4 = (bf16[264,1152]{1,0:T(8,128)(2,1)S(1)}, bf16[264,1152]{1,0:T(8,128)(2,1)S(1)}, u32[]{:S(2)}, u32[]{:S(2)}) collective-permute-start(bf16[264,1152]{1,0:T(8,128)(2,1)S(1)} %cast.1.text), channel_id=1, source_target_pairs={{0,2},{1,3},{2,4},{3,5},{4,6},{5,7},{6,8},{7,9},{8,10},{9,11},{10,... | collective-permute-start | bytes 1824776 | tf_op jit(solution)/shard_map/ppermute | solution.py:185
  5.1 2.1 %collective-permute-start.1 = (bf16[128,1152]{1,0:T(8,128)(2,1)S(1)}, bf16[128,1152]{1,0:T(8,128)(2,1)S(1)}, u32[]{:S(2)}, u32[]{:S(2)}) collective-permute-start(bf16[128,1152]{1,0:T(8,128)(2,1)S(1)} %get-tuple-element.36), channel_id=1, source_target_pairs={{0,1},{1,0},{2,3},{3,2},{4,5},{5,4},{6,7},{7,6},{8,9},{9,8},{10,11... | collective-permute-start | bytes 884744 | tf_op jit(solution)/shard_map/ppermute | solution.py:188
  5.2 2.0 %collective-permute-start.2 = (bf16[128,1152]{1,0:T(8,128)(2,1)S(1)}, bf16[128,1152]{1,0:T(8,128)(2,1)S(1)}, u32[]{:S(2)}, u32[]{:S(2)}) collective-permute-start(bf16[128,1152]{1,0:T(8,128)(2,1)S(1)} %get-tuple-element.35), channel_id=1, source_target_pairs={{0,1},{1,0},{2,3},{3,2},{4,5},{5,4},{6,7},{7,6},{8,9},{9,8},{10,11... | collective-permute-start | bytes 884744 | tf_op jit(solution)/shard_map/ppermute | solution.py:188
  5.7 1.5 %collective-permute-start = (s32[1,256]{1,0:T(1,128)S(1)}, s32[1,256]{1,0:T(1,128)S(1)}, u32[]{:S(2)}, u32[]{:S(2)}) collective-permute-start(s32[1,256]{1,0:T(1,128)S(1)} %bitcast.4), channel_id=1, source_target_pairs={{0,1},{1,0},{2,3},{3,2},{4,5},{5,4},{6,7},{7,6},{8,9},{9,8},{10,11... | collective-permute-start | bytes 3080 | tf_op jit(solution)/shard_map/ppermute | solution.py:188
  7.2 1.3 %copy-start.1 = (f32[256,1152]{1,0:T(8,128)S(1)}, f32[256,1152]{1,0:T(8,128)}, u32[]{:S(2)}) copy-start(f32[256,1152]{1,0:T(8,128)} %accum.1) | copy-start | bytes 3538948
  11.6 2.2 %collective-permute-start.3 = (bf16[96,1152]{1,0:T(8,128)(2,1)S(1)}, bf16[96,1152]{1,0:T(8,128)(2,1)S(1)}, u32[]{:S(2)}, u32[]{:S(2)}) collective-permute-start(bf16[96,1152]{1,0:T(8,128)(2,1)S(1)} %get-tuple-element.22), channel_id=1, source_target_pairs={{30,28}} | collective-permute-start | bytes 663560 | tf_op jit(solution)/shard_map/ppermute | solution.py:219
  12.3 18.8 %collective-permute-start.9 = (bf16[160,1152]{1,0:T(8,128)(2,1)S(1)}, bf16[160,1152]{1,0:T(8,128)(2,1)S(1)}, u32[]{:S(2)}, u32[]{:S(2)}) collective-permute-start(bf16[160,1152]{1,0:T(8,128)(2,1)S(1)} %get-tuple-element.34), channel_id=1, source_target_pairs={{0,2},{1,3},{2,4},{3,5},{4,6},{5,7},{6,8},{7,9},{8,10},{9,11},{10,... | collective-permute-start | bytes 1105928 | tf_op jit(solution)/shard_map/ppermute | solution.py:185
  23.6 5.0 %collective-permute-start.6 = (bf16[136,1152]{1,0:T(8,128)(2,1)S(1)}, bf16[136,1152]{1,0:T(8,128)(2,1)S(1)}, u32[]{:S(2)}, u32[]{:S(2)}) collective-permute-start(bf16[136,1152]{1,0:T(8,128)(2,1)S(1)} %get-tuple-element.25), channel_id=1, source_target_pairs={{0,1},{1,0},{2,3},{3,2},{4,5},{5,4},{6,7},{7,6},{8,9},{9,8},{10,11... | collective-permute-start | bytes 940040 | tf_op jit(solution)/shard_map/ppermute | solution.py:188
  23.7 4.9 %collective-permute-start.5 = (bf16[128,1152]{1,0:T(8,128)(2,1)S(1)}, bf16[128,1152]{1,0:T(8,128)(2,1)S(1)}, u32[]{:S(2)}, u32[]{:S(2)}) collective-permute-start(bf16[128,1152]{1,0:T(8,128)(2,1)S(1)} %get-tuple-element.24), channel_id=1, source_target_pairs={{0,1},{1,0},{2,3},{3,2},{4,5},{5,4},{6,7},{7,6},{8,9},{9,8},{10,11... | collective-permute-start | bytes 884744 | tf_op jit(solution)/shard_map/ppermute | solution.py:188
  24.2 7.8 %collective-permute-start.7 = (bf16[96,1152]{1,0:T(8,128)(2,1)S(1)}, bf16[96,1152]{1,0:T(8,128)(2,1)S(1)}, u32[]{:S(2)}, u32[]{:S(2)}) collective-permute-start(bf16[96,1152]{1,0:T(8,128)(2,1)S(1)} %get-tuple-element.22), channel_id=1, source_target_pairs={{0,2},{1,3},{2,4},{3,5},{4,6},{5,7},{6,8},{7,9},{8,10},{9,11},{10,... | collective-permute-start | bytes 663560 | tf_op jit(solution)/shard_map/ppermute | solution.py:221
  25.5 16.9 %collective-permute-start.8 = (bf16[96,1152]{1,0:T(8,128)(2,1)S(1)}, bf16[96,1152]{1,0:T(8,128)(2,1)S(1)}, u32[]{:S(2)}, u32[]{:S(2)}) collective-permute-start(bf16[96,1152]{1,0:T(8,128)(2,1)S(1)} %collective-permute-done.3), channel_id=1, source_target_pairs={{28,0}} | collective-permute-start | bytes 663560 | tf_op jit(solution)/shard_map/ppermute | solution.py:220

commit v10 on v8

--- a/solution.py
+++ b/solution.py
@@ -67,13 +67,21 @@
     out[rows:, :rows] = parts.astype(jnp.float32).astype(out.dtype)
 
 
-def add_kernel(start, chunks, count, late, *refs):
-    arrived, (out, staged, sems) = refs[:count], refs[-3:]
+def add_kernel(start, chunks, late, arrived, *refs):
+    flag_turned, (out, staged, sems) = refs[:2], refs[-3:]
     step = staged.shape[0] // chunks
     copies = []
     for k in range(chunks):
         here, there = pl.ds(k * step, step), pl.ds(start + k * step, step)
-        staged[here, :] = sum((part[here, :].astype(staged.dtype) for part in arrived), late[there, :])
+        staged[here, :] = arrived[here, :].astype(staged.dtype) + late[there, :]
+        if start:
+            flag, turned = flag_turned
+
+            @pl.when(flag[0] == 1)
+            def _():
+                part = turned[pl.ds(staged.shape[0] + k * step, step), :]
+                staged[here, :] = part.astype(staged.dtype) + late[there, :]
+
         copies.append(pltpu.make_async_copy(staged.at[here], out.at[there], sems.at[k]))
         copies[-1].start()
     for copy in copies:
@@ -155,18 +163,18 @@
     )(*scalars, *operands)
 
 
-def add_part(name, start, chunks, late, arrived, *before):
+def add_part(name, start, chunks, late, arrived, *more):
     return pl.pallas_call(
-        functools.partial(add_kernel, start, chunks, len(arrived)),
+        functools.partial(add_kernel, start, chunks),
         out_shape=jax.ShapeDtypeStruct(late.shape, late.dtype),
-        in_specs=[VMEM] * (1 + len(arrived)) + [HBM] * len(before),
+        in_specs=[VMEM, VMEM] + ([SMEM, VMEM, HBM] if more else []),
         out_specs=HBM,
-        scratch_shapes=[pltpu.VMEM(arrived[0].shape, late.dtype), pltpu.SemaphoreType.DMA((chunks,))],
-        input_output_aliases={1 + len(arrived): 0} if before else {},
+        scratch_shapes=[pltpu.VMEM(arrived.shape, late.dtype), pltpu.SemaphoreType.DMA((chunks,))],
+        input_output_aliases={4: 0} if more else {},
         compiler_params=pltpu.CompilerParams(vmem_limit_bytes=16 * 1024 * 1024),
         cost_estimate=pl.CostEstimate(flops=0, bytes_accessed=0, transcendentals=0),
         name=name,
-    )(late, *arrived, *before)
+    )(late, arrived, *more)
 
 
 def body(image_emb, text_emb, text_accum, pair_ids, log_scale, bias):
@@ -216,13 +224,17 @@
     )
     turn = count - 4
     arrived_a = ahead(out_a)
-    to_turn = lax.ppermute(out_b, AXES, [(count - 2, turn), (count - 1, turn + 1)])
-    turned = lax.ppermute(to_turn, AXES, [(turn, 0), (turn + 1, 1)])
+    pairs = [[i, i + 1] for i in range(0, count, 2)]
+    first_legs = pairs[:-2] + [[turn, count - 2], [turn + 1, count - 1]]
+    second_legs = pairs[1:-2] + [[0, turn], [1, turn + 1], [count - 2, count - 1]]
+    to_turn = lax.all_gather(out_b, AXES, axis_index_groups=first_legs)[1]
+    turned = lax.all_gather(to_turn, AXES, axis_index_groups=second_legs, tiled=True)
+    at_start = (lax.axis_index(AXES) < 2).astype(jnp.int32).reshape(1)
     arrived_b = lax.ppermute(out_b, AXES, skip[:-2])
 
     passed_a, passed_b = call(
         relay_kernel, "relay", [((half, width), bf16), ((rows + PAD - half, width), bf16)],
-        (flags,), lax.optimization_barrier((loss, to_turn))[0], text, far,
+        (flags,), to_turn, text, far,
     )
     near_a, near_b = across(passed_a), across(passed_b)
     late, image_sum, loss = call(
@@ -234,8 +246,8 @@
         (params,), ids, image_emb, near_a, near_b, image_sum, loss,
     )
     late, image_grad = lax.optimization_barrier((late, image_grad))
-    text_grad = add_part("add_a", 0, 2, late, (arrived_a,))
-    text_grad = add_part("add_b", cut, 1, late, (arrived_b, turned), text_grad)
+    text_grad = add_part("add_a", 0, 2, late, arrived_a)
+    text_grad = add_part("add_b", cut, 1, late, arrived_b, at_start, turned, text_grad)
     return (loss.reshape(rows), image_grad, text_grad)
 
 

time: 45.1 us -> 53 us (1.18)
  blocking collectives: 0 us -> 20.5 us
  waiting for transfers between devices: 22 us -> 6.27 us
  local copies, waits for them, and re-layouts: 1.32 us -> 3.96 us
  Pallas kernels: 10.5 us -> 12.9 us
  starting transfers between devices: 8.95 us -> 6.89 us
    all_gather x0 -> x2, blocking collectives: none -> 20.5 us  [the longest x1 18.4 us: body(): lax.all_gather(to_turn, AXES, axis_index_groups=second_legs, tiled=True)]
    ppermute x2 -> x0, waiting for transfers between devices: 10.2 us -> none  [the longest x1 10.2 us: body(): turned = lax.ppermute(to_turn, AXES, [(turn, 0), (turn + 1, 1)])]
    ppermute x2, waiting for transfers between devices: 11.7 us -> 6.22 us  [ahead(): return lax.ppermute(value, AXES, skip)]
    unnamed x6 -> x12, local copies, waits for them, and re-layouts: 1.28 us -> 3.91 us
    ppermute x2 -> x0, starting transfers between devices: 1.95 us -> none  [the longest x1 1.29 us: body(): turned = lax.ppermute(to_turn, AXES, [(turn, 0), (turn + 1, 1)])]
    pallas_call x4, Pallas kernels: 7.44 us -> 8.73 us  [call(): pl.pallas_call(kernel, out_shape=[jax.ShapeDtypeStruct(s, d) for s, d in...]
    pallas_call x2, Pallas kernels: 1.73 us -> 2.78 us  [add_part(): pl.pallas_call(functools.partial(add_kernel, start, chunks), out_shape=ja...]
  transfers between devices with their start and end apart: 10 -> 8, of which waited for: 3 -> 1; matrix products, arithmetic and copies ran while one was open for 0% -> 0% of each run, Pallas kernels for 19% -> 20%
where the time goes in v10:
time: 53 us; the launch traced here: 52.6 us
  blocking collectives  20.5 us (39%)
  Pallas kernels  12.9 us (24%)
  starting transfers between devices  6.89 us (13%)
  waiting for transfers between devices  6.27 us (12%)
  local copies, waits for them, and re-layouts  3.96 us (7%)
  between operations  2.04 us (4%)
    all_gather x1, blocking collectives, body(): lax.all_gather(to_turn, AXES, axis_index_groups=second_legs, tiled=True)  18.4 us
    pallas_call x4, Pallas kernels, call(): pl.pallas_call(kernel, out_shape=[jax.ShapeDtypeStruct(s, d) for s, d in...  8.73 us
    ppermute x2, waiting for transfers between devices, ahead(): return lax.ppermute(value, AXES, skip)  6.22 us
    ppermute x2, starting transfers between devices, ahead(): return lax.ppermute(value, AXES, skip)  4.45 us
    unnamed x12, local copies, waits for them, and re-layouts  3.91 us
    pallas_call x2, Pallas kernels, add_part(): pl.pallas_call(functools.partial(add_kernel, start, chunks), out_shape=ja...  2.78 us
    all_gather x1, blocking collectives, body(): to_turn = lax.all_gather(out_b, AXES, axis_index_groups=first_legs)[1]  2.16 us
    pallas_call x1, Pallas kernels, body(): pl.pallas_call(cast_kernel, out_shape=jax.ShapeDtypeStruct((rows + PAD, w...  1.36 us
  transfers between devices with their start and end apart: 8, of which 1 were waited for; matrix products, arithmetic and copies ran while one was open for 0% of the time, Pallas kernels for 20%

profile of v10, /device:TPU:0, one launch (start us, length us, event | category | flops | bytes accessed | tf_op | source)
XLA Modules:
  0.0 52.6 jit_solution(3207350155427960614)
XLA Ops:
  0.6 0.0 copy-start
  0.6 0.0 copy-start.5
  0.7 1.4 %cast.1.text = bf16[264,1152]{1,0:T(8,128)(2,1)S(1)} custom-call(s32[1,256]{1,0:T(1,128)} %bitcast.4, f32[256,1152]{1,0:T(8,128)} %text.1), custom_call_target="tpu_custom_call" | custom-call | tf_op jit(solution)/shard_map/cast/pallas_call | solution.py:198
  2.0 3.0 %collective-permute-start.3 = (bf16[264,1152]{1,0:T(8,128)(2,1)S(1)}, bf16[264,1152]{1,0:T(8,128)(2,1)S(1)}, u32[]{:S(2)}, u32[]{:S(2)}) collective-permute-start(bf16[264,1152]{1,0:T(8,128)(2,1)S(1)} %cast.1.text), channel_id=1, source_target_pairs={{0,2},{1,3},{2,4},{3,5},{4,6},{5,7},{6,8},{7,9},{8,10},{9,11},{10,... | collective-permute-start | bytes 1824776 | tf_op jit(solution)/shard_map/ppermute | solution.py:193
  5.0 0.0 copy-done
  5.1 0.1 collective-permute-start.1
  5.2 0.5 collective-permute-start.2
  5.7 0.0 copy-done.5
  5.7 0.1 collective-permute-start
  7.0 0.1 pad_maximum_fusion.params
  7.1 0.0 collective-permute-done.mate_ids
  7.2 0.0 collective-permute-done.1.mate_a
  7.2 0.0 collective-permute-done.2.mate_b
  7.2 0.0 copy-start.1
  7.2 0.7 %copy-done.1 = bf16[128,1152]{1,0:T(8,128)(2,1)} copy-done((bf16[128,1152]{1,0:T(8,128)(2,1)}, bf16[128,1152]{1,0:T(8,128)(2,1)S(1)}, u32[]{:S(2)}) %copy-start.1) | copy-done | bytes 294936
  7.9 0.0 copy-start.2
  7.9 1.0 %copy-done.2 = bf16[128,1152]{1,0:T(8,128)(2,1)S(1)} copy-done((bf16[128,1152]{1,0:T(8,128)(2,1)S(1)}, bf16[128,1152]{1,0:T(8,128)(2,1)}, u32[]{:S(2)}) %copy-start.2) | copy-done | bytes 294936
  8.8 0.0 copy-start.4
  8.8 1.3 %copy-done.4 = f32[256,1152]{1,0:T(8,128)S(1)} copy-done((f32[256,1152]{1,0:T(8,128)S(1)}, f32[256,1152]{1,0:T(8,128)}, u32[]{:S(2)}) %copy-start.4) | copy-done | bytes 1179672
  10.1 3.6 %own.1 = (bf16[208,1152]{1,0:T(8,128)(2,1)}, bf16[48,1152]{1,0:T(8,128)(2,1)}, f32[256,1152]{1,0:T(8,128)S(1)}, f32[1,256]{1,0:T(1,128)S(1)}) custom-call(s32[1]{0:T(128)} %bitcast.1.flags, f32[2]{0:T(128)S(1)} %pad_maximum_fusion.params, s32[1,256]{1,0:T(1,128)S(1)} %bitcast.6, s32[1,256]{1,0:T(1,128)S(1)} %collective-permute-done.mate_ids, ...), custom_call_target="tpu_custom_call" | custom-call | tf_op jit(solution)/shard_map/own/pallas_call | solution.py:155
  13.7 1.4 %collective-permute-start.7 = (bf16[208,1152]{1,0:T(8,128)(2,1)}, bf16[208,1152]{1,0:T(8,128)(2,1)}, u32[]{:S(2)}, u32[]{:S(2)}) collective-permute-start(bf16[208,1152]{1,0:T(8,128)(2,1)} %get-tuple-element.32), channel_id=1, source_target_pairs={{0,2},{1,3},{2,4},{3,5},{4,6},{5,7},{6,8},{7,9},{8,10},{9,11},{10,... | collective-permute-start | bytes 1437704 | tf_op jit(solution)/shard_map/ppermute | solution.py:193
  15.2 2.2 %all-gather = bf16[96,1152]{1,0:T(8,128)(2,1)S(1)} all-gather(bf16[48,1152]{1,0:T(8,128)(2,1)} %get-tuple-element.20), channel_id=2, replica_groups={{0,1},{2,3},{4,5},{6,7},{8,9},{10,11},{12,13},{14,15},{16,17},{18,19},{..., dimensions={0}, use_global_device_ids=true | all-gather | bytes 331776 | tf_op jit(solution)/shard_map/all_gather | solution.py:230
  17.3 6.2 %collective-permute-done.3.far = bf16[264,1152]{1,0:T(8,128)(2,1)S(1)} collective-permute-done((bf16[264,1152]{1,0:T(8,128)(2,1)S(1)}, bf16[264,1152]{1,0:T(8,128)(2,1)S(1)}, u32[]{:S(2)}, u32[]{:S(2)}) %collective-permute-start.3) | collective-permute-done | bytes 608288 | tf_op jit(solution)/shard_map/ppermute | solution.py:193
  23.6 0.9 %relay.1 = (bf16[128,1152]{1,0:T(8,128)(2,1)}, bf16[136,1152]{1,0:T(8,128)(2,1)}) custom-call(s32[1]{0:T(128)} %bitcast.1.flags, bf16[48,1152]{1,0:T(8,128)(2,1)S(1)} %slice.13.token, bf16[264,1152]{1,0:T(8,128)(2,1)S(1)} %cast.1.text, bf16[264,1152]{1,0:T(8,128)(2,1)S(1)} %collective-permute-done.3.far), custom_call_target="tpu_custom_call" | custom-call | tf_op jit(solution)/shard_map/relay/pallas_call | solution.py:155
  24.4 0.0 collective-permute-start.5
  24.4 0.5 collective-permute-start.4
  24.9 1.3 %collective-permute-start.6 = (bf16[48,1152]{1,0:T(8,128)(2,1)}, bf16[48,1152]{1,0:T(8,128)(2,1)S(1)}, u32[]{:S(2)}, u32[]{:S(2)}) collective-permute-start(bf16[48,1152]{1,0:T(8,128)(2,1)} %get-tuple-element.20), channel_id=1, source_target_pairs={{0,2},{1,3},{2,4},{3,5},{4,6},{5,7},{6,8},{7,9},{8,10},{9,11},{10,... | collective-permute-start | bytes 331784 | tf_op jit(solution)/shard_map/ppermute | solution.py:233
  26.2 18.4 %all-gather.2.refs_1_ = bf16[96,1152]{1,0:T(8,128)(2,1)S(1)} all-gather(bf16[48,1152]{1,0:T(8,128)(2,1)S(1)} %slice.13.token), channel_id=4, replica_groups={{2,3},{4,5},{6,7},{8,9},{10,11},{12,13},{14,15},{16,17},{18,19},{20,21}..., dimensions={0}, use_global_device_ids=true | all-gather | bytes 331776 | tf_op jit(solution)/shard_map/all_gather | solution.py:231
  44.6 0.0 copy-start.3
  44.6 1.0 %copy-done.3 = bf16[128,1152]{1,0:T(8,128)(2,1)S(1)} copy-done((bf16[128,1152]{1,0:T(8,128)(2,1)S(1)}, bf16[128,1152]{1,0:T(8,128)(2,1)}, u32[]{:S(2)}) %copy-start.3) | copy-done | bytes 294936
  45.6 1.8 %far.1 = (f32[256,1152]{1,0:T(8,128)S(1)}, f32[256,1152]{1,0:T(8,128)S(1)}, f32[1,256]{1,0:T(1,128)S(1)}) custom-call(s32[1]{0:T(128)} %bitcast.1.flags, f32[2]{0:T(128)S(1)} %pad_maximum_fusion.params, s32[1,256]{1,0:T(1,128)S(1)} %bitcast.7, s32[1,256]{1,0:T(1,128)S(1)} %collective-permute-done.mate_ids, bf16[256,1152]{1,0:T(8,128)(2,1)S(1)} %copy-done, ...), custom_call_target="tpu_custom_call" | custom-call | tf_op jit(solution)/shard_map/far/pallas_call | solution.py:155
  47.4 0.0 collective-permute-done.4.near_a
  47.4 0.0 collective-permute-done.5.near_b
  47.4 2.4 %near.1 = (bf16[256,1152]{1,0:T(8,128)(2,1)}, f32[1,256]{1,0:T(1,128)}) custom-call(f32[2]{0:T(128)S(1)} %pad_maximum_fusion.params, s32[1,256]{1,0:T(1,128)S(1)} %bitcast.8, bf16[256,1152]{1,0:T(8,128)(2,1)S(1)} %copy-done, bf16[128,1152]{1,0:T(8,128)(2,1)S(1)} %collective-permute-done.4.near_a, bf16[136,1152]{1,0:T(8,128)(2,1)S(1)} %collective-permute-done.5.near_b, ...), custom_call_target="tpu_custom_call" | custom-call | tf_op jit(solution)/shard_map/near/pallas_call | solution.py:155
  49.8 0.0 collective-permute-done.7.arrived
  49.8 2.0 %add_a.1.refs_2_ = f32[256,1152]{1,0:T(8,128)} custom-call(f32[256,1152]{1,0:T(8,128)S(1)} %get-tuple-element.31.late, bf16[208,1152]{1,0:T(8,128)(2,1)} %collective-permute-done.7.arrived), custom_call_target="tpu_custom_call" | custom-call | tf_op jit(solution)/shard_map/add_a/pallas_call | solution.py:167
  51.9 0.0 collective-permute-done.6.arrived
  51.9 0.8 %add_b.1 = f32[256,1152]{1,0:T(8,128)} custom-call(f32[256,1152]{1,0:T(8,128)S(1)} %get-tuple-element.31.late, bf16[48,1152]{1,0:T(8,128)(2,1)S(1)} %collective-permute-done.6.arrived, s32[1]{0:T(128)} %bitcast.3.refs_0_, bf16[96,1152]{1,0:T(8,128)(2,1)S(1)} %all-gather.2.refs_1_, f32[256,1152]{1,0:T(8,128)} %add_a.1.refs_2_), custom_call_target="tpu_custom_call", output_to_operand_aliasing={{}: (4, {})} | custom-call | tf_op jit(solution)/shard_map/add_b/pallas_call | solution.py:167
  (2 shorter events, 0.1 us)
Async XLA Ops:
  0.6 4.4 %copy-start = (bf16[256,1152]{1,0:T(8,128)(2,1)S(1)}, bf16[256,1152]{1,0:T(8,128)(2,1)}, u32[]{:S(2)}) copy-start(bf16[256,1152]{1,0:T(8,128)(2,1)} %image.2) | copy-start | bytes 1769476
  0.6 5.0 %copy-start.5 = (s32[256]{0:T(256)S(1)}, s32[256]{0:T(256)}, u32[]{:S(2)}) copy-start(s32[256]{0:T(256)} %param.9) | copy-start | bytes 3076
  2.0 21.5 %collective-permute-start.3 = (bf16[264,1152]{1,0:T(8,128)(2,1)S(1)}, bf16[264,1152]{1,0:T(8,128)(2,1)S(1)}, u32[]{:S(2)}, u32[]{:S(2)}) collective-permute-start(bf16[264,1152]{1,0:T(8,128)(2,1)S(1)} %cast.1.text), channel_id=1, source_target_pairs={{0,2},{1,3},{2,4},{3,5},{4,6},{5,7},{6,8},{7,9},{8,10},{9,11},{10,... | collective-permute-start | bytes 1824776 | tf_op jit(solution)/shard_map/ppermute | solution.py:193
  5.1 2.1 %collective-permute-start.1 = (bf16[128,1152]{1,0:T(8,128)(2,1)S(1)}, bf16[128,1152]{1,0:T(8,128)(2,1)S(1)}, u32[]{:S(2)}, u32[]{:S(2)}) collective-permute-start(bf16[128,1152]{1,0:T(8,128)(2,1)S(1)} %get-tuple-element.34), channel_id=1, source_target_pairs={{0,1},{1,0},{2,3},{3,2},{4,5},{5,4},{6,7},{7,6},{8,9},{9,8},{10,11... | collective-permute-start | bytes 884744 | tf_op jit(solution)/shard_map/ppermute | solution.py:196
  5.2 2.0 %collective-permute-start.2 = (bf16[128,1152]{1,0:T(8,128)(2,1)S(1)}, bf16[128,1152]{1,0:T(8,128)(2,1)S(1)}, u32[]{:S(2)}, u32[]{:S(2)}) collective-permute-start(bf16[128,1152]{1,0:T(8,128)(2,1)S(1)} %get-tuple-element.33), channel_id=1, source_target_pairs={{0,1},{1,0},{2,3},{3,2},{4,5},{5,4},{6,7},{7,6},{8,9},{9,8},{10,11... | collective-permute-start | bytes 884744 | tf_op jit(solution)/shard_map/ppermute | solution.py:196
  5.7 1.5 %collective-permute-start = (s32[1,256]{1,0:T(1,128)S(1)}, s32[1,256]{1,0:T(1,128)S(1)}, u32[]{:S(2)}, u32[]{:S(2)}) collective-permute-start(s32[1,256]{1,0:T(1,128)S(1)} %bitcast.5), channel_id=1, source_target_pairs={{0,1},{1,0},{2,3},{3,2},{4,5},{5,4},{6,7},{7,6},{8,9},{9,8},{10,11... | collective-permute-start | bytes 3080 | tf_op jit(solution)/shard_map/ppermute | solution.py:196
  7.2 0.7 %copy-start.1 = (bf16[128,1152]{1,0:T(8,128)(2,1)}, bf16[128,1152]{1,0:T(8,128)(2,1)S(1)}, u32[]{:S(2)}) copy-start(bf16[128,1152]{1,0:T(8,128)(2,1)S(1)} %collective-permute-done.2.mate_b) | copy-start | bytes 884740
  7.9 1.0 %copy-start.2 = (bf16[128,1152]{1,0:T(8,128)(2,1)S(1)}, bf16[128,1152]{1,0:T(8,128)(2,1)}, u32[]{:S(2)}) copy-start(bf16[128,1152]{1,0:T(8,128)(2,1)} %copy-done.1) | copy-start | bytes 884740
  8.8 1.3 %copy-start.4 = (f32[256,1152]{1,0:T(8,128)S(1)}, f32[256,1152]{1,0:T(8,128)}, u32[]{:S(2)}) copy-start(f32[256,1152]{1,0:T(8,128)} %accum.1) | copy-start | bytes 3538948
  13.7 36.1 %collective-permute-start.7 = (bf16[208,1152]{1,0:T(8,128)(2,1)}, bf16[208,1152]{1,0:T(8,128)(2,1)}, u32[]{:S(2)}, u32[]{:S(2)}) collective-permute-start(bf16[208,1152]{1,0:T(8,128)(2,1)} %get-tuple-element.32), channel_id=1, source_target_pairs={{0,2},{1,3},{2,4},{3,5},{4,6},{5,7},{6,8},{7,9},{8,10},{9,11},{10,... | collective-permute-start | bytes 1437704 | tf_op jit(solution)/shard_map/ppermute | solution.py:193
  24.4 23.0 %collective-permute-start.5 = (bf16[136,1152]{1,0:T(8,128)(2,1)}, bf16[136,1152]{1,0:T(8,128)(2,1)S(1)}, u32[]{:S(2)}, u32[]{:S(2)}) collective-permute-start(bf16[136,1152]{1,0:T(8,128)(2,1)} %get-tuple-element.22), channel_id=1, source_target_pairs={{0,1},{1,0},{2,3},{3,2},{4,5},{5,4},{6,7},{7,6},{8,9},{9,8},{10,11... | collective-permute-start | bytes 940040 | tf_op jit(solution)/shard_map/ppermute | solution.py:196
  24.4 23.0 %collective-permute-start.4 = (bf16[128,1152]{1,0:T(8,128)(2,1)}, bf16[128,1152]{1,0:T(8,128)(2,1)S(1)}, u32[]{:S(2)}, u32[]{:S(2)}) collective-permute-start(bf16[128,1152]{1,0:T(8,128)(2,1)} %get-tuple-element.21), channel_id=1, source_target_pairs={{0,1},{1,0},{2,3},{3,2},{4,5},{5,4},{6,7},{7,6},{8,9},{9,8},{10,11... | collective-permute-start | bytes 884744 | tf_op jit(solution)/shard_map/ppermute | solution.py:196
  24.9 27.0 %collective-permute-start.6 = (bf16[48,1152]{1,0:T(8,128)(2,1)}, bf16[48,1152]{1,0:T(8,128)(2,1)S(1)}, u32[]{:S(2)}, u32[]{:S(2)}) collective-permute-start(bf16[48,1152]{1,0:T(8,128)(2,1)} %get-tuple-element.20), channel_id=1, source_target_pairs={{0,2},{1,3},{2,4},{3,5},{4,6},{5,7},{6,8},{7,9},{8,10},{9,11},{10,... | collective-permute-start | bytes 331784 | tf_op jit(solution)/shard_map/ppermute | solution.py:233
  44.6 1.0 %copy-start.3 = (bf16[128,1152]{1,0:T(8,128)(2,1)S(1)}, bf16[128,1152]{1,0:T(8,128)(2,1)}, u32[]{:S(2)}) copy-start(bf16[128,1152]{1,0:T(8,128)(2,1)} %copy-done.1) | copy-start | bytes 884740

commit v11 on v7

--- a/solution.py
+++ b/solution.py
@@ -9,7 +9,6 @@
 
 SHIFTS = 2
 AXES = ("dp", "group")
-PAD = 8
 CHUNKS = 4
 VMEM = pl.BlockSpec(memory_space=pltpu.VMEM)
 SMEM = pl.BlockSpec(memory_space=pltpu.SMEM)
@@ -18,11 +17,6 @@
 
 def dot(a, b, contract):
     return lax.dot_general(a, b, ((contract[:1], contract[1:]), ((), ())), preferred_element_type=jnp.float32)
-
-
-def ids_of(text, at, rows):
-    parts = text[at:, :rows].astype(jnp.float32).astype(jnp.int32)
-    return parts[0:1] + parts[1:2] * 256 + parts[2:3] * 65536 + parts[3:4] * 16777216
 
 
 def pair(images, texts, image_ids, text_ids, params):
@@ -43,28 +37,15 @@
     return coef.astype(jnp.bfloat16)
 
 
-def cast_kernel(ids, text, out, staged, ids_in, sems, ids_sem):
-    rows, width = text.shape
-    step = rows // CHUNKS
-    ids_copy = pltpu.make_async_copy(ids, ids_in, ids_sem)
-    copies = [
-        pltpu.make_async_copy(text.at[pl.ds(k * step, step)], staged.at[pl.ds(k * step, step)], sems.at[k])
-        for k in range(CHUNKS)
-    ]
+def cast_kernel(text, out, staged, sems):
+    step = text.shape[0] // CHUNKS
+    parts = [pl.ds(k * step, step) for k in range(CHUNKS)]
+    copies = [pltpu.make_async_copy(text.at[part], staged.at[part], sems.at[k]) for k, part in enumerate(parts)]
     for copy in copies:
         copy.start()
-    ids_copy.start()
-    out[rows:, :] = jnp.zeros((PAD, width), out.dtype)
-    for k, copy in enumerate(copies):
+    for part, copy in zip(parts, copies):
         copy.wait()
-        out[k * step:(k + 1) * step, :] = staged[k * step:(k + 1) * step, :].astype(out.dtype)
-    ids_copy.wait()
-    row = lax.broadcasted_iota(jnp.int32, (PAD, rows), 0)
-    spread = jnp.broadcast_to(ids_in[...], (PAD, rows))
-    parts = jnp.zeros((PAD, rows), jnp.int32)
-    for k in range(4):
-        parts = jnp.where(row == k, (spread >> (8 * k)) & 255, parts)
-    out[rows:, :rows] = parts.astype(jnp.float32).astype(out.dtype)
+        out[part, :] = staged[part, :].astype(out.dtype)
 
 
 def add_kernel(start, chunks, arrived, late, *refs):
@@ -81,8 +62,7 @@
 
 
 def own_kernel(flags, params, ids, mate_ids, image, mate_a, mate_b, text, accum, out_a, out_b, image_sum, loss):
-    rows = image.shape[0]
-    own_loss, coef = pair(image[...], text[:rows, :], ids[...], ids[...], params)
+    own_loss, coef = pair(image[...], text[...], ids[...], ids[...], params)
     loss[...] = own_loss
     total = accum[...] + dot(low(coef.T), image[...], (1, 0))
     cut = out_a.shape[0]
@@ -94,14 +74,14 @@
     @pl.when(flags[0] == 0)
     def _():
         mate = jnp.concatenate([mate_a[...], mate_b[...]], axis=0)
-        _, mate_coef = pair(mate, text[:rows, :], mate_ids[...], ids[...], params)
+        _, mate_coef = pair(mate, text[...], mate_ids[...], ids[...], params)
         give(total + dot(low(mate_coef.T), mate, (1, 0)))
 
     @pl.when(flags[0] == 1)
     def _():
         give(total)
 
-    image_sum[...] = dot(low(coef), text[:rows, :], (1, 0))
+    image_sum[...] = dot(low(coef), text[...], (1, 0))
 
 
 def relay_kernel(flags, token, text, far, out_a, out_b):
@@ -115,12 +95,11 @@
     pl.when(flags[0] == 1)(lambda: fill(far))
 
 
-def far_kernel(flags, params, ids, mate_ids, image, mate_a, mate_b, far, image_in, loss_in, late, image_sum, loss):
-    rows = image.shape[0]
-    far_ids = ids_of(far, rows, rows)
-    more, coef = pair(image[...], far[:rows, :], ids[...], far_ids, params)
+def far_kernel(flags, params, ids, mate_ids, far_ids, image, mate_a, mate_b, far, image_in, loss_in,
+               late, image_sum, loss):
+    more, coef = pair(image[...], far[...], ids[...], far_ids[...], params)
     loss[...] = loss_in[...] + more
-    image_sum[...] = image_in[...] + dot(low(coef), far[:rows, :], (1, 0))
+    image_sum[...] = image_in[...] + dot(low(coef), far[...], (1, 0))
     part = dot(low(coef.T), image[...], (1, 0))
 
     @pl.when(flags[0] == 0)
@@ -130,16 +109,14 @@
     @pl.when(flags[0] == 1)
     def _():
         mate = jnp.concatenate([mate_a[...], mate_b[...]], axis=0)
-        _, mate_coef = pair(mate, far[:rows, :], mate_ids[...], far_ids, params)
+        _, mate_coef = pair(mate, far[...], mate_ids[...], far_ids[...], params)
         late[...] = part + dot(low(mate_coef.T), mate, (1, 0))
 
 
-def near_kernel(params, ids, image, near_a, near_b, image_in, loss_in, image_grad, loss):
-    rows = image.shape[0]
-    rest = rows - near_a.shape[0]
-    near = jnp.concatenate([near_a[...], near_b[:rest, :]], axis=0)
-    more, coef = pair(image[...], near, ids[...], ids_of(near_b, rest, rows), params)
-    loss[...] = (loss_in[...] + more) * (1.0 / ((SHIFTS + 1) * rows))
+def near_kernel(params, ids, near_ids, image, near_a, near_b, image_in, loss_in, image_grad, loss):
+    near = jnp.concatenate([near_a[...], near_b[...]], axis=0)
+    more, coef = pair(image[...], near, ids[...], near_ids[...], params)
+    loss[...] = (loss_in[...] + more) * (1.0 / ((SHIFTS + 1) * image.shape[0]))
     image_grad[...] = (image_in[...] + dot(low(coef), near, (1, 0))).astype(image_grad.dtype)
 
 
@@ -189,49 +166,46 @@
 
     text = pl.pallas_call(
         cast_kernel,
-        out_shape=jax.ShapeDtypeStruct((rows + PAD, width), bf16),
-        in_specs=[HBM, HBM],
+        out_shape=jax.ShapeDtypeStruct((rows, width), bf16),
+        in_specs=[HBM],
         out_specs=VMEM,
-        scratch_shapes=[
-            pltpu.VMEM((rows, width), f32),
-            pltpu.VMEM((1, rows), jnp.int32),
-            pltpu.SemaphoreType.DMA((CHUNKS,)),
-            pltpu.SemaphoreType.DMA,
-        ],
+        scratch_shapes=[pltpu.VMEM((rows, width), f32), pltpu.SemaphoreType.DMA((CHUNKS,))],
         compiler_params=pltpu.CompilerParams(vmem_limit_bytes=16 * 1024 * 1024),
         cost_estimate=pl.CostEstimate(flops=0, bytes_accessed=0, transcendentals=0),
         name="cast",
-    )(*(pltpu.with_memory_space_constraint(value, pltpu.HBM) for value in (ids, text_emb)))
+    )(pltpu.with_memory_space_constraint(text_emb, pltpu.HBM))
     far = ahead(text)
 
     image, text = lax.optimization_barrier((image_emb, text))
     image_emb = image
     mate_a, mate_b = across(image[:half]), across(image[half:])
     mate_ids = across(ids)
-
-    cut = rows - rows // 4
+    both_ids = ahead(jnp.concatenate([ids, mate_ids]))
+
+    cut = rows - rows // 8
     out_a, out_b, image_sum, loss = call(
         own_kernel, "own", [((cut, width), bf16), ((rows - cut, width), bf16), ((rows, width), f32), ((1, rows), f32)],
         (flags, params), ids, mate_ids, image_emb, mate_a, mate_b, text, text_accum,
     )
     arrived_a, arrived_b = ahead(out_a), ahead(out_b)
 
+    far_ids, near_ids = both_ids[:1], jnp.where(flags[0] == 0, both_ids[1:], mate_ids)
     passed_a, passed_b = call(
-        relay_kernel, "relay", [((half, width), bf16), ((rows + PAD - half, width), bf16)],
-        (flags,), loss, text, far,
+        relay_kernel, "relay", [((cut - 16, width), bf16), ((rows - cut + 16, width), bf16)],
+        (flags,), far_ids, text, far,
     )
     near_a, near_b = across(passed_a), across(passed_b)
     late, image_sum, loss = call(
         far_kernel, "far", [((rows, width), f32), ((rows, width), f32), ((1, rows), f32)],
-        (flags, params), ids, mate_ids, image_emb, mate_a, mate_b, far, image_sum, loss,
+        (flags, params), ids, mate_ids, far_ids, image_emb, mate_a, mate_b, far, image_sum, loss,
     )
     image_grad, loss = call(
         near_kernel, "near", [((rows, width), bf16), ((1, rows), f32)],
-        (params,), ids, image_emb, near_a, near_b, image_sum, loss,
+        (params,), ids, near_ids, image_emb, near_a, near_b, image_sum, loss,
     )
     late, image_grad = lax.optimization_barrier((late, image_grad))
     text_grad = add_part("add_a", 0, CHUNKS, arrived_a, late)
-    text_grad = add_part("add_b", cut, 2, arrived_b, late, text_grad)
+    text_grad = add_part("add_b", cut, 1, arrived_b, late, text_grad)
     return (loss.reshape(rows), image_grad, text_grad)
 
 

time: 36.3 us -> 36.2 us (level)
  waiting for transfers between devices: 16.4 us -> 14.6 us
  starting transfers between devices: 5.72 us -> 7.11 us
  other arithmetic: 0.08 us -> 0.85 us
  local copies, waits for them, and re-layouts: 1.32 us -> 0.87 us
    ppermute x3 -> x4, waiting for transfers between devices: 16.4 us -> 14.4 us  [ahead(): return lax.ppermute(value, AXES, skip)]
    ppermute x3 -> x4, starting transfers between devices: 4.51 us -> 6.03 us  [ahead(): return lax.ppermute(value, AXES, skip)]
    unnamed x6, local copies, waits for them, and re-layouts: 1.28 us -> 0.01 us
    slice x1, local copies, waits for them, and re-layouts: 0.05 us -> 0.86 us  [body(): mate_a, mate_b = (across(image[:half]), across(image[half:]))]
    slice x0 -> x1, other arithmetic: none -> 0.76 us  [body(): both_ids[:1]]
  transfers between devices with their start and end apart: 8 -> 9, of which waited for: 3 -> 3; matrix products, arithmetic and copies ran while one was open for 0% -> 5% of each run, Pallas kernels for 23% -> 23%
where the time goes in v11:
time: 36.2 us; the launch traced here: 36 us
  waiting for transfers between devices  14.6 us (40%)
  Pallas kernels  10.5 us (29%)
  starting transfers between devices  7.11 us (20%)
  between operations  2.04 us (6%)
  local copies, waits for them, and re-layouts  0.87 us (2%)
  other arithmetic  0.85 us (2%)
    ppermute x4, waiting for transfers between devices, ahead(): return lax.ppermute(value, AXES, skip)  14.4 us
    pallas_call x4, Pallas kernels, call(): pl.pallas_call(kernel, out_shape=[jax.ShapeDtypeStruct(s, d) for s, d in...  7.43 us
    ppermute x4, starting transfers between devices, ahead(): return lax.ppermute(value, AXES, skip)  6.03 us
    pallas_call x2, Pallas kernels, add_part(): pl.pallas_call(functools.partial(add_kernel, start, chunks), out_shape=ja...  1.7 us
    pallas_call x1, Pallas kernels, body(): pl.pallas_call(cast_kernel, out_shape=jax.ShapeDtypeStruct((rows, width),...  1.4 us
    ppermute x5, starting transfers between devices, across(): return lax.ppermute(value, AXES, swap)  1.08 us
    slice x1, local copies, waits for them, and re-layouts, body(): mate_a, mate_b = (across(image[:half]), across(image[half:]))  0.86 us
    slice x1, other arithmetic, body(): both_ids[:1]  0.76 us
  transfers between devices with their start and end apart: 9, of which 3 were waited for; matrix products, arithmetic and copies ran while one was open for 5% of the time, Pallas kernels for 23%

profile of v11, /device:TPU:0, one launch (start us, length us, event | category | flops | bytes accessed | tf_op | source)
XLA Modules:
  0.0 36.0 jit_solution(3190205849146875537)
XLA Ops:
  0.6 0.0 copy-start
  0.6 0.0 copy-start.2
  0.7 0.0 copy-start.1
  0.7 1.4 %cast.1.text = bf16[256,1152]{1,0:T(8,128)(2,1)S(1)} custom-call(f32[256,1152]{1,0:T(8,128)} %text.1), custom_call_target="tpu_custom_call" | custom-call | tf_op jit(solution)/shard_map/cast/pallas_call | solution.py:167
  2.1 3.0 %collective-permute-start.2 = (bf16[256,1152]{1,0:T(8,128)(2,1)S(1)}, bf16[256,1152]{1,0:T(8,128)(2,1)S(1)}, u32[]{:S(2)}, u32[]{:S(2)}) collective-permute-start(bf16[256,1152]{1,0:T(8,128)(2,1)S(1)} %cast.1.text), channel_id=1, source_target_pairs={{0,2},{1,3},{2,4},{3,5},{4,6},{5,7},{6,8},{7,9},{8,10},{9,11},{10,... | collective-permute-start | bytes 1769480 | tf_op jit(solution)/shard_map/ppermute | solution.py:162
  5.1 0.0 copy-done
  5.1 0.9 %fusion = (bf16[128,1152]{1,0:T(8,128)(2,1)}, bf16[128,1152]{1,0:T(8,128)(2,1)}) fusion(bf16[256,1152]{1,0:T(8,128)(2,1)S(1)} %copy-done), kind=kLoop, calls=%fused_computation.3 | loop fusion | bytes 1179648 | tf_op jit(solution)/shard_map/slice | solution.py:181
  6.0 0.0 collective-permute-start.6
  6.0 0.5 %collective-permute-start.5 = (bf16[128,1152]{1,0:T(8,128)(2,1)}, bf16[128,1152]{1,0:T(8,128)(2,1)S(1)}, u32[]{:S(2)}, u32[]{:S(2)}) collective-permute-start(bf16[128,1152]{1,0:T(8,128)(2,1)} %get-tuple-element.34), channel_id=1, source_target_pairs={{0,1},{1,0},{2,3},{3,2},{4,5},{5,4},{6,7},{7,6},{8,9},{9,8},{10,11... | collective-permute-start | bytes 884744 | tf_op jit(solution)/shard_map/ppermute | solution.py:165
  6.5 0.0 copy-done.2
  6.5 0.0 collective-permute-start
  7.8 0.2 collective-permute-done.mate_ids
  7.9 1.4 %collective-permute-start.1 = (s32[2,256]{1,0:T(2,128)S(1)}, s32[2,256]{1,0:T(2,128)}, u32[]{:S(2)}, u32[]{:S(2)}) collective-permute-start(s32[2,256]{1,0:T(2,128)S(1)} %pad_add_fusion), channel_id=1, source_target_pairs={{0,2},{1,3},{2,4},{3,5},{4,6},{5,7},{6,8},{7,9},{8,10},{9,11},{10,... | collective-permute-start | bytes 6152 | tf_op jit(solution)/shard_map/ppermute | solution.py:162
  9.4 0.1 pad_maximum_fusion.params
  9.5 0.0 collective-permute-done.6.mate_b
  9.5 0.0 collective-permute-done.5.mate_a
  9.5 0.0 copy-done.1
  9.5 3.1 %own.1 = (bf16[224,1152]{1,0:T(8,128)(2,1)S(1)}, bf16[32,1152]{1,0:T(8,128)(2,1)S(1)}, f32[256,1152]{1,0:T(8,128)S(1)}, f32[1,256]{1,0:T(1,128)S(1)}) custom-call(s32[1]{0:T(128)} %bitcast.1.flags, f32[2]{0:T(128)S(1)} %pad_maximum_fusion.params, s32[1,256]{1,0:T(1,128)S(1)} %bitcast.5, s32[1,256]{1,0:T(1,128)S(1)} %collective-permute-done.mate_ids, ...), custom_call_target="tpu_custom_call" | custom-call | tf_op jit(solution)/shard_map/own/pallas_call | solution.py:124
  12.6 1.6 %collective-permute-start.8 = (bf16[224,1152]{1,0:T(8,128)(2,1)S(1)}, bf16[224,1152]{1,0:T(8,128)(2,1)S(1)}, u32[]{:S(2)}, u32[]{:S(2)}) collective-permute-start(bf16[224,1152]{1,0:T(8,128)(2,1)S(1)} %get-tuple-element.32), channel_id=1, source_target_pairs={{0,2},{1,3},{2,4},{3,5},{4,6},{5,7},{6,8},{7,9},{8,10},{9,11},{10,... | collective-permute-start | bytes 1548296 | tf_op jit(solution)/shard_map/ppermute | solution.py:162
  14.2 9.2 %collective-permute-done.1 = s32[2,256]{1,0:T(2,128)} collective-permute-done((s32[2,256]{1,0:T(2,128)S(1)}, s32[2,256]{1,0:T(2,128)}, u32[]{:S(2)}, u32[]{:S(2)}) %collective-permute-start.1) | collective-permute-done | bytes 2080 | tf_op jit(solution)/shard_map/ppermute | solution.py:162
  23.4 0.8 %fusion.1 = (s32[1,256]{1,0:T(1,128)S(1)}, s32[1,256]{1,0:T(1,128)S(1)}) fusion(s32[2,256]{1,0:T(2,128)} %collective-permute-done.1, s32[1,256]{1,0:T(1,128)S(1)} %collective-permute-done.mate_ids, pred[]{:T(512)S(6)} %eq.5), kind=kLoop, calls=%fused_computation.4 | loop fusion | flops 256 | bytes 5121 | tf_op jit(solution)/shard_map/slice | solution.py:192
  24.1 0.0 collective-permute-done.2.far
  24.2 0.1 collective-permute-start.3
  24.3 0.5 %collective-permute-start.4 = (bf16[48,1152]{1,0:T(8,128)(2,1)S(1)}, bf16[48,1152]{1,0:T(8,128)(2,1)S(1)}, u32[]{:S(2)}, u32[]{:S(2)}) collective-permute-start(bf16[48,1152]{1,0:T(8,128)(2,1)S(1)} %get-tuple-element.21), channel_id=1, source_target_pairs={{0,1},{1,0},{2,3},{3,2},{4,5},{5,4},{6,7},{7,6},{8,9},{9,8},{10,11... | collective-permute-start | bytes 331784 | tf_op jit(solution)/shard_map/ppermute | solution.py:165
  24.8 0.0 collective-permute-start.7
  24.8 1.8 %far.1 = (f32[256,1152]{1,0:T(8,128)S(1)}, f32[256,1152]{1,0:T(8,128)S(1)}, f32[1,256]{1,0:T(1,128)S(1)}) custom-call(s32[1]{0:T(128)} %bitcast.1.flags, f32[2]{0:T(128)S(1)} %pad_maximum_fusion.params, s32[1,256]{1,0:T(1,128)S(1)} %bitcast.6, s32[1,256]{1,0:T(1,128)S(1)} %collective-permute-done.mate_ids, s32[1,256]{1,0:T(1,128)S(1)} %get-tuple-element.35.token.far_ids, ...), custom_call_target="tpu_custom_call" | custom-call | tf_op jit(solution)/shard_map/far/pallas_call | solution.py:124
  26.6 0.0 collective-permute-done.4.near_b
  26.6 0.0 collective-permute-done.3.near_a
  26.6 2.4 %near.1 = (bf16[256,1152]{1,0:T(8,128)(2,1)}, f32[1,256]{1,0:T(1,128)}) custom-call(f32[2]{0:T(128)S(1)} %pad_maximum_fusion.params, s32[1,256]{1,0:T(1,128)S(1)} %bitcast.7, s32[1,256]{1,0:T(1,128)S(1)} %get-tuple-element.36.near_ids, bf16[256,1152]{1,0:T(8,128)(2,1)S(1)} %copy-done, bf16[208,1152]{1,0:T(8,128)(2,1)S(1)} %collective-permute-done.3.near_a, ...), custom_call_target="tpu_custom_call" | custom-call | tf_op jit(solution)/shard_map/near/pallas_call | solution.py:124
  29.0 5.2 %collective-permute-done.8.arrived = bf16[224,1152]{1,0:T(8,128)(2,1)S(1)} collective-permute-done((bf16[224,1152]{1,0:T(8,128)(2,1)S(1)}, bf16[224,1152]{1,0:T(8,128)(2,1)S(1)}, u32[]{:S(2)}, u32[]{:S(2)}) %collective-permute-start.8) | collective-permute-done | bytes 516128 | tf_op jit(solution)/shard_map/ppermute | solution.py:162
  34.3 1.0 %add_a.1.refs_0_ = f32[256,1152]{1,0:T(8,128)} custom-call(bf16[224,1152]{1,0:T(8,128)(2,1)S(1)} %collective-permute-done.8.arrived, f32[256,1152]{1,0:T(8,128)S(1)} %get-tuple-element.31.late), custom_call_target="tpu_custom_call" | custom-call | tf_op jit(solution)/shard_map/add_a/pallas_call | solution.py:136
  35.3 0.0 collective-permute-done.7.arrived
  35.3 0.7 %add_b.1 = f32[256,1152]{1,0:T(8,128)} custom-call(bf16[32,1152]{1,0:T(8,128)(2,1)S(1)} %collective-permute-done.7.arrived, f32[256,1152]{1,0:T(8,128)S(1)} %get-tuple-element.31.late, f32[256,1152]{1,0:T(8,128)} %add_a.1.refs_0_), custom_call_target="tpu_custom_call", output_to_operand_aliasing={{}: (2, {})} | custom-call | tf_op jit(solution)/shard_map/add_b/pallas_call | solution.py:136
  (2 shorter events, 0.1 us)
Async XLA Ops:
  0.6 4.5 %copy-start = (bf16[256,1152]{1,0:T(8,128)(2,1)S(1)}, bf16[256,1152]{1,0:T(8,128)(2,1)}, u32[]{:S(2)}) copy-start(bf16[256,1152]{1,0:T(8,128)(2,1)} %image.2) | copy-start | bytes 1769476
  0.6 5.8 %copy-start.2 = (s32[256]{0:T(256)S(1)}, s32[256]{0:T(256)}, u32[]{:S(2)}) copy-start(s32[256]{0:T(256)} %param.9) | copy-start | bytes 3076
  0.7 8.8 %copy-start.1 = (f32[256,1152]{1,0:T(8,128)S(1)}, f32[256,1152]{1,0:T(8,128)}, u32[]{:S(2)}) copy-start(f32[256,1152]{1,0:T(8,128)} %accum.1) | copy-start | bytes 3538948
  2.1 22.1 %collective-permute-start.2 = (bf16[256,1152]{1,0:T(8,128)(2,1)S(1)}, bf16[256,1152]{1,0:T(8,128)(2,1)S(1)}, u32[]{:S(2)}, u32[]{:S(2)}) collective-permute-start(bf16[256,1152]{1,0:T(8,128)(2,1)S(1)} %cast.1.text), channel_id=1, source_target_pairs={{0,2},{1,3},{2,4},{3,5},{4,6},{5,7},{6,8},{7,9},{8,10},{9,11},{10,... | collective-permute-start | bytes 1769480 | tf_op jit(solution)/shard_map/ppermute | solution.py:162
  6.0 3.5 %collective-permute-start.6 = (bf16[128,1152]{1,0:T(8,128)(2,1)}, bf16[128,1152]{1,0:T(8,128)(2,1)S(1)}, u32[]{:S(2)}, u32[]{:S(2)}) collective-permute-start(bf16[128,1152]{1,0:T(8,128)(2,1)} %get-tuple-element.33), channel_id=1, source_target_pairs={{0,1},{1,0},{2,3},{3,2},{4,5},{5,4},{6,7},{7,6},{8,9},{9,8},{10,11... | collective-permute-start | bytes 884744 | tf_op jit(solution)/shard_map/ppermute | solution.py:165
  6.0 3.5 %collective-permute-start.5 = (bf16[128,1152]{1,0:T(8,128)(2,1)}, bf16[128,1152]{1,0:T(8,128)(2,1)S(1)}, u32[]{:S(2)}, u32[]{:S(2)}) collective-permute-start(bf16[128,1152]{1,0:T(8,128)(2,1)} %get-tuple-element.34), channel_id=1, source_target_pairs={{0,1},{1,0},{2,3},{3,2},{4,5},{5,4},{6,7},{7,6},{8,9},{9,8},{10,11... | collective-permute-start | bytes 884744 | tf_op jit(solution)/shard_map/ppermute | solution.py:165
  6.5 1.5 %collective-permute-start = (s32[1,256]{1,0:T(1,128)S(1)}, s32[1,256]{1,0:T(1,128)S(1)}, u32[]{:S(2)}, u32[]{:S(2)}) collective-permute-start(s32[1,256]{1,0:T(1,128)S(1)} %bitcast.3), channel_id=1, source_target_pairs={{0,1},{1,0},{2,3},{3,2},{4,5},{5,4},{6,7},{7,6},{8,9},{9,8},{10,11... | collective-permute-start | bytes 3080 | tf_op jit(solution)/shard_map/ppermute | solution.py:165
  7.9 15.4 %collective-permute-start.1 = (s32[2,256]{1,0:T(2,128)S(1)}, s32[2,256]{1,0:T(2,128)}, u32[]{:S(2)}, u32[]{:S(2)}) collective-permute-start(s32[2,256]{1,0:T(2,128)S(1)} %pad_add_fusion), channel_id=1, source_target_pairs={{0,2},{1,3},{2,4},{3,5},{4,6},{5,7},{6,8},{7,9},{8,10},{9,11},{10,... | collective-permute-start | bytes 6152 | tf_op jit(solution)/shard_map/ppermute | solution.py:162
  12.6 21.7 %collective-permute-start.8 = (bf16[224,1152]{1,0:T(8,128)(2,1)S(1)}, bf16[224,1152]{1,0:T(8,128)(2,1)S(1)}, u32[]{:S(2)}, u32[]{:S(2)}) collective-permute-start(bf16[224,1152]{1,0:T(8,128)(2,1)S(1)} %get-tuple-element.32), channel_id=1, source_target_pairs={{0,2},{1,3},{2,4},{3,5},{4,6},{5,7},{6,8},{7,9},{8,10},{9,11},{10,... | collective-permute-start | bytes 1548296 | tf_op jit(solution)/shard_map/ppermute | solution.py:162
  24.2 2.4 %collective-permute-start.3 = (bf16[208,1152]{1,0:T(8,128)(2,1)S(1)}, bf16[208,1152]{1,0:T(8,128)(2,1)S(1)}, u32[]{:S(2)}, u32[]{:S(2)}) collective-permute-start(bf16[208,1152]{1,0:T(8,128)(2,1)S(1)} %get-tuple-element.20), channel_id=1, source_target_pairs={{0,1},{1,0},{2,3},{3,2},{4,5},{5,4},{6,7},{7,6},{8,9},{9,8},{10,11... | collective-permute-start | bytes 1437704 | tf_op jit(solution)/shard_map/ppermute | solution.py:165
  24.3 2.3 %collective-permute-start.4 = (bf16[48,1152]{1,0:T(8,128)(2,1)S(1)}, bf16[48,1152]{1,0:T(8,128)(2,1)S(1)}, u32[]{:S(2)}, u32[]{:S(2)}) collective-permute-start(bf16[48,1152]{1,0:T(8,128)(2,1)S(1)} %get-tuple-element.21), channel_id=1, source_target_pairs={{0,1},{1,0},{2,3},{3,2},{4,5},{5,4},{6,7},{7,6},{8,9},{9,8},{10,11... | collective-permute-start | bytes 331784 | tf_op jit(solution)/shard_map/ppermute | solution.py:165
  24.8 10.5 %collective-permute-start.7 = (bf16[32,1152]{1,0:T(8,128)(2,1)S(1)}, bf16[32,1152]{1,0:T(8,128)(2,1)S(1)}, u32[]{:S(2)}, u32[]{:S(2)}) collective-permute-start(bf16[32,1152]{1,0:T(8,128)(2,1)S(1)} %get-tuple-element.30), channel_id=1, source_target_pairs={{0,2},{1,3},{2,4},{3,5},{4,6},{5,7},{6,8},{7,9},{8,10},{9,11},{10,... | collective-permute-start | bytes 221192 | tf_op jit(solution)/shard_map/ppermute | solution.py:162

commit v12 on v11

--- a/solution.py
+++ b/solution.py
@@ -12,6 +12,7 @@
 CHUNKS = 4
 VMEM = pl.BlockSpec(memory_space=pltpu.VMEM)
 SMEM = pl.BlockSpec(memory_space=pltpu.SMEM)
+ANY = pl.BlockSpec(memory_space=pl.ANY)
 HBM = pl.BlockSpec(memory_space=pltpu.HBM)
 
 
@@ -48,6 +49,19 @@
         out[part, :] = staged[part, :].astype(out.dtype)
 
 
+def load_kernel(text, image, out, half_a, half_b, sems):
+    half = half_a.shape[0]
+    copies = [
+        pltpu.make_async_copy(image.at[pl.ds(0, half)], half_a, sems.at[0]),
+        pltpu.make_async_copy(image.at[pl.ds(half, half)], half_b, sems.at[1]),
+        pltpu.make_async_copy(image, out, sems.at[2]),
+    ]
+    for copy in copies:
+        copy.start()
+    for copy in copies:
+        copy.wait()
+
+
 def add_kernel(start, chunks, arrived, late, *refs):
     out, staged, sems = refs[-3:]
     step = arrived.shape[0] // chunks
@@ -61,10 +75,15 @@
         copy.wait()
 
 
-def own_kernel(flags, params, ids, mate_ids, image, mate_a, mate_b, text, accum, out_a, out_b, image_sum, loss):
+def own_kernel(flags, params, ids, mate_ids, image, mate_a, mate_b, text, accum_in, out_a, out_b, image_sum, loss,
+               accum, sem):
+    copy = pltpu.make_async_copy(accum_in, accum, sem)
+    copy.start()
     own_loss, coef = pair(image[...], text[...], ids[...], ids[...], params)
     loss[...] = own_loss
-    total = accum[...] + dot(low(coef.T), image[...], (1, 0))
+    part = dot(low(coef.T), image[...], (1, 0))
+    copy.wait()
+    total = accum[...] + part
     cut = out_a.shape[0]
 
     def give(value):
@@ -95,9 +114,9 @@
     pl.when(flags[0] == 1)(lambda: fill(far))
 
 
-def far_kernel(flags, params, ids, mate_ids, far_ids, image, mate_a, mate_b, far, image_in, loss_in,
+def far_kernel(flags, params, ids, mate_ids, both_ids, image, mate_a, mate_b, far, image_in, loss_in,
                late, image_sum, loss):
-    more, coef = pair(image[...], far[...], ids[...], far_ids[...], params)
+    more, coef = pair(image[...], far[...], ids[...], both_ids[:1, :], params)
     loss[...] = loss_in[...] + more
     image_sum[...] = image_in[...] + dot(low(coef), far[...], (1, 0))
     part = dot(low(coef.T), image[...], (1, 0))
@@ -109,25 +128,26 @@
     @pl.when(flags[0] == 1)
     def _():
         mate = jnp.concatenate([mate_a[...], mate_b[...]], axis=0)
-        _, mate_coef = pair(mate, far[...], mate_ids[...], far_ids[...], params)
+        _, mate_coef = pair(mate, far[...], mate_ids[...], both_ids[:1, :], params)
         late[...] = part + dot(low(mate_coef.T), mate, (1, 0))
 
 
-def near_kernel(params, ids, near_ids, image, near_a, near_b, image_in, loss_in, image_grad, loss):
+def near_kernel(flags, params, ids, mate_ids, both_ids, image, near_a, near_b, image_in, loss_in, image_grad, loss):
+    near_ids = jnp.where(flags[0] == 0, both_ids[1:, :], mate_ids[...])
     near = jnp.concatenate([near_a[...], near_b[...]], axis=0)
-    more, coef = pair(image[...], near, ids[...], near_ids[...], params)
+    more, coef = pair(image[...], near, ids[...], near_ids, params)
     loss[...] = (loss_in[...] + more) * (1.0 / ((SHIFTS + 1) * image.shape[0]))
     image_grad[...] = (image_in[...] + dot(low(coef), near, (1, 0))).astype(image_grad.dtype)
 
 
-def call(kernel, name, outs, scalars, *operands):
+def call(kernel, name, outs, scalars, *operands, flops=0):
     return pl.pallas_call(
         kernel,
         out_shape=[jax.ShapeDtypeStruct(s, d) for s, d in outs],
         in_specs=[SMEM] * len(scalars) + [VMEM] * len(operands),
         out_specs=[VMEM] * len(outs),
         compiler_params=pltpu.CompilerParams(vmem_limit_bytes=16 * 1024 * 1024),
-        cost_estimate=pl.CostEstimate(flops=0, bytes_accessed=0, transcendentals=0),
+        cost_estimate=pl.CostEstimate(flops=flops, bytes_accessed=0, transcendentals=0),
         name=name,
     )(*scalars, *operands)
 
@@ -176,35 +196,54 @@
     )(pltpu.with_memory_space_constraint(text_emb, pltpu.HBM))
     far = ahead(text)
 
-    image, text = lax.optimization_barrier((image_emb, text))
-    image_emb = image
-    mate_a, mate_b = across(image[:half]), across(image[half:])
+    image, half_a, half_b = pl.pallas_call(
+        load_kernel,
+        out_shape=[jax.ShapeDtypeStruct((n, width), bf16) for n in (rows, half, rows - half)],
+        in_specs=[ANY, HBM],
+        out_specs=[VMEM] * 3,
+        scratch_shapes=[pltpu.SemaphoreType.DMA((3,))],
+        compiler_params=pltpu.CompilerParams(vmem_limit_bytes=16 * 1024 * 1024),
+        cost_estimate=pl.CostEstimate(flops=0, bytes_accessed=0, transcendentals=0),
+        name="load",
+    )(text, pltpu.with_memory_space_constraint(image_emb, pltpu.HBM))
+    mate_a, mate_b = across(half_a), across(half_b)
     mate_ids = across(ids)
     both_ids = ahead(jnp.concatenate([ids, mate_ids]))
 
-    cut = rows - rows // 8
-    out_a, out_b, image_sum, loss = call(
-        own_kernel, "own", [((cut, width), bf16), ((rows - cut, width), bf16), ((rows, width), f32), ((1, rows), f32)],
-        (flags, params), ids, mate_ids, image_emb, mate_a, mate_b, text, text_accum,
-    )
+    cut = rows - rows * 3 // 16
+    out_a, out_b, image_sum, loss = pl.pallas_call(
+        own_kernel,
+        out_shape=[
+            jax.ShapeDtypeStruct((cut, width), bf16),
+            jax.ShapeDtypeStruct((rows - cut, width), bf16),
+            jax.ShapeDtypeStruct((rows, width), f32),
+            jax.ShapeDtypeStruct((1, rows), f32),
+        ],
+        in_specs=[SMEM] * 2 + [VMEM] * 6 + [HBM],
+        out_specs=[VMEM] * 4,
+        scratch_shapes=[pltpu.VMEM((rows, width), f32), pltpu.SemaphoreType.DMA],
+        compiler_params=pltpu.CompilerParams(vmem_limit_bytes=16 * 1024 * 1024),
+        cost_estimate=pl.CostEstimate(flops=0, bytes_accessed=0, transcendentals=0),
+        name="own",
+    )(flags, params, ids, mate_ids, image, mate_a, mate_b, text,
+      pltpu.with_memory_space_constraint(text_accum, pltpu.HBM))
     arrived_a, arrived_b = ahead(out_a), ahead(out_b)
 
-    far_ids, near_ids = both_ids[:1], jnp.where(flags[0] == 0, both_ids[1:], mate_ids)
     passed_a, passed_b = call(
         relay_kernel, "relay", [((cut - 16, width), bf16), ((rows - cut + 16, width), bf16)],
-        (flags,), far_ids, text, far,
+        (flags,), both_ids, text, far, flops=1 << 30,
     )
     near_a, near_b = across(passed_a), across(passed_b)
     late, image_sum, loss = call(
         far_kernel, "far", [((rows, width), f32), ((rows, width), f32), ((1, rows), f32)],
-        (flags, params), ids, mate_ids, far_ids, image_emb, mate_a, mate_b, far, image_sum, loss,
+        (flags, params), ids, mate_ids, both_ids, image, mate_a, mate_b, far, image_sum, loss,
     )
     image_grad, loss = call(
         near_kernel, "near", [((rows, width), bf16), ((1, rows), f32)],
-        (params,), ids, near_ids, image_emb, near_a, near_b, image_sum, loss,
+        (flags, params), ids, mate_ids, both_ids, image, near_a, near_b, image_sum, loss,
     )
     late, image_grad = lax.optimization_barrier((late, image_grad))
-    text_grad = add_part("add_a", 0, CHUNKS, arrived_a, late)
+    text_grad = add_part("add_a", 0, 2, arrived_a, late)
     text_grad = add_part("add_b", cut, 1, arrived_b, late, text_grad)
     return (loss.reshape(rows), image_grad, text_grad)
 

time: 36.2 us -> 35.9 us (level)
  Pallas kernels: 10.5 us -> 13 us
  waiting for transfers between devices: 14.6 us -> 13.2 us
  local copies, waits for them, and re-layouts: 0.87 us -> 0.01 us
  other arithmetic: 0.85 us -> 0.08 us
    pallas_call x0 -> x2, Pallas kernels: none -> 5.71 us  [the longest x1 4.41 us: body(): pl.pallas_call(own_kernel, out_shape=[jax.ShapeDtypeStruct((cut, width),...]
    pallas_call x4 -> x3, Pallas kernels: 7.43 us -> 4.3 us  [call(): pl.pallas_call(kernel, out_shape=[jax.ShapeDtypeStruct(s, d) for s, d in...]
    ppermute x4, waiting for transfers between devices: 14.4 us -> 13.1 us  [ahead(): return lax.ppermute(value, AXES, skip)]
    slice x1 -> x0, local copies, waits for them, and re-layouts: 0.86 us -> none  [body(): mate_a, mate_b = (across(image[:half]), across(image[half:]))]
    slice x1 -> x0, other arithmetic: 0.76 us -> none  [body(): both_ids[:1]]
  transfers between devices with their start and end apart: 9 -> 9, of which waited for: 3 -> 4; matrix products, arithmetic and copies ran while one was open for 5% -> 0% of each run, Pallas kernels for 23% -> 31%
where the time goes in v12:
time: 35.9 us; the launch traced here: 35.6 us
  waiting for transfers between devices  13.2 us (37%)
  Pallas kernels  13 us (36%)
  starting transfers between devices  7.27 us (20%)
  between operations  2.03 us (6%)
    ppermute x4, waiting for transfers between devices, ahead(): return lax.ppermute(value, AXES, skip)  13.1 us
    ppermute x4, starting transfers between devices, ahead(): return lax.ppermute(value, AXES, skip)  6.05 us
    pallas_call x1, Pallas kernels, body(): pl.pallas_call(own_kernel, out_shape=[jax.ShapeDtypeStruct((cut, width),...  4.41 us
    pallas_call x3, Pallas kernels, call(): pl.pallas_call(kernel, out_shape=[jax.ShapeDtypeStruct(s, d) for s, d in...  4.3 us
    pallas_call x2, Pallas kernels, add_part(): pl.pallas_call(functools.partial(add_kernel, start, chunks), out_shape=ja...  1.72 us
    pallas_call x1, Pallas kernels, body(): pl.pallas_call(load_kernel, out_shape=[jax.ShapeDtypeStruct((n, width), b...  1.31 us
    pallas_call x1, Pallas kernels, body(): pl.pallas_call(cast_kernel, out_shape=jax.ShapeDtypeStruct((rows, width),...  1.28 us
    ppermute x5, starting transfers between devices, across(): return lax.ppermute(value, AXES, swap)  1.21 us
  transfers between devices with their start and end apart: 9, of which 4 were waited for; matrix products, arithmetic and copies ran while one was open for 0% of the time, Pallas kernels for 31%

profile of v12, /device:TPU:0, one launch (start us, length us, event | category | flops | bytes accessed | tf_op | source)
XLA Modules:
  0.0 35.6 jit_solution(4324944160004461426)
XLA Ops:
  0.6 0.0 copy-start
  0.6 1.3 %cast.1.text = bf16[256,1152]{1,0:T(8,128)(2,1)S(1)} custom-call(f32[256,1152]{1,0:T(8,128)} %text.1), custom_call_target="tpu_custom_call" | custom-call | tf_op jit(solution)/shard_map/cast/pallas_call | solution.py:187
  1.9 3.0 %collective-permute-start.2 = (bf16[256,1152]{1,0:T(8,128)(2,1)S(1)}, bf16[256,1152]{1,0:T(8,128)(2,1)S(1)}, u32[]{:S(2)}, u32[]{:S(2)}) collective-permute-start(bf16[256,1152]{1,0:T(8,128)(2,1)S(1)} %cast.1.text), channel_id=1, source_target_pairs={{0,2},{1,3},{2,4},{3,5},{4,6},{5,7},{6,8},{7,9},{8,10},{9,11},{10,... | collective-permute-start | bytes 1769480 | tf_op jit(solution)/shard_map/ppermute | solution.py:182
  5.0 1.3 %load.1 = (bf16[256,1152]{1,0:T(8,128)(2,1)S(1)}, bf16[128,1152]{1,0:T(8,128)(2,1)S(1)}, bf16[128,1152]{1,0:T(8,128)(2,1)S(1)}) custom-call(bf16[256,1152]{1,0:T(8,128)(2,1)S(1)} %cast.1.text, bf16[256,1152]{1,0:T(8,128)(2,1)} %image.1), custom_call_target="tpu_custom_call" | custom-call | tf_op jit(solution)/shard_map/load/pallas_call | solution.py:199
  6.3 0.1 collective-permute-start.5
  6.3 0.5 %collective-permute-start.6 = (bf16[128,1152]{1,0:T(8,128)(2,1)S(1)}, bf16[128,1152]{1,0:T(8,128)(2,1)S(1)}, u32[]{:S(2)}, u32[]{:S(2)}) collective-permute-start(bf16[128,1152]{1,0:T(8,128)(2,1)S(1)} %get-tuple-element.23), channel_id=1, source_target_pairs={{0,1},{1,0},{2,3},{3,2},{4,5},{5,4},{6,7},{7,6},{8,9},{9,8},{10,11... | collective-permute-start | bytes 884744 | tf_op jit(solution)/shard_map/ppermute | solution.py:185
  6.8 0.0 copy-done
  6.8 0.1 collective-permute-start
  8.2 0.1 collective-permute-done.mate_ids
  8.3 1.5 %collective-permute-start.1 = (s32[2,256]{1,0:T(2,128)S(1)}, s32[2,256]{1,0:T(2,128)S(1)}, u32[]{:S(2)}, u32[]{:S(2)}) collective-permute-start(s32[2,256]{1,0:T(2,128)S(1)} %pad_add_fusion), channel_id=1, source_target_pairs={{0,2},{1,3},{2,4},{3,5},{4,6},{5,7},{6,8},{7,9},{8,10},{9,11},{10,... | collective-permute-start | bytes 6152 | tf_op jit(solution)/shard_map/ppermute | solution.py:182
  9.8 0.1 pad_maximum_fusion.params
  9.9 0.0 collective-permute-done.5.mate_a
  9.9 0.0 collective-permute-done.6.mate_b
  9.9 4.4 %own.1 = (bf16[208,1152]{1,0:T(8,128)(2,1)S(1)}, bf16[48,1152]{1,0:T(8,128)(2,1)S(1)}, f32[256,1152]{1,0:T(8,128)S(1)}, f32[1,256]{1,0:T(1,128)S(1)}) custom-call(s32[1]{0:T(128)} %bitcast.flags, f32[2]{0:T(128)S(1)} %pad_maximum_fusion.params, s32[1,256]{1,0:T(1,128)S(1)} %bitcast.5, s32[1,256]{1,0:T(1,128)S(1)} %collective-permute-done.mate_ids, ...), custom_call_target="tpu_custom_call" | custom-call | tf_op jit(solution)/shard_map/own/pallas_call | solution.py:214
  14.3 1.6 %collective-permute-start.8 = (bf16[208,1152]{1,0:T(8,128)(2,1)S(1)}, bf16[208,1152]{1,0:T(8,128)(2,1)S(1)}, u32[]{:S(2)}, u32[]{:S(2)}) collective-permute-start(bf16[208,1152]{1,0:T(8,128)(2,1)S(1)} %get-tuple-element.34), channel_id=1, source_target_pairs={{0,2},{1,3},{2,4},{3,5},{4,6},{5,7},{6,8},{7,9},{8,10},{9,11},{10,... | collective-permute-start | bytes 1437704 | tf_op jit(solution)/shard_map/ppermute | solution.py:182
  15.9 7.2 %collective-permute-done.1.token.both_ids = s32[2,256]{1,0:T(2,128)S(1)} collective-permute-done((s32[2,256]{1,0:T(2,128)S(1)}, s32[2,256]{1,0:T(2,128)S(1)}, u32[]{:S(2)}, u32[]{:S(2)}) %collective-permute-start.1) | collective-permute-done | bytes 2080 | tf_op jit(solution)/shard_map/ppermute | solution.py:182
  23.1 0.0 collective-permute-done.2.far
  23.2 0.1 collective-permute-start.3
  23.3 0.5 %collective-permute-start.4 = (bf16[64,1152]{1,0:T(8,128)(2,1)S(1)}, bf16[64,1152]{1,0:T(8,128)(2,1)S(1)}, u32[]{:S(2)}, u32[]{:S(2)}) collective-permute-start(bf16[64,1152]{1,0:T(8,128)(2,1)S(1)} %get-tuple-element.21), channel_id=1, source_target_pairs={{0,1},{1,0},{2,3},{3,2},{4,5},{5,4},{6,7},{7,6},{8,9},{9,8},{10,11... | collective-permute-start | bytes 442376 | tf_op jit(solution)/shard_map/ppermute | solution.py:185
  23.8 0.0 collective-permute-start.7
  23.8 1.8 %far.1 = (f32[256,1152]{1,0:T(8,128)S(1)}, f32[256,1152]{1,0:T(8,128)S(1)}, f32[1,256]{1,0:T(1,128)S(1)}) custom-call(s32[1]{0:T(128)} %bitcast.flags, f32[2]{0:T(128)S(1)} %pad_maximum_fusion.params, s32[1,256]{1,0:T(1,128)S(1)} %bitcast.6, s32[1,256]{1,0:T(1,128)S(1)} %collective-permute-done.mate_ids, s32[2,256]{1,0:T(2,128)S(1)} %collective-permute-done.1.token.both_ids, ...), custom_call_target="tpu_custom_call" | custom-call | tf_op jit(solution)/shard_map/far/pallas_call | solution.py:144
  25.6 0.0 collective-permute-done.4.near_b
  25.6 0.0 collective-permute-done.3.near_a
  25.6 2.4 %near.1 = (bf16[256,1152]{1,0:T(8,128)(2,1)}, f32[1,256]{1,0:T(1,128)}) custom-call(s32[1]{0:T(128)} %bitcast.flags, f32[2]{0:T(128)S(1)} %pad_maximum_fusion.params, s32[1,256]{1,0:T(1,128)S(1)} %bitcast.7, s32[1,256]{1,0:T(1,128)S(1)} %collective-permute-done.mate_ids, s32[2,256]{1,0:T(2,128)S(1)} %collective-permute-done.1.token.both_ids, ...), custom_call_target="tpu_custom_call" | custom-call | tf_op jit(solution)/shard_map/near/pallas_call | solution.py:144
  28.0 5.3 %collective-permute-done.8.arrived = bf16[208,1152]{1,0:T(8,128)(2,1)S(1)} collective-permute-done((bf16[208,1152]{1,0:T(8,128)(2,1)S(1)}, bf16[208,1152]{1,0:T(8,128)(2,1)S(1)}, u32[]{:S(2)}, u32[]{:S(2)}) %collective-permute-start.8) | collective-permute-done | bytes 479264 | tf_op jit(solution)/shard_map/ppermute | solution.py:182
  33.4 1.0 %add_a.1.refs_0_ = f32[256,1152]{1,0:T(8,128)} custom-call(bf16[208,1152]{1,0:T(8,128)(2,1)S(1)} %collective-permute-done.8.arrived, f32[256,1152]{1,0:T(8,128)S(1)} %get-tuple-element.33.late), custom_call_target="tpu_custom_call" | custom-call | tf_op jit(solution)/shard_map/add_a/pallas_call | solution.py:156
  34.4 0.5 %collective-permute-done.7.arrived = bf16[48,1152]{1,0:T(8,128)(2,1)S(1)} collective-permute-done((bf16[48,1152]{1,0:T(8,128)(2,1)S(1)}, bf16[48,1152]{1,0:T(8,128)(2,1)S(1)}, u32[]{:S(2)}, u32[]{:S(2)}) %collective-permute-start.7) | collective-permute-done | bytes 110624 | tf_op jit(solution)/shard_map/ppermute | solution.py:182
  34.9 0.7 %add_b.1 = f32[256,1152]{1,0:T(8,128)} custom-call(bf16[48,1152]{1,0:T(8,128)(2,1)S(1)} %collective-permute-done.7.arrived, f32[256,1152]{1,0:T(8,128)S(1)} %get-tuple-element.33.late, f32[256,1152]{1,0:T(8,128)} %add_a.1.refs_0_), custom_call_target="tpu_custom_call", output_to_operand_aliasing={{}: (2, {})} | custom-call | tf_op jit(solution)/shard_map/add_b/pallas_call | solution.py:156
  (2 shorter events, 0.1 us)
Async XLA Ops:
  0.6 6.2 %copy-start = (s32[256]{0:T(256)S(1)}, s32[256]{0:T(256)}, u32[]{:S(2)}) copy-start(s32[256]{0:T(256)} %param.9) | copy-start | bytes 3076
  1.9 21.2 %collective-permute-start.2 = (bf16[256,1152]{1,0:T(8,128)(2,1)S(1)}, bf16[256,1152]{1,0:T(8,128)(2,1)S(1)}, u32[]{:S(2)}, u32[]{:S(2)}) collective-permute-start(bf16[256,1152]{1,0:T(8,128)(2,1)S(1)} %cast.1.text), channel_id=1, source_target_pairs={{0,2},{1,3},{2,4},{3,5},{4,6},{5,7},{6,8},{7,9},{8,10},{9,11},{10,... | collective-permute-start | bytes 1769480 | tf_op jit(solution)/shard_map/ppermute | solution.py:182
  6.3 3.6 %collective-permute-start.5 = (bf16[128,1152]{1,0:T(8,128)(2,1)S(1)}, bf16[128,1152]{1,0:T(8,128)(2,1)S(1)}, u32[]{:S(2)}, u32[]{:S(2)}) collective-permute-start(bf16[128,1152]{1,0:T(8,128)(2,1)S(1)} %get-tuple-element.22), channel_id=1, source_target_pairs={{0,1},{1,0},{2,3},{3,2},{4,5},{5,4},{6,7},{7,6},{8,9},{9,8},{10,11... | collective-permute-start | bytes 884744 | tf_op jit(solution)/shard_map/ppermute | solution.py:185
  6.3 3.5 %collective-permute-start.6 = (bf16[128,1152]{1,0:T(8,128)(2,1)S(1)}, bf16[128,1152]{1,0:T(8,128)(2,1)S(1)}, u32[]{:S(2)}, u32[]{:S(2)}) collective-permute-start(bf16[128,1152]{1,0:T(8,128)(2,1)S(1)} %get-tuple-element.23), channel_id=1, source_target_pairs={{0,1},{1,0},{2,3},{3,2},{4,5},{5,4},{6,7},{7,6},{8,9},{9,8},{10,11... | collective-permute-start | bytes 884744 | tf_op jit(solution)/shard_map/ppermute | solution.py:185
  6.8 1.5 %collective-permute-start = (s32[1,256]{1,0:T(1,128)S(1)}, s32[1,256]{1,0:T(1,128)S(1)}, u32[]{:S(2)}, u32[]{:S(2)}) collective-permute-start(s32[1,256]{1,0:T(1,128)S(1)} %bitcast.3), channel_id=1, source_target_pairs={{0,1},{1,0},{2,3},{3,2},{4,5},{5,4},{6,7},{7,6},{8,9},{9,8},{10,11... | collective-permute-start | bytes 3080 | tf_op jit(solution)/shard_map/ppermute | solution.py:185
  8.3 14.8 %collective-permute-start.1 = (s32[2,256]{1,0:T(2,128)S(1)}, s32[2,256]{1,0:T(2,128)S(1)}, u32[]{:S(2)}, u32[]{:S(2)}) collective-permute-start(s32[2,256]{1,0:T(2,128)S(1)} %pad_add_fusion), channel_id=1, source_target_pairs={{0,2},{1,3},{2,4},{3,5},{4,6},{5,7},{6,8},{7,9},{8,10},{9,11},{10,... | collective-permute-start | bytes 6152 | tf_op jit(solution)/shard_map/ppermute | solution.py:182
  14.3 19.1 %collective-permute-start.8 = (bf16[208,1152]{1,0:T(8,128)(2,1)S(1)}, bf16[208,1152]{1,0:T(8,128)(2,1)S(1)}, u32[]{:S(2)}, u32[]{:S(2)}) collective-permute-start(bf16[208,1152]{1,0:T(8,128)(2,1)S(1)} %get-tuple-element.34), channel_id=1, source_target_pairs={{0,2},{1,3},{2,4},{3,5},{4,6},{5,7},{6,8},{7,9},{8,10},{9,11},{10,... | collective-permute-start | bytes 1437704 | tf_op jit(solution)/shard_map/ppermute | solution.py:182
  23.2 2.4 %collective-permute-start.3 = (bf16[192,1152]{1,0:T(8,128)(2,1)S(1)}, bf16[192,1152]{1,0:T(8,128)(2,1)S(1)}, u32[]{:S(2)}, u32[]{:S(2)}) collective-permute-start(bf16[192,1152]{1,0:T(8,128)(2,1)S(1)} %get-tuple-element.20), channel_id=1, source_target_pairs={{0,1},{1,0},{2,3},{3,2},{4,5},{5,4},{6,7},{7,6},{8,9},{9,8},{10,11... | collective-permute-start | bytes 1327112 | tf_op jit(solution)/shard_map/ppermute | solution.py:185
  23.3 2.3 %collective-permute-start.4 = (bf16[64,1152]{1,0:T(8,128)(2,1)S(1)}, bf16[64,1152]{1,0:T(8,128)(2,1)S(1)}, u32[]{:S(2)}, u32[]{:S(2)}) collective-permute-start(bf16[64,1152]{1,0:T(8,128)(2,1)S(1)} %get-tuple-element.21), channel_id=1, source_target_pairs={{0,1},{1,0},{2,3},{3,2},{4,5},{5,4},{6,7},{7,6},{8,9},{9,8},{10,11... | collective-permute-start | bytes 442376 | tf_op jit(solution)/shard_map/ppermute | solution.py:185
  23.8 11.2 %collective-permute-start.7 = (bf16[48,1152]{1,0:T(8,128)(2,1)S(1)}, bf16[48,1152]{1,0:T(8,128)(2,1)S(1)}, u32[]{:S(2)}, u32[]{:S(2)}) collective-permute-start(bf16[48,1152]{1,0:T(8,128)(2,1)S(1)} %get-tuple-element.32), channel_id=1, source_target_pairs={{0,2},{1,3},{2,4},{3,5},{4,6},{5,7},{6,8},{7,9},{8,10},{9,11},{10,... | collective-permute-start | bytes 331784 | tf_op jit(solution)/shard_map/ppermute | solution.py:182

commit v13 on v12

--- a/solution.py
+++ b/solution.py
@@ -9,7 +9,7 @@
 
 SHIFTS = 2
 AXES = ("dp", "group")
-CHUNKS = 4
+STEP = 16
 VMEM = pl.BlockSpec(memory_space=pltpu.VMEM)
 SMEM = pl.BlockSpec(memory_space=pltpu.SMEM)
 ANY = pl.BlockSpec(memory_space=pl.ANY)
@@ -34,27 +34,23 @@
     return jnp.sum(loss.T, axis=0, keepdims=True), coef
 
 
+def whole(a, b):
+    return jnp.concatenate([a[...], b[...]], axis=0)
+
+
 def low(coef):
     return coef.astype(jnp.bfloat16)
 
 
-def cast_kernel(text, out, staged, sems):
-    step = text.shape[0] // CHUNKS
-    parts = [pl.ds(k * step, step) for k in range(CHUNKS)]
-    copies = [pltpu.make_async_copy(text.at[part], staged.at[part], sems.at[k]) for k, part in enumerate(parts)]
-    for copy in copies:
-        copy.start()
-    for part, copy in zip(parts, copies):
-        copy.wait()
-        out[part, :] = staged[part, :].astype(out.dtype)
-
-
-def load_kernel(text, image, out, half_a, half_b, sems):
-    half = half_a.shape[0]
+def cast_kernel(text, out):
+    out[...] = text[...].astype(out.dtype)
+
+
+def load_kernel(text, image, out_a, out_b, sems):
+    half = out_a.shape[0]
     copies = [
-        pltpu.make_async_copy(image.at[pl.ds(0, half)], half_a, sems.at[0]),
-        pltpu.make_async_copy(image.at[pl.ds(half, half)], half_b, sems.at[1]),
-        pltpu.make_async_copy(image, out, sems.at[2]),
+        pltpu.make_async_copy(image.at[pl.ds(0, half)], out_a, sems.at[0]),
+        pltpu.make_async_copy(image.at[pl.ds(half, half)], out_b, sems.at[1]),
     ]
     for copy in copies:
         copy.start()
@@ -75,15 +71,15 @@
         copy.wait()
 
 
-def own_kernel(flags, params, ids, mate_ids, image, mate_a, mate_b, text, accum_in, out_a, out_b, image_sum, loss,
+def own_kernel(flags, params, ids, mate_ids, image_a, image_b, mate_a, mate_b, text, accum_in, out_a, out_b, image_sum, loss,
                accum, sem):
     copy = pltpu.make_async_copy(accum_in, accum, sem)
     copy.start()
-    own_loss, coef = pair(image[...], text[...], ids[...], ids[...], params)
+    image = whole(image_a, image_b)
+    own_loss, coef = pair(image, text[...], ids[...], ids[...], params)
     loss[...] = own_loss
-    part = dot(low(coef.T), image[...], (1, 0))
     copy.wait()
-    total = accum[...] + part
+    total = accum[...] + dot(low(coef.T), image, (1, 0))
     cut = out_a.shape[0]
 
     def give(value):
@@ -92,7 +88,7 @@
 
     @pl.when(flags[0] == 0)
     def _():
-        mate = jnp.concatenate([mate_a[...], mate_b[...]], axis=0)
+        mate = whole(mate_a, mate_b)
         _, mate_coef = pair(mate, text[...], mate_ids[...], ids[...], params)
         give(total + dot(low(mate_coef.T), mate, (1, 0)))
 
@@ -114,12 +110,13 @@
     pl.when(flags[0] == 1)(lambda: fill(far))
 
 
-def far_kernel(flags, params, ids, mate_ids, both_ids, image, mate_a, mate_b, far, image_in, loss_in,
-               late, image_sum, loss):
-    more, coef = pair(image[...], far[...], ids[...], both_ids[:1, :], params)
+def far_kernel(flags, params, ids, mate_ids, both_ids, image_a, image_b, mate_a, mate_b, far, image_in,
+               loss_in, late, image_sum, loss):
+    image = whole(image_a, image_b)
+    more, coef = pair(image, far[...], ids[...], both_ids[:1, :], params)
     loss[...] = loss_in[...] + more
     image_sum[...] = image_in[...] + dot(low(coef), far[...], (1, 0))
-    part = dot(low(coef.T), image[...], (1, 0))
+    part = dot(low(coef.T), image, (1, 0))
 
     @pl.when(flags[0] == 0)
     def _():
@@ -127,15 +124,17 @@
 
     @pl.when(flags[0] == 1)
     def _():
-        mate = jnp.concatenate([mate_a[...], mate_b[...]], axis=0)
+        mate = whole(mate_a, mate_b)
         _, mate_coef = pair(mate, far[...], mate_ids[...], both_ids[:1, :], params)
         late[...] = part + dot(low(mate_coef.T), mate, (1, 0))
 
 
-def near_kernel(flags, params, ids, mate_ids, both_ids, image, near_a, near_b, image_in, loss_in, image_grad, loss):
+def near_kernel(flags, params, ids, mate_ids, both_ids, image_a, image_b, near_a, near_b, image_in, loss_in,
+                image_grad, loss):
+    image = whole(image_a, image_b)
     near_ids = jnp.where(flags[0] == 0, both_ids[1:, :], mate_ids[...])
-    near = jnp.concatenate([near_a[...], near_b[...]], axis=0)
-    more, coef = pair(image[...], near, ids[...], near_ids, params)
+    near = whole(near_a, near_b)
+    more, coef = pair(image, near, ids[...], near_ids, params)
     loss[...] = (loss_in[...] + more) * (1.0 / ((SHIFTS + 1) * image.shape[0]))
     image_grad[...] = (image_in[...] + dot(low(coef), near, (1, 0))).astype(image_grad.dtype)
 
@@ -184,29 +183,20 @@
     def across(value):
         return lax.ppermute(value, AXES, swap)
 
-    text = pl.pallas_call(
-        cast_kernel,
-        out_shape=jax.ShapeDtypeStruct((rows, width), bf16),
-        in_specs=[HBM],
-        out_specs=VMEM,
-        scratch_shapes=[pltpu.VMEM((rows, width), f32), pltpu.SemaphoreType.DMA((CHUNKS,))],
-        compiler_params=pltpu.CompilerParams(vmem_limit_bytes=16 * 1024 * 1024),
-        cost_estimate=pl.CostEstimate(flops=0, bytes_accessed=0, transcendentals=0),
-        name="cast",
-    )(pltpu.with_memory_space_constraint(text_emb, pltpu.HBM))
+    (text,) = call(cast_kernel, "cast", [((rows, width), bf16)], (), text_emb)
     far = ahead(text)
 
-    image, half_a, half_b = pl.pallas_call(
+    image_a, image_b = pl.pallas_call(
         load_kernel,
-        out_shape=[jax.ShapeDtypeStruct((n, width), bf16) for n in (rows, half, rows - half)],
+        out_shape=[jax.ShapeDtypeStruct((n, width), bf16) for n in (half, rows - half)],
         in_specs=[ANY, HBM],
-        out_specs=[VMEM] * 3,
-        scratch_shapes=[pltpu.SemaphoreType.DMA((3,))],
+        out_specs=[VMEM] * 2,
+        scratch_shapes=[pltpu.SemaphoreType.DMA((2,))],
         compiler_params=pltpu.CompilerParams(vmem_limit_bytes=16 * 1024 * 1024),
         cost_estimate=pl.CostEstimate(flops=0, bytes_accessed=0, transcendentals=0),
         name="load",
     )(text, pltpu.with_memory_space_constraint(image_emb, pltpu.HBM))
-    mate_a, mate_b = across(half_a), across(half_b)
+    mate_a, mate_b = across(image_a), across(image_b)
     mate_ids = across(ids)
     both_ids = ahead(jnp.concatenate([ids, mate_ids]))
 
@@ -219,13 +209,13 @@
             jax.ShapeDtypeStruct((rows, width), f32),
             jax.ShapeDtypeStruct((1, rows), f32),
         ],
-        in_specs=[SMEM] * 2 + [VMEM] * 6 + [HBM],
+        in_specs=[SMEM] * 2 + [VMEM] * 7 + [HBM],
         out_specs=[VMEM] * 4,
         scratch_shapes=[pltpu.VMEM((rows, width), f32), pltpu.SemaphoreType.DMA],
         compiler_params=pltpu.CompilerParams(vmem_limit_bytes=16 * 1024 * 1024),
         cost_estimate=pl.CostEstimate(flops=0, bytes_accessed=0, transcendentals=0),
         name="own",
-    )(flags, params, ids, mate_ids, image, mate_a, mate_b, text,
+    )(flags, params, ids, mate_ids, image_a, image_b, mate_a, mate_b, text,
       pltpu.with_memory_space_constraint(text_accum, pltpu.HBM))
     arrived_a, arrived_b = ahead(out_a), ahead(out_b)
 
@@ -236,15 +226,16 @@
     near_a, near_b = across(passed_a), across(passed_b)
     late, image_sum, loss = call(
         far_kernel, "far", [((rows, width), f32), ((rows, width), f32), ((1, rows), f32)],
-        (flags, params), ids, mate_ids, both_ids, image, mate_a, mate_b, far, image_sum, loss,
+        (flags, params), ids, mate_ids, both_ids, image_a, image_b, mate_a, mate_b, far, image_sum,
+        loss,
     )
     image_grad, loss = call(
         near_kernel, "near", [((rows, width), bf16), ((1, rows), f32)],
-        (flags, params), ids, mate_ids, both_ids, image, near_a, near_b, image_sum, loss,
+        (flags, params), ids, mate_ids, both_ids, image_a, image_b, near_a, near_b, image_sum, loss,
     )
     late, image_grad = lax.optimization_barrier((late, image_grad))
-    text_grad = add_part("add_a", 0, 2, arrived_a, late)
-    text_grad = add_part("add_b", cut, 1, arrived_b, late, text_grad)
+    text_grad = add_part("add_a", 0, cut // STEP, arrived_a, late)
+    text_grad = add_part("add_b", cut, (rows - cut) // STEP, arrived_b, late, text_grad)
     return (loss.reshape(rows), image_grad, text_grad)
 
 

time: 35.9 us -> 35.9 us (level)
  Pallas kernels: 13 us -> 11 us
  local copies, waits for them, and re-layouts: 0.01 us -> 1.27 us
  waiting for transfers between devices: 13.2 us -> 14 us
    pallas_call x1 -> x0, Pallas kernels: 1.28 us -> none  [body(): pl.pallas_call(cast_kernel, out_shape=jax.ShapeDtypeStruct((rows, width),...]
    unnamed x2 -> x4, local copies, waits for them, and re-layouts: 0.01 us -> 1.27 us
    ppermute x4, waiting for transfers between devices: 13.1 us -> 13.9 us  [ahead(): return lax.ppermute(value, AXES, skip)]
    pallas_call x1, Pallas kernels: 4.41 us -> 3.82 us  [body(): pl.pallas_call(own_kernel, out_shape=[jax.ShapeDtypeStruct((cut, width),...]
    pallas_call x3 -> x4, Pallas kernels: 4.3 us -> 4.36 us  [call(): pl.pallas_call(kernel, out_shape=[jax.ShapeDtypeStruct(s, d) for s, d in...]
  transfers between devices with their start and end apart: 9 -> 9, of which waited for: 4 -> 4; matrix products, arithmetic and copies ran while one was open for 0% -> 0% of each run, Pallas kernels for 31% -> 29%
where the time goes in v13:
time: 35.9 us; the launch traced here: 35.7 us
  waiting for transfers between devices  14 us (39%)
  Pallas kernels  11 us (31%)
  starting transfers between devices  7.27 us (20%)
  between operations  2.02 us (6%)
  local copies, waits for them, and re-layouts  1.27 us (4%)
    ppermute x4, waiting for transfers between devices, ahead(): return lax.ppermute(value, AXES, skip)  13.9 us
    ppermute x4, starting transfers between devices, ahead(): return lax.ppermute(value, AXES, skip)  6.05 us
    pallas_call x4, Pallas kernels, call(): pl.pallas_call(kernel, out_shape=[jax.ShapeDtypeStruct(s, d) for s, d in...  4.36 us
    pallas_call x1, Pallas kernels, body(): pl.pallas_call(own_kernel, out_shape=[jax.ShapeDtypeStruct((cut, width),...  3.82 us
    pallas_call x2, Pallas kernels, add_part(): pl.pallas_call(functools.partial(add_kernel, start, chunks), out_shape=ja...  1.76 us
    unnamed x4, local copies, waits for them, and re-layouts  1.27 us
    ppermute x5, starting transfers between devices, across(): return lax.ppermute(value, AXES, swap)  1.21 us
    pallas_call x1, Pallas kernels, body(): pl.pallas_call(load_kernel, out_shape=[jax.ShapeDtypeStruct((n, width), b...  1.07 us
  transfers between devices with their start and end apart: 9, of which 4 were waited for; matrix products, arithmetic and copies ran while one was open for 0% of the time, Pallas kernels for 29%

profile of v13, /device:TPU:0, one launch (start us, length us, event | category | flops | bytes accessed | tf_op | source)
XLA Modules:
  0.0 35.7 jit_solution(11597755795404340397)
XLA Ops:
  0.6 0.0 copy-start
  0.6 1.3 %copy-done = f32[256,1152]{1,0:T(8,128)S(1)} copy-done((f32[256,1152]{1,0:T(8,128)S(1)}, f32[256,1152]{1,0:T(8,128)}, u32[]{:S(2)}) %copy-start) | copy-done | bytes 1179672
  1.9 0.0 copy-start.1
  1.9 0.1 cast.1.text
  2.0 3.0 %collective-permute-start.2 = (bf16[256,1152]{1,0:T(8,128)(2,1)S(1)}, bf16[256,1152]{1,0:T(8,128)(2,1)S(1)}, u32[]{:S(2)}, u32[]{:S(2)}) collective-permute-start(bf16[256,1152]{1,0:T(8,128)(2,1)S(1)} %cast.1.text), channel_id=1, source_target_pairs={{0,2},{1,3},{2,4},{3,5},{4,6},{5,7},{6,8},{7,9},{8,10},{9,11},{10,... | collective-permute-start | bytes 1769480 | tf_op jit(solution)/shard_map/ppermute | solution.py:181
  5.0 1.1 %load.1 = (bf16[128,1152]{1,0:T(8,128)(2,1)S(1)}, bf16[128,1152]{1,0:T(8,128)(2,1)S(1)}) custom-call(bf16[256,1152]{1,0:T(8,128)(2,1)S(1)} %cast.1.text, bf16[256,1152]{1,0:T(8,128)(2,1)} %image.1), custom_call_target="tpu_custom_call" | custom-call | tf_op jit(solution)/shard_map/load/pallas_call | solution.py:189
  6.1 0.1 collective-permute-start.5
  6.1 0.5 %collective-permute-start.6 = (bf16[128,1152]{1,0:T(8,128)(2,1)S(1)}, bf16[128,1152]{1,0:T(8,128)(2,1)S(1)}, u32[]{:S(2)}, u32[]{:S(2)}) collective-permute-start(bf16[128,1152]{1,0:T(8,128)(2,1)S(1)} %get-tuple-element.19.image_b), channel_id=1, source_target_pairs={{0,1},{1,0},{2,3},{3,2},{4,5},{5,4},{6,7},{7,6},{8,9},{9,8},{10,11... | collective-permute-start | bytes 884744 | tf_op jit(solution)/shard_map/ppermute | solution.py:184
  6.6 0.0 copy-done.1
  6.6 0.1 collective-permute-start
  8.0 0.1 collective-permute-done.mate_ids
  8.1 1.5 %collective-permute-start.1 = (s32[2,256]{1,0:T(2,128)S(1)}, s32[2,256]{1,0:T(2,128)S(1)}, u32[]{:S(2)}, u32[]{:S(2)}) collective-permute-start(s32[2,256]{1,0:T(2,128)S(1)} %pad_add_fusion), channel_id=1, source_target_pairs={{0,2},{1,3},{2,4},{3,5},{4,6},{5,7},{6,8},{7,9},{8,10},{9,11},{10,... | collective-permute-start | bytes 6152 | tf_op jit(solution)/shard_map/ppermute | solution.py:181
  9.6 0.1 pad_maximum_fusion.params
  9.7 0.0 collective-permute-done.5.mate_a
  9.7 0.0 collective-permute-done.6.mate_b
  9.7 3.8 %own.1 = (bf16[208,1152]{1,0:T(8,128)(2,1)S(1)}, bf16[48,1152]{1,0:T(8,128)(2,1)S(1)}, f32[256,1152]{1,0:T(8,128)S(1)}, f32[1,256]{1,0:T(1,128)S(1)}) custom-call(s32[1]{0:T(128)} %bitcast.flags, f32[2]{0:T(128)S(1)} %pad_maximum_fusion.params, s32[1,256]{1,0:T(1,128)S(1)} %bitcast.5, s32[1,256]{1,0:T(1,128)S(1)} %collective-permute-done.mate_ids, ...), custom_call_target="tpu_custom_call" | custom-call | tf_op jit(solution)/shard_map/own/pallas_call | solution.py:204
  13.5 1.6 %collective-permute-start.8 = (bf16[208,1152]{1,0:T(8,128)(2,1)S(1)}, bf16[208,1152]{1,0:T(8,128)(2,1)S(1)}, u32[]{:S(2)}, u32[]{:S(2)}) collective-permute-start(bf16[208,1152]{1,0:T(8,128)(2,1)S(1)} %get-tuple-element.32), channel_id=1, source_target_pairs={{0,2},{1,3},{2,4},{3,5},{4,6},{5,7},{6,8},{7,9},{8,10},{9,11},{10,... | collective-permute-start | bytes 1437704 | tf_op jit(solution)/shard_map/ppermute | solution.py:181
  15.1 8.1 %collective-permute-done.1.token.both_ids = s32[2,256]{1,0:T(2,128)S(1)} collective-permute-done((s32[2,256]{1,0:T(2,128)S(1)}, s32[2,256]{1,0:T(2,128)S(1)}, u32[]{:S(2)}, u32[]{:S(2)}) %collective-permute-start.1) | collective-permute-done | bytes 2080 | tf_op jit(solution)/shard_map/ppermute | solution.py:181
  23.2 0.0 collective-permute-done.2.far
  23.2 0.1 collective-permute-start.3
  23.3 0.5 %collective-permute-start.4 = (bf16[64,1152]{1,0:T(8,128)(2,1)S(1)}, bf16[64,1152]{1,0:T(8,128)(2,1)S(1)}, u32[]{:S(2)}, u32[]{:S(2)}) collective-permute-start(bf16[64,1152]{1,0:T(8,128)(2,1)S(1)} %get-tuple-element.21), channel_id=1, source_target_pairs={{0,1},{1,0},{2,3},{3,2},{4,5},{5,4},{6,7},{7,6},{8,9},{9,8},{10,11... | collective-permute-start | bytes 442376 | tf_op jit(solution)/shard_map/ppermute | solution.py:184
  23.8 0.0 collective-permute-start.7
  23.8 1.8 %far.1 = (f32[256,1152]{1,0:T(8,128)S(1)}, f32[256,1152]{1,0:T(8,128)S(1)}, f32[1,256]{1,0:T(1,128)S(1)}) custom-call(s32[1]{0:T(128)} %bitcast.flags, f32[2]{0:T(128)S(1)} %pad_maximum_fusion.params, s32[1,256]{1,0:T(1,128)S(1)} %bitcast.6, s32[1,256]{1,0:T(1,128)S(1)} %collective-permute-done.mate_ids, s32[2,256]{1,0:T(2,128)S(1)} %collective-permute-done.1.token.both_ids, ...), custom_call_target="tpu_custom_call" | custom-call | tf_op jit(solution)/shard_map/far/pallas_call | solution.py:143
  25.6 0.0 collective-permute-done.4.near_b
  25.6 0.0 collective-permute-done.3.near_a
  25.6 2.4 %near.1 = (bf16[256,1152]{1,0:T(8,128)(2,1)}, f32[1,256]{1,0:T(1,128)}) custom-call(s32[1]{0:T(128)} %bitcast.flags, f32[2]{0:T(128)S(1)} %pad_maximum_fusion.params, s32[1,256]{1,0:T(1,128)S(1)} %bitcast.7, s32[1,256]{1,0:T(1,128)S(1)} %collective-permute-done.mate_ids, s32[2,256]{1,0:T(2,128)S(1)} %collective-permute-done.1.token.both_ids, ...), custom_call_target="tpu_custom_call" | custom-call | tf_op jit(solution)/shard_map/near/pallas_call | solution.py:143
  28.1 5.4 %collective-permute-done.8.arrived = bf16[208,1152]{1,0:T(8,128)(2,1)S(1)} collective-permute-done((bf16[208,1152]{1,0:T(8,128)(2,1)S(1)}, bf16[208,1152]{1,0:T(8,128)(2,1)S(1)}, u32[]{:S(2)}, u32[]{:S(2)}) %collective-permute-start.8) | collective-permute-done | bytes 479264 | tf_op jit(solution)/shard_map/ppermute | solution.py:181
  33.4 1.1 %add_a.1.refs_0_ = f32[256,1152]{1,0:T(8,128)} custom-call(bf16[208,1152]{1,0:T(8,128)(2,1)S(1)} %collective-permute-done.8.arrived, f32[256,1152]{1,0:T(8,128)S(1)} %get-tuple-element.31.late), custom_call_target="tpu_custom_call" | custom-call | tf_op jit(solution)/shard_map/add_a/pallas_call | solution.py:155
  34.5 0.5 %collective-permute-done.7.arrived = bf16[48,1152]{1,0:T(8,128)(2,1)S(1)} collective-permute-done((bf16[48,1152]{1,0:T(8,128)(2,1)S(1)}, bf16[48,1152]{1,0:T(8,128)(2,1)S(1)}, u32[]{:S(2)}, u32[]{:S(2)}) %collective-permute-start.7) | collective-permute-done | bytes 110624 | tf_op jit(solution)/shard_map/ppermute | solution.py:181
  35.0 0.7 %add_b.1 = f32[256,1152]{1,0:T(8,128)} custom-call(bf16[48,1152]{1,0:T(8,128)(2,1)S(1)} %collective-permute-done.7.arrived, f32[256,1152]{1,0:T(8,128)S(1)} %get-tuple-element.31.late, f32[256,1152]{1,0:T(8,128)} %add_a.1.refs_0_), custom_call_target="tpu_custom_call", output_to_operand_aliasing={{}: (2, {})} | custom-call | tf_op jit(solution)/shard_map/add_b/pallas_call | solution.py:155
  (2 shorter events, 0.1 us)
Async XLA Ops:
  0.6 1.3 %copy-start = (f32[256,1152]{1,0:T(8,128)S(1)}, f32[256,1152]{1,0:T(8,128)}, u32[]{:S(2)}) copy-start(f32[256,1152]{1,0:T(8,128)} %text.1) | copy-start | bytes 3538948
  1.9 4.7 %copy-start.1 = (s32[256]{0:T(256)S(1)}, s32[256]{0:T(256)}, u32[]{:S(2)}) copy-start(s32[256]{0:T(256)} %param.9) | copy-start | bytes 3076
  2.0 21.2 %collective-permute-start.2 = (bf16[256,1152]{1,0:T(8,128)(2,1)S(1)}, bf16[256,1152]{1,0:T(8,128)(2,1)S(1)}, u32[]{:S(2)}, u32[]{:S(2)}) collective-permute-start(bf16[256,1152]{1,0:T(8,128)(2,1)S(1)} %cast.1.text), channel_id=1, source_target_pairs={{0,2},{1,3},{2,4},{3,5},{4,6},{5,7},{6,8},{7,9},{8,10},{9,11},{10,... | collective-permute-start | bytes 1769480 | tf_op jit(solution)/shard_map/ppermute | solution.py:181
  6.1 3.6 %collective-permute-start.5 = (bf16[128,1152]{1,0:T(8,128)(2,1)S(1)}, bf16[128,1152]{1,0:T(8,128)(2,1)S(1)}, u32[]{:S(2)}, u32[]{:S(2)}) collective-permute-start(bf16[128,1152]{1,0:T(8,128)(2,1)S(1)} %get-tuple-element.18.image_a), channel_id=1, source_target_pairs={{0,1},{1,0},{2,3},{3,2},{4,5},{5,4},{6,7},{7,6},{8,9},{9,8},{10,11... | collective-permute-start | bytes 884744 | tf_op jit(solution)/shard_map/ppermute | solution.py:184
  6.1 3.5 %collective-permute-start.6 = (bf16[128,1152]{1,0:T(8,128)(2,1)S(1)}, bf16[128,1152]{1,0:T(8,128)(2,1)S(1)}, u32[]{:S(2)}, u32[]{:S(2)}) collective-permute-start(bf16[128,1152]{1,0:T(8,128)(2,1)S(1)} %get-tuple-element.19.image_b), channel_id=1, source_target_pairs={{0,1},{1,0},{2,3},{3,2},{4,5},{5,4},{6,7},{7,6},{8,9},{9,8},{10,11... | collective-permute-start | bytes 884744 | tf_op jit(solution)/shard_map/ppermute | solution.py:184
  6.6 1.5 %collective-permute-start = (s32[1,256]{1,0:T(1,128)S(1)}, s32[1,256]{1,0:T(1,128)S(1)}, u32[]{:S(2)}, u32[]{:S(2)}) collective-permute-start(s32[1,256]{1,0:T(1,128)S(1)} %bitcast.3), channel_id=1, source_target_pairs={{0,1},{1,0},{2,3},{3,2},{4,5},{5,4},{6,7},{7,6},{8,9},{9,8},{10,11... | collective-permute-start | bytes 3080 | tf_op jit(solution)/shard_map/ppermute | solution.py:184
  8.1 15.0 %collective-permute-start.1 = (s32[2,256]{1,0:T(2,128)S(1)}, s32[2,256]{1,0:T(2,128)S(1)}, u32[]{:S(2)}, u32[]{:S(2)}) collective-permute-start(s32[2,256]{1,0:T(2,128)S(1)} %pad_add_fusion), channel_id=1, source_target_pairs={{0,2},{1,3},{2,4},{3,5},{4,6},{5,7},{6,8},{7,9},{8,10},{9,11},{10,... | collective-permute-start | bytes 6152 | tf_op jit(solution)/shard_map/ppermute | solution.py:181
  13.5 19.9 %collective-permute-start.8 = (bf16[208,1152]{1,0:T(8,128)(2,1)S(1)}, bf16[208,1152]{1,0:T(8,128)(2,1)S(1)}, u32[]{:S(2)}, u32[]{:S(2)}) collective-permute-start(bf16[208,1152]{1,0:T(8,128)(2,1)S(1)} %get-tuple-element.32), channel_id=1, source_target_pairs={{0,2},{1,3},{2,4},{3,5},{4,6},{5,7},{6,8},{7,9},{8,10},{9,11},{10,... | collective-permute-start | bytes 1437704 | tf_op jit(solution)/shard_map/ppermute | solution.py:181
  23.2 2.4 %collective-permute-start.3 = (bf16[192,1152]{1,0:T(8,128)(2,1)S(1)}, bf16[192,1152]{1,0:T(8,128)(2,1)S(1)}, u32[]{:S(2)}, u32[]{:S(2)}) collective-permute-start(bf16[192,1152]{1,0:T(8,128)(2,1)S(1)} %get-tuple-element.20), channel_id=1, source_target_pairs={{0,1},{1,0},{2,3},{3,2},{4,5},{5,4},{6,7},{7,6},{8,9},{9,8},{10,11... | collective-permute-start | bytes 1327112 | tf_op jit(solution)/shard_map/ppermute | solution.py:184
  23.3 2.3 %collective-permute-start.4 = (bf16[64,1152]{1,0:T(8,128)(2,1)S(1)}, bf16[64,1152]{1,0:T(8,128)(2,1)S(1)}, u32[]{:S(2)}, u32[]{:S(2)}) collective-permute-start(bf16[64,1152]{1,0:T(8,128)(2,1)S(1)} %get-tuple-element.21), channel_id=1, source_target_pairs={{0,1},{1,0},{2,3},{3,2},{4,5},{5,4},{6,7},{7,6},{8,9},{9,8},{10,11... | collective-permute-start | bytes 442376 | tf_op jit(solution)/shard_map/ppermute | solution.py:184
  23.8 11.2 %collective-permute-start.7 = (bf16[48,1152]{1,0:T(8,128)(2,1)S(1)}, bf16[48,1152]{1,0:T(8,128)(2,1)S(1)}, u32[]{:S(2)}, u32[]{:S(2)}) collective-permute-start(bf16[48,1152]{1,0:T(8,128)(2,1)S(1)} %get-tuple-element.30), channel_id=1, source_target_pairs={{0,2},{1,3},{2,4},{3,5},{4,6},{5,7},{6,8},{7,9},{8,10},{9,11},{10,... | collective-permute-start | bytes 331784 | tf_op jit(solution)/shard_map/ppermute | solution.py:181

commit v14 on v13

--- a/solution.py
+++ b/solution.py
@@ -42,11 +42,7 @@
     return coef.astype(jnp.bfloat16)
 
 
-def cast_kernel(text, out):
-    out[...] = text[...].astype(out.dtype)
-
-
-def load_kernel(text, image, out_a, out_b, sems):
+def fetch(image, out_a, out_b, sems):
     half = out_a.shape[0]
     copies = [
         pltpu.make_async_copy(image.at[pl.ds(0, half)], out_a, sems.at[0]),
@@ -56,6 +52,25 @@
         copy.start()
     for copy in copies:
         copy.wait()
+
+
+def cast_kernel(flags, text, image, out, image_a, image_b, sems):
+    out[...] = text[...].astype(out.dtype)
+
+    @pl.when(flags[0] == 1)
+    def _():
+        fetch(image, image_a, image_b, sems)
+
+
+def load_kernel(flags, early_a, early_b, image, image_a, image_b, sems):
+    @pl.when(flags[0] == 0)
+    def _():
+        fetch(image, image_a, image_b, sems)
+
+    @pl.when(flags[0] == 1)
+    def _():
+        image_a[...] = early_a[...]
+        image_b[...] = early_b[...]
 
 
 def add_kernel(start, chunks, arrived, late, *refs):
@@ -183,19 +198,30 @@
     def across(value):
         return lax.ppermute(value, AXES, swap)
 
-    (text,) = call(cast_kernel, "cast", [((rows, width), bf16)], (), text_emb)
+    fixed_image = pltpu.with_memory_space_constraint(image_emb, pltpu.HBM)
+    halves = [jax.ShapeDtypeStruct((n, width), bf16) for n in (half, rows - half)]
+    text, early_a, early_b = pl.pallas_call(
+        cast_kernel,
+        out_shape=[jax.ShapeDtypeStruct((rows, width), bf16)] + halves,
+        in_specs=[SMEM, VMEM, HBM],
+        out_specs=[VMEM] * 3,
+        scratch_shapes=[pltpu.SemaphoreType.DMA((2,))],
+        compiler_params=pltpu.CompilerParams(vmem_limit_bytes=16 * 1024 * 1024),
+        cost_estimate=pl.CostEstimate(flops=0, bytes_accessed=0, transcendentals=0),
+        name="cast",
+    )(flags, text_emb, fixed_image)
     far = ahead(text)
 
     image_a, image_b = pl.pallas_call(
         load_kernel,
-        out_shape=[jax.ShapeDtypeStruct((n, width), bf16) for n in (half, rows - half)],
-        in_specs=[ANY, HBM],
+        out_shape=halves,
+        in_specs=[SMEM, VMEM, VMEM, HBM],
         out_specs=[VMEM] * 2,
         scratch_shapes=[pltpu.SemaphoreType.DMA((2,))],
         compiler_params=pltpu.CompilerParams(vmem_limit_bytes=16 * 1024 * 1024),
         cost_estimate=pl.CostEstimate(flops=0, bytes_accessed=0, transcendentals=0),
         name="load",
-    )(text, pltpu.with_memory_space_constraint(image_emb, pltpu.HBM))
+    )(flags, early_a, early_b, fixed_image)
     mate_a, mate_b = across(image_a), across(image_b)
     mate_ids = across(ids)
     both_ids = ahead(jnp.concatenate([ids, mate_ids]))

time: 35.9 us -> 36.6 us (1.019)
  waiting for transfers between devices: 14 us -> 14.7 us
    ppermute x4, waiting for transfers between devices: 13.9 us -> 14.6 us  [ahead(): return lax.ppermute(value, AXES, skip)]
    pallas_call x1 -> x2, Pallas kernels: 1.07 us -> 1.14 us  [the longest x1 1.07 us: body(): pl.pallas_call(load_kernel, out_shape=halves, in_specs=[SMEM, VMEM, VMEM,...]
    pallas_call x4 -> x3, Pallas kernels: 4.36 us -> 4.3 us  [call(): pl.pallas_call(kernel, out_shape=[jax.ShapeDtypeStruct(s, d) for s, d in...]
  transfers between devices with their start and end apart: 9 -> 9, of which waited for: 4 -> 4; matrix products, arithmetic and copies ran while one was open for 0% -> 0% of each run, Pallas kernels for 29% -> 28%
where the time goes in v14:
time: 36.6 us; the launch traced here: 36.4 us
  waiting for transfers between devices  14.7 us (40%)
  Pallas kernels  11 us (30%)
  starting transfers between devices  7.28 us (20%)
  between operations  2.03 us (6%)
  local copies, waits for them, and re-layouts  1.27 us (3%)
    ppermute x4, waiting for transfers between devices, ahead(): return lax.ppermute(value, AXES, skip)  14.6 us
    ppermute x4, starting transfers between devices, ahead(): return lax.ppermute(value, AXES, skip)  6.05 us
    pallas_call x3, Pallas kernels, call(): pl.pallas_call(kernel, out_shape=[jax.ShapeDtypeStruct(s, d) for s, d in...  4.3 us
    pallas_call x1, Pallas kernels, body(): pl.pallas_call(own_kernel, out_shape=[jax.ShapeDtypeStruct((cut, width),...  3.83 us
    pallas_call x2, Pallas kernels, add_part(): pl.pallas_call(functools.partial(add_kernel, start, chunks), out_shape=ja...  1.77 us
    unnamed x4, local copies, waits for them, and re-layouts  1.27 us
    ppermute x5, starting transfers between devices, across(): return lax.ppermute(value, AXES, swap)  1.22 us
    pallas_call x1, Pallas kernels, body(): pl.pallas_call(load_kernel, out_shape=halves, in_specs=[SMEM, VMEM, VMEM,...  1.07 us
  transfers between devices with their start and end apart: 9, of which 4 were waited for; matrix products, arithmetic and copies ran while one was open for 0% of the time, Pallas kernels for 28%

profile of v14, /device:TPU:0, one launch (start us, length us, event | category | flops | bytes accessed | tf_op | source)
XLA Modules:
  0.0 36.4 jit_solution(12865176979880544932)
XLA Ops:
  0.6 0.0 copy-start
  0.7 1.3 %copy-done = f32[256,1152]{1,0:T(8,128)S(1)} copy-done((f32[256,1152]{1,0:T(8,128)S(1)}, f32[256,1152]{1,0:T(8,128)}, u32[]{:S(2)}) %copy-start) | copy-done | bytes 1179672
  1.9 0.0 copy-start.1
  1.9 0.1 cast.1
  2.0 3.0 %collective-permute-start.2 = (bf16[256,1152]{1,0:T(8,128)(2,1)S(1)}, bf16[256,1152]{1,0:T(8,128)(2,1)S(1)}, u32[]{:S(2)}, u32[]{:S(2)}) collective-permute-start(bf16[256,1152]{1,0:T(8,128)(2,1)S(1)} %get-tuple-element.25.text), channel_id=1, source_target_pairs={{0,2},{1,3},{2,4},{3,5},{4,6},{5,7},{6,8},{7,9},{8,10},{9,11},{10,... | collective-permute-start | bytes 1769480 | tf_op jit(solution)/shard_map/ppermute | solution.py:196
  5.0 1.1 %load.1 = (bf16[128,1152]{1,0:T(8,128)(2,1)S(1)}, bf16[128,1152]{1,0:T(8,128)(2,1)S(1)}) custom-call(s32[1]{0:T(128)} %bitcast.flags, bf16[128,1152]{1,0:T(8,128)(2,1)S(1)} %get-tuple-element.21.early_a, bf16[128,1152]{1,0:T(8,128)(2,1)S(1)} %get-tuple-element.22.early_b, bf16[256,1152]{1,0:T(8,128)(2,1)} %image.3), custom_call_target="tpu_custom_call" | custom-call | tf_op jit(solution)/shard_map/load/pallas_call | solution.py:215
  6.1 0.1 collective-permute-start.5
  6.2 0.5 %collective-permute-start.6 = (bf16[128,1152]{1,0:T(8,128)(2,1)S(1)}, bf16[128,1152]{1,0:T(8,128)(2,1)S(1)}, u32[]{:S(2)}, u32[]{:S(2)}) collective-permute-start(bf16[128,1152]{1,0:T(8,128)(2,1)S(1)} %get-tuple-element.24.image_b), channel_id=1, source_target_pairs={{0,1},{1,0},{2,3},{3,2},{4,5},{5,4},{6,7},{7,6},{8,9},{9,8},{10,11... | collective-permute-start | bytes 884744 | tf_op jit(solution)/shard_map/ppermute | solution.py:199
  6.7 0.0 copy-done.1
  6.7 0.1 collective-permute-start
  8.1 0.1 collective-permute-done.mate_ids
  8.2 1.5 %collective-permute-start.1 = (s32[2,256]{1,0:T(2,128)S(1)}, s32[2,256]{1,0:T(2,128)S(1)}, u32[]{:S(2)}, u32[]{:S(2)}) collective-permute-start(s32[2,256]{1,0:T(2,128)S(1)} %pad_add_fusion), channel_id=1, source_target_pairs={{0,2},{1,3},{2,4},{3,5},{4,6},{5,7},{6,8},{7,9},{8,10},{9,11},{10,... | collective-permute-start | bytes 6152 | tf_op jit(solution)/shard_map/ppermute | solution.py:196
  9.6 0.1 pad_maximum_fusion.params
  9.7 0.0 collective-permute-done.5.mate_a
  9.7 0.0 collective-permute-done.6.mate_b
  9.7 3.8 %own.1 = (bf16[208,1152]{1,0:T(8,128)(2,1)S(1)}, bf16[48,1152]{1,0:T(8,128)(2,1)S(1)}, f32[256,1152]{1,0:T(8,128)S(1)}, f32[1,256]{1,0:T(1,128)S(1)}) custom-call(s32[1]{0:T(128)} %bitcast.flags, f32[2]{0:T(128)S(1)} %pad_maximum_fusion.params, s32[1,256]{1,0:T(1,128)S(1)} %bitcast.5, s32[1,256]{1,0:T(1,128)S(1)} %collective-permute-done.mate_ids, ...), custom_call_target="tpu_custom_call" | custom-call | tf_op jit(solution)/shard_map/own/pallas_call | solution.py:230
  13.6 1.6 %collective-permute-start.8 = (bf16[208,1152]{1,0:T(8,128)(2,1)S(1)}, bf16[208,1152]{1,0:T(8,128)(2,1)S(1)}, u32[]{:S(2)}, u32[]{:S(2)}) collective-permute-start(bf16[208,1152]{1,0:T(8,128)(2,1)S(1)} %get-tuple-element.38), channel_id=1, source_target_pairs={{0,2},{1,3},{2,4},{3,5},{4,6},{5,7},{6,8},{7,9},{8,10},{9,11},{10,... | collective-permute-start | bytes 1437704 | tf_op jit(solution)/shard_map/ppermute | solution.py:196
  15.1 7.9 %collective-permute-done.1.token.both_ids = s32[2,256]{1,0:T(2,128)S(1)} collective-permute-done((s32[2,256]{1,0:T(2,128)S(1)}, s32[2,256]{1,0:T(2,128)S(1)}, u32[]{:S(2)}, u32[]{:S(2)}) %collective-permute-start.1) | collective-permute-done | bytes 2080 | tf_op jit(solution)/shard_map/ppermute | solution.py:196
  23.1 0.0 collective-permute-done.2.far
  23.1 0.5 %collective-permute-start.3 = (bf16[192,1152]{1,0:T(8,128)(2,1)S(1)}, bf16[192,1152]{1,0:T(8,128)(2,1)S(1)}, u32[]{:S(2)}, u32[]{:S(2)}) collective-permute-start(bf16[192,1152]{1,0:T(8,128)(2,1)S(1)} %get-tuple-element.26), channel_id=1, source_target_pairs={{0,1},{1,0},{2,3},{3,2},{4,5},{5,4},{6,7},{7,6},{8,9},{9,8},{10,11... | collective-permute-start | bytes 1327112 | tf_op jit(solution)/shard_map/ppermute | solution.py:199
  23.6 0.1 collective-permute-start.4
  23.7 0.0 collective-permute-start.7
  23.7 1.8 %far.1 = (f32[256,1152]{1,0:T(8,128)S(1)}, f32[256,1152]{1,0:T(8,128)S(1)}, f32[1,256]{1,0:T(1,128)S(1)}) custom-call(s32[1]{0:T(128)} %bitcast.flags, f32[2]{0:T(128)S(1)} %pad_maximum_fusion.params, s32[1,256]{1,0:T(1,128)S(1)} %bitcast.6, s32[1,256]{1,0:T(1,128)S(1)} %collective-permute-done.mate_ids, s32[2,256]{1,0:T(2,128)S(1)} %collective-permute-done.1.token.both_ids, ...), custom_call_target="tpu_custom_call" | custom-call | tf_op jit(solution)/shard_map/far/pallas_call | solution.py:158
  25.5 0.0 collective-permute-done.4.near_b
  25.5 0.0 collective-permute-done.3.near_a
  25.6 2.4 %near.1 = (bf16[256,1152]{1,0:T(8,128)(2,1)}, f32[1,256]{1,0:T(1,128)}) custom-call(s32[1]{0:T(128)} %bitcast.flags, f32[2]{0:T(128)S(1)} %pad_maximum_fusion.params, s32[1,256]{1,0:T(1,128)S(1)} %bitcast.7, s32[1,256]{1,0:T(1,128)S(1)} %collective-permute-done.mate_ids, s32[2,256]{1,0:T(2,128)S(1)} %collective-permute-done.1.token.both_ids, ...), custom_call_target="tpu_custom_call" | custom-call | tf_op jit(solution)/shard_map/near/pallas_call | solution.py:158
  28.0 5.3 %collective-permute-done.8.arrived = bf16[208,1152]{1,0:T(8,128)(2,1)S(1)} collective-permute-done((bf16[208,1152]{1,0:T(8,128)(2,1)S(1)}, bf16[208,1152]{1,0:T(8,128)(2,1)S(1)}, u32[]{:S(2)}, u32[]{:S(2)}) %collective-permute-start.8) | collective-permute-done | bytes 479264 | tf_op jit(solution)/shard_map/ppermute | solution.py:196
  33.3 1.1 %add_a.1.refs_0_ = f32[256,1152]{1,0:T(8,128)} custom-call(bf16[208,1152]{1,0:T(8,128)(2,1)S(1)} %collective-permute-done.8.arrived, f32[256,1152]{1,0:T(8,128)S(1)} %get-tuple-element.37.late), custom_call_target="tpu_custom_call" | custom-call | tf_op jit(solution)/shard_map/add_a/pallas_call | solution.py:170
  34.4 1.3 %collective-permute-done.7.arrived = bf16[48,1152]{1,0:T(8,128)(2,1)S(1)} collective-permute-done((bf16[48,1152]{1,0:T(8,128)(2,1)S(1)}, bf16[48,1152]{1,0:T(8,128)(2,1)S(1)}, u32[]{:S(2)}, u32[]{:S(2)}) %collective-permute-start.7) | collective-permute-done | bytes 110624 | tf_op jit(solution)/shard_map/ppermute | solution.py:196
  35.7 0.7 %add_b.1 = f32[256,1152]{1,0:T(8,128)} custom-call(bf16[48,1152]{1,0:T(8,128)(2,1)S(1)} %collective-permute-done.7.arrived, f32[256,1152]{1,0:T(8,128)S(1)} %get-tuple-element.37.late, f32[256,1152]{1,0:T(8,128)} %add_a.1.refs_0_), custom_call_target="tpu_custom_call", output_to_operand_aliasing={{}: (2, {})} | custom-call | tf_op jit(solution)/shard_map/add_b/pallas_call | solution.py:170
  (2 shorter events, 0.1 us)
Async XLA Ops:
  0.6 1.3 %copy-start = (f32[256,1152]{1,0:T(8,128)S(1)}, f32[256,1152]{1,0:T(8,128)}, u32[]{:S(2)}) copy-start(f32[256,1152]{1,0:T(8,128)} %text.1) | copy-start | bytes 3538948
  1.9 4.8 %copy-start.1 = (s32[256]{0:T(256)S(1)}, s32[256]{0:T(256)}, u32[]{:S(2)}) copy-start(s32[256]{0:T(256)} %param.9) | copy-start | bytes 3076
  2.0 21.1 %collective-permute-start.2 = (bf16[256,1152]{1,0:T(8,128)(2,1)S(1)}, bf16[256,1152]{1,0:T(8,128)(2,1)S(1)}, u32[]{:S(2)}, u32[]{:S(2)}) collective-permute-start(bf16[256,1152]{1,0:T(8,128)(2,1)S(1)} %get-tuple-element.25.text), channel_id=1, source_target_pairs={{0,2},{1,3},{2,4},{3,5},{4,6},{5,7},{6,8},{7,9},{8,10},{9,11},{10,... | collective-permute-start | bytes 1769480 | tf_op jit(solution)/shard_map/ppermute | solution.py:196
  6.1 3.6 %collective-permute-start.5 = (bf16[128,1152]{1,0:T(8,128)(2,1)S(1)}, bf16[128,1152]{1,0:T(8,128)(2,1)S(1)}, u32[]{:S(2)}, u32[]{:S(2)}) collective-permute-start(bf16[128,1152]{1,0:T(8,128)(2,1)S(1)} %get-tuple-element.23.image_a), channel_id=1, source_target_pairs={{0,1},{1,0},{2,3},{3,2},{4,5},{5,4},{6,7},{7,6},{8,9},{9,8},{10,11... | collective-permute-start | bytes 884744 | tf_op jit(solution)/shard_map/ppermute | solution.py:199
  6.2 3.5 %collective-permute-start.6 = (bf16[128,1152]{1,0:T(8,128)(2,1)S(1)}, bf16[128,1152]{1,0:T(8,128)(2,1)S(1)}, u32[]{:S(2)}, u32[]{:S(2)}) collective-permute-start(bf16[128,1152]{1,0:T(8,128)(2,1)S(1)} %get-tuple-element.24.image_b), channel_id=1, source_target_pairs={{0,1},{1,0},{2,3},{3,2},{4,5},{5,4},{6,7},{7,6},{8,9},{9,8},{10,11... | collective-permute-start | bytes 884744 | tf_op jit(solution)/shard_map/ppermute | solution.py:199
  6.7 1.5 %collective-permute-start = (s32[1,256]{1,0:T(1,128)S(1)}, s32[1,256]{1,0:T(1,128)S(1)}, u32[]{:S(2)}, u32[]{:S(2)}) collective-permute-start(s32[1,256]{1,0:T(1,128)S(1)} %bitcast.3), channel_id=1, source_target_pairs={{0,1},{1,0},{2,3},{3,2},{4,5},{5,4},{6,7},{7,6},{8,9},{9,8},{10,11... | collective-permute-start | bytes 3080 | tf_op jit(solution)/shard_map/ppermute | solution.py:199
  8.2 14.9 %collective-permute-start.1 = (s32[2,256]{1,0:T(2,128)S(1)}, s32[2,256]{1,0:T(2,128)S(1)}, u32[]{:S(2)}, u32[]{:S(2)}) collective-permute-start(s32[2,256]{1,0:T(2,128)S(1)} %pad_add_fusion), channel_id=1, source_target_pairs={{0,2},{1,3},{2,4},{3,5},{4,6},{5,7},{6,8},{7,9},{8,10},{9,11},{10,... | collective-permute-start | bytes 6152 | tf_op jit(solution)/shard_map/ppermute | solution.py:196
  13.6 19.8 %collective-permute-start.8 = (bf16[208,1152]{1,0:T(8,128)(2,1)S(1)}, bf16[208,1152]{1,0:T(8,128)(2,1)S(1)}, u32[]{:S(2)}, u32[]{:S(2)}) collective-permute-start(bf16[208,1152]{1,0:T(8,128)(2,1)S(1)} %get-tuple-element.38), channel_id=1, source_target_pairs={{0,2},{1,3},{2,4},{3,5},{4,6},{5,7},{6,8},{7,9},{8,10},{9,11},{10,... | collective-permute-start | bytes 1437704 | tf_op jit(solution)/shard_map/ppermute | solution.py:196
  23.1 2.4 %collective-permute-start.3 = (bf16[192,1152]{1,0:T(8,128)(2,1)S(1)}, bf16[192,1152]{1,0:T(8,128)(2,1)S(1)}, u32[]{:S(2)}, u32[]{:S(2)}) collective-permute-start(bf16[192,1152]{1,0:T(8,128)(2,1)S(1)} %get-tuple-element.26), channel_id=1, source_target_pairs={{0,1},{1,0},{2,3},{3,2},{4,5},{5,4},{6,7},{7,6},{8,9},{9,8},{10,11... | collective-permute-start | bytes 1327112 | tf_op jit(solution)/shard_map/ppermute | solution.py:199
  23.6 1.9 %collective-permute-start.4 = (bf16[64,1152]{1,0:T(8,128)(2,1)S(1)}, bf16[64,1152]{1,0:T(8,128)(2,1)S(1)}, u32[]{:S(2)}, u32[]{:S(2)}) collective-permute-start(bf16[64,1152]{1,0:T(8,128)(2,1)S(1)} %get-tuple-element.27), channel_id=1, source_target_pairs={{0,1},{1,0},{2,3},{3,2},{4,5},{5,4},{6,7},{7,6},{8,9},{9,8},{10,11... | collective-permute-start | bytes 442376 | tf_op jit(solution)/shard_map/ppermute | solution.py:199
  23.7 12.0 %collective-permute-start.7 = (bf16[48,1152]{1,0:T(8,128)(2,1)S(1)}, bf16[48,1152]{1,0:T(8,128)(2,1)S(1)}, u32[]{:S(2)}, u32[]{:S(2)}) collective-permute-start(bf16[48,1152]{1,0:T(8,128)(2,1)S(1)} %get-tuple-element.36), channel_id=1, source_target_pairs={{0,2},{1,3},{2,4},{3,5},{4,6},{5,7},{6,8},{7,9},{8,10},{9,11},{10,... | collective-permute-start | bytes 331784 | tf_op jit(solution)/shard_map/ppermute | solution.py:196

commit v15 on v13

--- a/solution.py
+++ b/solution.py
@@ -58,13 +58,13 @@
         copy.wait()
 
 
-def add_kernel(start, chunks, arrived, late, *refs):
-    out, staged, sems = refs[-3:]
-    step = arrived.shape[0] // chunks
+def add_kernel(start, chunks, count, late, *refs):
+    arrived, (out, staged, sems) = refs[:count], refs[-3:]
+    step = staged.shape[0] // chunks
     copies = []
     for k in range(chunks):
         here, there = pl.ds(k * step, step), pl.ds(start + k * step, step)
-        staged[here, :] = arrived[here, :].astype(staged.dtype) + late[there, :]
+        staged[here, :] = sum((part[here, :].astype(staged.dtype) for part in arrived), late[there, :])
         copies.append(pltpu.make_async_copy(staged.at[here], out.at[there], sems.at[k]))
         copies[-1].start()
     for copy in copies:
@@ -99,7 +99,11 @@
     image_sum[...] = dot(low(coef), text[...], (1, 0))
 
 
-def relay_kernel(flags, token, text, far, out_a, out_b):
+def ids_kernel(token, both_ids, out):
+    out[...] = both_ids[...]
+
+
+def relay_kernel(flags, token, leg, text, far, out_a, out_b):
     cut = out_a.shape[0]
 
     def fill(source):
@@ -151,18 +155,18 @@
     )(*scalars, *operands)
 
 
-def add_part(name, start, chunks, arrived, late, *before):
+def add_part(name, start, chunks, late, arrived, *before):
     return pl.pallas_call(
-        functools.partial(add_kernel, start, chunks),
+        functools.partial(add_kernel, start, chunks, len(arrived)),
         out_shape=jax.ShapeDtypeStruct(late.shape, late.dtype),
-        in_specs=[VMEM, VMEM] + [HBM] * len(before),
+        in_specs=[VMEM] * (1 + len(arrived)) + [HBM] * len(before),
         out_specs=HBM,
-        scratch_shapes=[pltpu.VMEM(arrived.shape, late.dtype), pltpu.SemaphoreType.DMA((chunks,))],
-        input_output_aliases={2: 0} if before else {},
+        scratch_shapes=[pltpu.VMEM(arrived[0].shape, late.dtype), pltpu.SemaphoreType.DMA((chunks,))],
+        input_output_aliases={1 + len(arrived): 0} if before else {},
         compiler_params=pltpu.CompilerParams(vmem_limit_bytes=16 * 1024 * 1024),
         cost_estimate=pl.CostEstimate(flops=0, bytes_accessed=0, transcendentals=0),
         name=name,
-    )(arrived, late, *before)
+    )(late, *arrived, *before)
 
 
 def body(image_emb, text_emb, text_accum, pair_ids, log_scale, bias):
@@ -200,7 +204,7 @@
     mate_ids = across(ids)
     both_ids = ahead(jnp.concatenate([ids, mate_ids]))
 
-    cut = rows - rows * 3 // 16
+    cut = rows - rows // 4
     out_a, out_b, image_sum, loss = pl.pallas_call(
         own_kernel,
         out_shape=[
@@ -217,11 +221,16 @@
         name="own",
     )(flags, params, ids, mate_ids, image_a, image_b, mate_a, mate_b, text,
       pltpu.with_memory_space_constraint(text_accum, pltpu.HBM))
-    arrived_a, arrived_b = ahead(out_a), ahead(out_b)
-
+    turn = lax.axis_size("group")
+    to_turn = lax.ppermute(out_b, AXES, [(count - 2, turn)])
+    turned = lax.ppermute(to_turn, AXES, [(turn, 0)])
+    arrived_a = ahead(out_a)
+    arrived_b = lax.ppermute(out_b, AXES, skip[:-2] + skip[-1:])
+
+    (both_ids,) = call(ids_kernel, "ids", [((2, rows), jnp.int32)], (), loss, both_ids, flops=2 << 30)
     passed_a, passed_b = call(
         relay_kernel, "relay", [((cut - 16, width), bf16), ((rows - cut + 16, width), bf16)],
-        (flags,), both_ids, text, far, flops=1 << 30,
+        (flags,), both_ids, to_turn, text, far, flops=1 << 30,
     )
     near_a, near_b = across(passed_a), across(passed_b)
     late, image_sum, loss = call(
@@ -234,8 +243,8 @@
         (flags, params), ids, mate_ids, both_ids, image_a, image_b, near_a, near_b, image_sum, loss,
     )
     late, image_grad = lax.optimization_barrier((late, image_grad))
-    text_grad = add_part("add_a", 0, cut // STEP, arrived_a, late)
-    text_grad = add_part("add_b", cut, (rows - cut) // STEP, arrived_b, late, text_grad)
+    text_grad = add_part("add_a", 0, cut // STEP, late, (arrived_a,))
+    text_grad = add_part("add_b", cut, (rows - cut) // STEP, late, (arrived_b, turned), text_grad)
     return (loss.reshape(rows), image_grad, text_grad)
 
 

time: 35.9 us -> 36.8 us (1.025)
  starting transfers between devices: 7.27 us -> 10.5 us
  waiting for transfers between devices: 14 us -> 11.6 us
    ppermute x0 -> x3, starting transfers between devices: none -> 3.25 us  [the longest x1 1.29 us: body(): turned = lax.ppermute(to_turn, AXES, [(turn, 0)])]
    ppermute x4 -> x3, waiting for transfers between devices: 13.9 us -> 11.4 us  [ahead(): return lax.ppermute(value, AXES, skip)]
    pallas_call x4 -> x5, Pallas kernels: 4.36 us -> 4.38 us  [call(): pl.pallas_call(kernel, out_shape=[jax.ShapeDtypeStruct(s, d) for s, d in...]
    ppermute x4 -> x3, starting transfers between devices: 6.05 us -> 6.05 us  [ahead(): return lax.ppermute(value, AXES, skip)]
  transfers between devices with their start and end apart: 9 -> 11, of which waited for: 4 -> 3; matrix products, arithmetic and copies ran while one was open for 0% -> 0% of each run, Pallas kernels for 29% -> 28%
where the time goes in v15:
time: 36.8 us; the launch traced here: 36.5 us
  waiting for transfers between devices  11.6 us (32%)
  Pallas kernels  11 us (30%)
  starting transfers between devices  10.5 us (29%)
  between operations  2.06 us (6%)
  local copies, waits for them, and re-layouts  1.27 us (3%)
    ppermute x3, waiting for transfers between devices, ahead(): return lax.ppermute(value, AXES, skip)  11.4 us
    ppermute x3, starting transfers between devices, ahead(): return lax.ppermute(value, AXES, skip)  6.05 us
    pallas_call x5, Pallas kernels, call(): pl.pallas_call(kernel, out_shape=[jax.ShapeDtypeStruct(s, d) for s, d in...  4.38 us
    pallas_call x1, Pallas kernels, body(): pl.pallas_call(own_kernel, out_shape=[jax.ShapeDtypeStruct((cut, width),...  3.82 us
    pallas_call x2, Pallas kernels, add_part(): pl.pallas_call(functools.partial(add_kernel, start, chunks, len(arrived))...  1.77 us
    ppermute x1, starting transfers between devices, body(): turned = lax.ppermute(to_turn, AXES, [(turn, 0)])  1.29 us
    ppermute x1, starting transfers between devices, body(): arrived_b = lax.ppermute(out_b, AXES, skip[:-2] + skip[-1:])  1.29 us
    unnamed x4, local copies, waits for them, and re-layouts  1.27 us
  transfers between devices with their start and end apart: 11, of which 3 were waited for; matrix products, arithmetic and copies ran while one was open for 0% of the time, Pallas kernels for 28%

profile of v15, /device:TPU:0, one launch (start us, length us, event | category | flops | bytes accessed | tf_op | source)
XLA Modules:
  0.0 36.5 jit_solution(3014598421937019090)
XLA Ops:
  0.6 0.0 copy-start
  0.6 1.3 %copy-done = f32[256,1152]{1,0:T(8,128)S(1)} copy-done((f32[256,1152]{1,0:T(8,128)S(1)}, f32[256,1152]{1,0:T(8,128)}, u32[]{:S(2)}) %copy-start) | copy-done | bytes 1179672
  1.9 0.0 copy-start.1
  1.9 0.1 cast.1.text
  2.0 3.0 %collective-permute-start.5 = (bf16[256,1152]{1,0:T(8,128)(2,1)S(1)}, bf16[256,1152]{1,0:T(8,128)(2,1)S(1)}, u32[]{:S(2)}, u32[]{:S(2)}) collective-permute-start(bf16[256,1152]{1,0:T(8,128)(2,1)S(1)} %cast.1.text), channel_id=1, source_target_pairs={{0,2},{1,3},{2,4},{3,5},{4,6},{5,7},{6,8},{7,9},{8,10},{9,11},{10,... | collective-permute-start | bytes 1769480 | tf_op jit(solution)/shard_map/ppermute | solution.py:185
  5.0 1.1 %load.1 = (bf16[128,1152]{1,0:T(8,128)(2,1)S(1)}, bf16[128,1152]{1,0:T(8,128)(2,1)S(1)}) custom-call(bf16[256,1152]{1,0:T(8,128)(2,1)S(1)} %cast.1.text, bf16[256,1152]{1,0:T(8,128)(2,1)} %image.1), custom_call_target="tpu_custom_call" | custom-call | tf_op jit(solution)/shard_map/load/pallas_call | solution.py:193
  6.1 0.1 collective-permute-start.1
  6.1 0.5 %collective-permute-start.2 = (bf16[128,1152]{1,0:T(8,128)(2,1)S(1)}, bf16[128,1152]{1,0:T(8,128)(2,1)S(1)}, u32[]{:S(2)}, u32[]{:S(2)}) collective-permute-start(bf16[128,1152]{1,0:T(8,128)(2,1)S(1)} %get-tuple-element.19.image_b), channel_id=1, source_target_pairs={{0,1},{1,0},{2,3},{3,2},{4,5},{5,4},{6,7},{7,6},{8,9},{9,8},{10,11... | collective-permute-start | bytes 884744 | tf_op jit(solution)/shard_map/ppermute | solution.py:188
  6.6 0.0 copy-done.1
  6.6 0.1 collective-permute-start
  8.0 0.1 collective-permute-done.mate_ids
  8.1 1.5 %collective-permute-start.3 = (s32[2,256]{1,0:T(2,128)S(1)}, s32[2,256]{1,0:T(2,128)S(1)}, u32[]{:S(2)}, u32[]{:S(2)}) collective-permute-start(s32[2,256]{1,0:T(2,128)S(1)} %pad_add_fusion), channel_id=1, source_target_pairs={{0,2},{1,3},{2,4},{3,5},{4,6},{5,7},{6,8},{7,9},{8,10},{9,11},{10,... | collective-permute-start | bytes 6152 | tf_op jit(solution)/shard_map/ppermute | solution.py:185
  9.6 0.1 pad_maximum_fusion.params
  9.7 0.0 collective-permute-done.1.mate_a
  9.7 0.0 collective-permute-done.2.mate_b
  9.7 3.8 %own.1 = (bf16[192,1152]{1,0:T(8,128)(2,1)S(1)}, bf16[64,1152]{1,0:T(8,128)(2,1)S(1)}, f32[256,1152]{1,0:T(8,128)S(1)}, f32[1,256]{1,0:T(1,128)S(1)}) custom-call(s32[1]{0:T(128)} %bitcast.flags, f32[2]{0:T(128)S(1)} %pad_maximum_fusion.params, s32[1,256]{1,0:T(1,128)S(1)} %bitcast.5, s32[1,256]{1,0:T(1,128)S(1)} %collective-permute-done.mate_ids, ...), custom_call_target="tpu_custom_call" | custom-call | tf_op jit(solution)/shard_map/own/pallas_call | solution.py:208
  13.5 0.7 %collective-permute-start.4 = (bf16[64,1152]{1,0:T(8,128)(2,1)S(1)}, bf16[64,1152]{1,0:T(8,128)(2,1)S(1)}, u32[]{:S(2)}, u32[]{:S(2)}) collective-permute-start(bf16[64,1152]{1,0:T(8,128)(2,1)S(1)} %get-tuple-element.21), channel_id=1, source_target_pairs={{30,4}} | collective-permute-start | bytes 442376 | tf_op jit(solution)/shard_map/ppermute | solution.py:225
  14.2 1.6 %collective-permute-start.10 = (bf16[192,1152]{1,0:T(8,128)(2,1)S(1)}, bf16[192,1152]{1,0:T(8,128)(2,1)S(1)}, u32[]{:S(2)}, u32[]{:S(2)}) collective-permute-start(bf16[192,1152]{1,0:T(8,128)(2,1)S(1)} %get-tuple-element.32), channel_id=1, source_target_pairs={{0,2},{1,3},{2,4},{3,5},{4,6},{5,7},{6,8},{7,9},{8,10},{9,11},{10,... | collective-permute-start | bytes 1327112 | tf_op jit(solution)/shard_map/ppermute | solution.py:185
  15.8 7.4 %collective-permute-done.3.both_ids = s32[2,256]{1,0:T(2,128)S(1)} collective-permute-done((s32[2,256]{1,0:T(2,128)S(1)}, s32[2,256]{1,0:T(2,128)S(1)}, u32[]{:S(2)}, u32[]{:S(2)}) %collective-permute-start.3) | collective-permute-done | bytes 2080 | tf_op jit(solution)/shard_map/ppermute | solution.py:185
  23.2 0.0 collective-permute-done.4.leg
  23.2 0.0 collective-permute-done.5.far
  23.2 0.1 relay.1
  23.2 0.1 collective-permute-start.6
  23.3 0.5 %collective-permute-start.7 = (bf16[80,1152]{1,0:T(8,128)(2,1)S(1)}, bf16[80,1152]{1,0:T(8,128)(2,1)S(1)}, u32[]{:S(2)}, u32[]{:S(2)}) collective-permute-start(bf16[80,1152]{1,0:T(8,128)(2,1)S(1)} %get-tuple-element.23), channel_id=1, source_target_pairs={{0,1},{1,0},{2,3},{3,2},{4,5},{5,4},{6,7},{7,6},{8,9},{9,8},{10,11... | collective-permute-start | bytes 552968 | tf_op jit(solution)/shard_map/ppermute | solution.py:188
  23.8 1.3 %collective-permute-start.8 = (bf16[64,1152]{1,0:T(8,128)(2,1)S(1)}, bf16[64,1152]{1,0:T(8,128)(2,1)S(1)}, u32[]{:S(2)}, u32[]{:S(2)}) collective-permute-start(bf16[64,1152]{1,0:T(8,128)(2,1)S(1)} %get-tuple-element.21), channel_id=1, source_target_pairs={{0,2},{1,3},{2,4},{3,5},{4,6},{5,7},{6,8},{7,9},{8,10},{9,11},{10,... | collective-permute-start | bytes 442376 | tf_op jit(solution)/shard_map/ppermute | solution.py:228
  25.1 1.3 %collective-permute-start.9 = (bf16[64,1152]{1,0:T(8,128)(2,1)S(1)}, bf16[64,1152]{1,0:T(8,128)(2,1)S(1)}, u32[]{:S(2)}, u32[]{:S(2)}) collective-permute-start(bf16[64,1152]{1,0:T(8,128)(2,1)S(1)} %collective-permute-done.4.leg), channel_id=1, source_target_pairs={{4,0}} | collective-permute-start | bytes 442376 | tf_op jit(solution)/shard_map/ppermute | solution.py:226
  26.4 1.8 %far.1 = (f32[256,1152]{1,0:T(8,128)S(1)}, f32[256,1152]{1,0:T(8,128)S(1)}, f32[1,256]{1,0:T(1,128)S(1)}) custom-call(s32[1]{0:T(128)} %bitcast.flags, f32[2]{0:T(128)S(1)} %pad_maximum_fusion.params, s32[1,256]{1,0:T(1,128)S(1)} %bitcast.6, s32[1,256]{1,0:T(1,128)S(1)} %collective-permute-done.mate_ids, s32[2,256]{1,0:T(2,128)S(1)} %ids.1.token.both_ids, ...), custom_call_target="tpu_custom_call" | custom-call | tf_op jit(solution)/shard_map/far/pallas_call | solution.py:147
  28.2 0.0 collective-permute-done.7.near_b
  28.2 0.0 collective-permute-done.6.near_a
  28.3 2.4 %near.1 = (bf16[256,1152]{1,0:T(8,128)(2,1)}, f32[1,256]{1,0:T(1,128)}) custom-call(s32[1]{0:T(128)} %bitcast.flags, f32[2]{0:T(128)S(1)} %pad_maximum_fusion.params, s32[1,256]{1,0:T(1,128)S(1)} %bitcast.7, s32[1,256]{1,0:T(1,128)S(1)} %collective-permute-done.mate_ids, s32[2,256]{1,0:T(2,128)S(1)} %ids.1.token.both_ids, ...), custom_call_target="tpu_custom_call" | custom-call | tf_op jit(solution)/shard_map/near/pallas_call | solution.py:147
  30.7 4.1 %collective-permute-done.10.refs_0_ = bf16[192,1152]{1,0:T(8,128)(2,1)S(1)} collective-permute-done((bf16[192,1152]{1,0:T(8,128)(2,1)S(1)}, bf16[192,1152]{1,0:T(8,128)(2,1)S(1)}, u32[]{:S(2)}, u32[]{:S(2)}) %collective-permute-start.10) | collective-permute-done | bytes 442400 | tf_op jit(solution)/shard_map/ppermute | solution.py:185
  34.7 1.0 %add_a.1.refs_2_ = f32[256,1152]{1,0:T(8,128)} custom-call(f32[256,1152]{1,0:T(8,128)S(1)} %get-tuple-element.31.late, bf16[192,1152]{1,0:T(8,128)(2,1)S(1)} %collective-permute-done.10.refs_0_), custom_call_target="tpu_custom_call" | custom-call | tf_op jit(solution)/shard_map/add_a/pallas_call | solution.py:159
  35.8 0.0 collective-permute-done.8.refs_0_
  35.8 0.0 collective-permute-done.9.refs_1_
  35.8 0.8 %add_b.1 = f32[256,1152]{1,0:T(8,128)} custom-call(f32[256,1152]{1,0:T(8,128)S(1)} %get-tuple-element.31.late, bf16[64,1152]{1,0:T(8,128)(2,1)S(1)} %collective-permute-done.8.refs_0_, bf16[64,1152]{1,0:T(8,128)(2,1)S(1)} %collective-permute-done.9.refs_1_, f32[256,1152]{1,0:T(8,128)} %add_a.1.refs_2_), custom_call_target="tpu_custom_call", output_to_operand_aliasing={{}: (3, {})} | custom-call | tf_op jit(solution)/shard_map/add_b/pallas_call | solution.py:159
  (2 shorter events, 0.0 us)
Async XLA Ops:
  0.6 1.3 %copy-start = (f32[256,1152]{1,0:T(8,128)S(1)}, f32[256,1152]{1,0:T(8,128)}, u32[]{:S(2)}) copy-start(f32[256,1152]{1,0:T(8,128)} %text.1) | copy-start | bytes 3538948
  1.9 4.7 %copy-start.1 = (s32[256]{0:T(256)S(1)}, s32[256]{0:T(256)}, u32[]{:S(2)}) copy-start(s32[256]{0:T(256)} %param.9) | copy-start | bytes 3076
  2.0 21.2 %collective-permute-start.5 = (bf16[256,1152]{1,0:T(8,128)(2,1)S(1)}, bf16[256,1152]{1,0:T(8,128)(2,1)S(1)}, u32[]{:S(2)}, u32[]{:S(2)}) collective-permute-start(bf16[256,1152]{1,0:T(8,128)(2,1)S(1)} %cast.1.text), channel_id=1, source_target_pairs={{0,2},{1,3},{2,4},{3,5},{4,6},{5,7},{6,8},{7,9},{8,10},{9,11},{10,... | collective-permute-start | bytes 1769480 | tf_op jit(solution)/shard_map/ppermute | solution.py:185
  6.1 3.6 %collective-permute-start.1 = (bf16[128,1152]{1,0:T(8,128)(2,1)S(1)}, bf16[128,1152]{1,0:T(8,128)(2,1)S(1)}, u32[]{:S(2)}, u32[]{:S(2)}) collective-permute-start(bf16[128,1152]{1,0:T(8,128)(2,1)S(1)} %get-tuple-element.18.image_a), channel_id=1, source_target_pairs={{0,1},{1,0},{2,3},{3,2},{4,5},{5,4},{6,7},{7,6},{8,9},{9,8},{10,11... | collective-permute-start | bytes 884744 | tf_op jit(solution)/shard_map/ppermute | solution.py:188
  6.1 3.5 %collective-permute-start.2 = (bf16[128,1152]{1,0:T(8,128)(2,1)S(1)}, bf16[128,1152]{1,0:T(8,128)(2,1)S(1)}, u32[]{:S(2)}, u32[]{:S(2)}) collective-permute-start(bf16[128,1152]{1,0:T(8,128)(2,1)S(1)} %get-tuple-element.19.image_b), channel_id=1, source_target_pairs={{0,1},{1,0},{2,3},{3,2},{4,5},{5,4},{6,7},{7,6},{8,9},{9,8},{10,11... | collective-permute-start | bytes 884744 | tf_op jit(solution)/shard_map/ppermute | solution.py:188
  6.6 1.5 %collective-permute-start = (s32[1,256]{1,0:T(1,128)S(1)}, s32[1,256]{1,0:T(1,128)S(1)}, u32[]{:S(2)}, u32[]{:S(2)}) collective-permute-start(s32[1,256]{1,0:T(1,128)S(1)} %bitcast.3), channel_id=1, source_target_pairs={{0,1},{1,0},{2,3},{3,2},{4,5},{5,4},{6,7},{7,6},{8,9},{9,8},{10,11... | collective-permute-start | bytes 3080 | tf_op jit(solution)/shard_map/ppermute | solution.py:188
  8.1 15.0 %collective-permute-start.3 = (s32[2,256]{1,0:T(2,128)S(1)}, s32[2,256]{1,0:T(2,128)S(1)}, u32[]{:S(2)}, u32[]{:S(2)}) collective-permute-start(s32[2,256]{1,0:T(2,128)S(1)} %pad_add_fusion), channel_id=1, source_target_pairs={{0,2},{1,3},{2,4},{3,5},{4,6},{5,7},{6,8},{7,9},{8,10},{9,11},{10,... | collective-permute-start | bytes 6152 | tf_op jit(solution)/shard_map/ppermute | solution.py:185
  13.5 9.6 %collective-permute-start.4 = (bf16[64,1152]{1,0:T(8,128)(2,1)S(1)}, bf16[64,1152]{1,0:T(8,128)(2,1)S(1)}, u32[]{:S(2)}, u32[]{:S(2)}) collective-permute-start(bf16[64,1152]{1,0:T(8,128)(2,1)S(1)} %get-tuple-element.21), channel_id=1, source_target_pairs={{30,4}} | collective-permute-start | bytes 442376 | tf_op jit(solution)/shard_map/ppermute | solution.py:225
  14.2 20.6 %collective-permute-start.10 = (bf16[192,1152]{1,0:T(8,128)(2,1)S(1)}, bf16[192,1152]{1,0:T(8,128)(2,1)S(1)}, u32[]{:S(2)}, u32[]{:S(2)}) collective-permute-start(bf16[192,1152]{1,0:T(8,128)(2,1)S(1)} %get-tuple-element.32), channel_id=1, source_target_pairs={{0,2},{1,3},{2,4},{3,5},{4,6},{5,7},{6,8},{7,9},{8,10},{9,11},{10,... | collective-permute-start | bytes 1327112 | tf_op jit(solution)/shard_map/ppermute | solution.py:185
  23.2 5.0 %collective-permute-start.6 = (bf16[176,1152]{1,0:T(8,128)(2,1)S(1)}, bf16[176,1152]{1,0:T(8,128)(2,1)S(1)}, u32[]{:S(2)}, u32[]{:S(2)}) collective-permute-start(bf16[176,1152]{1,0:T(8,128)(2,1)S(1)} %get-tuple-element.22), channel_id=1, source_target_pairs={{0,1},{1,0},{2,3},{3,2},{4,5},{5,4},{6,7},{7,6},{8,9},{9,8},{10,11... | collective-permute-start | bytes 1216520 | tf_op jit(solution)/shard_map/ppermute | solution.py:188
  23.3 4.9 %collective-permute-start.7 = (bf16[80,1152]{1,0:T(8,128)(2,1)S(1)}, bf16[80,1152]{1,0:T(8,128)(2,1)S(1)}, u32[]{:S(2)}, u32[]{:S(2)}) collective-permute-start(bf16[80,1152]{1,0:T(8,128)(2,1)S(1)} %get-tuple-element.23), channel_id=1, source_target_pairs={{0,1},{1,0},{2,3},{3,2},{4,5},{5,4},{6,7},{7,6},{8,9},{9,8},{10,11... | collective-permute-start | bytes 552968 | tf_op jit(solution)/shard_map/ppermute | solution.py:188
  23.8 12.0 %collective-permute-start.8 = (bf16[64,1152]{1,0:T(8,128)(2,1)S(1)}, bf16[64,1152]{1,0:T(8,128)(2,1)S(1)}, u32[]{:S(2)}, u32[]{:S(2)}) collective-permute-start(bf16[64,1152]{1,0:T(8,128)(2,1)S(1)} %get-tuple-element.21), channel_id=1, source_target_pairs={{0,2},{1,3},{2,4},{3,5},{4,6},{5,7},{6,8},{7,9},{8,10},{9,11},{10,... | collective-permute-start | bytes 442376 | tf_op jit(solution)/shard_map/ppermute | solution.py:228
  25.1 10.7 %collective-permute-start.9 = (bf16[64,1152]{1,0:T(8,128)(2,1)S(1)}, bf16[64,1152]{1,0:T(8,128)(2,1)S(1)}, u32[]{:S(2)}, u32[]{:S(2)}) collective-permute-start(bf16[64,1152]{1,0:T(8,128)(2,1)S(1)} %collective-permute-done.4.leg), channel_id=1, source_target_pairs={{4,0}} | collective-permute-start | bytes 442376 | tf_op jit(solution)/shard_map/ppermute | solution.py:226

commit v16 on v15

--- a/solution.py
+++ b/solution.py
@@ -10,6 +10,7 @@
 SHIFTS = 2
 AXES = ("dp", "group")
 STEP = 16
+PIECES = 4
 VMEM = pl.BlockSpec(memory_space=pltpu.VMEM)
 SMEM = pl.BlockSpec(memory_space=pltpu.SMEM)
 ANY = pl.BlockSpec(memory_space=pl.ANY)
@@ -34,8 +35,8 @@
     return jnp.sum(loss.T, axis=0, keepdims=True), coef
 
 
-def whole(a, b):
-    return jnp.concatenate([a[...], b[...]], axis=0)
+def whole(*parts):
+    return jnp.concatenate([part[...] for part in parts], axis=0)
 
 
 def low(coef):
@@ -103,12 +104,12 @@
     out[...] = both_ids[...]
 
 
-def relay_kernel(flags, token, leg, text, far, out_a, out_b):
-    cut = out_a.shape[0]
+def relay_kernel(flags, token, text, far, *outs):
+    step = outs[0].shape[0]
 
     def fill(source):
-        out_a[...] = source[:cut, :]
-        out_b[...] = source[cut:, :]
+        for k, out in enumerate(outs):
+            out[...] = source[k * step:(k + 1) * step, :]
 
     pl.when(flags[0] == 0)(lambda: fill(text))
     pl.when(flags[0] == 1)(lambda: fill(far))
@@ -133,11 +134,11 @@
         late[...] = part + dot(low(mate_coef.T), mate, (1, 0))
 
 
-def near_kernel(flags, params, ids, mate_ids, both_ids, image_a, image_b, near_a, near_b, image_in, loss_in,
-                image_grad, loss):
+def near_kernel(flags, params, ids, mate_ids, both_ids, image_a, image_b, image_in, loss_in, *refs):
+    image_grad, loss = refs[PIECES:]
     image = whole(image_a, image_b)
     near_ids = jnp.where(flags[0] == 0, both_ids[1:, :], mate_ids[...])
-    near = whole(near_a, near_b)
+    near = whole(*refs[:PIECES])
     more, coef = pair(image, near, ids[...], near_ids, params)
     loss[...] = (loss_in[...] + more) * (1.0 / ((SHIFTS + 1) * image.shape[0]))
     image_grad[...] = (image_in[...] + dot(low(coef), near, (1, 0))).astype(image_grad.dtype)
@@ -204,7 +205,7 @@
     mate_ids = across(ids)
     both_ids = ahead(jnp.concatenate([ids, mate_ids]))
 
-    cut = rows - rows // 4
+    cut = rows - rows * 3 // 8
     out_a, out_b, image_sum, loss = pl.pallas_call(
         own_kernel,
         out_shape=[
@@ -228,11 +229,11 @@
     arrived_b = lax.ppermute(out_b, AXES, skip[:-2] + skip[-1:])
 
     (both_ids,) = call(ids_kernel, "ids", [((2, rows), jnp.int32)], (), loss, both_ids, flops=2 << 30)
-    passed_a, passed_b = call(
-        relay_kernel, "relay", [((cut - 16, width), bf16), ((rows - cut + 16, width), bf16)],
-        (flags,), both_ids, to_turn, text, far, flops=1 << 30,
+    passed = call(
+        relay_kernel, "relay", [((rows // PIECES, width), bf16)] * PIECES,
+        (flags,), both_ids, text, far, flops=1 << 30,
     )
-    near_a, near_b = across(passed_a), across(passed_b)
+    near = [across(piece) for piece in passed]
     late, image_sum, loss = call(
         far_kernel, "far", [((rows, width), f32), ((rows, width), f32), ((1, rows), f32)],
         (flags, params), ids, mate_ids, both_ids, image_a, image_b, mate_a, mate_b, far, image_sum,
@@ -240,11 +241,11 @@
     )
     image_grad, loss = call(
         near_kernel, "near", [((rows, width), bf16), ((1, rows), f32)],
-        (flags, params), ids, mate_ids, both_ids, image_a, image_b, near_a, near_b, image_sum, loss,
+        (flags, params), ids, mate_ids, both_ids, image_a, image_b, image_sum, loss, *near,
     )
     late, image_grad = lax.optimization_barrier((late, image_grad))
-    text_grad = add_part("add_a", 0, cut // STEP, late, (arrived_a,))
-    text_grad = add_part("add_b", cut, (rows - cut) // STEP, late, (arrived_b, turned), text_grad)
+    text_grad = add_part("add_b", cut, (rows - cut) // STEP, late, (arrived_b, turned))
+    text_grad = add_part("add_a", 0, cut // STEP, late, (arrived_a,), text_grad)
     return (loss.reshape(rows), image_grad, text_grad)
 
 

time: 36.8 us -> 36.6 us (level)
  waiting for transfers between devices: 11.6 us -> 10.8 us
  starting transfers between devices: 10.5 us -> 11.1 us
    ppermute x3, waiting for transfers between devices: 11.4 us -> 7.39 us  [ahead(): return lax.ppermute(value, AXES, skip)]
    ppermute x1, waiting for transfers between devices: 0.01 us -> 3.26 us  [body(): turned = lax.ppermute(to_turn, AXES, [(turn, 0)])]
    ppermute x5 -> x7, starting transfers between devices: 1.21 us -> 1.79 us  [across(): return lax.ppermute(value, AXES, swap)]
  transfers between devices with their start and end apart: 11 -> 13, of which waited for: 3 -> 3; matrix products, arithmetic and copies ran while one was open for 0% -> 0% of each run, Pallas kernels for 28% -> 28%
where the time goes in v16:
time: 36.6 us; the launch traced here: 36.3 us
  starting transfers between devices  11.1 us (30%)
  Pallas kernels  11 us (30%)
  waiting for transfers between devices  10.8 us (30%)
  between operations  2.07 us (6%)
  local copies, waits for them, and re-layouts  1.27 us (3%)
    ppermute x3, waiting for transfers between devices, ahead(): return lax.ppermute(value, AXES, skip)  7.39 us
    ppermute x3, starting transfers between devices, ahead(): return lax.ppermute(value, AXES, skip)  6.05 us
    pallas_call x5, Pallas kernels, call(): pl.pallas_call(kernel, out_shape=[jax.ShapeDtypeStruct(s, d) for s, d in...  4.36 us
    pallas_call x1, Pallas kernels, body(): pl.pallas_call(own_kernel, out_shape=[jax.ShapeDtypeStruct((cut, width),...  3.82 us
    ppermute x1, waiting for transfers between devices, body(): turned = lax.ppermute(to_turn, AXES, [(turn, 0)])  3.26 us
    ppermute x7, starting transfers between devices, across(): return lax.ppermute(value, AXES, swap)  1.79 us
    pallas_call x2, Pallas kernels, add_part(): pl.pallas_call(functools.partial(add_kernel, start, chunks, len(arrived))...  1.78 us
    ppermute x1, starting transfers between devices, body(): turned = lax.ppermute(to_turn, AXES, [(turn, 0)])  1.29 us
  transfers between devices with their start and end apart: 13, of which 3 were waited for; matrix products, arithmetic and copies ran while one was open for 0% of the time, Pallas kernels for 28%

profile of v16, /device:TPU:0, one launch (start us, length us, event | category | flops | bytes accessed | tf_op | source)
XLA Modules:
  0.0 36.3 jit_solution(5945301865416881411)
XLA Ops:
  0.6 0.0 copy-start
  0.6 1.3 %copy-done = f32[256,1152]{1,0:T(8,128)S(1)} copy-done((f32[256,1152]{1,0:T(8,128)S(1)}, f32[256,1152]{1,0:T(8,128)}, u32[]{:S(2)}) %copy-start) | copy-done | bytes 1179672
  1.9 0.0 copy-start.1
  1.9 0.1 cast.1.text
  2.0 3.0 %collective-permute-start.4 = (bf16[256,1152]{1,0:T(8,128)(2,1)S(1)}, bf16[256,1152]{1,0:T(8,128)(2,1)S(1)}, u32[]{:S(2)}, u32[]{:S(2)}) collective-permute-start(bf16[256,1152]{1,0:T(8,128)(2,1)S(1)} %cast.1.text), channel_id=1, source_target_pairs={{0,2},{1,3},{2,4},{3,5},{4,6},{5,7},{6,8},{7,9},{8,10},{9,11},{10,... | collective-permute-start | bytes 1769480 | tf_op jit(solution)/shard_map/ppermute | solution.py:186
  5.0 1.1 %load.1 = (bf16[128,1152]{1,0:T(8,128)(2,1)S(1)}, bf16[128,1152]{1,0:T(8,128)(2,1)S(1)}) custom-call(bf16[256,1152]{1,0:T(8,128)(2,1)S(1)} %cast.1.text, bf16[256,1152]{1,0:T(8,128)(2,1)} %image.1), custom_call_target="tpu_custom_call" | custom-call | tf_op jit(solution)/shard_map/load/pallas_call | solution.py:194
  6.1 0.1 collective-permute-start.1
  6.1 0.5 %collective-permute-start.2 = (bf16[128,1152]{1,0:T(8,128)(2,1)S(1)}, bf16[128,1152]{1,0:T(8,128)(2,1)S(1)}, u32[]{:S(2)}, u32[]{:S(2)}) collective-permute-start(bf16[128,1152]{1,0:T(8,128)(2,1)S(1)} %get-tuple-element.21.image_b), channel_id=1, source_target_pairs={{0,1},{1,0},{2,3},{3,2},{4,5},{5,4},{6,7},{7,6},{8,9},{9,8},{10,11... | collective-permute-start | bytes 884744 | tf_op jit(solution)/shard_map/ppermute | solution.py:189
  6.6 0.0 copy-done.1
  6.6 0.1 collective-permute-start
  8.0 0.1 collective-permute-done.mate_ids
  8.1 1.5 %collective-permute-start.3 = (s32[2,256]{1,0:T(2,128)S(1)}, s32[2,256]{1,0:T(2,128)S(1)}, u32[]{:S(2)}, u32[]{:S(2)}) collective-permute-start(s32[2,256]{1,0:T(2,128)S(1)} %pad_add_fusion), channel_id=1, source_target_pairs={{0,2},{1,3},{2,4},{3,5},{4,6},{5,7},{6,8},{7,9},{8,10},{9,11},{10,... | collective-permute-start | bytes 6152 | tf_op jit(solution)/shard_map/ppermute | solution.py:186
  9.6 0.1 pad_maximum_fusion.params
  9.7 0.0 collective-permute-done.1.mate_a
  9.7 0.0 collective-permute-done.2.mate_b
  9.7 3.8 %own.1 = (bf16[160,1152]{1,0:T(8,128)(2,1)S(1)}, bf16[96,1152]{1,0:T(8,128)(2,1)S(1)}, f32[256,1152]{1,0:T(8,128)S(1)}, f32[1,256]{1,0:T(1,128)S(1)}) custom-call(s32[1]{0:T(128)} %bitcast.flags, f32[2]{0:T(128)S(1)} %pad_maximum_fusion.params, s32[1,256]{1,0:T(1,128)S(1)} %bitcast.5, s32[1,256]{1,0:T(1,128)S(1)} %collective-permute-done.mate_ids, ...), custom_call_target="tpu_custom_call" | custom-call | tf_op jit(solution)/shard_map/own/pallas_call | solution.py:209
  13.5 0.7 %collective-permute-start.11 = (bf16[96,1152]{1,0:T(8,128)(2,1)S(1)}, bf16[96,1152]{1,0:T(8,128)(2,1)S(1)}, u32[]{:S(2)}, u32[]{:S(2)}) collective-permute-start(bf16[96,1152]{1,0:T(8,128)(2,1)S(1)} %get-tuple-element.36), channel_id=1, source_target_pairs={{30,4}} | collective-permute-start | bytes 663560 | tf_op jit(solution)/shard_map/ppermute | solution.py:226
  14.2 1.6 %collective-permute-start.9 = (bf16[160,1152]{1,0:T(8,128)(2,1)S(1)}, bf16[160,1152]{1,0:T(8,128)(2,1)S(1)}, u32[]{:S(2)}, u32[]{:S(2)}) collective-permute-start(bf16[160,1152]{1,0:T(8,128)(2,1)S(1)} %get-tuple-element.35), channel_id=1, source_target_pairs={{0,2},{1,3},{2,4},{3,5},{4,6},{5,7},{6,8},{7,9},{8,10},{9,11},{10,... | collective-permute-start | bytes 1105928 | tf_op jit(solution)/shard_map/ppermute | solution.py:186
  15.8 7.4 %collective-permute-done.3.both_ids = s32[2,256]{1,0:T(2,128)S(1)} collective-permute-done((s32[2,256]{1,0:T(2,128)S(1)}, s32[2,256]{1,0:T(2,128)S(1)}, u32[]{:S(2)}, u32[]{:S(2)}) %collective-permute-start.3) | collective-permute-done | bytes 2080 | tf_op jit(solution)/shard_map/ppermute | solution.py:186
  23.2 0.0 collective-permute-done.4.far
  23.2 0.1 collective-permute-start.5
  23.3 0.5 %collective-permute-start.6 = (bf16[64,1152]{1,0:T(8,128)(2,1)S(1)}, bf16[64,1152]{1,0:T(8,128)(2,1)S(1)}, u32[]{:S(2)}, u32[]{:S(2)}) collective-permute-start(bf16[64,1152]{1,0:T(8,128)(2,1)S(1)} %get-tuple-element.27), channel_id=1, source_target_pairs={{0,1},{1,0},{2,3},{3,2},{4,5},{5,4},{6,7},{7,6},{8,9},{9,8},{10,11... | collective-permute-start | bytes 442376 | tf_op jit(solution)/shard_map/ppermute | solution.py:189
  23.8 1.3 %collective-permute-start.10 = (bf16[96,1152]{1,0:T(8,128)(2,1)S(1)}, bf16[96,1152]{1,0:T(8,128)(2,1)S(1)}, u32[]{:S(2)}, u32[]{:S(2)}) collective-permute-start(bf16[96,1152]{1,0:T(8,128)(2,1)S(1)} %get-tuple-element.36), channel_id=1, source_target_pairs={{0,2},{1,3},{2,4},{3,5},{4,6},{5,7},{6,8},{7,9},{8,10},{9,11},{10,... | collective-permute-start | bytes 663560 | tf_op jit(solution)/shard_map/ppermute | solution.py:229
  25.1 0.0 collective-permute-done.11
  25.1 1.3 %collective-permute-start.12 = (bf16[96,1152]{1,0:T(8,128)(2,1)S(1)}, bf16[96,1152]{1,0:T(8,128)(2,1)S(1)}, u32[]{:S(2)}, u32[]{:S(2)}) collective-permute-start(bf16[96,1152]{1,0:T(8,128)(2,1)S(1)} %collective-permute-done.11), channel_id=1, source_target_pairs={{4,0}} | collective-permute-start | bytes 663560 | tf_op jit(solution)/shard_map/ppermute | solution.py:227
  26.4 0.0 collective-permute-done.5.refs_0_
  26.4 0.1 collective-permute-start.7
  26.6 0.0 collective-permute-done.6.refs_1_
  26.6 0.4 %collective-permute-start.8 = (bf16[64,1152]{1,0:T(8,128)(2,1)S(1)}, bf16[64,1152]{1,0:T(8,128)(2,1)S(1)}, u32[]{:S(2)}, u32[]{:S(2)}) collective-permute-start(bf16[64,1152]{1,0:T(8,128)(2,1)S(1)} %get-tuple-element.29), channel_id=1, source_target_pairs={{0,1},{1,0},{2,3},{3,2},{4,5},{5,4},{6,7},{7,6},{8,9},{9,8},{10,11... | collective-permute-start | bytes 442376 | tf_op jit(solution)/shard_map/ppermute | solution.py:189
  27.0 1.8 %far.1 = (f32[256,1152]{1,0:T(8,128)S(1)}, f32[256,1152]{1,0:T(8,128)S(1)}, f32[1,256]{1,0:T(1,128)S(1)}) custom-call(s32[1]{0:T(128)} %bitcast.flags, f32[2]{0:T(128)S(1)} %pad_maximum_fusion.params, s32[1,256]{1,0:T(1,128)S(1)} %bitcast.6, s32[1,256]{1,0:T(1,128)S(1)} %collective-permute-done.mate_ids, s32[2,256]{1,0:T(2,128)S(1)} %ids.1.both_ids.token, ...), custom_call_target="tpu_custom_call" | custom-call | tf_op jit(solution)/shard_map/far/pallas_call | solution.py:148
  28.8 0.0 collective-permute-done.7.refs_2_
  28.8 0.0 collective-permute-done.8.refs_3_
  28.8 2.4 %near.1 = (bf16[256,1152]{1,0:T(8,128)(2,1)}, f32[1,256]{1,0:T(1,128)}) custom-call(s32[1]{0:T(128)} %bitcast.flags, f32[2]{0:T(128)S(1)} %pad_maximum_fusion.params, s32[1,256]{1,0:T(1,128)S(1)} %bitcast.7, s32[1,256]{1,0:T(1,128)S(1)} %collective-permute-done.mate_ids, s32[2,256]{1,0:T(2,128)S(1)} %ids.1.both_ids.token, ...), custom_call_target="tpu_custom_call" | custom-call | tf_op jit(solution)/shard_map/near/pallas_call | solution.py:148
  31.3 0.0 collective-permute-done.10.refs_0_
  31.3 3.3 %collective-permute-done.12.refs_1_ = bf16[96,1152]{1,0:T(8,128)(2,1)S(1)} collective-permute-done((bf16[96,1152]{1,0:T(8,128)(2,1)S(1)}, bf16[96,1152]{1,0:T(8,128)(2,1)S(1)}, u32[]{:S(2)}, u32[]{:S(2)}) %collective-permute-start.12) | collective-permute-done | bytes 221216 | tf_op jit(solution)/shard_map/ppermute | solution.py:227
  34.5 0.8 %add_b.1.refs_1_ = f32[256,1152]{1,0:T(8,128)} custom-call(f32[256,1152]{1,0:T(8,128)S(1)} %get-tuple-element.34.late, bf16[96,1152]{1,0:T(8,128)(2,1)S(1)} %collective-permute-done.10.refs_0_, bf16[96,1152]{1,0:T(8,128)(2,1)S(1)} %collective-permute-done.12.refs_1_), custom_call_target="tpu_custom_call" | custom-call | tf_op jit(solution)/shard_map/add_b/pallas_call | solution.py:160
  35.4 0.0 collective-permute-done.9.refs_0_
  35.4 1.0 %add_a.1 = f32[256,1152]{1,0:T(8,128)} custom-call(f32[256,1152]{1,0:T(8,128)S(1)} %get-tuple-element.34.late, bf16[160,1152]{1,0:T(8,128)(2,1)S(1)} %collective-permute-done.9.refs_0_, f32[256,1152]{1,0:T(8,128)} %add_b.1.refs_1_), custom_call_target="tpu_custom_call", output_to_operand_aliasing={{}: (2, {})} | custom-call | tf_op jit(solution)/shard_map/add_a/pallas_call | solution.py:160
  (3 shorter events, 0.1 us)
Async XLA Ops:
  0.6 1.3 %copy-start = (f32[256,1152]{1,0:T(8,128)S(1)}, f32[256,1152]{1,0:T(8,128)}, u32[]{:S(2)}) copy-start(f32[256,1152]{1,0:T(8,128)} %text.1) | copy-start | bytes 3538948
  1.9 4.7 %copy-start.1 = (s32[256]{0:T(256)S(1)}, s32[256]{0:T(256)}, u32[]{:S(2)}) copy-start(s32[256]{0:T(256)} %param.9) | copy-start | bytes 3076
  2.0 21.2 %collective-permute-start.4 = (bf16[256,1152]{1,0:T(8,128)(2,1)S(1)}, bf16[256,1152]{1,0:T(8,128)(2,1)S(1)}, u32[]{:S(2)}, u32[]{:S(2)}) collective-permute-start(bf16[256,1152]{1,0:T(8,128)(2,1)S(1)} %cast.1.text), channel_id=1, source_target_pairs={{0,2},{1,3},{2,4},{3,5},{4,6},{5,7},{6,8},{7,9},{8,10},{9,11},{10,... | collective-permute-start | bytes 1769480 | tf_op jit(solution)/shard_map/ppermute | solution.py:186
  6.1 3.6 %collective-permute-start.1 = (bf16[128,1152]{1,0:T(8,128)(2,1)S(1)}, bf16[128,1152]{1,0:T(8,128)(2,1)S(1)}, u32[]{:S(2)}, u32[]{:S(2)}) collective-permute-start(bf16[128,1152]{1,0:T(8,128)(2,1)S(1)} %get-tuple-element.20.image_a), channel_id=1, source_target_pairs={{0,1},{1,0},{2,3},{3,2},{4,5},{5,4},{6,7},{7,6},{8,9},{9,8},{10,11... | collective-permute-start | bytes 884744 | tf_op jit(solution)/shard_map/ppermute | solution.py:189
  6.1 3.5 %collective-permute-start.2 = (bf16[128,1152]{1,0:T(8,128)(2,1)S(1)}, bf16[128,1152]{1,0:T(8,128)(2,1)S(1)}, u32[]{:S(2)}, u32[]{:S(2)}) collective-permute-start(bf16[128,1152]{1,0:T(8,128)(2,1)S(1)} %get-tuple-element.21.image_b), channel_id=1, source_target_pairs={{0,1},{1,0},{2,3},{3,2},{4,5},{5,4},{6,7},{7,6},{8,9},{9,8},{10,11... | collective-permute-start | bytes 884744 | tf_op jit(solution)/shard_map/ppermute | solution.py:189
  6.6 1.5 %collective-permute-start = (s32[1,256]{1,0:T(1,128)S(1)}, s32[1,256]{1,0:T(1,128)S(1)}, u32[]{:S(2)}, u32[]{:S(2)}) collective-permute-start(s32[1,256]{1,0:T(1,128)S(1)} %bitcast.3), channel_id=1, source_target_pairs={{0,1},{1,0},{2,3},{3,2},{4,5},{5,4},{6,7},{7,6},{8,9},{9,8},{10,11... | collective-permute-start | bytes 3080 | tf_op jit(solution)/shard_map/ppermute | solution.py:189
  8.1 15.0 %collective-permute-start.3 = (s32[2,256]{1,0:T(2,128)S(1)}, s32[2,256]{1,0:T(2,128)S(1)}, u32[]{:S(2)}, u32[]{:S(2)}) collective-permute-start(s32[2,256]{1,0:T(2,128)S(1)} %pad_add_fusion), channel_id=1, source_target_pairs={{0,2},{1,3},{2,4},{3,5},{4,6},{5,7},{6,8},{7,9},{8,10},{9,11},{10,... | collective-permute-start | bytes 6152 | tf_op jit(solution)/shard_map/ppermute | solution.py:186
  13.5 11.6 %collective-permute-start.11 = (bf16[96,1152]{1,0:T(8,128)(2,1)S(1)}, bf16[96,1152]{1,0:T(8,128)(2,1)S(1)}, u32[]{:S(2)}, u32[]{:S(2)}) collective-permute-start(bf16[96,1152]{1,0:T(8,128)(2,1)S(1)} %get-tuple-element.36), channel_id=1, source_target_pairs={{30,4}} | collective-permute-start | bytes 663560 | tf_op jit(solution)/shard_map/ppermute | solution.py:226
  14.2 21.2 %collective-permute-start.9 = (bf16[160,1152]{1,0:T(8,128)(2,1)S(1)}, bf16[160,1152]{1,0:T(8,128)(2,1)S(1)}, u32[]{:S(2)}, u32[]{:S(2)}) collective-permute-start(bf16[160,1152]{1,0:T(8,128)(2,1)S(1)} %get-tuple-element.35), channel_id=1, source_target_pairs={{0,2},{1,3},{2,4},{3,5},{4,6},{5,7},{6,8},{7,9},{8,10},{9,11},{10,... | collective-permute-start | bytes 1105928 | tf_op jit(solution)/shard_map/ppermute | solution.py:186
  23.2 3.2 %collective-permute-start.5 = (bf16[64,1152]{1,0:T(8,128)(2,1)S(1)}, bf16[64,1152]{1,0:T(8,128)(2,1)S(1)}, u32[]{:S(2)}, u32[]{:S(2)}) collective-permute-start(bf16[64,1152]{1,0:T(8,128)(2,1)S(1)} %get-tuple-element.26), channel_id=1, source_target_pairs={{0,1},{1,0},{2,3},{3,2},{4,5},{5,4},{6,7},{7,6},{8,9},{9,8},{10,11... | collective-permute-start | bytes 442376 | tf_op jit(solution)/shard_map/ppermute | solution.py:189
  23.3 3.3 %collective-permute-start.6 = (bf16[64,1152]{1,0:T(8,128)(2,1)S(1)}, bf16[64,1152]{1,0:T(8,128)(2,1)S(1)}, u32[]{:S(2)}, u32[]{:S(2)}) collective-permute-start(bf16[64,1152]{1,0:T(8,128)(2,1)S(1)} %get-tuple-element.27), channel_id=1, source_target_pairs={{0,1},{1,0},{2,3},{3,2},{4,5},{5,4},{6,7},{7,6},{8,9},{9,8},{10,11... | collective-permute-start | bytes 442376 | tf_op jit(solution)/shard_map/ppermute | solution.py:189
  23.8 7.5 %collective-permute-start.10 = (bf16[96,1152]{1,0:T(8,128)(2,1)S(1)}, bf16[96,1152]{1,0:T(8,128)(2,1)S(1)}, u32[]{:S(2)}, u32[]{:S(2)}) collective-permute-start(bf16[96,1152]{1,0:T(8,128)(2,1)S(1)} %get-tuple-element.36), channel_id=1, source_target_pairs={{0,2},{1,3},{2,4},{3,5},{4,6},{5,7},{6,8},{7,9},{8,10},{9,11},{10,... | collective-permute-start | bytes 663560 | tf_op jit(solution)/shard_map/ppermute | solution.py:229
  25.1 9.4 %collective-permute-start.12 = (bf16[96,1152]{1,0:T(8,128)(2,1)S(1)}, bf16[96,1152]{1,0:T(8,128)(2,1)S(1)}, u32[]{:S(2)}, u32[]{:S(2)}) collective-permute-start(bf16[96,1152]{1,0:T(8,128)(2,1)S(1)} %collective-permute-done.11), channel_id=1, source_target_pairs={{4,0}} | collective-permute-start | bytes 663560 | tf_op jit(solution)/shard_map/ppermute | solution.py:227
  26.4 2.4 %collective-permute-start.7 = (bf16[64,1152]{1,0:T(8,128)(2,1)S(1)}, bf16[64,1152]{1,0:T(8,128)(2,1)S(1)}, u32[]{:S(2)}, u32[]{:S(2)}) collective-permute-start(bf16[64,1152]{1,0:T(8,128)(2,1)S(1)} %get-tuple-element.28), channel_id=1, source_target_pairs={{0,1},{1,0},{2,3},{3,2},{4,5},{5,4},{6,7},{7,6},{8,9},{9,8},{10,11... | collective-permute-start | bytes 442376 | tf_op jit(solution)/shard_map/ppermute | solution.py:189
  26.6 2.3 %collective-permute-start.8 = (bf16[64,1152]{1,0:T(8,128)(2,1)S(1)}, bf16[64,1152]{1,0:T(8,128)(2,1)S(1)}, u32[]{:S(2)}, u32[]{:S(2)}) collective-permute-start(bf16[64,1152]{1,0:T(8,128)(2,1)S(1)} %get-tuple-element.29), channel_id=1, source_target_pairs={{0,1},{1,0},{2,3},{3,2},{4,5},{5,4},{6,7},{7,6},{8,9},{9,8},{10,11... | collective-permute-start | bytes 442376 | tf_op jit(solution)/shard_map/ppermute | solution.py:189

commit v17 on v15

--- a/solution.py
+++ b/solution.py
@@ -1,5 +1,3 @@
-import functools
-
 import jax
 import jax.numpy as jnp
 from jax import lax
@@ -58,14 +56,18 @@
         copy.wait()
 
 
-def add_kernel(start, chunks, count, late, *refs):
-    arrived, (out, staged, sems) = refs[:count], refs[-3:]
-    step = staged.shape[0] // chunks
+def add_kernel(first, second, turned, late, out, staged, sems):
+    cut = first.shape[0]
     copies = []
-    for k in range(chunks):
-        here, there = pl.ds(k * step, step), pl.ds(start + k * step, step)
-        staged[here, :] = sum((part[here, :].astype(staged.dtype) for part in arrived), late[there, :])
-        copies.append(pltpu.make_async_copy(staged.at[here], out.at[there], sems.at[k]))
+    for k in range(out.shape[0] // STEP):
+        rows = pl.ds(k * STEP, STEP)
+        if k * STEP < cut:
+            arrived = first[rows, :].astype(staged.dtype)
+        else:
+            part = pl.ds(k * STEP - cut, STEP)
+            arrived = second[part, :].astype(staged.dtype) + turned[part, :].astype(staged.dtype)
+        staged[rows, :] = arrived + late[rows, :]
+        copies.append(pltpu.make_async_copy(staged.at[rows], out.at[rows], sems.at[k]))
         copies[-1].start()
     for copy in copies:
         copy.wait()
@@ -155,20 +157,6 @@
     )(*scalars, *operands)
 
 
-def add_part(name, start, chunks, late, arrived, *before):
-    return pl.pallas_call(
-        functools.partial(add_kernel, start, chunks, len(arrived)),
-        out_shape=jax.ShapeDtypeStruct(late.shape, late.dtype),
-        in_specs=[VMEM] * (1 + len(arrived)) + [HBM] * len(before),
-        out_specs=HBM,
-        scratch_shapes=[pltpu.VMEM(arrived[0].shape, late.dtype), pltpu.SemaphoreType.DMA((chunks,))],
-        input_output_aliases={1 + len(arrived): 0} if before else {},
-        compiler_params=pltpu.CompilerParams(vmem_limit_bytes=16 * 1024 * 1024),
-        cost_estimate=pl.CostEstimate(flops=0, bytes_accessed=0, transcendentals=0),
-        name=name,
-    )(late, *arrived, *before)
-
-
 def body(image_emb, text_emb, text_accum, pair_ids, log_scale, bias):
     count = lax.axis_size(AXES)
     rows, width = image_emb.shape
@@ -204,7 +192,7 @@
     mate_ids = across(ids)
     both_ids = ahead(jnp.concatenate([ids, mate_ids]))
 
-    cut = rows - rows // 4
+    cut = rows - rows * 3 // 16
     out_a, out_b, image_sum, loss = pl.pallas_call(
         own_kernel,
         out_shape=[
@@ -243,8 +231,16 @@
         (flags, params), ids, mate_ids, both_ids, image_a, image_b, near_a, near_b, image_sum, loss,
     )
     late, image_grad = lax.optimization_barrier((late, image_grad))
-    text_grad = add_part("add_a", 0, cut // STEP, late, (arrived_a,))
-    text_grad = add_part("add_b", cut, (rows - cut) // STEP, late, (arrived_b, turned), text_grad)
+    text_grad = pl.pallas_call(
+        add_kernel,
+        out_shape=jax.ShapeDtypeStruct((rows, width), f32),
+        in_specs=[VMEM] * 4,
+        out_specs=HBM,
+        scratch_shapes=[pltpu.VMEM((rows, width), f32), pltpu.SemaphoreType.DMA((rows // STEP,))],
+        compiler_params=pltpu.CompilerParams(vmem_limit_bytes=16 * 1024 * 1024),
+        cost_estimate=pl.CostEstimate(flops=0, bytes_accessed=0, transcendentals=0),
+        name="add",
+    )(arrived_a, arrived_b, turned, late)
     return (loss.reshape(rows), image_grad, text_grad)
 
 

time: 36.8 us -> 36.4 us (0.989)
  Pallas kernels: 11 us -> 10.4 us
    ppermute x1, waiting for transfers between devices: 0.01 us -> 2.7 us  [body(): turned = lax.ppermute(to_turn, AXES, [(turn, 0)])]
    ppermute x3, waiting for transfers between devices: 11.4 us -> 8.97 us  [ahead(): return lax.ppermute(value, AXES, skip)]
    pallas_call x2 -> x1, Pallas kernels: 1.77 us -> 1.15 us  [body(): pl.pallas_call(add_kernel, out_shape=jax.ShapeDtypeStruct((rows, width),...]
  transfers between devices with their start and end apart: 11 -> 11, of which waited for: 3 -> 4; matrix products, arithmetic and copies ran while one was open for 0% -> 0% of each run, Pallas kernels for 28% -> 26%
where the time goes in v17:
time: 36.4 us; the launch traced here: 36.1 us
  waiting for transfers between devices  11.8 us (32%)
  starting transfers between devices  10.5 us (29%)
  Pallas kernels  10.4 us (29%)
  between operations  2.04 us (6%)
  local copies, waits for them, and re-layouts  1.27 us (3%)
    ppermute x3, waiting for transfers between devices, ahead(): return lax.ppermute(value, AXES, skip)  8.97 us
    ppermute x3, starting transfers between devices, ahead(): return lax.ppermute(value, AXES, skip)  6.05 us
    pallas_call x5, Pallas kernels, call(): pl.pallas_call(kernel, out_shape=[jax.ShapeDtypeStruct(s, d) for s, d in...  4.38 us
    pallas_call x1, Pallas kernels, body(): pl.pallas_call(own_kernel, out_shape=[jax.ShapeDtypeStruct((cut, width),...  3.82 us
    ppermute x1, waiting for transfers between devices, body(): turned = lax.ppermute(to_turn, AXES, [(turn, 0)])  2.7 us
    ppermute x1, starting transfers between devices, body(): turned = lax.ppermute(to_turn, AXES, [(turn, 0)])  1.29 us
    ppermute x1, starting transfers between devices, body(): arrived_b = lax.ppermute(out_b, AXES, skip[:-2] + skip[-1:])  1.28 us
    unnamed x4, local copies, waits for them, and re-layouts  1.27 us
  transfers between devices with their start and end apart: 11, of which 4 were waited for; matrix products, arithmetic and copies ran while one was open for 0% of the time, Pallas kernels for 26%

profile of v17, /device:TPU:0, one launch (start us, length us, event | category | flops | bytes accessed | tf_op | source)
XLA Modules:
  0.0 36.1 jit_solution(2311345803668253904)
XLA Ops:
  0.6 0.0 copy-start
  0.6 1.3 %copy-done = f32[256,1152]{1,0:T(8,128)S(1)} copy-done((f32[256,1152]{1,0:T(8,128)S(1)}, f32[256,1152]{1,0:T(8,128)}, u32[]{:S(2)}) %copy-start) | copy-done | bytes 1179672
  1.9 0.0 copy-start.1
  1.9 0.1 cast.1.text
  2.0 3.0 %collective-permute-start.5 = (bf16[256,1152]{1,0:T(8,128)(2,1)S(1)}, bf16[256,1152]{1,0:T(8,128)(2,1)S(1)}, u32[]{:S(2)}, u32[]{:S(2)}) collective-permute-start(bf16[256,1152]{1,0:T(8,128)(2,1)S(1)} %cast.1.text), channel_id=1, source_target_pairs={{0,2},{1,3},{2,4},{3,5},{4,6},{5,7},{6,8},{7,9},{8,10},{9,11},{10,... | collective-permute-start | bytes 1769480 | tf_op jit(solution)/shard_map/ppermute | solution.py:173
  5.0 1.1 %load.1 = (bf16[128,1152]{1,0:T(8,128)(2,1)S(1)}, bf16[128,1152]{1,0:T(8,128)(2,1)S(1)}) custom-call(bf16[256,1152]{1,0:T(8,128)(2,1)S(1)} %cast.1.text, bf16[256,1152]{1,0:T(8,128)(2,1)} %image.1), custom_call_target="tpu_custom_call" | custom-call | tf_op jit(solution)/shard_map/load/pallas_call | solution.py:181
  6.1 0.1 collective-permute-start.1
  6.1 0.5 %collective-permute-start.2 = (bf16[128,1152]{1,0:T(8,128)(2,1)S(1)}, bf16[128,1152]{1,0:T(8,128)(2,1)S(1)}, u32[]{:S(2)}, u32[]{:S(2)}) collective-permute-start(bf16[128,1152]{1,0:T(8,128)(2,1)S(1)} %get-tuple-element.19.image_b), channel_id=1, source_target_pairs={{0,1},{1,0},{2,3},{3,2},{4,5},{5,4},{6,7},{7,6},{8,9},{9,8},{10,11... | collective-permute-start | bytes 884744 | tf_op jit(solution)/shard_map/ppermute | solution.py:176
  6.6 0.0 copy-done.1
  6.6 0.1 collective-permute-start
  8.0 0.1 collective-permute-done.mate_ids
  8.1 1.5 %collective-permute-start.3 = (s32[2,256]{1,0:T(2,128)S(1)}, s32[2,256]{1,0:T(2,128)S(1)}, u32[]{:S(2)}, u32[]{:S(2)}) collective-permute-start(s32[2,256]{1,0:T(2,128)S(1)} %pad_add_fusion), channel_id=1, source_target_pairs={{0,2},{1,3},{2,4},{3,5},{4,6},{5,7},{6,8},{7,9},{8,10},{9,11},{10,... | collective-permute-start | bytes 6152 | tf_op jit(solution)/shard_map/ppermute | solution.py:173
  9.6 0.1 pad_maximum_fusion.params
  9.7 0.0 collective-permute-done.1.mate_a
  9.7 0.0 collective-permute-done.2.mate_b
  9.7 3.8 %own.1 = (bf16[208,1152]{1,0:T(8,128)(2,1)S(1)}, bf16[48,1152]{1,0:T(8,128)(2,1)S(1)}, f32[256,1152]{1,0:T(8,128)S(1)}, f32[1,256]{1,0:T(1,128)S(1)}) custom-call(s32[1]{0:T(128)} %bitcast.flags, f32[2]{0:T(128)S(1)} %pad_maximum_fusion.params, s32[1,256]{1,0:T(1,128)S(1)} %bitcast.5, s32[1,256]{1,0:T(1,128)S(1)} %collective-permute-done.mate_ids, ...), custom_call_target="tpu_custom_call" | custom-call | tf_op jit(solution)/shard_map/own/pallas_call | solution.py:196
  13.5 0.7 %collective-permute-start.4 = (bf16[48,1152]{1,0:T(8,128)(2,1)S(1)}, bf16[48,1152]{1,0:T(8,128)(2,1)S(1)}, u32[]{:S(2)}, u32[]{:S(2)}) collective-permute-start(bf16[48,1152]{1,0:T(8,128)(2,1)S(1)} %get-tuple-element.21), channel_id=1, source_target_pairs={{30,4}} | collective-permute-start | bytes 331784 | tf_op jit(solution)/shard_map/ppermute | solution.py:213
  14.2 1.6 %collective-permute-start.8 = (bf16[208,1152]{1,0:T(8,128)(2,1)S(1)}, bf16[208,1152]{1,0:T(8,128)(2,1)S(1)}, u32[]{:S(2)}, u32[]{:S(2)}) collective-permute-start(bf16[208,1152]{1,0:T(8,128)(2,1)S(1)} %get-tuple-element.31), channel_id=1, source_target_pairs={{0,2},{1,3},{2,4},{3,5},{4,6},{5,7},{6,8},{7,9},{8,10},{9,11},{10,... | collective-permute-start | bytes 1437704 | tf_op jit(solution)/shard_map/ppermute | solution.py:173
  15.8 7.4 %collective-permute-done.3.both_ids = s32[2,256]{1,0:T(2,128)S(1)} collective-permute-done((s32[2,256]{1,0:T(2,128)S(1)}, s32[2,256]{1,0:T(2,128)S(1)}, u32[]{:S(2)}, u32[]{:S(2)}) %collective-permute-start.3) | collective-permute-done | bytes 2080 | tf_op jit(solution)/shard_map/ppermute | solution.py:173
  23.2 0.0 collective-permute-done.4.leg
  23.2 0.0 collective-permute-done.5.far
  23.2 0.1 relay.1
  23.2 0.1 collective-permute-start.6
  23.3 0.5 %collective-permute-start.7 = (bf16[64,1152]{1,0:T(8,128)(2,1)S(1)}, bf16[64,1152]{1,0:T(8,128)(2,1)S(1)}, u32[]{:S(2)}, u32[]{:S(2)}) collective-permute-start(bf16[64,1152]{1,0:T(8,128)(2,1)S(1)} %get-tuple-element.23), channel_id=1, source_target_pairs={{0,1},{1,0},{2,3},{3,2},{4,5},{5,4},{6,7},{7,6},{8,9},{9,8},{10,11... | collective-permute-start | bytes 442376 | tf_op jit(solution)/shard_map/ppermute | solution.py:176
  23.8 1.3 %collective-permute-start.9 = (bf16[48,1152]{1,0:T(8,128)(2,1)S(1)}, bf16[48,1152]{1,0:T(8,128)(2,1)S(1)}, u32[]{:S(2)}, u32[]{:S(2)}) collective-permute-start(bf16[48,1152]{1,0:T(8,128)(2,1)S(1)} %get-tuple-element.21), channel_id=1, source_target_pairs={{0,2},{1,3},{2,4},{3,5},{4,6},{5,7},{6,8},{7,9},{8,10},{9,11},{10,... | collective-permute-start | bytes 331784 | tf_op jit(solution)/shard_map/ppermute | solution.py:216
  25.1 1.3 %collective-permute-start.10 = (bf16[48,1152]{1,0:T(8,128)(2,1)S(1)}, bf16[48,1152]{1,0:T(8,128)(2,1)S(1)}, u32[]{:S(2)}, u32[]{:S(2)}) collective-permute-start(bf16[48,1152]{1,0:T(8,128)(2,1)S(1)} %collective-permute-done.4.leg), channel_id=1, source_target_pairs={{4,0}} | collective-permute-start | bytes 331784 | tf_op jit(solution)/shard_map/ppermute | solution.py:214
  26.4 1.8 %far.1 = (f32[256,1152]{1,0:T(8,128)S(1)}, f32[256,1152]{1,0:T(8,128)S(1)}, f32[1,256]{1,0:T(1,128)S(1)}) custom-call(s32[1]{0:T(128)} %bitcast.flags, f32[2]{0:T(128)S(1)} %pad_maximum_fusion.params, s32[1,256]{1,0:T(1,128)S(1)} %bitcast.6, s32[1,256]{1,0:T(1,128)S(1)} %collective-permute-done.mate_ids, s32[2,256]{1,0:T(2,128)S(1)} %ids.1.token.both_ids, ...), custom_call_target="tpu_custom_call" | custom-call | tf_op jit(solution)/shard_map/far/pallas_call | solution.py:149
  28.2 0.0 collective-permute-done.7.near_b
  28.2 0.0 collective-permute-done.6.near_a
  28.3 2.4 %near.1 = (bf16[256,1152]{1,0:T(8,128)(2,1)}, f32[1,256]{1,0:T(1,128)}) custom-call(s32[1]{0:T(128)} %bitcast.flags, f32[2]{0:T(128)S(1)} %pad_maximum_fusion.params, s32[1,256]{1,0:T(1,128)S(1)} %bitcast.7, s32[1,256]{1,0:T(1,128)S(1)} %collective-permute-done.mate_ids, s32[2,256]{1,0:T(2,128)S(1)} %ids.1.token.both_ids, ...), custom_call_target="tpu_custom_call" | custom-call | tf_op jit(solution)/shard_map/near/pallas_call | solution.py:149
  30.7 0.0 collective-permute-done.9.second
  30.7 2.7 %collective-permute-done.10.turned = bf16[48,1152]{1,0:T(8,128)(2,1)S(1)} collective-permute-done((bf16[48,1152]{1,0:T(8,128)(2,1)S(1)}, bf16[48,1152]{1,0:T(8,128)(2,1)S(1)}, u32[]{:S(2)}, u32[]{:S(2)}) %collective-permute-start.10) | collective-permute-done | bytes 110624 | tf_op jit(solution)/shard_map/ppermute | solution.py:214
  33.4 1.6 %collective-permute-done.8.first = bf16[208,1152]{1,0:T(8,128)(2,1)S(1)} collective-permute-done((bf16[208,1152]{1,0:T(8,128)(2,1)S(1)}, bf16[208,1152]{1,0:T(8,128)(2,1)S(1)}, u32[]{:S(2)}, u32[]{:S(2)}) %collective-permute-start.8) | collective-permute-done | bytes 479264 | tf_op jit(solution)/shard_map/ppermute | solution.py:173
  35.0 1.2 %add.8 = f32[256,1152]{1,0:T(8,128)} custom-call(bf16[208,1152]{1,0:T(8,128)(2,1)S(1)} %collective-permute-done.8.first, bf16[48,1152]{1,0:T(8,128)(2,1)S(1)} %collective-permute-done.9.second, bf16[48,1152]{1,0:T(8,128)(2,1)S(1)} %collective-permute-done.10.turned, f32[256,1152]{1,0:T(8,128)S(1)} %get-tuple-element.32.late), custom_call_target="tpu_custom_call" | custom-call | tf_op jit(solution)/shard_map/add/pallas_call | solution.py:234
  (2 shorter events, 0.0 us)
Async XLA Ops:
  0.6 1.3 %copy-start = (f32[256,1152]{1,0:T(8,128)S(1)}, f32[256,1152]{1,0:T(8,128)}, u32[]{:S(2)}) copy-start(f32[256,1152]{1,0:T(8,128)} %text.1) | copy-start | bytes 3538948
  1.9 4.7 %copy-start.1 = (s32[256]{0:T(256)S(1)}, s32[256]{0:T(256)}, u32[]{:S(2)}) copy-start(s32[256]{0:T(256)} %param.9) | copy-start | bytes 3076
  2.0 21.2 %collective-permute-start.5 = (bf16[256,1152]{1,0:T(8,128)(2,1)S(1)}, bf16[256,1152]{1,0:T(8,128)(2,1)S(1)}, u32[]{:S(2)}, u32[]{:S(2)}) collective-permute-start(bf16[256,1152]{1,0:T(8,128)(2,1)S(1)} %cast.1.text), channel_id=1, source_target_pairs={{0,2},{1,3},{2,4},{3,5},{4,6},{5,7},{6,8},{7,9},{8,10},{9,11},{10,... | collective-permute-start | bytes 1769480 | tf_op jit(solution)/shard_map/ppermute | solution.py:173
  6.1 3.6 %collective-permute-start.1 = (bf16[128,1152]{1,0:T(8,128)(2,1)S(1)}, bf16[128,1152]{1,0:T(8,128)(2,1)S(1)}, u32[]{:S(2)}, u32[]{:S(2)}) collective-permute-start(bf16[128,1152]{1,0:T(8,128)(2,1)S(1)} %get-tuple-element.18.image_a), channel_id=1, source_target_pairs={{0,1},{1,0},{2,3},{3,2},{4,5},{5,4},{6,7},{7,6},{8,9},{9,8},{10,11... | collective-permute-start | bytes 884744 | tf_op jit(solution)/shard_map/ppermute | solution.py:176
  6.1 3.5 %collective-permute-start.2 = (bf16[128,1152]{1,0:T(8,128)(2,1)S(1)}, bf16[128,1152]{1,0:T(8,128)(2,1)S(1)}, u32[]{:S(2)}, u32[]{:S(2)}) collective-permute-start(bf16[128,1152]{1,0:T(8,128)(2,1)S(1)} %get-tuple-element.19.image_b), channel_id=1, source_target_pairs={{0,1},{1,0},{2,3},{3,2},{4,5},{5,4},{6,7},{7,6},{8,9},{9,8},{10,11... | collective-permute-start | bytes 884744 | tf_op jit(solution)/shard_map/ppermute | solution.py:176
  6.6 1.5 %collective-permute-start = (s32[1,256]{1,0:T(1,128)S(1)}, s32[1,256]{1,0:T(1,128)S(1)}, u32[]{:S(2)}, u32[]{:S(2)}) collective-permute-start(s32[1,256]{1,0:T(1,128)S(1)} %bitcast.3), channel_id=1, source_target_pairs={{0,1},{1,0},{2,3},{3,2},{4,5},{5,4},{6,7},{7,6},{8,9},{9,8},{10,11... | collective-permute-start | bytes 3080 | tf_op jit(solution)/shard_map/ppermute | solution.py:176
  8.1 15.0 %collective-permute-start.3 = (s32[2,256]{1,0:T(2,128)S(1)}, s32[2,256]{1,0:T(2,128)S(1)}, u32[]{:S(2)}, u32[]{:S(2)}) collective-permute-start(s32[2,256]{1,0:T(2,128)S(1)} %pad_add_fusion), channel_id=1, source_target_pairs={{0,2},{1,3},{2,4},{3,5},{4,6},{5,7},{6,8},{7,9},{8,10},{9,11},{10,... | collective-permute-start | bytes 6152 | tf_op jit(solution)/shard_map/ppermute | solution.py:173
  13.5 9.6 %collective-permute-start.4 = (bf16[48,1152]{1,0:T(8,128)(2,1)S(1)}, bf16[48,1152]{1,0:T(8,128)(2,1)S(1)}, u32[]{:S(2)}, u32[]{:S(2)}) collective-permute-start(bf16[48,1152]{1,0:T(8,128)(2,1)S(1)} %get-tuple-element.21), channel_id=1, source_target_pairs={{30,4}} | collective-permute-start | bytes 331784 | tf_op jit(solution)/shard_map/ppermute | solution.py:213
  14.2 20.8 %collective-permute-start.8 = (bf16[208,1152]{1,0:T(8,128)(2,1)S(1)}, bf16[208,1152]{1,0:T(8,128)(2,1)S(1)}, u32[]{:S(2)}, u32[]{:S(2)}) collective-permute-start(bf16[208,1152]{1,0:T(8,128)(2,1)S(1)} %get-tuple-element.31), channel_id=1, source_target_pairs={{0,2},{1,3},{2,4},{3,5},{4,6},{5,7},{6,8},{7,9},{8,10},{9,11},{10,... | collective-permute-start | bytes 1437704 | tf_op jit(solution)/shard_map/ppermute | solution.py:173
  23.2 5.0 %collective-permute-start.6 = (bf16[192,1152]{1,0:T(8,128)(2,1)S(1)}, bf16[192,1152]{1,0:T(8,128)(2,1)S(1)}, u32[]{:S(2)}, u32[]{:S(2)}) collective-permute-start(bf16[192,1152]{1,0:T(8,128)(2,1)S(1)} %get-tuple-element.22), channel_id=1, source_target_pairs={{0,1},{1,0},{2,3},{3,2},{4,5},{5,4},{6,7},{7,6},{8,9},{9,8},{10,11... | collective-permute-start | bytes 1327112 | tf_op jit(solution)/shard_map/ppermute | solution.py:176
  23.3 4.9 %collective-permute-start.7 = (bf16[64,1152]{1,0:T(8,128)(2,1)S(1)}, bf16[64,1152]{1,0:T(8,128)(2,1)S(1)}, u32[]{:S(2)}, u32[]{:S(2)}) collective-permute-start(bf16[64,1152]{1,0:T(8,128)(2,1)S(1)} %get-tuple-element.23), channel_id=1, source_target_pairs={{0,1},{1,0},{2,3},{3,2},{4,5},{5,4},{6,7},{7,6},{8,9},{9,8},{10,11... | collective-permute-start | bytes 442376 | tf_op jit(solution)/shard_map/ppermute | solution.py:176
  23.8 6.9 %collective-permute-start.9 = (bf16[48,1152]{1,0:T(8,128)(2,1)S(1)}, bf16[48,1152]{1,0:T(8,128)(2,1)S(1)}, u32[]{:S(2)}, u32[]{:S(2)}) collective-permute-start(bf16[48,1152]{1,0:T(8,128)(2,1)S(1)} %get-tuple-element.21), channel_id=1, source_target_pairs={{0,2},{1,3},{2,4},{3,5},{4,6},{5,7},{6,8},{7,9},{8,10},{9,11},{10,... | collective-permute-start | bytes 331784 | tf_op jit(solution)/shard_map/ppermute | solution.py:216
  25.1 8.3 %collective-permute-start.10 = (bf16[48,1152]{1,0:T(8,128)(2,1)S(1)}, bf16[48,1152]{1,0:T(8,128)(2,1)S(1)}, u32[]{:S(2)}, u32[]{:S(2)}) collective-permute-start(bf16[48,1152]{1,0:T(8,128)(2,1)S(1)} %collective-permute-done.4.leg), channel_id=1, source_target_pairs={{4,0}} | collective-permute-start | bytes 331784 | tf_op jit(solution)/shard_map/ppermute | solution.py:214

commit v18 on v13

--- a/solution.py
+++ b/solution.py
@@ -99,7 +99,11 @@
     image_sum[...] = dot(low(coef), text[...], (1, 0))
 
 
-def relay_kernel(flags, token, text, far, out_a, out_b):
+def ids_kernel(token, both_ids, out):
+    out[...] = both_ids[...]
+
+
+def relay_kernel(flags, token, before, text, far, out_a, out_b):
     cut = out_a.shape[0]
 
     def fill(source):
@@ -217,11 +221,15 @@
         name="own",
     )(flags, params, ids, mate_ids, image_a, image_b, mate_a, mate_b, text,
       pltpu.with_memory_space_constraint(text_accum, pltpu.HBM))
-    arrived_a, arrived_b = ahead(out_a), ahead(out_b)
-
+    crossed = [(i, target ^ 1) for i, target in skip]
+    arrived_a = ahead(out_a)
+    mate_rows = across(out_b)
+    arrived_b = lax.ppermute(mate_rows, AXES, crossed)
+
+    (both_ids,) = call(ids_kernel, "ids", [((2, rows), jnp.int32)], (), loss, both_ids, flops=2 << 30)
     passed_a, passed_b = call(
         relay_kernel, "relay", [((cut - 16, width), bf16), ((rows - cut + 16, width), bf16)],
-        (flags,), both_ids, text, far, flops=1 << 30,
+        (flags,), both_ids, mate_rows, text, far, flops=1 << 30,
     )
     near_a, near_b = across(passed_a), across(passed_b)
     late, image_sum, loss = call(

time: 35.9 us -> 35.4 us (0.986)
  waiting for transfers between devices: 14 us -> 13.4 us
    ppermute x4 -> x3, waiting for transfers between devices: 13.9 us -> 13.3 us  [ahead(): return lax.ppermute(value, AXES, skip)]
    ppermute x5 -> x6, starting transfers between devices: 1.21 us -> 1.29 us  [across(): return lax.ppermute(value, AXES, swap)]
    pallas_call x4 -> x5, Pallas kernels: 4.36 us -> 4.37 us  [call(): pl.pallas_call(kernel, out_shape=[jax.ShapeDtypeStruct(s, d) for s, d in...]
    ppermute x4 -> x3, starting transfers between devices: 6.05 us -> 6.05 us  [ahead(): return lax.ppermute(value, AXES, skip)]
  transfers between devices with their start and end apart: 9 -> 10, of which waited for: 4 -> 3; matrix products, arithmetic and copies ran while one was open for 0% -> 0% of each run, Pallas kernels for 29% -> 29%
where the time goes in v18:
time: 35.4 us; the launch traced here: 35.2 us
  waiting for transfers between devices  13.4 us (38%)
  Pallas kernels  11 us (31%)
  starting transfers between devices  7.34 us (21%)
  between operations  2.04 us (6%)
  local copies, waits for them, and re-layouts  1.27 us (4%)
    ppermute x3, waiting for transfers between devices, ahead(): return lax.ppermute(value, AXES, skip)  13.3 us
    ppermute x3, starting transfers between devices, ahead(): return lax.ppermute(value, AXES, skip)  6.05 us
    pallas_call x5, Pallas kernels, call(): pl.pallas_call(kernel, out_shape=[jax.ShapeDtypeStruct(s, d) for s, d in...  4.37 us
    pallas_call x1, Pallas kernels, body(): pl.pallas_call(own_kernel, out_shape=[jax.ShapeDtypeStruct((cut, width),...  3.82 us
    pallas_call x2, Pallas kernels, add_part(): pl.pallas_call(functools.partial(add_kernel, start, chunks), out_shape=ja...  1.77 us
    ppermute x6, starting transfers between devices, across(): return lax.ppermute(value, AXES, swap)  1.29 us
    unnamed x4, local copies, waits for them, and re-layouts  1.27 us
    pallas_call x1, Pallas kernels, body(): pl.pallas_call(load_kernel, out_shape=[jax.ShapeDtypeStruct((n, width), b...  1.07 us
  transfers between devices with their start and end apart: 10, of which 3 were waited for; matrix products, arithmetic and copies ran while one was open for 0% of the time, Pallas kernels for 29%

profile of v18, /device:TPU:0, one launch (start us, length us, event | category | flops | bytes accessed | tf_op | source)
XLA Modules:
  0.0 35.2 jit_solution(11607124377463106552)
XLA Ops:
  0.6 0.0 copy-start
  0.6 1.3 %copy-done = f32[256,1152]{1,0:T(8,128)S(1)} copy-done((f32[256,1152]{1,0:T(8,128)S(1)}, f32[256,1152]{1,0:T(8,128)}, u32[]{:S(2)}) %copy-start) | copy-done | bytes 1179672
  1.9 0.0 copy-start.1
  1.9 0.1 cast.1.text
  2.0 3.0 %collective-permute-start.5 = (bf16[256,1152]{1,0:T(8,128)(2,1)S(1)}, bf16[256,1152]{1,0:T(8,128)(2,1)S(1)}, u32[]{:S(2)}, u32[]{:S(2)}) collective-permute-start(bf16[256,1152]{1,0:T(8,128)(2,1)S(1)} %cast.1.text), channel_id=1, source_target_pairs={{0,2},{1,3},{2,4},{3,5},{4,6},{5,7},{6,8},{7,9},{8,10},{9,11},{10,... | collective-permute-start | bytes 1769480 | tf_op jit(solution)/shard_map/ppermute | solution.py:185
  5.0 1.1 %load.1 = (bf16[128,1152]{1,0:T(8,128)(2,1)S(1)}, bf16[128,1152]{1,0:T(8,128)(2,1)S(1)}) custom-call(bf16[256,1152]{1,0:T(8,128)(2,1)S(1)} %cast.1.text, bf16[256,1152]{1,0:T(8,128)(2,1)} %image.1), custom_call_target="tpu_custom_call" | custom-call | tf_op jit(solution)/shard_map/load/pallas_call | solution.py:193
  6.1 0.1 collective-permute-start.1
  6.1 0.5 %collective-permute-start.2 = (bf16[128,1152]{1,0:T(8,128)(2,1)S(1)}, bf16[128,1152]{1,0:T(8,128)(2,1)S(1)}, u32[]{:S(2)}, u32[]{:S(2)}) collective-permute-start(bf16[128,1152]{1,0:T(8,128)(2,1)S(1)} %get-tuple-element.19.image_b), channel_id=1, source_target_pairs={{0,1},{1,0},{2,3},{3,2},{4,5},{5,4},{6,7},{7,6},{8,9},{9,8},{10,11... | collective-permute-start | bytes 884744 | tf_op jit(solution)/shard_map/ppermute | solution.py:188
  6.6 0.0 copy-done.1
  6.6 0.1 collective-permute-start
  8.0 0.1 collective-permute-done.mate_ids
  8.1 1.5 %collective-permute-start.3 = (s32[2,256]{1,0:T(2,128)S(1)}, s32[2,256]{1,0:T(2,128)S(1)}, u32[]{:S(2)}, u32[]{:S(2)}) collective-permute-start(s32[2,256]{1,0:T(2,128)S(1)} %pad_add_fusion), channel_id=1, source_target_pairs={{0,2},{1,3},{2,4},{3,5},{4,6},{5,7},{6,8},{7,9},{8,10},{9,11},{10,... | collective-permute-start | bytes 6152 | tf_op jit(solution)/shard_map/ppermute | solution.py:185
  9.6 0.1 pad_maximum_fusion.params
  9.7 0.0 collective-permute-done.1.mate_a
  9.7 0.0 collective-permute-done.2.mate_b
  9.7 3.8 %own.1 = (bf16[208,1152]{1,0:T(8,128)(2,1)S(1)}, bf16[48,1152]{1,0:T(8,128)(2,1)S(1)}, f32[256,1152]{1,0:T(8,128)S(1)}, f32[1,256]{1,0:T(1,128)S(1)}) custom-call(s32[1]{0:T(128)} %bitcast.flags, f32[2]{0:T(128)S(1)} %pad_maximum_fusion.params, s32[1,256]{1,0:T(1,128)S(1)} %bitcast.5, s32[1,256]{1,0:T(1,128)S(1)} %collective-permute-done.mate_ids, ...), custom_call_target="tpu_custom_call" | custom-call | tf_op jit(solution)/shard_map/own/pallas_call | solution.py:208
  13.5 0.1 collective-permute-start.4
  13.6 1.6 %collective-permute-start.9 = (bf16[208,1152]{1,0:T(8,128)(2,1)S(1)}, bf16[208,1152]{1,0:T(8,128)(2,1)S(1)}, u32[]{:S(2)}, u32[]{:S(2)}) collective-permute-start(bf16[208,1152]{1,0:T(8,128)(2,1)S(1)} %get-tuple-element.32), channel_id=1, source_target_pairs={{0,2},{1,3},{2,4},{3,5},{4,6},{5,7},{6,8},{7,9},{8,10},{9,11},{10,... | collective-permute-start | bytes 1437704 | tf_op jit(solution)/shard_map/ppermute | solution.py:185
  15.2 8.0 %collective-permute-done.3.both_ids = s32[2,256]{1,0:T(2,128)S(1)} collective-permute-done((s32[2,256]{1,0:T(2,128)S(1)}, s32[2,256]{1,0:T(2,128)S(1)}, u32[]{:S(2)}, u32[]{:S(2)}) %collective-permute-start.3) | collective-permute-done | bytes 2080 | tf_op jit(solution)/shard_map/ppermute | solution.py:185
  23.2 0.0 collective-permute-done.4.before
  23.2 0.0 collective-permute-done.5.far
  23.2 0.1 relay.1
  23.2 0.1 collective-permute-start.6
  23.3 0.5 %collective-permute-start.7 = (bf16[64,1152]{1,0:T(8,128)(2,1)S(1)}, bf16[64,1152]{1,0:T(8,128)(2,1)S(1)}, u32[]{:S(2)}, u32[]{:S(2)}) collective-permute-start(bf16[64,1152]{1,0:T(8,128)(2,1)S(1)} %get-tuple-element.23), channel_id=1, source_target_pairs={{0,1},{1,0},{2,3},{3,2},{4,5},{5,4},{6,7},{7,6},{8,9},{9,8},{10,11... | collective-permute-start | bytes 442376 | tf_op jit(solution)/shard_map/ppermute | solution.py:188
  23.8 0.0 collective-permute-start.8
  23.8 1.8 %far.1 = (f32[256,1152]{1,0:T(8,128)S(1)}, f32[256,1152]{1,0:T(8,128)S(1)}, f32[1,256]{1,0:T(1,128)S(1)}) custom-call(s32[1]{0:T(128)} %bitcast.flags, f32[2]{0:T(128)S(1)} %pad_maximum_fusion.params, s32[1,256]{1,0:T(1,128)S(1)} %bitcast.6, s32[1,256]{1,0:T(1,128)S(1)} %collective-permute-done.mate_ids, s32[2,256]{1,0:T(2,128)S(1)} %ids.1.token.both_ids, ...), custom_call_target="tpu_custom_call" | custom-call | tf_op jit(solution)/shard_map/far/pallas_call | solution.py:147
  25.6 0.0 collective-permute-done.7.near_b
  25.7 0.0 collective-permute-done.6.near_a
  25.7 2.4 %near.1 = (bf16[256,1152]{1,0:T(8,128)(2,1)}, f32[1,256]{1,0:T(1,128)}) custom-call(s32[1]{0:T(128)} %bitcast.flags, f32[2]{0:T(128)S(1)} %pad_maximum_fusion.params, s32[1,256]{1,0:T(1,128)S(1)} %bitcast.7, s32[1,256]{1,0:T(1,128)S(1)} %collective-permute-done.mate_ids, s32[2,256]{1,0:T(2,128)S(1)} %ids.1.token.both_ids, ...), custom_call_target="tpu_custom_call" | custom-call | tf_op jit(solution)/shard_map/near/pallas_call | solution.py:147
  28.1 5.3 %collective-permute-done.9.arrived = bf16[208,1152]{1,0:T(8,128)(2,1)S(1)} collective-permute-done((bf16[208,1152]{1,0:T(8,128)(2,1)S(1)}, bf16[208,1152]{1,0:T(8,128)(2,1)S(1)}, u32[]{:S(2)}, u32[]{:S(2)}) %collective-permute-start.9) | collective-permute-done | bytes 479264 | tf_op jit(solution)/shard_map/ppermute | solution.py:185
  33.4 1.1 %add_a.1.refs_0_ = f32[256,1152]{1,0:T(8,128)} custom-call(bf16[208,1152]{1,0:T(8,128)(2,1)S(1)} %collective-permute-done.9.arrived, f32[256,1152]{1,0:T(8,128)S(1)} %get-tuple-element.31.late), custom_call_target="tpu_custom_call" | custom-call | tf_op jit(solution)/shard_map/add_a/pallas_call | solution.py:159
  34.5 0.0 collective-permute-done.8.arrived
  34.5 0.7 %add_b.1 = f32[256,1152]{1,0:T(8,128)} custom-call(bf16[48,1152]{1,0:T(8,128)(2,1)S(1)} %collective-permute-done.8.arrived, f32[256,1152]{1,0:T(8,128)S(1)} %get-tuple-element.31.late, f32[256,1152]{1,0:T(8,128)} %add_a.1.refs_0_), custom_call_target="tpu_custom_call", output_to_operand_aliasing={{}: (2, {})} | custom-call | tf_op jit(solution)/shard_map/add_b/pallas_call | solution.py:159
  (2 shorter events, 0.0 us)
Async XLA Ops:
  0.6 1.3 %copy-start = (f32[256,1152]{1,0:T(8,128)S(1)}, f32[256,1152]{1,0:T(8,128)}, u32[]{:S(2)}) copy-start(f32[256,1152]{1,0:T(8,128)} %text.1) | copy-start | bytes 3538948
  1.9 4.7 %copy-start.1 = (s32[256]{0:T(256)S(1)}, s32[256]{0:T(256)}, u32[]{:S(2)}) copy-start(s32[256]{0:T(256)} %param.9) | copy-start | bytes 3076
  2.0 21.2 %collective-permute-start.5 = (bf16[256,1152]{1,0:T(8,128)(2,1)S(1)}, bf16[256,1152]{1,0:T(8,128)(2,1)S(1)}, u32[]{:S(2)}, u32[]{:S(2)}) collective-permute-start(bf16[256,1152]{1,0:T(8,128)(2,1)S(1)} %cast.1.text), channel_id=1, source_target_pairs={{0,2},{1,3},{2,4},{3,5},{4,6},{5,7},{6,8},{7,9},{8,10},{9,11},{10,... | collective-permute-start | bytes 1769480 | tf_op jit(solution)/shard_map/ppermute | solution.py:185
  6.1 3.6 %collective-permute-start.1 = (bf16[128,1152]{1,0:T(8,128)(2,1)S(1)}, bf16[128,1152]{1,0:T(8,128)(2,1)S(1)}, u32[]{:S(2)}, u32[]{:S(2)}) collective-permute-start(bf16[128,1152]{1,0:T(8,128)(2,1)S(1)} %get-tuple-element.18.image_a), channel_id=1, source_target_pairs={{0,1},{1,0},{2,3},{3,2},{4,5},{5,4},{6,7},{7,6},{8,9},{9,8},{10,11... | collective-permute-start | bytes 884744 | tf_op jit(solution)/shard_map/ppermute | solution.py:188
  6.1 3.5 %collective-permute-start.2 = (bf16[128,1152]{1,0:T(8,128)(2,1)S(1)}, bf16[128,1152]{1,0:T(8,128)(2,1)S(1)}, u32[]{:S(2)}, u32[]{:S(2)}) collective-permute-start(bf16[128,1152]{1,0:T(8,128)(2,1)S(1)} %get-tuple-element.19.image_b), channel_id=1, source_target_pairs={{0,1},{1,0},{2,3},{3,2},{4,5},{5,4},{6,7},{7,6},{8,9},{9,8},{10,11... | collective-permute-start | bytes 884744 | tf_op jit(solution)/shard_map/ppermute | solution.py:188
  6.6 1.5 %collective-permute-start = (s32[1,256]{1,0:T(1,128)S(1)}, s32[1,256]{1,0:T(1,128)S(1)}, u32[]{:S(2)}, u32[]{:S(2)}) collective-permute-start(s32[1,256]{1,0:T(1,128)S(1)} %bitcast.3), channel_id=1, source_target_pairs={{0,1},{1,0},{2,3},{3,2},{4,5},{5,4},{6,7},{7,6},{8,9},{9,8},{10,11... | collective-permute-start | bytes 3080 | tf_op jit(solution)/shard_map/ppermute | solution.py:188
  8.1 15.0 %collective-permute-start.3 = (s32[2,256]{1,0:T(2,128)S(1)}, s32[2,256]{1,0:T(2,128)S(1)}, u32[]{:S(2)}, u32[]{:S(2)}) collective-permute-start(s32[2,256]{1,0:T(2,128)S(1)} %pad_add_fusion), channel_id=1, source_target_pairs={{0,2},{1,3},{2,4},{3,5},{4,6},{5,7},{6,8},{7,9},{8,10},{9,11},{10,... | collective-permute-start | bytes 6152 | tf_op jit(solution)/shard_map/ppermute | solution.py:185
  13.5 9.6 %collective-permute-start.4 = (bf16[48,1152]{1,0:T(8,128)(2,1)S(1)}, bf16[48,1152]{1,0:T(8,128)(2,1)S(1)}, u32[]{:S(2)}, u32[]{:S(2)}) collective-permute-start(bf16[48,1152]{1,0:T(8,128)(2,1)S(1)} %get-tuple-element.21), channel_id=1, source_target_pairs={{0,1},{1,0},{2,3},{3,2},{4,5},{5,4},{6,7},{7,6},{8,9},{9,8},{10,11... | collective-permute-start | bytes 331784 | tf_op jit(solution)/shard_map/ppermute | solution.py:188
  13.6 19.8 %collective-permute-start.9 = (bf16[208,1152]{1,0:T(8,128)(2,1)S(1)}, bf16[208,1152]{1,0:T(8,128)(2,1)S(1)}, u32[]{:S(2)}, u32[]{:S(2)}) collective-permute-start(bf16[208,1152]{1,0:T(8,128)(2,1)S(1)} %get-tuple-element.32), channel_id=1, source_target_pairs={{0,2},{1,3},{2,4},{3,5},{4,6},{5,7},{6,8},{7,9},{8,10},{9,11},{10,... | collective-permute-start | bytes 1437704 | tf_op jit(solution)/shard_map/ppermute | solution.py:185
  23.2 2.4 %collective-permute-start.6 = (bf16[192,1152]{1,0:T(8,128)(2,1)S(1)}, bf16[192,1152]{1,0:T(8,128)(2,1)S(1)}, u32[]{:S(2)}, u32[]{:S(2)}) collective-permute-start(bf16[192,1152]{1,0:T(8,128)(2,1)S(1)} %get-tuple-element.22), channel_id=1, source_target_pairs={{0,1},{1,0},{2,3},{3,2},{4,5},{5,4},{6,7},{7,6},{8,9},{9,8},{10,11... | collective-permute-start | bytes 1327112 | tf_op jit(solution)/shard_map/ppermute | solution.py:188
  23.3 2.3 %collective-permute-start.7 = (bf16[64,1152]{1,0:T(8,128)(2,1)S(1)}, bf16[64,1152]{1,0:T(8,128)(2,1)S(1)}, u32[]{:S(2)}, u32[]{:S(2)}) collective-permute-start(bf16[64,1152]{1,0:T(8,128)(2,1)S(1)} %get-tuple-element.23), channel_id=1, source_target_pairs={{0,1},{1,0},{2,3},{3,2},{4,5},{5,4},{6,7},{7,6},{8,9},{9,8},{10,11... | collective-permute-start | bytes 442376 | tf_op jit(solution)/shard_map/ppermute | solution.py:188
  23.8 10.7 %collective-permute-start.8 = (bf16[48,1152]{1,0:T(8,128)(2,1)S(1)}, bf16[48,1152]{1,0:T(8,128)(2,1)S(1)}, u32[]{:S(2)}, u32[]{:S(2)}) collective-permute-start(bf16[48,1152]{1,0:T(8,128)(2,1)S(1)} %collective-permute-done.4.before), channel_id=1, source_target_pairs={{0,3},{1,2},{2,5},{3,4},{4,7},{5,6},{6,9},{7,8},{8,11},{9,10},{10,... | collective-permute-start | bytes 331784 | tf_op jit(solution)/shard_map/ppermute | solution.py:227

commit v19 on v18

--- a/solution.py
+++ b/solution.py
@@ -10,6 +10,7 @@
 SHIFTS = 2
 AXES = ("dp", "group")
 STEP = 16
+PIECES = 4
 VMEM = pl.BlockSpec(memory_space=pltpu.VMEM)
 SMEM = pl.BlockSpec(memory_space=pltpu.SMEM)
 ANY = pl.BlockSpec(memory_space=pl.ANY)
@@ -34,27 +35,32 @@
     return jnp.sum(loss.T, axis=0, keepdims=True), coef
 
 
-def whole(a, b):
-    return jnp.concatenate([a[...], b[...]], axis=0)
+def whole(*parts):
+    return jnp.concatenate([part[...] for part in parts], axis=0)
 
 
 def low(coef):
     return coef.astype(jnp.bfloat16)
 
 
-def cast_kernel(text, out):
-    out[...] = text[...].astype(out.dtype)
-
-
-def load_kernel(text, image, out_a, out_b, sems):
-    half = out_a.shape[0]
-    copies = [
-        pltpu.make_async_copy(image.at[pl.ds(0, half)], out_a, sems.at[0]),
-        pltpu.make_async_copy(image.at[pl.ds(half, half)], out_b, sems.at[1]),
-    ]
+def cast_kernel(text, out, staged, sem):
+    copy = pltpu.make_async_copy(text.at[pl.ds(0, out.shape[0])], staged, sem)
+    copy.start()
+    copy.wait()
+    out[...] = staged[...].astype(out.dtype)
+
+
+def load_kernel(before, text, image, out, *refs):
+    images, (staged, sems) = refs[:-2], refs[-2:]
+    step, rest = images[0].shape[0], out.shape[0]
+    copies = [pltpu.make_async_copy(text.at[pl.ds(text.shape[0] - rest, rest)], staged, sems.at[PIECES])]
+    for k, piece in enumerate(images):
+        copies.append(pltpu.make_async_copy(image.at[pl.ds(k * step, step)], piece, sems.at[k]))
     for copy in copies:
         copy.start()
-    for copy in copies:
+    copies[0].wait()
+    out[...] = staged[...].astype(out.dtype)
+    for copy in copies[1:]:
         copy.wait()
 
 
@@ -71,12 +77,13 @@
         copy.wait()
 
 
-def own_kernel(flags, params, ids, mate_ids, image_a, image_b, mate_a, mate_b, text, accum_in, out_a, out_b, image_sum, loss,
-               accum, sem):
+def own_kernel(flags, params, ids, mate_ids, text_a, text_b, accum_in, *refs):
+    images, mates = refs[:PIECES], refs[PIECES:2 * PIECES]
+    out_a, out_b, image_sum, loss, accum, sem = refs[2 * PIECES:]
     copy = pltpu.make_async_copy(accum_in, accum, sem)
     copy.start()
-    image = whole(image_a, image_b)
-    own_loss, coef = pair(image, text[...], ids[...], ids[...], params)
+    image, text = whole(*images), whole(text_a, text_b)
+    own_loss, coef = pair(image, text, ids[...], ids[...], params)
     loss[...] = own_loss
     copy.wait()
     total = accum[...] + dot(low(coef.T), image, (1, 0))
@@ -88,38 +95,40 @@
 
     @pl.when(flags[0] == 0)
     def _():
-        mate = whole(mate_a, mate_b)
-        _, mate_coef = pair(mate, text[...], mate_ids[...], ids[...], params)
+        mate = whole(*mates)
+        _, mate_coef = pair(mate, text, mate_ids[...], ids[...], params)
         give(total + dot(low(mate_coef.T), mate, (1, 0)))
 
     @pl.when(flags[0] == 1)
     def _():
         give(total)
 
-    image_sum[...] = dot(low(coef), text[...], (1, 0))
+    image_sum[...] = dot(low(coef), text, (1, 0))
 
 
 def ids_kernel(token, both_ids, out):
     out[...] = both_ids[...]
 
 
-def relay_kernel(flags, token, before, text, far, out_a, out_b):
-    cut = out_a.shape[0]
-
-    def fill(source):
-        out_a[...] = source[:cut, :]
-        out_b[...] = source[cut:, :]
-
-    pl.when(flags[0] == 0)(lambda: fill(text))
-    pl.when(flags[0] == 1)(lambda: fill(far))
-
-
-def far_kernel(flags, params, ids, mate_ids, both_ids, image_a, image_b, mate_a, mate_b, far, image_in,
-               loss_in, late, image_sum, loss):
-    image = whole(image_a, image_b)
-    more, coef = pair(image, far[...], ids[...], both_ids[:1, :], params)
+def relay_kernel(flags, token, before, text_a, text_b, far_a, far_b, out_a, out_b):
+    cut, top = out_a.shape[0], text_a.shape[0]
+
+    def fill(upper, lower):
+        out_a[:top, :] = upper[...]
+        out_a[top:, :] = lower[:cut - top, :]
+        out_b[...] = lower[cut - top:, :]
+
+    pl.when(flags[0] == 0)(lambda: fill(text_a, text_b))
+    pl.when(flags[0] == 1)(lambda: fill(far_a, far_b))
+
+
+def far_kernel(flags, params, ids, mate_ids, both_ids, far_a, far_b, image_in, loss_in, *refs):
+    images, mates = refs[:PIECES], refs[PIECES:2 * PIECES]
+    late, image_sum, loss = refs[2 * PIECES:]
+    image, far = whole(*images), whole(far_a, far_b)
+    more, coef = pair(image, far, ids[...], both_ids[:1, :], params)
     loss[...] = loss_in[...] + more
-    image_sum[...] = image_in[...] + dot(low(coef), far[...], (1, 0))
+    image_sum[...] = image_in[...] + dot(low(coef), far, (1, 0))
     part = dot(low(coef.T), image, (1, 0))
 
     @pl.when(flags[0] == 0)
@@ -128,14 +137,14 @@
 
     @pl.when(flags[0] == 1)
     def _():
-        mate = whole(mate_a, mate_b)
-        _, mate_coef = pair(mate, far[...], mate_ids[...], both_ids[:1, :], params)
+        mate = whole(*mates)
+        _, mate_coef = pair(mate, far, mate_ids[...], both_ids[:1, :], params)
         late[...] = part + dot(low(mate_coef.T), mate, (1, 0))
 
 
-def near_kernel(flags, params, ids, mate_ids, both_ids, image_a, image_b, near_a, near_b, image_in, loss_in,
-                image_grad, loss):
-    image = whole(image_a, image_b)
+def near_kernel(flags, params, ids, mate_ids, both_ids, near_a, near_b, image_in, loss_in, *refs):
+    image_grad, loss = refs[PIECES:]
+    image = whole(*refs[:PIECES])
     near_ids = jnp.where(flags[0] == 0, both_ids[1:, :], mate_ids[...])
     near = whole(near_a, near_b)
     more, coef = pair(image, near, ids[...], near_ids, params)
@@ -172,7 +181,6 @@
 def body(image_emb, text_emb, text_accum, pair_ids, log_scale, bias):
     count = lax.axis_size(AXES)
     rows, width = image_emb.shape
-    half = rows // 2
     f32, bf16 = jnp.float32, jnp.bfloat16
     flags = (lax.axis_index("group") % 2).astype(jnp.int32).reshape(1)
     params = jnp.concatenate([log_scale, bias])
@@ -187,20 +195,33 @@
     def across(value):
         return lax.ppermute(value, AXES, swap)
 
-    (text,) = call(cast_kernel, "cast", [((rows, width), bf16)], (), text_emb)
-    far = ahead(text)
-
-    image_a, image_b = pl.pallas_call(
+    top = rows * 176 // 256
+    fixed_text = pltpu.with_memory_space_constraint(text_emb, pltpu.HBM)
+    text_a = pl.pallas_call(
+        cast_kernel,
+        out_shape=jax.ShapeDtypeStruct((top, width), bf16),
+        in_specs=[HBM],
+        out_specs=VMEM,
+        scratch_shapes=[pltpu.VMEM((top, width), f32), pltpu.SemaphoreType.DMA],
+        compiler_params=pltpu.CompilerParams(vmem_limit_bytes=16 * 1024 * 1024),
+        cost_estimate=pl.CostEstimate(flops=0, bytes_accessed=0, transcendentals=0),
+        name="cast",
+    )(fixed_text)
+    text_b, *images = pl.pallas_call(
         load_kernel,
-        out_shape=[jax.ShapeDtypeStruct((n, width), bf16) for n in (half, rows - half)],
-        in_specs=[ANY, HBM],
-        out_specs=[VMEM] * 2,
-        scratch_shapes=[pltpu.SemaphoreType.DMA((2,))],
+        out_shape=[
+            jax.ShapeDtypeStruct((rows - top, width), bf16),
+            *[jax.ShapeDtypeStruct((rows // PIECES, width), bf16)] * PIECES,
+        ],
+        in_specs=[ANY, HBM, HBM],
+        out_specs=[VMEM] * (1 + PIECES),
+        scratch_shapes=[pltpu.VMEM((rows - top, width), f32), pltpu.SemaphoreType.DMA((PIECES + 1,))],
         compiler_params=pltpu.CompilerParams(vmem_limit_bytes=16 * 1024 * 1024),
         cost_estimate=pl.CostEstimate(flops=0, bytes_accessed=0, transcendentals=0),
         name="load",
-    )(text, pltpu.with_memory_space_constraint(image_emb, pltpu.HBM))
-    mate_a, mate_b = across(image_a), across(image_b)
+    )(text_a, fixed_text, pltpu.with_memory_space_constraint(image_emb, pltpu.HBM))
+    far_a, far_b = ahead(text_a), ahead(text_b)
+    mates = [across(piece) for piece in images]
     mate_ids = across(ids)
     both_ids = ahead(jnp.concatenate([ids, mate_ids]))
 
@@ -213,33 +234,32 @@
             jax.ShapeDtypeStruct((rows, width), f32),
             jax.ShapeDtypeStruct((1, rows), f32),
         ],
-        in_specs=[SMEM] * 2 + [VMEM] * 7 + [HBM],
+        in_specs=[SMEM] * 2 + [VMEM] * 4 + [HBM] + [VMEM] * 2 * PIECES,
         out_specs=[VMEM] * 4,
         scratch_shapes=[pltpu.VMEM((rows, width), f32), pltpu.SemaphoreType.DMA],
         compiler_params=pltpu.CompilerParams(vmem_limit_bytes=16 * 1024 * 1024),
         cost_estimate=pl.CostEstimate(flops=0, bytes_accessed=0, transcendentals=0),
         name="own",
-    )(flags, params, ids, mate_ids, image_a, image_b, mate_a, mate_b, text,
-      pltpu.with_memory_space_constraint(text_accum, pltpu.HBM))
+    )(flags, params, ids, mate_ids, text_a, text_b, pltpu.with_memory_space_constraint(text_accum, pltpu.HBM),
+      *images, *mates)
     crossed = [(i, target ^ 1) for i, target in skip]
     arrived_a = ahead(out_a)
     mate_rows = across(out_b)
     arrived_b = lax.ppermute(mate_rows, AXES, crossed)
 
-    (both_ids,) = call(ids_kernel, "ids", [((2, rows), jnp.int32)], (), loss, both_ids, flops=2 << 30)
+    (both_ids,) = call(ids_kernel, "ids", [((2, rows), jnp.int32)], (), loss, both_ids, flops=1300000000)
     passed_a, passed_b = call(
         relay_kernel, "relay", [((cut - 16, width), bf16), ((rows - cut + 16, width), bf16)],
-        (flags,), both_ids, mate_rows, text, far, flops=1 << 30,
+        (flags,), both_ids, mate_rows, text_a, text_b, far_a, far_b, flops=1 << 30,
     )
     near_a, near_b = across(passed_a), across(passed_b)
     late, image_sum, loss = call(
         far_kernel, "far", [((rows, width), f32), ((rows, width), f32), ((1, rows), f32)],
-        (flags, params), ids, mate_ids, both_ids, image_a, image_b, mate_a, mate_b, far, image_sum,
-        loss,
+        (flags, params), ids, mate_ids, both_ids, far_a, far_b, image_sum, loss, *images, *mates,
     )
     image_grad, loss = call(
         near_kernel, "near", [((rows, width), bf16), ((1, rows), f32)],
-        (flags, params), ids, mate_ids, both_ids, image_a, image_b, near_a, near_b, image_sum, loss,
+        (flags, params), ids, mate_ids, both_ids, near_a, near_b, image_sum, loss, *images,
     )
     late, image_grad = lax.optimization_barrier((late, image_grad))
     text_grad = add_part("add_a", 0, cut // STEP, arrived_a, late)

time: 35.4 us -> 36.1 us (1.020)
  starting transfers between devices: 7.34 us -> 9.43 us
  Pallas kernels: 11 us -> 13 us
  waiting for transfers between devices: 13.4 us -> 11.4 us
  local copies, waits for them, and re-layouts: 1.27 us -> 0.01 us
    ppermute x3 -> x4, waiting for transfers between devices: 13.3 us -> 10.9 us  [ahead(): return lax.ppermute(value, AXES, skip)]
    ppermute x3 -> x4, starting transfers between devices: 6.05 us -> 7.57 us  [ahead(): return lax.ppermute(value, AXES, skip)]
    pallas_call x1 -> x2, Pallas kernels: 1.07 us -> 2.44 us  [the longest x1 1.25 us: body(): pl.pallas_call(load_kernel, out_shape=[jax.ShapeDtypeStruct((rows - top,...]
    unnamed x4 -> x2, local copies, waits for them, and re-layouts: 1.27 us -> 0.01 us
    pallas_call x1, Pallas kernels: 3.82 us -> 4.44 us  [body(): pl.pallas_call(own_kernel, out_shape=[jax.ShapeDtypeStruct((cut, width),...]
    ppermute x6 -> x8, starting transfers between devices: 1.29 us -> 1.86 us  [across(): return lax.ppermute(value, AXES, swap)]
    ppermute x1, waiting for transfers between devices: 0.01 us -> 0.41 us  [body(): arrived_b = lax.ppermute(mate_rows, AXES, crossed)]
    pallas_call x5 -> x4, Pallas kernels: 4.37 us -> 4.3 us  [call(): pl.pallas_call(kernel, out_shape=[jax.ShapeDtypeStruct(s, d) for s, d in...]
  transfers between devices with their start and end apart: 10 -> 13, of which waited for: 3 -> 3; matrix products, arithmetic and copies ran while one was open for 0% -> 0% of each run, Pallas kernels for 29% -> 31%
where the time goes in v19:
time: 36.1 us; the launch traced here: 35.9 us
  Pallas kernels  13 us (36%)
  waiting for transfers between devices  11.4 us (32%)
  starting transfers between devices  9.43 us (26%)
  between operations  2.05 us (6%)
    ppermute x4, waiting for transfers between devices, ahead(): return lax.ppermute(value, AXES, skip)  10.9 us
    ppermute x4, starting transfers between devices, ahead(): return lax.ppermute(value, AXES, skip)  7.57 us
    pallas_call x1, Pallas kernels, body(): pl.pallas_call(own_kernel, out_shape=[jax.ShapeDtypeStruct((cut, width),...  4.44 us
    pallas_call x4, Pallas kernels, call(): pl.pallas_call(kernel, out_shape=[jax.ShapeDtypeStruct(s, d) for s, d in...  4.3 us
    ppermute x8, starting transfers between devices, across(): return lax.ppermute(value, AXES, swap)  1.86 us
    pallas_call x2, Pallas kernels, add_part(): pl.pallas_call(functools.partial(add_kernel, start, chunks), out_shape=ja...  1.77 us
    pallas_call x1, Pallas kernels, body(): pl.pallas_call(load_kernel, out_shape=[jax.ShapeDtypeStruct((rows - top,...  1.25 us
    pallas_call x1, Pallas kernels, body(): pl.pallas_call(cast_kernel, out_shape=jax.ShapeDtypeStruct((top, width),...  1.19 us
  transfers between devices with their start and end apart: 13, of which 3 were waited for; matrix products, arithmetic and copies ran while one was open for 0% of the time, Pallas kernels for 31%

profile of v19, /device:TPU:0, one launch (start us, length us, event | category | flops | bytes accessed | tf_op | source)
XLA Modules:
  0.0 35.9 jit_solution(10588874866676938266)
XLA Ops:
  0.6 1.2 %cast.1.before.text_a = bf16[176,1152]{1,0:T(8,128)(2,1)S(1)} custom-call(f32[256,1152]{1,0:T(8,128)} %text.3), custom_call_target="tpu_custom_call" | custom-call | tf_op jit(solution)/shard_map/cast/pallas_call | solution.py:200
  1.8 0.0 copy-start
  1.8 3.0 %collective-permute-start.7 = (bf16[176,1152]{1,0:T(8,128)(2,1)S(1)}, bf16[176,1152]{1,0:T(8,128)(2,1)S(1)}, u32[]{:S(2)}, u32[]{:S(2)}) collective-permute-start(bf16[176,1152]{1,0:T(8,128)(2,1)S(1)} %cast.1.before.text_a), channel_id=1, source_target_pairs={{0,2},{1,3},{2,4},{3,5},{4,6},{5,7},{6,8},{7,9},{8,10},{9,11},{10,... | collective-permute-start | bytes 1216520 | tf_op jit(solution)/shard_map/ppermute | solution.py:193
  4.9 1.2 %load.1 = (bf16[80,1152]{1,0:T(8,128)(2,1)S(1)}, bf16[64,1152]{1,0:T(8,128)(2,1)S(1)}, bf16[64,1152]{1,0:T(8,128)(2,1)S(1)}, bf16[64,1152]{1,0:T(8,128)(2,1)S(1)}, bf16[64,1152]{1,0:T(8,128)(2,1)S(1)}) custom-call(bf16[176,1152]{1,0:T(8,128)(2,1)S(1)} %cast.1.before.text_a, f32[256,1152]{1,0:T(8,128)} %text.3, bf16[256,1152]{1,0:T(8,128)(2,1)} %image.1), custom_call_target="tpu_custom_call" | custom-call | tf_op jit(solution)/shard_map/load/pallas_call | solution.py:210
  6.1 0.1 collective-permute-start.1
  6.2 0.5 %collective-permute-start.2 = (bf16[64,1152]{1,0:T(8,128)(2,1)S(1)}, bf16[64,1152]{1,0:T(8,128)(2,1)S(1)}, u32[]{:S(2)}, u32[]{:S(2)}) collective-permute-start(bf16[64,1152]{1,0:T(8,128)(2,1)S(1)} %get-tuple-element.23.refs_1_), channel_id=1, source_target_pairs={{0,1},{1,0},{2,3},{3,2},{4,5},{5,4},{6,7},{7,6},{8,9},{9,8},{10,11... | collective-permute-start | bytes 442376 | tf_op jit(solution)/shard_map/ppermute | solution.py:196
  6.7 0.0 copy-done
  6.7 0.1 collective-permute-start
  6.8 0.4 %collective-permute-start.3 = (bf16[64,1152]{1,0:T(8,128)(2,1)S(1)}, bf16[64,1152]{1,0:T(8,128)(2,1)S(1)}, u32[]{:S(2)}, u32[]{:S(2)}) collective-permute-start(bf16[64,1152]{1,0:T(8,128)(2,1)S(1)} %get-tuple-element.24.refs_2_), channel_id=1, source_target_pairs={{0,1},{1,0},{2,3},{3,2},{4,5},{5,4},{6,7},{7,6},{8,9},{9,8},{10,11... | collective-permute-start | bytes 442376 | tf_op jit(solution)/shard_map/ppermute | solution.py:196
  8.5 0.0 collective-permute-done.mate_ids
  8.5 0.1 collective-permute-start.4
  8.7 0.0 collective-permute-done.1.refs_4_
  8.7 1.5 %collective-permute-start.8 = (bf16[80,1152]{1,0:T(8,128)(2,1)S(1)}, bf16[80,1152]{1,0:T(8,128)(2,1)S(1)}, u32[]{:S(2)}, u32[]{:S(2)}) collective-permute-start(bf16[80,1152]{1,0:T(8,128)(2,1)S(1)} %get-tuple-element.21.text_b), channel_id=1, source_target_pairs={{0,2},{1,3},{2,4},{3,5},{4,6},{5,7},{6,8},{7,9},{8,10},{9,11},{10,... | collective-permute-start | bytes 552968 | tf_op jit(solution)/shard_map/ppermute | solution.py:193
  10.2 0.0 collective-permute-done.2.refs_5_
  10.2 1.5 %collective-permute-start.5 = (s32[2,256]{1,0:T(2,128)S(1)}, s32[2,256]{1,0:T(2,128)S(1)}, u32[]{:S(2)}, u32[]{:S(2)}) collective-permute-start(s32[2,256]{1,0:T(2,128)S(1)} %pad_add_fusion), channel_id=1, source_target_pairs={{0,2},{1,3},{2,4},{3,5},{4,6},{5,7},{6,8},{7,9},{8,10},{9,11},{10,... | collective-permute-start | bytes 6152 | tf_op jit(solution)/shard_map/ppermute | solution.py:193
  11.7 0.1 pad_maximum_fusion.params
  11.8 0.0 collective-permute-done.3.refs_6_
  11.8 0.0 collective-permute-done.4.refs_7_
  11.8 4.4 %own.1 = (bf16[208,1152]{1,0:T(8,128)(2,1)S(1)}, bf16[48,1152]{1,0:T(8,128)(2,1)S(1)}, f32[256,1152]{1,0:T(8,128)S(1)}, f32[1,256]{1,0:T(1,128)S(1)}) custom-call(s32[1]{0:T(128)} %bitcast.flags, f32[2]{0:T(128)S(1)} %pad_maximum_fusion.params, s32[1,256]{1,0:T(1,128)S(1)} %bitcast.5, s32[1,256]{1,0:T(1,128)S(1)} %collective-permute-done.mate_ids, ...), custom_call_target="tpu_custom_call" | custom-call | tf_op jit(solution)/shard_map/own/pallas_call | solution.py:229
  16.2 0.1 collective-permute-start.6
  16.3 1.5 %collective-permute-start.12 = (bf16[208,1152]{1,0:T(8,128)(2,1)S(1)}, bf16[208,1152]{1,0:T(8,128)(2,1)S(1)}, u32[]{:S(2)}, u32[]{:S(2)}) collective-permute-start(bf16[208,1152]{1,0:T(8,128)(2,1)S(1)} %get-tuple-element.38), channel_id=1, source_target_pairs={{0,2},{1,3},{2,4},{3,5},{4,6},{5,7},{6,8},{7,9},{8,10},{9,11},{10,... | collective-permute-start | bytes 1437704 | tf_op jit(solution)/shard_map/ppermute | solution.py:193
  17.8 4.4 %collective-permute-done.5.both_ids = s32[2,256]{1,0:T(2,128)S(1)} collective-permute-done((s32[2,256]{1,0:T(2,128)S(1)}, s32[2,256]{1,0:T(2,128)S(1)}, u32[]{:S(2)}, u32[]{:S(2)}) %collective-permute-start.5) | collective-permute-done | bytes 2080 | tf_op jit(solution)/shard_map/ppermute | solution.py:193
  22.2 0.0 collective-permute-done.8.far_b
  22.2 0.0 collective-permute-done.6.before
  22.2 0.0 collective-permute-done.7.far_a
  22.2 0.1 relay.1
  22.3 0.1 collective-permute-start.9
  22.4 0.5 %collective-permute-start.10 = (bf16[64,1152]{1,0:T(8,128)(2,1)S(1)}, bf16[64,1152]{1,0:T(8,128)(2,1)S(1)}, u32[]{:S(2)}, u32[]{:S(2)}) collective-permute-start(bf16[64,1152]{1,0:T(8,128)(2,1)S(1)} %get-tuple-element.29), channel_id=1, source_target_pairs={{0,1},{1,0},{2,3},{3,2},{4,5},{5,4},{6,7},{7,6},{8,9},{9,8},{10,11... | collective-permute-start | bytes 442376 | tf_op jit(solution)/shard_map/ppermute | solution.py:196
  22.9 0.0 collective-permute-start.11
  22.9 1.8 %far.1 = (f32[256,1152]{1,0:T(8,128)S(1)}, f32[256,1152]{1,0:T(8,128)S(1)}, f32[1,256]{1,0:T(1,128)S(1)}) custom-call(s32[1]{0:T(128)} %bitcast.flags, f32[2]{0:T(128)S(1)} %pad_maximum_fusion.params, s32[1,256]{1,0:T(1,128)S(1)} %bitcast.6, s32[1,256]{1,0:T(1,128)S(1)} %collective-permute-done.mate_ids, s32[2,256]{1,0:T(2,128)S(1)} %ids.1.token.both_ids, ...), custom_call_target="tpu_custom_call" | custom-call | tf_op jit(solution)/shard_map/far/pallas_call | solution.py:156
  24.7 0.0 collective-permute-done.10.near_b
  24.7 0.0 collective-permute-done.9.near_a
  24.7 2.4 %near.1 = (bf16[256,1152]{1,0:T(8,128)(2,1)}, f32[1,256]{1,0:T(1,128)}) custom-call(s32[1]{0:T(128)} %bitcast.flags, f32[2]{0:T(128)S(1)} %pad_maximum_fusion.params, s32[1,256]{1,0:T(1,128)S(1)} %bitcast.7, s32[1,256]{1,0:T(1,128)S(1)} %collective-permute-done.mate_ids, s32[2,256]{1,0:T(2,128)S(1)} %ids.1.token.both_ids, ...), custom_call_target="tpu_custom_call" | custom-call | tf_op jit(solution)/shard_map/near/pallas_call | solution.py:156
  27.1 6.6 %collective-permute-done.12.arrived = bf16[208,1152]{1,0:T(8,128)(2,1)S(1)} collective-permute-done((bf16[208,1152]{1,0:T(8,128)(2,1)S(1)}, bf16[208,1152]{1,0:T(8,128)(2,1)S(1)}, u32[]{:S(2)}, u32[]{:S(2)}) %collective-permute-start.12) | collective-permute-done | bytes 479264 | tf_op jit(solution)/shard_map/ppermute | solution.py:193
  33.7 1.1 %add_a.1.refs_0_ = f32[256,1152]{1,0:T(8,128)} custom-call(bf16[208,1152]{1,0:T(8,128)(2,1)S(1)} %collective-permute-done.12.arrived, f32[256,1152]{1,0:T(8,128)S(1)} %get-tuple-element.37.late), custom_call_target="tpu_custom_call" | custom-call | tf_op jit(solution)/shard_map/add_a/pallas_call | solution.py:168
  34.8 0.4 %collective-permute-done.11.arrived = bf16[48,1152]{1,0:T(8,128)(2,1)S(1)} collective-permute-done((bf16[48,1152]{1,0:T(8,128)(2,1)S(1)}, bf16[48,1152]{1,0:T(8,128)(2,1)S(1)}, u32[]{:S(2)}, u32[]{:S(2)}) %collective-permute-start.11) | collective-permute-done | bytes 110624 | tf_op jit(solution)/shard_map/ppermute | solution.py:248
  35.2 0.7 %add_b.1 = f32[256,1152]{1,0:T(8,128)} custom-call(bf16[48,1152]{1,0:T(8,128)(2,1)S(1)} %collective-permute-done.11.arrived, f32[256,1152]{1,0:T(8,128)S(1)} %get-tuple-element.37.late, f32[256,1152]{1,0:T(8,128)} %add_a.1.refs_0_), custom_call_target="tpu_custom_call", output_to_operand_aliasing={{}: (2, {})} | custom-call | tf_op jit(solution)/shard_map/add_b/pallas_call | solution.py:168
  (2 shorter events, 0.0 us)
Async XLA Ops:
  1.8 4.9 %copy-start = (s32[256]{0:T(256)S(1)}, s32[256]{0:T(256)}, u32[]{:S(2)}) copy-start(s32[256]{0:T(256)} %param.9) | copy-start | bytes 3076
  1.8 20.4 %collective-permute-start.7 = (bf16[176,1152]{1,0:T(8,128)(2,1)S(1)}, bf16[176,1152]{1,0:T(8,128)(2,1)S(1)}, u32[]{:S(2)}, u32[]{:S(2)}) collective-permute-start(bf16[176,1152]{1,0:T(8,128)(2,1)S(1)} %cast.1.before.text_a), channel_id=1, source_target_pairs={{0,2},{1,3},{2,4},{3,5},{4,6},{5,7},{6,8},{7,9},{8,10},{9,11},{10,... | collective-permute-start | bytes 1216520 | tf_op jit(solution)/shard_map/ppermute | solution.py:193
  6.1 2.6 %collective-permute-start.1 = (bf16[64,1152]{1,0:T(8,128)(2,1)S(1)}, bf16[64,1152]{1,0:T(8,128)(2,1)S(1)}, u32[]{:S(2)}, u32[]{:S(2)}) collective-permute-start(bf16[64,1152]{1,0:T(8,128)(2,1)S(1)} %get-tuple-element.22.refs_0_), channel_id=1, source_target_pairs={{0,1},{1,0},{2,3},{3,2},{4,5},{5,4},{6,7},{7,6},{8,9},{9,8},{10,11... | collective-permute-start | bytes 442376 | tf_op jit(solution)/shard_map/ppermute | solution.py:196
  6.2 4.0 %collective-permute-start.2 = (bf16[64,1152]{1,0:T(8,128)(2,1)S(1)}, bf16[64,1152]{1,0:T(8,128)(2,1)S(1)}, u32[]{:S(2)}, u32[]{:S(2)}) collective-permute-start(bf16[64,1152]{1,0:T(8,128)(2,1)S(1)} %get-tuple-element.23.refs_1_), channel_id=1, source_target_pairs={{0,1},{1,0},{2,3},{3,2},{4,5},{5,4},{6,7},{7,6},{8,9},{9,8},{10,11... | collective-permute-start | bytes 442376 | tf_op jit(solution)/shard_map/ppermute | solution.py:196
  6.7 1.8 %collective-permute-start = (s32[1,256]{1,0:T(1,128)S(1)}, s32[1,256]{1,0:T(1,128)S(1)}, u32[]{:S(2)}, u32[]{:S(2)}) collective-permute-start(s32[1,256]{1,0:T(1,128)S(1)} %bitcast.3), channel_id=1, source_target_pairs={{0,1},{1,0},{2,3},{3,2},{4,5},{5,4},{6,7},{7,6},{8,9},{9,8},{10,11... | collective-permute-start | bytes 3080 | tf_op jit(solution)/shard_map/ppermute | solution.py:196
  6.8 5.0 %collective-permute-start.3 = (bf16[64,1152]{1,0:T(8,128)(2,1)S(1)}, bf16[64,1152]{1,0:T(8,128)(2,1)S(1)}, u32[]{:S(2)}, u32[]{:S(2)}) collective-permute-start(bf16[64,1152]{1,0:T(8,128)(2,1)S(1)} %get-tuple-element.24.refs_2_), channel_id=1, source_target_pairs={{0,1},{1,0},{2,3},{3,2},{4,5},{5,4},{6,7},{7,6},{8,9},{9,8},{10,11... | collective-permute-start | bytes 442376 | tf_op jit(solution)/shard_map/ppermute | solution.py:196
  8.5 3.2 %collective-permute-start.4 = (bf16[64,1152]{1,0:T(8,128)(2,1)S(1)}, bf16[64,1152]{1,0:T(8,128)(2,1)S(1)}, u32[]{:S(2)}, u32[]{:S(2)}) collective-permute-start(bf16[64,1152]{1,0:T(8,128)(2,1)S(1)} %get-tuple-element.25.refs_3_), channel_id=1, source_target_pairs={{0,1},{1,0},{2,3},{3,2},{4,5},{5,4},{6,7},{7,6},{8,9},{9,8},{10,11... | collective-permute-start | bytes 442376 | tf_op jit(solution)/shard_map/ppermute | solution.py:196
  8.7 13.5 %collective-permute-start.8 = (bf16[80,1152]{1,0:T(8,128)(2,1)S(1)}, bf16[80,1152]{1,0:T(8,128)(2,1)S(1)}, u32[]{:S(2)}, u32[]{:S(2)}) collective-permute-start(bf16[80,1152]{1,0:T(8,128)(2,1)S(1)} %get-tuple-element.21.text_b), channel_id=1, source_target_pairs={{0,2},{1,3},{2,4},{3,5},{4,6},{5,7},{6,8},{7,9},{8,10},{9,11},{10,... | collective-permute-start | bytes 552968 | tf_op jit(solution)/shard_map/ppermute | solution.py:193
  10.2 12.0 %collective-permute-start.5 = (s32[2,256]{1,0:T(2,128)S(1)}, s32[2,256]{1,0:T(2,128)S(1)}, u32[]{:S(2)}, u32[]{:S(2)}) collective-permute-start(s32[2,256]{1,0:T(2,128)S(1)} %pad_add_fusion), channel_id=1, source_target_pairs={{0,2},{1,3},{2,4},{3,5},{4,6},{5,7},{6,8},{7,9},{8,10},{9,11},{10,... | collective-permute-start | bytes 6152 | tf_op jit(solution)/shard_map/ppermute | solution.py:193
  16.2 6.0 %collective-permute-start.6 = (bf16[48,1152]{1,0:T(8,128)(2,1)S(1)}, bf16[48,1152]{1,0:T(8,128)(2,1)S(1)}, u32[]{:S(2)}, u32[]{:S(2)}) collective-permute-start(bf16[48,1152]{1,0:T(8,128)(2,1)S(1)} %get-tuple-element.27), channel_id=1, source_target_pairs={{0,1},{1,0},{2,3},{3,2},{4,5},{5,4},{6,7},{7,6},{8,9},{9,8},{10,11... | collective-permute-start | bytes 331784 | tf_op jit(solution)/shard_map/ppermute | solution.py:196
  16.3 17.4 %collective-permute-start.12 = (bf16[208,1152]{1,0:T(8,128)(2,1)S(1)}, bf16[208,1152]{1,0:T(8,128)(2,1)S(1)}, u32[]{:S(2)}, u32[]{:S(2)}) collective-permute-start(bf16[208,1152]{1,0:T(8,128)(2,1)S(1)} %get-tuple-element.38), channel_id=1, source_target_pairs={{0,2},{1,3},{2,4},{3,5},{4,6},{5,7},{6,8},{7,9},{8,10},{9,11},{10,... | collective-permute-start | bytes 1437704 | tf_op jit(solution)/shard_map/ppermute | solution.py:193
  22.3 2.4 %collective-permute-start.9 = (bf16[192,1152]{1,0:T(8,128)(2,1)S(1)}, bf16[192,1152]{1,0:T(8,128)(2,1)S(1)}, u32[]{:S(2)}, u32[]{:S(2)}) collective-permute-start(bf16[192,1152]{1,0:T(8,128)(2,1)S(1)} %get-tuple-element.28), channel_id=1, source_target_pairs={{0,1},{1,0},{2,3},{3,2},{4,5},{5,4},{6,7},{7,6},{8,9},{9,8},{10,11... | collective-permute-start | bytes 1327112 | tf_op jit(solution)/shard_map/ppermute | solution.py:196
  22.4 2.3 %collective-permute-start.10 = (bf16[64,1152]{1,0:T(8,128)(2,1)S(1)}, bf16[64,1152]{1,0:T(8,128)(2,1)S(1)}, u32[]{:S(2)}, u32[]{:S(2)}) collective-permute-start(bf16[64,1152]{1,0:T(8,128)(2,1)S(1)} %get-tuple-element.29), channel_id=1, source_target_pairs={{0,1},{1,0},{2,3},{3,2},{4,5},{5,4},{6,7},{7,6},{8,9},{9,8},{10,11... | collective-permute-start | bytes 442376 | tf_op jit(solution)/shard_map/ppermute | solution.py:196
  22.9 12.3 %collective-permute-start.11 = (bf16[48,1152]{1,0:T(8,128)(2,1)S(1)}, bf16[48,1152]{1,0:T(8,128)(2,1)S(1)}, u32[]{:S(2)}, u32[]{:S(2)}) collective-permute-start(bf16[48,1152]{1,0:T(8,128)(2,1)S(1)} %collective-permute-done.6.before), channel_id=1, source_target_pairs={{0,3},{1,2},{2,5},{3,4},{4,7},{5,6},{6,9},{7,8},{8,11},{9,10},{10,... | collective-permute-start | bytes 331784 | tf_op jit(solution)/shard_map/ppermute | solution.py:248

commit v20 on v19

--- a/solution.py
+++ b/solution.py
@@ -85,8 +85,7 @@
     image, text = whole(*images), whole(text_a, text_b)
     own_loss, coef = pair(image, text, ids[...], ids[...], params)
     loss[...] = own_loss
-    copy.wait()
-    total = accum[...] + dot(low(coef.T), image, (1, 0))
+    image_sum[...] = dot(low(coef), text, (1, 0))
     cut = out_a.shape[0]
 
     def give(value):
@@ -97,13 +96,13 @@
     def _():
         mate = whole(*mates)
         _, mate_coef = pair(mate, text, mate_ids[...], ids[...], params)
-        give(total + dot(low(mate_coef.T), mate, (1, 0)))
+        copy.wait()
+        give(accum[...] + dot(low(coef.T), image, (1, 0)) + dot(low(mate_coef.T), mate, (1, 0)))
 
     @pl.when(flags[0] == 1)
     def _():
-        give(total)
-
-    image_sum[...] = dot(low(coef), text, (1, 0))
+        copy.wait()
+        give(accum[...] + dot(low(coef.T), image, (1, 0)))
 
 
 def ids_kernel(token, both_ids, out):

time: 36.1 us -> 35.2 us (0.975)
  Pallas kernels: 13 us -> 11.5 us
  waiting for transfers between devices: 11.4 us -> 11.9 us
    pallas_call x1, Pallas kernels: 4.44 us -> 2.96 us  [body(): pl.pallas_call(own_kernel, out_shape=[jax.ShapeDtypeStruct((cut, width),...]
    ppermute x4, waiting for transfers between devices: 10.9 us -> 11.8 us  [ahead(): return lax.ppermute(value, AXES, skip)]
  transfers between devices with their start and end apart: 13 -> 13, of which waited for: 3 -> 3; matrix products, arithmetic and copies ran while one was open for 0% -> 0% of each run, Pallas kernels for 31% -> 27%
where the time goes in v20:
time: 35.2 us; the launch traced here: 34.9 us
  waiting for transfers between devices  11.9 us (34%)
  Pallas kernels  11.5 us (33%)
  starting transfers between devices  9.43 us (27%)
  between operations  2.05 us (6%)
    ppermute x4, waiting for transfers between devices, ahead(): return lax.ppermute(value, AXES, skip)  11.8 us
    ppermute x4, starting transfers between devices, ahead(): return lax.ppermute(value, AXES, skip)  7.57 us
    pallas_call x4, Pallas kernels, call(): pl.pallas_call(kernel, out_shape=[jax.ShapeDtypeStruct(s, d) for s, d in...  4.3 us
    pallas_call x1, Pallas kernels, body(): pl.pallas_call(own_kernel, out_shape=[jax.ShapeDtypeStruct((cut, width),...  2.96 us
    ppermute x8, starting transfers between devices, across(): return lax.ppermute(value, AXES, swap)  1.86 us
    pallas_call x2, Pallas kernels, add_part(): pl.pallas_call(functools.partial(add_kernel, start, chunks), out_shape=ja...  1.77 us
    pallas_call x1, Pallas kernels, body(): pl.pallas_call(load_kernel, out_shape=[jax.ShapeDtypeStruct((rows - top,...  1.25 us
    pallas_call x1, Pallas kernels, body(): pl.pallas_call(cast_kernel, out_shape=jax.ShapeDtypeStruct((top, width),...  1.19 us
  transfers between devices with their start and end apart: 13, of which 3 were waited for; matrix products, arithmetic and copies ran while one was open for 0% of the time, Pallas kernels for 27%

profile of v20, /device:TPU:0, one launch (start us, length us, event | category | flops | bytes accessed | tf_op | source)
XLA Modules:
  0.0 34.9 jit_solution(9512945542122047608)
XLA Ops:
  0.6 1.2 %cast.1.before.text_a = bf16[176,1152]{1,0:T(8,128)(2,1)S(1)} custom-call(f32[256,1152]{1,0:T(8,128)} %text.3), custom_call_target="tpu_custom_call" | custom-call | tf_op jit(solution)/shard_map/cast/pallas_call | solution.py:199
  1.8 0.0 copy-start
  1.8 3.0 %collective-permute-start.7 = (bf16[176,1152]{1,0:T(8,128)(2,1)S(1)}, bf16[176,1152]{1,0:T(8,128)(2,1)S(1)}, u32[]{:S(2)}, u32[]{:S(2)}) collective-permute-start(bf16[176,1152]{1,0:T(8,128)(2,1)S(1)} %cast.1.before.text_a), channel_id=1, source_target_pairs={{0,2},{1,3},{2,4},{3,5},{4,6},{5,7},{6,8},{7,9},{8,10},{9,11},{10,... | collective-permute-start | bytes 1216520 | tf_op jit(solution)/shard_map/ppermute | solution.py:192
  4.9 1.2 %load.1 = (bf16[80,1152]{1,0:T(8,128)(2,1)S(1)}, bf16[64,1152]{1,0:T(8,128)(2,1)S(1)}, bf16[64,1152]{1,0:T(8,128)(2,1)S(1)}, bf16[64,1152]{1,0:T(8,128)(2,1)S(1)}, bf16[64,1152]{1,0:T(8,128)(2,1)S(1)}) custom-call(bf16[176,1152]{1,0:T(8,128)(2,1)S(1)} %cast.1.before.text_a, f32[256,1152]{1,0:T(8,128)} %text.3, bf16[256,1152]{1,0:T(8,128)(2,1)} %image.1), custom_call_target="tpu_custom_call" | custom-call | tf_op jit(solution)/shard_map/load/pallas_call | solution.py:209
  6.1 0.1 collective-permute-start.1
  6.2 0.5 %collective-permute-start.2 = (bf16[64,1152]{1,0:T(8,128)(2,1)S(1)}, bf16[64,1152]{1,0:T(8,128)(2,1)S(1)}, u32[]{:S(2)}, u32[]{:S(2)}) collective-permute-start(bf16[64,1152]{1,0:T(8,128)(2,1)S(1)} %get-tuple-element.23.refs_1_), channel_id=1, source_target_pairs={{0,1},{1,0},{2,3},{3,2},{4,5},{5,4},{6,7},{7,6},{8,9},{9,8},{10,11... | collective-permute-start | bytes 442376 | tf_op jit(solution)/shard_map/ppermute | solution.py:195
  6.7 0.0 copy-done
  6.7 0.1 collective-permute-start
  6.8 0.4 %collective-permute-start.3 = (bf16[64,1152]{1,0:T(8,128)(2,1)S(1)}, bf16[64,1152]{1,0:T(8,128)(2,1)S(1)}, u32[]{:S(2)}, u32[]{:S(2)}) collective-permute-start(bf16[64,1152]{1,0:T(8,128)(2,1)S(1)} %get-tuple-element.24.refs_2_), channel_id=1, source_target_pairs={{0,1},{1,0},{2,3},{3,2},{4,5},{5,4},{6,7},{7,6},{8,9},{9,8},{10,11... | collective-permute-start | bytes 442376 | tf_op jit(solution)/shard_map/ppermute | solution.py:195
  8.5 0.0 collective-permute-done.mate_ids
  8.5 0.1 collective-permute-start.4
  8.7 0.0 collective-permute-done.1.refs_4_
  8.7 1.5 %collective-permute-start.8 = (bf16[80,1152]{1,0:T(8,128)(2,1)S(1)}, bf16[80,1152]{1,0:T(8,128)(2,1)S(1)}, u32[]{:S(2)}, u32[]{:S(2)}) collective-permute-start(bf16[80,1152]{1,0:T(8,128)(2,1)S(1)} %get-tuple-element.21.text_b), channel_id=1, source_target_pairs={{0,2},{1,3},{2,4},{3,5},{4,6},{5,7},{6,8},{7,9},{8,10},{9,11},{10,... | collective-permute-start | bytes 552968 | tf_op jit(solution)/shard_map/ppermute | solution.py:192
  10.2 0.0 collective-permute-done.2.refs_5_
  10.2 1.5 %collective-permute-start.5 = (s32[2,256]{1,0:T(2,128)S(1)}, s32[2,256]{1,0:T(2,128)S(1)}, u32[]{:S(2)}, u32[]{:S(2)}) collective-permute-start(s32[2,256]{1,0:T(2,128)S(1)} %pad_add_fusion), channel_id=1, source_target_pairs={{0,2},{1,3},{2,4},{3,5},{4,6},{5,7},{6,8},{7,9},{8,10},{9,11},{10,... | collective-permute-start | bytes 6152 | tf_op jit(solution)/shard_map/ppermute | solution.py:192
  11.7 0.1 pad_maximum_fusion.params
  11.8 0.0 collective-permute-done.3.refs_6_
  11.8 0.0 collective-permute-done.4.refs_7_
  11.8 3.0 %own.1 = (bf16[208,1152]{1,0:T(8,128)(2,1)S(1)}, bf16[48,1152]{1,0:T(8,128)(2,1)S(1)}, f32[256,1152]{1,0:T(8,128)S(1)}, f32[1,256]{1,0:T(1,128)S(1)}) custom-call(s32[1]{0:T(128)} %bitcast.flags, f32[2]{0:T(128)S(1)} %pad_maximum_fusion.params, s32[1,256]{1,0:T(1,128)S(1)} %bitcast.5, s32[1,256]{1,0:T(1,128)S(1)} %collective-permute-done.mate_ids, ...), custom_call_target="tpu_custom_call" | custom-call | tf_op jit(solution)/shard_map/own/pallas_call | solution.py:228
  14.7 0.1 collective-permute-start.6
  14.8 1.5 %collective-permute-start.12 = (bf16[208,1152]{1,0:T(8,128)(2,1)S(1)}, bf16[208,1152]{1,0:T(8,128)(2,1)S(1)}, u32[]{:S(2)}, u32[]{:S(2)}) collective-permute-start(bf16[208,1152]{1,0:T(8,128)(2,1)S(1)} %get-tuple-element.38), channel_id=1, source_target_pairs={{0,2},{1,3},{2,4},{3,5},{4,6},{5,7},{6,8},{7,9},{8,10},{9,11},{10,... | collective-permute-start | bytes 1437704 | tf_op jit(solution)/shard_map/ppermute | solution.py:192
  16.4 6.5 %collective-permute-done.5.both_ids = s32[2,256]{1,0:T(2,128)S(1)} collective-permute-done((s32[2,256]{1,0:T(2,128)S(1)}, s32[2,256]{1,0:T(2,128)S(1)}, u32[]{:S(2)}, u32[]{:S(2)}) %collective-permute-start.5) | collective-permute-done | bytes 2080 | tf_op jit(solution)/shard_map/ppermute | solution.py:192
  22.8 0.0 collective-permute-done.8.far_b
  22.8 0.0 collective-permute-done.6.before
  22.8 0.0 collective-permute-done.7.far_a
  22.8 0.1 relay.1
  22.9 0.1 collective-permute-start.9
  23.0 0.5 %collective-permute-start.10 = (bf16[64,1152]{1,0:T(8,128)(2,1)S(1)}, bf16[64,1152]{1,0:T(8,128)(2,1)S(1)}, u32[]{:S(2)}, u32[]{:S(2)}) collective-permute-start(bf16[64,1152]{1,0:T(8,128)(2,1)S(1)} %get-tuple-element.29), channel_id=1, source_target_pairs={{0,1},{1,0},{2,3},{3,2},{4,5},{5,4},{6,7},{7,6},{8,9},{9,8},{10,11... | collective-permute-start | bytes 442376 | tf_op jit(solution)/shard_map/ppermute | solution.py:195
  23.5 0.0 collective-permute-start.11
  23.5 1.8 %far.1 = (f32[256,1152]{1,0:T(8,128)S(1)}, f32[256,1152]{1,0:T(8,128)S(1)}, f32[1,256]{1,0:T(1,128)S(1)}) custom-call(s32[1]{0:T(128)} %bitcast.flags, f32[2]{0:T(128)S(1)} %pad_maximum_fusion.params, s32[1,256]{1,0:T(1,128)S(1)} %bitcast.6, s32[1,256]{1,0:T(1,128)S(1)} %collective-permute-done.mate_ids, s32[2,256]{1,0:T(2,128)S(1)} %ids.1.token.both_ids, ...), custom_call_target="tpu_custom_call" | custom-call | tf_op jit(solution)/shard_map/far/pallas_call | solution.py:155
  25.3 0.0 collective-permute-done.10.near_b
  25.3 0.0 collective-permute-done.9.near_a
  25.3 2.4 %near.1 = (bf16[256,1152]{1,0:T(8,128)(2,1)}, f32[1,256]{1,0:T(1,128)}) custom-call(s32[1]{0:T(128)} %bitcast.flags, f32[2]{0:T(128)S(1)} %pad_maximum_fusion.params, s32[1,256]{1,0:T(1,128)S(1)} %bitcast.7, s32[1,256]{1,0:T(1,128)S(1)} %collective-permute-done.mate_ids, s32[2,256]{1,0:T(2,128)S(1)} %ids.1.token.both_ids, ...), custom_call_target="tpu_custom_call" | custom-call | tf_op jit(solution)/shard_map/near/pallas_call | solution.py:155
  27.8 5.3 %collective-permute-done.12.arrived = bf16[208,1152]{1,0:T(8,128)(2,1)S(1)} collective-permute-done((bf16[208,1152]{1,0:T(8,128)(2,1)S(1)}, bf16[208,1152]{1,0:T(8,128)(2,1)S(1)}, u32[]{:S(2)}, u32[]{:S(2)}) %collective-permute-start.12) | collective-permute-done | bytes 479264 | tf_op jit(solution)/shard_map/ppermute | solution.py:192
  33.1 1.1 %add_a.1.refs_0_ = f32[256,1152]{1,0:T(8,128)} custom-call(bf16[208,1152]{1,0:T(8,128)(2,1)S(1)} %collective-permute-done.12.arrived, f32[256,1152]{1,0:T(8,128)S(1)} %get-tuple-element.37.late), custom_call_target="tpu_custom_call" | custom-call | tf_op jit(solution)/shard_map/add_a/pallas_call | solution.py:167
  34.2 0.1 collective-permute-done.11.arrived
  34.2 0.7 %add_b.1 = f32[256,1152]{1,0:T(8,128)} custom-call(bf16[48,1152]{1,0:T(8,128)(2,1)S(1)} %collective-permute-done.11.arrived, f32[256,1152]{1,0:T(8,128)S(1)} %get-tuple-element.37.late, f32[256,1152]{1,0:T(8,128)} %add_a.1.refs_0_), custom_call_target="tpu_custom_call", output_to_operand_aliasing={{}: (2, {})} | custom-call | tf_op jit(solution)/shard_map/add_b/pallas_call | solution.py:167
  (2 shorter events, 0.0 us)
Async XLA Ops:
  1.8 4.9 %copy-start = (s32[256]{0:T(256)S(1)}, s32[256]{0:T(256)}, u32[]{:S(2)}) copy-start(s32[256]{0:T(256)} %param.9) | copy-start | bytes 3076
  1.8 21.0 %collective-permute-start.7 = (bf16[176,1152]{1,0:T(8,128)(2,1)S(1)}, bf16[176,1152]{1,0:T(8,128)(2,1)S(1)}, u32[]{:S(2)}, u32[]{:S(2)}) collective-permute-start(bf16[176,1152]{1,0:T(8,128)(2,1)S(1)} %cast.1.before.text_a), channel_id=1, source_target_pairs={{0,2},{1,3},{2,4},{3,5},{4,6},{5,7},{6,8},{7,9},{8,10},{9,11},{10,... | collective-permute-start | bytes 1216520 | tf_op jit(solution)/shard_map/ppermute | solution.py:192
  6.1 2.6 %collective-permute-start.1 = (bf16[64,1152]{1,0:T(8,128)(2,1)S(1)}, bf16[64,1152]{1,0:T(8,128)(2,1)S(1)}, u32[]{:S(2)}, u32[]{:S(2)}) collective-permute-start(bf16[64,1152]{1,0:T(8,128)(2,1)S(1)} %get-tuple-element.22.refs_0_), channel_id=1, source_target_pairs={{0,1},{1,0},{2,3},{3,2},{4,5},{5,4},{6,7},{7,6},{8,9},{9,8},{10,11... | collective-permute-start | bytes 442376 | tf_op jit(solution)/shard_map/ppermute | solution.py:195
  6.2 4.0 %collective-permute-start.2 = (bf16[64,1152]{1,0:T(8,128)(2,1)S(1)}, bf16[64,1152]{1,0:T(8,128)(2,1)S(1)}, u32[]{:S(2)}, u32[]{:S(2)}) collective-permute-start(bf16[64,1152]{1,0:T(8,128)(2,1)S(1)} %get-tuple-element.23.refs_1_), channel_id=1, source_target_pairs={{0,1},{1,0},{2,3},{3,2},{4,5},{5,4},{6,7},{7,6},{8,9},{9,8},{10,11... | collective-permute-start | bytes 442376 | tf_op jit(solution)/shard_map/ppermute | solution.py:195
  6.7 1.8 %collective-permute-start = (s32[1,256]{1,0:T(1,128)S(1)}, s32[1,256]{1,0:T(1,128)S(1)}, u32[]{:S(2)}, u32[]{:S(2)}) collective-permute-start(s32[1,256]{1,0:T(1,128)S(1)} %bitcast.3), channel_id=1, source_target_pairs={{0,1},{1,0},{2,3},{3,2},{4,5},{5,4},{6,7},{7,6},{8,9},{9,8},{10,11... | collective-permute-start | bytes 3080 | tf_op jit(solution)/shard_map/ppermute | solution.py:195
  6.8 5.0 %collective-permute-start.3 = (bf16[64,1152]{1,0:T(8,128)(2,1)S(1)}, bf16[64,1152]{1,0:T(8,128)(2,1)S(1)}, u32[]{:S(2)}, u32[]{:S(2)}) collective-permute-start(bf16[64,1152]{1,0:T(8,128)(2,1)S(1)} %get-tuple-element.24.refs_2_), channel_id=1, source_target_pairs={{0,1},{1,0},{2,3},{3,2},{4,5},{5,4},{6,7},{7,6},{8,9},{9,8},{10,11... | collective-permute-start | bytes 442376 | tf_op jit(solution)/shard_map/ppermute | solution.py:195
  8.5 3.2 %collective-permute-start.4 = (bf16[64,1152]{1,0:T(8,128)(2,1)S(1)}, bf16[64,1152]{1,0:T(8,128)(2,1)S(1)}, u32[]{:S(2)}, u32[]{:S(2)}) collective-permute-start(bf16[64,1152]{1,0:T(8,128)(2,1)S(1)} %get-tuple-element.25.refs_3_), channel_id=1, source_target_pairs={{0,1},{1,0},{2,3},{3,2},{4,5},{5,4},{6,7},{7,6},{8,9},{9,8},{10,11... | collective-permute-start | bytes 442376 | tf_op jit(solution)/shard_map/ppermute | solution.py:195
  8.7 14.2 %collective-permute-start.8 = (bf16[80,1152]{1,0:T(8,128)(2,1)S(1)}, bf16[80,1152]{1,0:T(8,128)(2,1)S(1)}, u32[]{:S(2)}, u32[]{:S(2)}) collective-permute-start(bf16[80,1152]{1,0:T(8,128)(2,1)S(1)} %get-tuple-element.21.text_b), channel_id=1, source_target_pairs={{0,2},{1,3},{2,4},{3,5},{4,6},{5,7},{6,8},{7,9},{8,10},{9,11},{10,... | collective-permute-start | bytes 552968 | tf_op jit(solution)/shard_map/ppermute | solution.py:192
  10.2 12.7 %collective-permute-start.5 = (s32[2,256]{1,0:T(2,128)S(1)}, s32[2,256]{1,0:T(2,128)S(1)}, u32[]{:S(2)}, u32[]{:S(2)}) collective-permute-start(s32[2,256]{1,0:T(2,128)S(1)} %pad_add_fusion), channel_id=1, source_target_pairs={{0,2},{1,3},{2,4},{3,5},{4,6},{5,7},{6,8},{7,9},{8,10},{9,11},{10,... | collective-permute-start | bytes 6152 | tf_op jit(solution)/shard_map/ppermute | solution.py:192
  14.7 8.1 %collective-permute-start.6 = (bf16[48,1152]{1,0:T(8,128)(2,1)S(1)}, bf16[48,1152]{1,0:T(8,128)(2,1)S(1)}, u32[]{:S(2)}, u32[]{:S(2)}) collective-permute-start(bf16[48,1152]{1,0:T(8,128)(2,1)S(1)} %get-tuple-element.27), channel_id=1, source_target_pairs={{0,1},{1,0},{2,3},{3,2},{4,5},{5,4},{6,7},{7,6},{8,9},{9,8},{10,11... | collective-permute-start | bytes 331784 | tf_op jit(solution)/shard_map/ppermute | solution.py:195
  14.8 18.3 %collective-permute-start.12 = (bf16[208,1152]{1,0:T(8,128)(2,1)S(1)}, bf16[208,1152]{1,0:T(8,128)(2,1)S(1)}, u32[]{:S(2)}, u32[]{:S(2)}) collective-permute-start(bf16[208,1152]{1,0:T(8,128)(2,1)S(1)} %get-tuple-element.38), channel_id=1, source_target_pairs={{0,2},{1,3},{2,4},{3,5},{4,6},{5,7},{6,8},{7,9},{8,10},{9,11},{10,... | collective-permute-start | bytes 1437704 | tf_op jit(solution)/shard_map/ppermute | solution.py:192
  22.9 2.4 %collective-permute-start.9 = (bf16[192,1152]{1,0:T(8,128)(2,1)S(1)}, bf16[192,1152]{1,0:T(8,128)(2,1)S(1)}, u32[]{:S(2)}, u32[]{:S(2)}) collective-permute-start(bf16[192,1152]{1,0:T(8,128)(2,1)S(1)} %get-tuple-element.28), channel_id=1, source_target_pairs={{0,1},{1,0},{2,3},{3,2},{4,5},{5,4},{6,7},{7,6},{8,9},{9,8},{10,11... | collective-permute-start | bytes 1327112 | tf_op jit(solution)/shard_map/ppermute | solution.py:195
  23.0 2.3 %collective-permute-start.10 = (bf16[64,1152]{1,0:T(8,128)(2,1)S(1)}, bf16[64,1152]{1,0:T(8,128)(2,1)S(1)}, u32[]{:S(2)}, u32[]{:S(2)}) collective-permute-start(bf16[64,1152]{1,0:T(8,128)(2,1)S(1)} %get-tuple-element.29), channel_id=1, source_target_pairs={{0,1},{1,0},{2,3},{3,2},{4,5},{5,4},{6,7},{7,6},{8,9},{9,8},{10,11... | collective-permute-start | bytes 442376 | tf_op jit(solution)/shard_map/ppermute | solution.py:195
  23.5 10.7 %collective-permute-start.11 = (bf16[48,1152]{1,0:T(8,128)(2,1)S(1)}, bf16[48,1152]{1,0:T(8,128)(2,1)S(1)}, u32[]{:S(2)}, u32[]{:S(2)}) collective-permute-start(bf16[48,1152]{1,0:T(8,128)(2,1)S(1)} %collective-permute-done.6.before), channel_id=1, source_target_pairs={{0,3},{1,2},{2,5},{3,4},{4,7},{5,6},{6,9},{7,8},{8,11},{9,10},{10,... | collective-permute-start | bytes 331784 | tf_op jit(solution)/shard_map/ppermute | solution.py:247

commit v21 on v18

--- a/solution.py
+++ b/solution.py
@@ -78,8 +78,7 @@
     image = whole(image_a, image_b)
     own_loss, coef = pair(image, text[...], ids[...], ids[...], params)
     loss[...] = own_loss
-    copy.wait()
-    total = accum[...] + dot(low(coef.T), image, (1, 0))
+    image_sum[...] = dot(low(coef), text[...], (1, 0))
     cut = out_a.shape[0]
 
     def give(value):
@@ -90,13 +89,13 @@
     def _():
         mate = whole(mate_a, mate_b)
         _, mate_coef = pair(mate, text[...], mate_ids[...], ids[...], params)
-        give(total + dot(low(mate_coef.T), mate, (1, 0)))
+        copy.wait()
+        give(accum[...] + dot(low(coef.T), image, (1, 0)) + dot(low(mate_coef.T), mate, (1, 0)))
 
     @pl.when(flags[0] == 1)
     def _():
-        give(total)
-
-    image_sum[...] = dot(low(coef), text[...], (1, 0))
+        copy.wait()
+        give(accum[...] + dot(low(coef.T), image, (1, 0)))
 
 
 def ids_kernel(token, both_ids, out):

time: 35.4 us -> 35.4 us (level)
  waiting for transfers between devices: 13.4 us -> 14.3 us
  Pallas kernels: 11 us -> 10.2 us
    ppermute x3, waiting for transfers between devices: 13.3 us -> 14.2 us  [ahead(): return lax.ppermute(value, AXES, skip)]
    pallas_call x1, Pallas kernels: 3.82 us -> 2.96 us  [body(): pl.pallas_call(own_kernel, out_shape=[jax.ShapeDtypeStruct((cut, width),...]
  transfers between devices with their start and end apart: 10 -> 10, of which waited for: 3 -> 3; matrix products, arithmetic and copies ran while one was open for 0% -> 0% of each run, Pallas kernels for 29% -> 27%
where the time goes in v21:
time: 35.4 us; the launch traced here: 35.2 us
  waiting for transfers between devices  14.3 us (40%)
  Pallas kernels  10.2 us (29%)
  starting transfers between devices  7.34 us (21%)
  between operations  2.04 us (6%)
  local copies, waits for them, and re-layouts  1.27 us (4%)
    ppermute x3, waiting for transfers between devices, ahead(): return lax.ppermute(value, AXES, skip)  14.2 us
    ppermute x3, starting transfers between devices, ahead(): return lax.ppermute(value, AXES, skip)  6.05 us
    pallas_call x5, Pallas kernels, call(): pl.pallas_call(kernel, out_shape=[jax.ShapeDtypeStruct(s, d) for s, d in...  4.37 us
    pallas_call x1, Pallas kernels, body(): pl.pallas_call(own_kernel, out_shape=[jax.ShapeDtypeStruct((cut, width),...  2.96 us
    pallas_call x2, Pallas kernels, add_part(): pl.pallas_call(functools.partial(add_kernel, start, chunks), out_shape=ja...  1.77 us
    ppermute x6, starting transfers between devices, across(): return lax.ppermute(value, AXES, swap)  1.29 us
    unnamed x4, local copies, waits for them, and re-layouts  1.27 us
    pallas_call x1, Pallas kernels, body(): pl.pallas_call(load_kernel, out_shape=[jax.ShapeDtypeStruct((n, width), b...  1.07 us
  transfers between devices with their start and end apart: 10, of which 3 were waited for; matrix products, arithmetic and copies ran while one was open for 0% of the time, Pallas kernels for 27%

profile of v21, /device:TPU:0, one launch (start us, length us, event | category | flops | bytes accessed | tf_op | source)
XLA Modules:
  0.0 35.2 jit_solution(15467078594449363880)
XLA Ops:
  0.6 0.0 copy-start
  0.6 1.3 %copy-done = f32[256,1152]{1,0:T(8,128)S(1)} copy-done((f32[256,1152]{1,0:T(8,128)S(1)}, f32[256,1152]{1,0:T(8,128)}, u32[]{:S(2)}) %copy-start) | copy-done | bytes 1179672
  1.9 0.0 copy-start.1
  1.9 0.1 cast.1.text
  2.0 3.0 %collective-permute-start.5 = (bf16[256,1152]{1,0:T(8,128)(2,1)S(1)}, bf16[256,1152]{1,0:T(8,128)(2,1)S(1)}, u32[]{:S(2)}, u32[]{:S(2)}) collective-permute-start(bf16[256,1152]{1,0:T(8,128)(2,1)S(1)} %cast.1.text), channel_id=1, source_target_pairs={{0,2},{1,3},{2,4},{3,5},{4,6},{5,7},{6,8},{7,9},{8,10},{9,11},{10,... | collective-permute-start | bytes 1769480 | tf_op jit(solution)/shard_map/ppermute | solution.py:184
  5.0 1.1 %load.1 = (bf16[128,1152]{1,0:T(8,128)(2,1)S(1)}, bf16[128,1152]{1,0:T(8,128)(2,1)S(1)}) custom-call(bf16[256,1152]{1,0:T(8,128)(2,1)S(1)} %cast.1.text, bf16[256,1152]{1,0:T(8,128)(2,1)} %image.1), custom_call_target="tpu_custom_call" | custom-call | tf_op jit(solution)/shard_map/load/pallas_call | solution.py:192
  6.1 0.1 collective-permute-start.1
  6.1 0.5 %collective-permute-start.2 = (bf16[128,1152]{1,0:T(8,128)(2,1)S(1)}, bf16[128,1152]{1,0:T(8,128)(2,1)S(1)}, u32[]{:S(2)}, u32[]{:S(2)}) collective-permute-start(bf16[128,1152]{1,0:T(8,128)(2,1)S(1)} %get-tuple-element.19.image_b), channel_id=1, source_target_pairs={{0,1},{1,0},{2,3},{3,2},{4,5},{5,4},{6,7},{7,6},{8,9},{9,8},{10,11... | collective-permute-start | bytes 884744 | tf_op jit(solution)/shard_map/ppermute | solution.py:187
  6.6 0.0 copy-done.1
  6.6 0.1 collective-permute-start
  8.0 0.1 collective-permute-done.mate_ids
  8.1 1.5 %collective-permute-start.3 = (s32[2,256]{1,0:T(2,128)S(1)}, s32[2,256]{1,0:T(2,128)S(1)}, u32[]{:S(2)}, u32[]{:S(2)}) collective-permute-start(s32[2,256]{1,0:T(2,128)S(1)} %pad_add_fusion), channel_id=1, source_target_pairs={{0,2},{1,3},{2,4},{3,5},{4,6},{5,7},{6,8},{7,9},{8,10},{9,11},{10,... | collective-permute-start | bytes 6152 | tf_op jit(solution)/shard_map/ppermute | solution.py:184
  9.6 0.1 pad_maximum_fusion.params
  9.7 0.0 collective-permute-done.1.mate_a
  9.7 0.0 collective-permute-done.2.mate_b
  9.7 3.0 %own.1 = (bf16[208,1152]{1,0:T(8,128)(2,1)S(1)}, bf16[48,1152]{1,0:T(8,128)(2,1)S(1)}, f32[256,1152]{1,0:T(8,128)S(1)}, f32[1,256]{1,0:T(1,128)S(1)}) custom-call(s32[1]{0:T(128)} %bitcast.flags, f32[2]{0:T(128)S(1)} %pad_maximum_fusion.params, s32[1,256]{1,0:T(1,128)S(1)} %bitcast.5, s32[1,256]{1,0:T(1,128)S(1)} %collective-permute-done.mate_ids, ...), custom_call_target="tpu_custom_call" | custom-call | tf_op jit(solution)/shard_map/own/pallas_call | solution.py:207
  12.6 0.1 collective-permute-start.4
  12.7 1.6 %collective-permute-start.9 = (bf16[208,1152]{1,0:T(8,128)(2,1)S(1)}, bf16[208,1152]{1,0:T(8,128)(2,1)S(1)}, u32[]{:S(2)}, u32[]{:S(2)}) collective-permute-start(bf16[208,1152]{1,0:T(8,128)(2,1)S(1)} %get-tuple-element.32), channel_id=1, source_target_pairs={{0,2},{1,3},{2,4},{3,5},{4,6},{5,7},{6,8},{7,9},{8,10},{9,11},{10,... | collective-permute-start | bytes 1437704 | tf_op jit(solution)/shard_map/ppermute | solution.py:184
  14.3 8.9 %collective-permute-done.3.both_ids = s32[2,256]{1,0:T(2,128)S(1)} collective-permute-done((s32[2,256]{1,0:T(2,128)S(1)}, s32[2,256]{1,0:T(2,128)S(1)}, u32[]{:S(2)}, u32[]{:S(2)}) %collective-permute-start.3) | collective-permute-done | bytes 2080 | tf_op jit(solution)/shard_map/ppermute | solution.py:184
  23.2 0.0 collective-permute-done.4.before
  23.2 0.0 collective-permute-done.5.far
  23.2 0.1 relay.1
  23.2 0.1 collective-permute-start.6
  23.3 0.5 %collective-permute-start.7 = (bf16[64,1152]{1,0:T(8,128)(2,1)S(1)}, bf16[64,1152]{1,0:T(8,128)(2,1)S(1)}, u32[]{:S(2)}, u32[]{:S(2)}) collective-permute-start(bf16[64,1152]{1,0:T(8,128)(2,1)S(1)} %get-tuple-element.23), channel_id=1, source_target_pairs={{0,1},{1,0},{2,3},{3,2},{4,5},{5,4},{6,7},{7,6},{8,9},{9,8},{10,11... | collective-permute-start | bytes 442376 | tf_op jit(solution)/shard_map/ppermute | solution.py:187
  23.8 0.0 collective-permute-start.8
  23.8 1.8 %far.1 = (f32[256,1152]{1,0:T(8,128)S(1)}, f32[256,1152]{1,0:T(8,128)S(1)}, f32[1,256]{1,0:T(1,128)S(1)}) custom-call(s32[1]{0:T(128)} %bitcast.flags, f32[2]{0:T(128)S(1)} %pad_maximum_fusion.params, s32[1,256]{1,0:T(1,128)S(1)} %bitcast.6, s32[1,256]{1,0:T(1,128)S(1)} %collective-permute-done.mate_ids, s32[2,256]{1,0:T(2,128)S(1)} %ids.1.token.both_ids, ...), custom_call_target="tpu_custom_call" | custom-call | tf_op jit(solution)/shard_map/far/pallas_call | solution.py:146
  25.6 0.0 collective-permute-done.7.near_b
  25.7 0.0 collective-permute-done.6.near_a
  25.7 2.4 %near.1 = (bf16[256,1152]{1,0:T(8,128)(2,1)}, f32[1,256]{1,0:T(1,128)}) custom-call(s32[1]{0:T(128)} %bitcast.flags, f32[2]{0:T(128)S(1)} %pad_maximum_fusion.params, s32[1,256]{1,0:T(1,128)S(1)} %bitcast.7, s32[1,256]{1,0:T(1,128)S(1)} %collective-permute-done.mate_ids, s32[2,256]{1,0:T(2,128)S(1)} %ids.1.token.both_ids, ...), custom_call_target="tpu_custom_call" | custom-call | tf_op jit(solution)/shard_map/near/pallas_call | solution.py:146
  28.1 5.3 %collective-permute-done.9.arrived = bf16[208,1152]{1,0:T(8,128)(2,1)S(1)} collective-permute-done((bf16[208,1152]{1,0:T(8,128)(2,1)S(1)}, bf16[208,1152]{1,0:T(8,128)(2,1)S(1)}, u32[]{:S(2)}, u32[]{:S(2)}) %collective-permute-start.9) | collective-permute-done | bytes 479264 | tf_op jit(solution)/shard_map/ppermute | solution.py:184
  33.4 1.1 %add_a.1.refs_0_ = f32[256,1152]{1,0:T(8,128)} custom-call(bf16[208,1152]{1,0:T(8,128)(2,1)S(1)} %collective-permute-done.9.arrived, f32[256,1152]{1,0:T(8,128)S(1)} %get-tuple-element.31.late), custom_call_target="tpu_custom_call" | custom-call | tf_op jit(solution)/shard_map/add_a/pallas_call | solution.py:158
  34.5 0.0 collective-permute-done.8.arrived
  34.5 0.7 %add_b.1 = f32[256,1152]{1,0:T(8,128)} custom-call(bf16[48,1152]{1,0:T(8,128)(2,1)S(1)} %collective-permute-done.8.arrived, f32[256,1152]{1,0:T(8,128)S(1)} %get-tuple-element.31.late, f32[256,1152]{1,0:T(8,128)} %add_a.1.refs_0_), custom_call_target="tpu_custom_call", output_to_operand_aliasing={{}: (2, {})} | custom-call | tf_op jit(solution)/shard_map/add_b/pallas_call | solution.py:158
  (2 shorter events, 0.0 us)
Async XLA Ops:
  0.6 1.3 %copy-start = (f32[256,1152]{1,0:T(8,128)S(1)}, f32[256,1152]{1,0:T(8,128)}, u32[]{:S(2)}) copy-start(f32[256,1152]{1,0:T(8,128)} %text.1) | copy-start | bytes 3538948
  1.9 4.7 %copy-start.1 = (s32[256]{0:T(256)S(1)}, s32[256]{0:T(256)}, u32[]{:S(2)}) copy-start(s32[256]{0:T(256)} %param.9) | copy-start | bytes 3076
  2.0 21.2 %collective-permute-start.5 = (bf16[256,1152]{1,0:T(8,128)(2,1)S(1)}, bf16[256,1152]{1,0:T(8,128)(2,1)S(1)}, u32[]{:S(2)}, u32[]{:S(2)}) collective-permute-start(bf16[256,1152]{1,0:T(8,128)(2,1)S(1)} %cast.1.text), channel_id=1, source_target_pairs={{0,2},{1,3},{2,4},{3,5},{4,6},{5,7},{6,8},{7,9},{8,10},{9,11},{10,... | collective-permute-start | bytes 1769480 | tf_op jit(solution)/shard_map/ppermute | solution.py:184
  6.1 3.6 %collective-permute-start.1 = (bf16[128,1152]{1,0:T(8,128)(2,1)S(1)}, bf16[128,1152]{1,0:T(8,128)(2,1)S(1)}, u32[]{:S(2)}, u32[]{:S(2)}) collective-permute-start(bf16[128,1152]{1,0:T(8,128)(2,1)S(1)} %get-tuple-element.18.image_a), channel_id=1, source_target_pairs={{0,1},{1,0},{2,3},{3,2},{4,5},{5,4},{6,7},{7,6},{8,9},{9,8},{10,11... | collective-permute-start | bytes 884744 | tf_op jit(solution)/shard_map/ppermute | solution.py:187
  6.1 3.5 %collective-permute-start.2 = (bf16[128,1152]{1,0:T(8,128)(2,1)S(1)}, bf16[128,1152]{1,0:T(8,128)(2,1)S(1)}, u32[]{:S(2)}, u32[]{:S(2)}) collective-permute-start(bf16[128,1152]{1,0:T(8,128)(2,1)S(1)} %get-tuple-element.19.image_b), channel_id=1, source_target_pairs={{0,1},{1,0},{2,3},{3,2},{4,5},{5,4},{6,7},{7,6},{8,9},{9,8},{10,11... | collective-permute-start | bytes 884744 | tf_op jit(solution)/shard_map/ppermute | solution.py:187
  6.6 1.5 %collective-permute-start = (s32[1,256]{1,0:T(1,128)S(1)}, s32[1,256]{1,0:T(1,128)S(1)}, u32[]{:S(2)}, u32[]{:S(2)}) collective-permute-start(s32[1,256]{1,0:T(1,128)S(1)} %bitcast.3), channel_id=1, source_target_pairs={{0,1},{1,0},{2,3},{3,2},{4,5},{5,4},{6,7},{7,6},{8,9},{9,8},{10,11... | collective-permute-start | bytes 3080 | tf_op jit(solution)/shard_map/ppermute | solution.py:187
  8.1 15.0 %collective-permute-start.3 = (s32[2,256]{1,0:T(2,128)S(1)}, s32[2,256]{1,0:T(2,128)S(1)}, u32[]{:S(2)}, u32[]{:S(2)}) collective-permute-start(s32[2,256]{1,0:T(2,128)S(1)} %pad_add_fusion), channel_id=1, source_target_pairs={{0,2},{1,3},{2,4},{3,5},{4,6},{5,7},{6,8},{7,9},{8,10},{9,11},{10,... | collective-permute-start | bytes 6152 | tf_op jit(solution)/shard_map/ppermute | solution.py:184
  12.6 10.5 %collective-permute-start.4 = (bf16[48,1152]{1,0:T(8,128)(2,1)S(1)}, bf16[48,1152]{1,0:T(8,128)(2,1)S(1)}, u32[]{:S(2)}, u32[]{:S(2)}) collective-permute-start(bf16[48,1152]{1,0:T(8,128)(2,1)S(1)} %get-tuple-element.21), channel_id=1, source_target_pairs={{0,1},{1,0},{2,3},{3,2},{4,5},{5,4},{6,7},{7,6},{8,9},{9,8},{10,11... | collective-permute-start | bytes 331784 | tf_op jit(solution)/shard_map/ppermute | solution.py:187
  12.7 20.7 %collective-permute-start.9 = (bf16[208,1152]{1,0:T(8,128)(2,1)S(1)}, bf16[208,1152]{1,0:T(8,128)(2,1)S(1)}, u32[]{:S(2)}, u32[]{:S(2)}) collective-permute-start(bf16[208,1152]{1,0:T(8,128)(2,1)S(1)} %get-tuple-element.32), channel_id=1, source_target_pairs={{0,2},{1,3},{2,4},{3,5},{4,6},{5,7},{6,8},{7,9},{8,10},{9,11},{10,... | collective-permute-start | bytes 1437704 | tf_op jit(solution)/shard_map/ppermute | solution.py:184
  23.2 2.4 %collective-permute-start.6 = (bf16[192,1152]{1,0:T(8,128)(2,1)S(1)}, bf16[192,1152]{1,0:T(8,128)(2,1)S(1)}, u32[]{:S(2)}, u32[]{:S(2)}) collective-permute-start(bf16[192,1152]{1,0:T(8,128)(2,1)S(1)} %get-tuple-element.22), channel_id=1, source_target_pairs={{0,1},{1,0},{2,3},{3,2},{4,5},{5,4},{6,7},{7,6},{8,9},{9,8},{10,11... | collective-permute-start | bytes 1327112 | tf_op jit(solution)/shard_map/ppermute | solution.py:187
  23.3 2.3 %collective-permute-start.7 = (bf16[64,1152]{1,0:T(8,128)(2,1)S(1)}, bf16[64,1152]{1,0:T(8,128)(2,1)S(1)}, u32[]{:S(2)}, u32[]{:S(2)}) collective-permute-start(bf16[64,1152]{1,0:T(8,128)(2,1)S(1)} %get-tuple-element.23), channel_id=1, source_target_pairs={{0,1},{1,0},{2,3},{3,2},{4,5},{5,4},{6,7},{7,6},{8,9},{9,8},{10,11... | collective-permute-start | bytes 442376 | tf_op jit(solution)/shard_map/ppermute | solution.py:187
  23.8 10.7 %collective-permute-start.8 = (bf16[48,1152]{1,0:T(8,128)(2,1)S(1)}, bf16[48,1152]{1,0:T(8,128)(2,1)S(1)}, u32[]{:S(2)}, u32[]{:S(2)}) collective-permute-start(bf16[48,1152]{1,0:T(8,128)(2,1)S(1)} %collective-permute-done.4.before), channel_id=1, source_target_pairs={{0,3},{1,2},{2,5},{3,4},{4,7},{5,6},{6,9},{7,8},{8,11},{9,10},{10,... | collective-permute-start | bytes 331784 | tf_op jit(solution)/shard_map/ppermute | solution.py:226

commit v22 on v18

--- a/solution.py
+++ b/solution.py
@@ -204,7 +204,7 @@
     mate_ids = across(ids)
     both_ids = ahead(jnp.concatenate([ids, mate_ids]))
 
-    cut = rows - rows * 3 // 16
+    cut = rows - rows // 4
     out_a, out_b, image_sum, loss = pl.pallas_call(
         own_kernel,
         out_shape=[

time: 35.4 us -> 35.3 us (level)
    ppermute x3, waiting for transfers between devices: 13.3 us -> 12.5 us  [ahead(): return lax.ppermute(value, AXES, skip)]
    ppermute x1, waiting for transfers between devices: 0.01 us -> 0.47 us  [body(): arrived_b = lax.ppermute(mate_rows, AXES, crossed)]
  transfers between devices with their start and end apart: 10 -> 10, of which waited for: 3 -> 4; matrix products, arithmetic and copies ran while one was open for 0% -> 0% of each run, Pallas kernels for 29% -> 29%
where the time goes in v22:
time: 35.3 us; the launch traced here: 34.9 us
  waiting for transfers between devices  13.1 us (37%)
  Pallas kernels  11 us (31%)
  starting transfers between devices  7.34 us (21%)
  between operations  2.03 us (6%)
  local copies, waits for them, and re-layouts  1.27 us (4%)
    ppermute x3, waiting for transfers between devices, ahead(): return lax.ppermute(value, AXES, skip)  12.5 us
    ppermute x3, starting transfers between devices, ahead(): return lax.ppermute(value, AXES, skip)  6.05 us
    pallas_call x5, Pallas kernels, call(): pl.pallas_call(kernel, out_shape=[jax.ShapeDtypeStruct(s, d) for s, d in...  4.37 us
    pallas_call x1, Pallas kernels, body(): pl.pallas_call(own_kernel, out_shape=[jax.ShapeDtypeStruct((cut, width),...  3.82 us
    pallas_call x2, Pallas kernels, add_part(): pl.pallas_call(functools.partial(add_kernel, start, chunks), out_shape=ja...  1.77 us
    ppermute x6, starting transfers between devices, across(): return lax.ppermute(value, AXES, swap)  1.29 us
    unnamed x4, local copies, waits for them, and re-layouts  1.27 us
    pallas_call x1, Pallas kernels, body(): pl.pallas_call(load_kernel, out_shape=[jax.ShapeDtypeStruct((n, width), b...  1.07 us
  transfers between devices with their start and end apart: 10, of which 4 were waited for; matrix products, arithmetic and copies ran while one was open for 0% of the time, Pallas kernels for 29%

profile of v22, /device:TPU:0, one launch (start us, length us, event | category | flops | bytes accessed | tf_op | source)
XLA Modules:
  0.0 34.9 jit_solution(280630294470781022)
XLA Ops:
  0.6 0.0 copy-start
  0.6 1.3 %copy-done = f32[256,1152]{1,0:T(8,128)S(1)} copy-done((f32[256,1152]{1,0:T(8,128)S(1)}, f32[256,1152]{1,0:T(8,128)}, u32[]{:S(2)}) %copy-start) | copy-done | bytes 1179672
  1.9 0.0 copy-start.1
  1.9 0.1 cast.1.text
  2.0 3.0 %collective-permute-start.5 = (bf16[256,1152]{1,0:T(8,128)(2,1)S(1)}, bf16[256,1152]{1,0:T(8,128)(2,1)S(1)}, u32[]{:S(2)}, u32[]{:S(2)}) collective-permute-start(bf16[256,1152]{1,0:T(8,128)(2,1)S(1)} %cast.1.text), channel_id=1, source_target_pairs={{0,2},{1,3},{2,4},{3,5},{4,6},{5,7},{6,8},{7,9},{8,10},{9,11},{10,... | collective-permute-start | bytes 1769480 | tf_op jit(solution)/shard_map/ppermute | solution.py:185
  5.0 1.1 %load.1 = (bf16[128,1152]{1,0:T(8,128)(2,1)S(1)}, bf16[128,1152]{1,0:T(8,128)(2,1)S(1)}) custom-call(bf16[256,1152]{1,0:T(8,128)(2,1)S(1)} %cast.1.text, bf16[256,1152]{1,0:T(8,128)(2,1)} %image.1), custom_call_target="tpu_custom_call" | custom-call | tf_op jit(solution)/shard_map/load/pallas_call | solution.py:193
  6.1 0.1 collective-permute-start.1
  6.1 0.5 %collective-permute-start.2 = (bf16[128,1152]{1,0:T(8,128)(2,1)S(1)}, bf16[128,1152]{1,0:T(8,128)(2,1)S(1)}, u32[]{:S(2)}, u32[]{:S(2)}) collective-permute-start(bf16[128,1152]{1,0:T(8,128)(2,1)S(1)} %get-tuple-element.19.image_b), channel_id=1, source_target_pairs={{0,1},{1,0},{2,3},{3,2},{4,5},{5,4},{6,7},{7,6},{8,9},{9,8},{10,11... | collective-permute-start | bytes 884744 | tf_op jit(solution)/shard_map/ppermute | solution.py:188
  6.6 0.0 copy-done.1
  6.6 0.1 collective-permute-start
  8.0 0.1 collective-permute-done.mate_ids
  8.1 1.5 %collective-permute-start.3 = (s32[2,256]{1,0:T(2,128)S(1)}, s32[2,256]{1,0:T(2,128)S(1)}, u32[]{:S(2)}, u32[]{:S(2)}) collective-permute-start(s32[2,256]{1,0:T(2,128)S(1)} %pad_add_fusion), channel_id=1, source_target_pairs={{0,2},{1,3},{2,4},{3,5},{4,6},{5,7},{6,8},{7,9},{8,10},{9,11},{10,... | collective-permute-start | bytes 6152 | tf_op jit(solution)/shard_map/ppermute | solution.py:185
  9.6 0.1 pad_maximum_fusion.params
  9.7 0.0 collective-permute-done.1.mate_a
  9.7 0.0 collective-permute-done.2.mate_b
  9.7 3.8 %own.1 = (bf16[192,1152]{1,0:T(8,128)(2,1)S(1)}, bf16[64,1152]{1,0:T(8,128)(2,1)S(1)}, f32[256,1152]{1,0:T(8,128)S(1)}, f32[1,256]{1,0:T(1,128)S(1)}) custom-call(s32[1]{0:T(128)} %bitcast.flags, f32[2]{0:T(128)S(1)} %pad_maximum_fusion.params, s32[1,256]{1,0:T(1,128)S(1)} %bitcast.5, s32[1,256]{1,0:T(1,128)S(1)} %collective-permute-done.mate_ids, ...), custom_call_target="tpu_custom_call" | custom-call | tf_op jit(solution)/shard_map/own/pallas_call | solution.py:208
  13.5 0.1 collective-permute-start.4
  13.6 1.6 %collective-permute-start.9 = (bf16[192,1152]{1,0:T(8,128)(2,1)S(1)}, bf16[192,1152]{1,0:T(8,128)(2,1)S(1)}, u32[]{:S(2)}, u32[]{:S(2)}) collective-permute-start(bf16[192,1152]{1,0:T(8,128)(2,1)S(1)} %get-tuple-element.32), channel_id=1, source_target_pairs={{0,2},{1,3},{2,4},{3,5},{4,6},{5,7},{6,8},{7,9},{8,10},{9,11},{10,... | collective-permute-start | bytes 1327112 | tf_op jit(solution)/shard_map/ppermute | solution.py:185
  15.2 8.0 %collective-permute-done.3.both_ids = s32[2,256]{1,0:T(2,128)S(1)} collective-permute-done((s32[2,256]{1,0:T(2,128)S(1)}, s32[2,256]{1,0:T(2,128)S(1)}, u32[]{:S(2)}, u32[]{:S(2)}) %collective-permute-start.3) | collective-permute-done | bytes 2080 | tf_op jit(solution)/shard_map/ppermute | solution.py:185
  23.2 0.0 collective-permute-done.4.before
  23.2 0.0 collective-permute-done.5.far
  23.2 0.1 relay.1
  23.2 0.1 collective-permute-start.6
  23.3 0.5 %collective-permute-start.7 = (bf16[80,1152]{1,0:T(8,128)(2,1)S(1)}, bf16[80,1152]{1,0:T(8,128)(2,1)S(1)}, u32[]{:S(2)}, u32[]{:S(2)}) collective-permute-start(bf16[80,1152]{1,0:T(8,128)(2,1)S(1)} %get-tuple-element.23), channel_id=1, source_target_pairs={{0,1},{1,0},{2,3},{3,2},{4,5},{5,4},{6,7},{7,6},{8,9},{9,8},{10,11... | collective-permute-start | bytes 552968 | tf_op jit(solution)/shard_map/ppermute | solution.py:188
  23.8 0.0 collective-permute-start.8
  23.8 1.8 %far.1 = (f32[256,1152]{1,0:T(8,128)S(1)}, f32[256,1152]{1,0:T(8,128)S(1)}, f32[1,256]{1,0:T(1,128)S(1)}) custom-call(s32[1]{0:T(128)} %bitcast.flags, f32[2]{0:T(128)S(1)} %pad_maximum_fusion.params, s32[1,256]{1,0:T(1,128)S(1)} %bitcast.6, s32[1,256]{1,0:T(1,128)S(1)} %collective-permute-done.mate_ids, s32[2,256]{1,0:T(2,128)S(1)} %ids.1.token.both_ids, ...), custom_call_target="tpu_custom_call" | custom-call | tf_op jit(solution)/shard_map/far/pallas_call | solution.py:147
  25.6 0.0 collective-permute-done.7.near_b
  25.7 0.0 collective-permute-done.6.near_a
  25.7 2.4 %near.1 = (bf16[256,1152]{1,0:T(8,128)(2,1)}, f32[1,256]{1,0:T(1,128)}) custom-call(s32[1]{0:T(128)} %bitcast.flags, f32[2]{0:T(128)S(1)} %pad_maximum_fusion.params, s32[1,256]{1,0:T(1,128)S(1)} %bitcast.7, s32[1,256]{1,0:T(1,128)S(1)} %collective-permute-done.mate_ids, s32[2,256]{1,0:T(2,128)S(1)} %ids.1.token.both_ids, ...), custom_call_target="tpu_custom_call" | custom-call | tf_op jit(solution)/shard_map/near/pallas_call | solution.py:147
  28.1 4.5 %collective-permute-done.9.arrived = bf16[192,1152]{1,0:T(8,128)(2,1)S(1)} collective-permute-done((bf16[192,1152]{1,0:T(8,128)(2,1)S(1)}, bf16[192,1152]{1,0:T(8,128)(2,1)S(1)}, u32[]{:S(2)}, u32[]{:S(2)}) %collective-permute-start.9) | collective-permute-done | bytes 442400 | tf_op jit(solution)/shard_map/ppermute | solution.py:185
  32.6 1.0 %add_a.1.refs_0_ = f32[256,1152]{1,0:T(8,128)} custom-call(bf16[192,1152]{1,0:T(8,128)(2,1)S(1)} %collective-permute-done.9.arrived, f32[256,1152]{1,0:T(8,128)S(1)} %get-tuple-element.31.late), custom_call_target="tpu_custom_call" | custom-call | tf_op jit(solution)/shard_map/add_a/pallas_call | solution.py:159
  33.7 0.5 %collective-permute-done.8.arrived = bf16[64,1152]{1,0:T(8,128)(2,1)S(1)} collective-permute-done((bf16[64,1152]{1,0:T(8,128)(2,1)S(1)}, bf16[64,1152]{1,0:T(8,128)(2,1)S(1)}, u32[]{:S(2)}, u32[]{:S(2)}) %collective-permute-start.8) | collective-permute-done | bytes 147488 | tf_op jit(solution)/shard_map/ppermute | solution.py:227
  34.1 0.7 %add_b.1 = f32[256,1152]{1,0:T(8,128)} custom-call(bf16[64,1152]{1,0:T(8,128)(2,1)S(1)} %collective-permute-done.8.arrived, f32[256,1152]{1,0:T(8,128)S(1)} %get-tuple-element.31.late, f32[256,1152]{1,0:T(8,128)} %add_a.1.refs_0_), custom_call_target="tpu_custom_call", output_to_operand_aliasing={{}: (2, {})} | custom-call | tf_op jit(solution)/shard_map/add_b/pallas_call | solution.py:159
  (2 shorter events, 0.0 us)
Async XLA Ops:
  0.6 1.3 %copy-start = (f32[256,1152]{1,0:T(8,128)S(1)}, f32[256,1152]{1,0:T(8,128)}, u32[]{:S(2)}) copy-start(f32[256,1152]{1,0:T(8,128)} %text.1) | copy-start | bytes 3538948
  1.9 4.7 %copy-start.1 = (s32[256]{0:T(256)S(1)}, s32[256]{0:T(256)}, u32[]{:S(2)}) copy-start(s32[256]{0:T(256)} %param.9) | copy-start | bytes 3076
  2.0 21.2 %collective-permute-start.5 = (bf16[256,1152]{1,0:T(8,128)(2,1)S(1)}, bf16[256,1152]{1,0:T(8,128)(2,1)S(1)}, u32[]{:S(2)}, u32[]{:S(2)}) collective-permute-start(bf16[256,1152]{1,0:T(8,128)(2,1)S(1)} %cast.1.text), channel_id=1, source_target_pairs={{0,2},{1,3},{2,4},{3,5},{4,6},{5,7},{6,8},{7,9},{8,10},{9,11},{10,... | collective-permute-start | bytes 1769480 | tf_op jit(solution)/shard_map/ppermute | solution.py:185
  6.1 3.6 %collective-permute-start.1 = (bf16[128,1152]{1,0:T(8,128)(2,1)S(1)}, bf16[128,1152]{1,0:T(8,128)(2,1)S(1)}, u32[]{:S(2)}, u32[]{:S(2)}) collective-permute-start(bf16[128,1152]{1,0:T(8,128)(2,1)S(1)} %get-tuple-element.18.image_a), channel_id=1, source_target_pairs={{0,1},{1,0},{2,3},{3,2},{4,5},{5,4},{6,7},{7,6},{8,9},{9,8},{10,11... | collective-permute-start | bytes 884744 | tf_op jit(solution)/shard_map/ppermute | solution.py:188
  6.1 3.5 %collective-permute-start.2 = (bf16[128,1152]{1,0:T(8,128)(2,1)S(1)}, bf16[128,1152]{1,0:T(8,128)(2,1)S(1)}, u32[]{:S(2)}, u32[]{:S(2)}) collective-permute-start(bf16[128,1152]{1,0:T(8,128)(2,1)S(1)} %get-tuple-element.19.image_b), channel_id=1, source_target_pairs={{0,1},{1,0},{2,3},{3,2},{4,5},{5,4},{6,7},{7,6},{8,9},{9,8},{10,11... | collective-permute-start | bytes 884744 | tf_op jit(solution)/shard_map/ppermute | solution.py:188
  6.6 1.5 %collective-permute-start = (s32[1,256]{1,0:T(1,128)S(1)}, s32[1,256]{1,0:T(1,128)S(1)}, u32[]{:S(2)}, u32[]{:S(2)}) collective-permute-start(s32[1,256]{1,0:T(1,128)S(1)} %bitcast.3), channel_id=1, source_target_pairs={{0,1},{1,0},{2,3},{3,2},{4,5},{5,4},{6,7},{7,6},{8,9},{9,8},{10,11... | collective-permute-start | bytes 3080 | tf_op jit(solution)/shard_map/ppermute | solution.py:188
  8.1 15.0 %collective-permute-start.3 = (s32[2,256]{1,0:T(2,128)S(1)}, s32[2,256]{1,0:T(2,128)S(1)}, u32[]{:S(2)}, u32[]{:S(2)}) collective-permute-start(s32[2,256]{1,0:T(2,128)S(1)} %pad_add_fusion), channel_id=1, source_target_pairs={{0,2},{1,3},{2,4},{3,5},{4,6},{5,7},{6,8},{7,9},{8,10},{9,11},{10,... | collective-permute-start | bytes 6152 | tf_op jit(solution)/shard_map/ppermute | solution.py:185
  13.5 9.6 %collective-permute-start.4 = (bf16[64,1152]{1,0:T(8,128)(2,1)S(1)}, bf16[64,1152]{1,0:T(8,128)(2,1)S(1)}, u32[]{:S(2)}, u32[]{:S(2)}) collective-permute-start(bf16[64,1152]{1,0:T(8,128)(2,1)S(1)} %get-tuple-element.21), channel_id=1, source_target_pairs={{0,1},{1,0},{2,3},{3,2},{4,5},{5,4},{6,7},{7,6},{8,9},{9,8},{10,11... | collective-permute-start | bytes 442376 | tf_op jit(solution)/shard_map/ppermute | solution.py:188
  13.6 19.0 %collective-permute-start.9 = (bf16[192,1152]{1,0:T(8,128)(2,1)S(1)}, bf16[192,1152]{1,0:T(8,128)(2,1)S(1)}, u32[]{:S(2)}, u32[]{:S(2)}) collective-permute-start(bf16[192,1152]{1,0:T(8,128)(2,1)S(1)} %get-tuple-element.32), channel_id=1, source_target_pairs={{0,2},{1,3},{2,4},{3,5},{4,6},{5,7},{6,8},{7,9},{8,10},{9,11},{10,... | collective-permute-start | bytes 1327112 | tf_op jit(solution)/shard_map/ppermute | solution.py:185
  23.2 2.4 %collective-permute-start.6 = (bf16[176,1152]{1,0:T(8,128)(2,1)S(1)}, bf16[176,1152]{1,0:T(8,128)(2,1)S(1)}, u32[]{:S(2)}, u32[]{:S(2)}) collective-permute-start(bf16[176,1152]{1,0:T(8,128)(2,1)S(1)} %get-tuple-element.22), channel_id=1, source_target_pairs={{0,1},{1,0},{2,3},{3,2},{4,5},{5,4},{6,7},{7,6},{8,9},{9,8},{10,11... | collective-permute-start | bytes 1216520 | tf_op jit(solution)/shard_map/ppermute | solution.py:188
  23.3 2.3 %collective-permute-start.7 = (bf16[80,1152]{1,0:T(8,128)(2,1)S(1)}, bf16[80,1152]{1,0:T(8,128)(2,1)S(1)}, u32[]{:S(2)}, u32[]{:S(2)}) collective-permute-start(bf16[80,1152]{1,0:T(8,128)(2,1)S(1)} %get-tuple-element.23), channel_id=1, source_target_pairs={{0,1},{1,0},{2,3},{3,2},{4,5},{5,4},{6,7},{7,6},{8,9},{9,8},{10,11... | collective-permute-start | bytes 552968 | tf_op jit(solution)/shard_map/ppermute | solution.py:188
  23.8 10.3 %collective-permute-start.8 = (bf16[64,1152]{1,0:T(8,128)(2,1)S(1)}, bf16[64,1152]{1,0:T(8,128)(2,1)S(1)}, u32[]{:S(2)}, u32[]{:S(2)}) collective-permute-start(bf16[64,1152]{1,0:T(8,128)(2,1)S(1)} %collective-permute-done.4.before), channel_id=1, source_target_pairs={{0,3},{1,2},{2,5},{3,4},{4,7},{5,6},{6,9},{7,8},{8,11},{9,10},{10,... | collective-permute-start | bytes 442376 | tf_op jit(solution)/shard_map/ppermute | solution.py:227

commit v23 on v22

--- a/solution.py
+++ b/solution.py
@@ -71,8 +71,8 @@
         copy.wait()
 
 
-def own_kernel(flags, params, ids, mate_ids, image_a, image_b, mate_a, mate_b, text, accum_in, out_a, out_b, image_sum, loss,
-               accum, sem):
+def own_kernel(flags, params, ids, mate_ids, image_a, image_b, mate_a, mate_b, text, accum_in, out_a, out_b, out_c,
+               image_sum, loss, accum, sem):
     copy = pltpu.make_async_copy(accum_in, accum, sem)
     copy.start()
     image = whole(image_a, image_b)
@@ -84,7 +84,8 @@
 
     def give(value):
         out_a[...] = value[:cut, :].astype(out_a.dtype)
-        out_b[...] = value[cut:, :].astype(out_b.dtype)
+        out_b[...] = value[cut:cut + out_b.shape[0], :].astype(out_b.dtype)
+        out_c[...] = value[cut + out_b.shape[0]:, :].astype(out_c.dtype)
 
     @pl.when(flags[0] == 0)
     def _():
@@ -103,7 +104,7 @@
     out[...] = both_ids[...]
 
 
-def relay_kernel(flags, token, before, text, far, out_a, out_b):
+def relay_kernel(flags, token, before_b, before_c, text, far, out_a, out_b):
     cut = out_a.shape[0]
 
     def fill(source):
@@ -205,16 +206,17 @@
     both_ids = ahead(jnp.concatenate([ids, mate_ids]))
 
     cut = rows - rows // 4
-    out_a, out_b, image_sum, loss = pl.pallas_call(
+    out_a, out_b, out_c, image_sum, loss = pl.pallas_call(
         own_kernel,
         out_shape=[
             jax.ShapeDtypeStruct((cut, width), bf16),
-            jax.ShapeDtypeStruct((rows - cut, width), bf16),
+            jax.ShapeDtypeStruct((rows - cut - STEP, width), bf16),
+            jax.ShapeDtypeStruct((STEP, width), bf16),
             jax.ShapeDtypeStruct((rows, width), f32),
             jax.ShapeDtypeStruct((1, rows), f32),
         ],
         in_specs=[SMEM] * 2 + [VMEM] * 7 + [HBM],
-        out_specs=[VMEM] * 4,
+        out_specs=[VMEM] * 5,
         scratch_shapes=[pltpu.VMEM((rows, width), f32), pltpu.SemaphoreType.DMA],
         compiler_params=pltpu.CompilerParams(vmem_limit_bytes=16 * 1024 * 1024),
         cost_estimate=pl.CostEstimate(flops=0, bytes_accessed=0, transcendentals=0),
@@ -223,13 +225,13 @@
       pltpu.with_memory_space_constraint(text_accum, pltpu.HBM))
     crossed = [(i, target ^ 1) for i, target in skip]
     arrived_a = ahead(out_a)
-    mate_rows = across(out_b)
-    arrived_b = lax.ppermute(mate_rows, AXES, crossed)
+    mate_rows, mate_last = across(out_b), across(out_c)
+    arrived_b, arrived_c = (lax.ppermute(part, AXES, crossed) for part in (mate_rows, mate_last))
 
     (both_ids,) = call(ids_kernel, "ids", [((2, rows), jnp.int32)], (), loss, both_ids, flops=2 << 30)
     passed_a, passed_b = call(
         relay_kernel, "relay", [((cut - 16, width), bf16), ((rows - cut + 16, width), bf16)],
-        (flags,), both_ids, mate_rows, text, far, flops=1 << 30,
+        (flags,), both_ids, mate_rows, mate_last, text, far, flops=1 << 30,
     )
     near_a, near_b = across(passed_a), across(passed_b)
     late, image_sum, loss = call(
@@ -243,7 +245,8 @@
     )
     late, image_grad = lax.optimization_barrier((late, image_grad))
     text_grad = add_part("add_a", 0, cut // STEP, arrived_a, late)
-    text_grad = add_part("add_b", cut, (rows - cut) // STEP, arrived_b, late, text_grad)
+    text_grad = add_part("add_b", cut, (rows - cut) // STEP - 1, arrived_b, late, text_grad)
+    text_grad = add_part("add_c", rows - STEP, 1, arrived_c, late, text_grad)
     return (loss.reshape(rows), image_grad, text_grad)
 
 

time: 35.3 us -> 35.6 us (level)
  waiting for transfers between devices: 13.1 us -> 12.1 us
  Pallas kernels: 11 us -> 11.7 us
  starting transfers between devices: 7.34 us -> 7.94 us
    pallas_call x2 -> x3, Pallas kernels: 1.77 us -> 2.4 us  [add_part(): pl.pallas_call(functools.partial(add_kernel, start, chunks), out_shape=ja...]
    ppermute x3, waiting for transfers between devices: 12.5 us -> 11.9 us  [ahead(): return lax.ppermute(value, AXES, skip)]
    ppermute x6 -> x7, starting transfers between devices: 1.29 us -> 1.78 us  [across(): return lax.ppermute(value, AXES, swap)]
    ppermute x1 -> x2, waiting for transfers between devices: 0.47 us -> 0.01 us  [body(): lax.ppermute(part, AXES, crossed)]
  transfers between devices with their start and end apart: 10 -> 12, of which waited for: 4 -> 3; matrix products, arithmetic and copies ran while one was open for 0% -> 0% of each run, Pallas kernels for 29% -> 31%
where the time goes in v23:
time: 35.6 us; the launch traced here: 35.1 us
  waiting for transfers between devices  12.1 us (34%)
  Pallas kernels  11.7 us (33%)
  starting transfers between devices  7.94 us (22%)
  between operations  2.07 us (6%)
  local copies, waits for them, and re-layouts  1.27 us (4%)
    ppermute x3, waiting for transfers between devices, ahead(): return lax.ppermute(value, AXES, skip)  11.9 us
    ppermute x3, starting transfers between devices, ahead(): return lax.ppermute(value, AXES, skip)  6 us
    pallas_call x5, Pallas kernels, call(): pl.pallas_call(kernel, out_shape=[jax.ShapeDtypeStruct(s, d) for s, d in...  4.37 us
    pallas_call x1, Pallas kernels, body(): pl.pallas_call(own_kernel, out_shape=[jax.ShapeDtypeStruct((cut, width),...  3.82 us
    pallas_call x3, Pallas kernels, add_part(): pl.pallas_call(functools.partial(add_kernel, start, chunks), out_shape=ja...  2.4 us
    ppermute x7, starting transfers between devices, across(): return lax.ppermute(value, AXES, swap)  1.78 us
    unnamed x4, local copies, waits for them, and re-layouts  1.27 us
    pallas_call x1, Pallas kernels, body(): pl.pallas_call(load_kernel, out_shape=[jax.ShapeDtypeStruct((n, width), b...  1.07 us
  transfers between devices with their start and end apart: 12, of which 3 were waited for; matrix products, arithmetic and copies ran while one was open for 0% of the time, Pallas kernels for 31%

profile of v23, /device:TPU:0, one launch (start us, length us, event | category | flops | bytes accessed | tf_op | source)
XLA Modules:
  0.0 35.1 jit_solution(404510454108979562)
XLA Ops:
  0.6 0.0 copy-start
  0.6 1.3 %copy-done = f32[256,1152]{1,0:T(8,128)S(1)} copy-done((f32[256,1152]{1,0:T(8,128)S(1)}, f32[256,1152]{1,0:T(8,128)}, u32[]{:S(2)}) %copy-start) | copy-done | bytes 1179672
  1.9 0.0 copy-start.1
  1.9 0.1 cast.1.text
  2.0 3.0 %collective-permute-start.6 = (bf16[256,1152]{1,0:T(8,128)(2,1)S(1)}, bf16[256,1152]{1,0:T(8,128)(2,1)S(1)}, u32[]{:S(2)}, u32[]{:S(2)}) collective-permute-start(bf16[256,1152]{1,0:T(8,128)(2,1)S(1)} %cast.1.text), channel_id=1, source_target_pairs={{0,2},{1,3},{2,4},{3,5},{4,6},{5,7},{6,8},{7,9},{8,10},{9,11},{10,... | collective-permute-start | bytes 1769480 | tf_op jit(solution)/shard_map/ppermute | solution.py:186
  5.0 1.1 %load.1 = (bf16[128,1152]{1,0:T(8,128)(2,1)S(1)}, bf16[128,1152]{1,0:T(8,128)(2,1)S(1)}) custom-call(bf16[256,1152]{1,0:T(8,128)(2,1)S(1)} %cast.1.text, bf16[256,1152]{1,0:T(8,128)(2,1)} %image.1), custom_call_target="tpu_custom_call" | custom-call | tf_op jit(solution)/shard_map/load/pallas_call | solution.py:194
  6.1 0.1 collective-permute-start.1
  6.1 0.5 %collective-permute-start.2 = (bf16[128,1152]{1,0:T(8,128)(2,1)S(1)}, bf16[128,1152]{1,0:T(8,128)(2,1)S(1)}, u32[]{:S(2)}, u32[]{:S(2)}) collective-permute-start(bf16[128,1152]{1,0:T(8,128)(2,1)S(1)} %get-tuple-element.20.image_b), channel_id=1, source_target_pairs={{0,1},{1,0},{2,3},{3,2},{4,5},{5,4},{6,7},{7,6},{8,9},{9,8},{10,11... | collective-permute-start | bytes 884744 | tf_op jit(solution)/shard_map/ppermute | solution.py:189
  6.6 0.0 copy-done.1
  6.6 0.1 collective-permute-start
  8.0 0.1 collective-permute-done.mate_ids
  8.1 1.5 %collective-permute-start.3 = (s32[2,256]{1,0:T(2,128)S(1)}, s32[2,256]{1,0:T(2,128)S(1)}, u32[]{:S(2)}, u32[]{:S(2)}) collective-permute-start(s32[2,256]{1,0:T(2,128)S(1)} %pad_add_fusion), channel_id=1, source_target_pairs={{0,2},{1,3},{2,4},{3,5},{4,6},{5,7},{6,8},{7,9},{8,10},{9,11},{10,... | collective-permute-start | bytes 6152 | tf_op jit(solution)/shard_map/ppermute | solution.py:186
  9.6 0.1 pad_maximum_fusion.params
  9.7 0.0 collective-permute-done.1.mate_a
  9.7 0.0 collective-permute-done.2.mate_b
  9.7 3.8 %own.1 = (bf16[192,1152]{1,0:T(8,128)(2,1)S(1)}, bf16[48,1152]{1,0:T(8,128)(2,1)S(1)}, bf16[16,1152]{1,0:T(8,128)(2,1)S(1)}, f32[256,1152]{1,0:T(8,128)S(1)}, f32[1,256]{1,0:T(1,128)S(1)}) custom-call(s32[1]{0:T(128)} %bitcast.flags, f32[2]{0:T(128)S(1)} %pad_maximum_fusion.params, s32[1,256]{1,0:T(1,128)S(1)} %bitcast.5, ...), custom_call_target="tpu_custom_call" | custom-call | tf_op jit(solution)/shard_map/own/pallas_call | solution.py:209
  13.5 0.1 collective-permute-start.5
  13.6 0.5 %collective-permute-start.4 = (bf16[48,1152]{1,0:T(8,128)(2,1)S(1)}, bf16[48,1152]{1,0:T(8,128)(2,1)S(1)}, u32[]{:S(2)}, u32[]{:S(2)}) collective-permute-start(bf16[48,1152]{1,0:T(8,128)(2,1)S(1)} %get-tuple-element.22), channel_id=1, source_target_pairs={{0,1},{1,0},{2,3},{3,2},{4,5},{5,4},{6,7},{7,6},{8,9},{9,8},{10,11... | collective-permute-start | bytes 331784 | tf_op jit(solution)/shard_map/ppermute | solution.py:189
  14.1 1.5 %collective-permute-start.11 = (bf16[192,1152]{1,0:T(8,128)(2,1)S(1)}, bf16[192,1152]{1,0:T(8,128)(2,1)S(1)}, u32[]{:S(2)}, u32[]{:S(2)}) collective-permute-start(bf16[192,1152]{1,0:T(8,128)(2,1)S(1)} %get-tuple-element.34), channel_id=1, source_target_pairs={{0,2},{1,3},{2,4},{3,5},{4,6},{5,7},{6,8},{7,9},{8,10},{9,11},{10,... | collective-permute-start | bytes 1327112 | tf_op jit(solution)/shard_map/ppermute | solution.py:186
  15.6 7.5 %collective-permute-done.3.both_ids = s32[2,256]{1,0:T(2,128)S(1)} collective-permute-done((s32[2,256]{1,0:T(2,128)S(1)}, s32[2,256]{1,0:T(2,128)S(1)}, u32[]{:S(2)}, u32[]{:S(2)}) %collective-permute-start.3) | collective-permute-done | bytes 2080 | tf_op jit(solution)/shard_map/ppermute | solution.py:186
  23.2 0.0 collective-permute-done.5.before_c
  23.2 0.0 collective-permute-done.4.before_b
  23.2 0.0 collective-permute-done.6.far
  23.2 0.1 relay.1
  23.2 0.1 collective-permute-start.7
  23.3 0.5 %collective-permute-start.8 = (bf16[80,1152]{1,0:T(8,128)(2,1)S(1)}, bf16[80,1152]{1,0:T(8,128)(2,1)S(1)}, u32[]{:S(2)}, u32[]{:S(2)}) collective-permute-start(bf16[80,1152]{1,0:T(8,128)(2,1)S(1)} %get-tuple-element.25), channel_id=1, source_target_pairs={{0,1},{1,0},{2,3},{3,2},{4,5},{5,4},{6,7},{7,6},{8,9},{9,8},{10,11... | collective-permute-start | bytes 552968 | tf_op jit(solution)/shard_map/ppermute | solution.py:189
  23.8 0.0 collective-permute-start.10
  23.8 0.2 collective-permute-start.9
  24.0 1.8 %far.1 = (f32[256,1152]{1,0:T(8,128)S(1)}, f32[256,1152]{1,0:T(8,128)S(1)}, f32[1,256]{1,0:T(1,128)S(1)}) custom-call(s32[1]{0:T(128)} %bitcast.flags, f32[2]{0:T(128)S(1)} %pad_maximum_fusion.params, s32[1,256]{1,0:T(1,128)S(1)} %bitcast.6, s32[1,256]{1,0:T(1,128)S(1)} %collective-permute-done.mate_ids, s32[2,256]{1,0:T(2,128)S(1)} %ids.1.token.both_ids, ...), custom_call_target="tpu_custom_call" | custom-call | tf_op jit(solution)/shard_map/far/pallas_call | solution.py:148
  25.8 0.0 collective-permute-done.8.near_b
  25.8 0.0 collective-permute-done.7.near_a
  25.8 2.4 %near.1 = (bf16[256,1152]{1,0:T(8,128)(2,1)}, f32[1,256]{1,0:T(1,128)}) custom-call(s32[1]{0:T(128)} %bitcast.flags, f32[2]{0:T(128)S(1)} %pad_maximum_fusion.params, s32[1,256]{1,0:T(1,128)S(1)} %bitcast.7, s32[1,256]{1,0:T(1,128)S(1)} %collective-permute-done.mate_ids, s32[2,256]{1,0:T(2,128)S(1)} %ids.1.token.both_ids, ...), custom_call_target="tpu_custom_call" | custom-call | tf_op jit(solution)/shard_map/near/pallas_call | solution.py:148
  28.3 4.4 %collective-permute-done.11.arrived = bf16[192,1152]{1,0:T(8,128)(2,1)S(1)} collective-permute-done((bf16[192,1152]{1,0:T(8,128)(2,1)S(1)}, bf16[192,1152]{1,0:T(8,128)(2,1)S(1)}, u32[]{:S(2)}, u32[]{:S(2)}) %collective-permute-start.11) | collective-permute-done | bytes 442400 | tf_op jit(solution)/shard_map/ppermute | solution.py:186
  32.6 1.0 %add_a.1.refs_0_ = f32[256,1152]{1,0:T(8,128)} custom-call(bf16[192,1152]{1,0:T(8,128)(2,1)S(1)} %collective-permute-done.11.arrived, f32[256,1152]{1,0:T(8,128)S(1)} %get-tuple-element.33.late), custom_call_target="tpu_custom_call" | custom-call | tf_op jit(solution)/shard_map/add_a/pallas_call | solution.py:160
  33.7 0.0 collective-permute-done.10.arrived
  33.7 0.7 %add_b.1.refs_0_ = f32[256,1152]{1,0:T(8,128)} custom-call(bf16[48,1152]{1,0:T(8,128)(2,1)S(1)} %collective-permute-done.10.arrived, f32[256,1152]{1,0:T(8,128)S(1)} %get-tuple-element.33.late, f32[256,1152]{1,0:T(8,128)} %add_a.1.refs_0_), custom_call_target="tpu_custom_call", output_to_operand_aliasing={{}: (2, {})} | custom-call | tf_op jit(solution)/shard_map/add_b/pallas_call | solution.py:160
  34.4 0.0 collective-permute-done.9.arrived
  34.4 0.7 %add_c.1 = f32[256,1152]{1,0:T(8,128)} custom-call(bf16[16,1152]{1,0:T(8,128)(2,1)S(1)} %collective-permute-done.9.arrived, f32[256,1152]{1,0:T(8,128)S(1)} %get-tuple-element.33.late, f32[256,1152]{1,0:T(8,128)} %add_b.1.refs_0_), custom_call_target="tpu_custom_call", output_to_operand_aliasing={{}: (2, {})} | custom-call | tf_op jit(solution)/shard_map/add_c/pallas_call | solution.py:160
  (2 shorter events, 0.0 us)
Async XLA Ops:
  0.6 1.3 %copy-start = (f32[256,1152]{1,0:T(8,128)S(1)}, f32[256,1152]{1,0:T(8,128)}, u32[]{:S(2)}) copy-start(f32[256,1152]{1,0:T(8,128)} %text.1) | copy-start | bytes 3538948
  1.9 4.7 %copy-start.1 = (s32[256]{0:T(256)S(1)}, s32[256]{0:T(256)}, u32[]{:S(2)}) copy-start(s32[256]{0:T(256)} %param.9) | copy-start | bytes 3076
  2.0 21.2 %collective-permute-start.6 = (bf16[256,1152]{1,0:T(8,128)(2,1)S(1)}, bf16[256,1152]{1,0:T(8,128)(2,1)S(1)}, u32[]{:S(2)}, u32[]{:S(2)}) collective-permute-start(bf16[256,1152]{1,0:T(8,128)(2,1)S(1)} %cast.1.text), channel_id=1, source_target_pairs={{0,2},{1,3},{2,4},{3,5},{4,6},{5,7},{6,8},{7,9},{8,10},{9,11},{10,... | collective-permute-start | bytes 1769480 | tf_op jit(solution)/shard_map/ppermute | solution.py:186
  6.1 3.6 %collective-permute-start.1 = (bf16[128,1152]{1,0:T(8,128)(2,1)S(1)}, bf16[128,1152]{1,0:T(8,128)(2,1)S(1)}, u32[]{:S(2)}, u32[]{:S(2)}) collective-permute-start(bf16[128,1152]{1,0:T(8,128)(2,1)S(1)} %get-tuple-element.19.image_a), channel_id=1, source_target_pairs={{0,1},{1,0},{2,3},{3,2},{4,5},{5,4},{6,7},{7,6},{8,9},{9,8},{10,11... | collective-permute-start | bytes 884744 | tf_op jit(solution)/shard_map/ppermute | solution.py:189
  6.1 3.5 %collective-permute-start.2 = (bf16[128,1152]{1,0:T(8,128)(2,1)S(1)}, bf16[128,1152]{1,0:T(8,128)(2,1)S(1)}, u32[]{:S(2)}, u32[]{:S(2)}) collective-permute-start(bf16[128,1152]{1,0:T(8,128)(2,1)S(1)} %get-tuple-element.20.image_b), channel_id=1, source_target_pairs={{0,1},{1,0},{2,3},{3,2},{4,5},{5,4},{6,7},{7,6},{8,9},{9,8},{10,11... | collective-permute-start | bytes 884744 | tf_op jit(solution)/shard_map/ppermute | solution.py:189
  6.6 1.5 %collective-permute-start = (s32[1,256]{1,0:T(1,128)S(1)}, s32[1,256]{1,0:T(1,128)S(1)}, u32[]{:S(2)}, u32[]{:S(2)}) collective-permute-start(s32[1,256]{1,0:T(1,128)S(1)} %bitcast.3), channel_id=1, source_target_pairs={{0,1},{1,0},{2,3},{3,2},{4,5},{5,4},{6,7},{7,6},{8,9},{9,8},{10,11... | collective-permute-start | bytes 3080 | tf_op jit(solution)/shard_map/ppermute | solution.py:189
  8.1 15.0 %collective-permute-start.3 = (s32[2,256]{1,0:T(2,128)S(1)}, s32[2,256]{1,0:T(2,128)S(1)}, u32[]{:S(2)}, u32[]{:S(2)}) collective-permute-start(s32[2,256]{1,0:T(2,128)S(1)} %pad_add_fusion), channel_id=1, source_target_pairs={{0,2},{1,3},{2,4},{3,5},{4,6},{5,7},{6,8},{7,9},{8,10},{9,11},{10,... | collective-permute-start | bytes 6152 | tf_op jit(solution)/shard_map/ppermute | solution.py:186
  13.5 9.6 %collective-permute-start.5 = (bf16[16,1152]{1,0:T(8,128)(2,1)S(1)}, bf16[16,1152]{1,0:T(8,128)(2,1)S(1)}, u32[]{:S(2)}, u32[]{:S(2)}) collective-permute-start(bf16[16,1152]{1,0:T(8,128)(2,1)S(1)} %get-tuple-element.23), channel_id=1, source_target_pairs={{0,1},{1,0},{2,3},{3,2},{4,5},{5,4},{6,7},{7,6},{8,9},{9,8},{10,11... | collective-permute-start | bytes 110600 | tf_op jit(solution)/shard_map/ppermute | solution.py:189
  13.6 9.6 %collective-permute-start.4 = (bf16[48,1152]{1,0:T(8,128)(2,1)S(1)}, bf16[48,1152]{1,0:T(8,128)(2,1)S(1)}, u32[]{:S(2)}, u32[]{:S(2)}) collective-permute-start(bf16[48,1152]{1,0:T(8,128)(2,1)S(1)} %get-tuple-element.22), channel_id=1, source_target_pairs={{0,1},{1,0},{2,3},{3,2},{4,5},{5,4},{6,7},{7,6},{8,9},{9,8},{10,11... | collective-permute-start | bytes 331784 | tf_op jit(solution)/shard_map/ppermute | solution.py:189
  14.1 18.5 %collective-permute-start.11 = (bf16[192,1152]{1,0:T(8,128)(2,1)S(1)}, bf16[192,1152]{1,0:T(8,128)(2,1)S(1)}, u32[]{:S(2)}, u32[]{:S(2)}) collective-permute-start(bf16[192,1152]{1,0:T(8,128)(2,1)S(1)} %get-tuple-element.34), channel_id=1, source_target_pairs={{0,2},{1,3},{2,4},{3,5},{4,6},{5,7},{6,8},{7,9},{8,10},{9,11},{10,... | collective-permute-start | bytes 1327112 | tf_op jit(solution)/shard_map/ppermute | solution.py:186
  23.2 2.6 %collective-permute-start.7 = (bf16[176,1152]{1,0:T(8,128)(2,1)S(1)}, bf16[176,1152]{1,0:T(8,128)(2,1)S(1)}, u32[]{:S(2)}, u32[]{:S(2)}) collective-permute-start(bf16[176,1152]{1,0:T(8,128)(2,1)S(1)} %get-tuple-element.24), channel_id=1, source_target_pairs={{0,1},{1,0},{2,3},{3,2},{4,5},{5,4},{6,7},{7,6},{8,9},{9,8},{10,11... | collective-permute-start | bytes 1216520 | tf_op jit(solution)/shard_map/ppermute | solution.py:189
  23.3 2.5 %collective-permute-start.8 = (bf16[80,1152]{1,0:T(8,128)(2,1)S(1)}, bf16[80,1152]{1,0:T(8,128)(2,1)S(1)}, u32[]{:S(2)}, u32[]{:S(2)}) collective-permute-start(bf16[80,1152]{1,0:T(8,128)(2,1)S(1)} %get-tuple-element.25), channel_id=1, source_target_pairs={{0,1},{1,0},{2,3},{3,2},{4,5},{5,4},{6,7},{7,6},{8,9},{9,8},{10,11... | collective-permute-start | bytes 552968 | tf_op jit(solution)/shard_map/ppermute | solution.py:189
  23.8 9.8 %collective-permute-start.10 = (bf16[48,1152]{1,0:T(8,128)(2,1)S(1)}, bf16[48,1152]{1,0:T(8,128)(2,1)S(1)}, u32[]{:S(2)}, u32[]{:S(2)}) collective-permute-start(bf16[48,1152]{1,0:T(8,128)(2,1)S(1)} %collective-permute-done.4.before_b), channel_id=1, source_target_pairs={{0,3},{1,2},{2,5},{3,4},{4,7},{5,6},{6,9},{7,8},{8,11},{9,10},{10,... | collective-permute-start | bytes 331784 | tf_op jit(solution)/shard_map/ppermute | solution.py:229
  23.8 10.6 %collective-permute-start.9 = (bf16[16,1152]{1,0:T(8,128)(2,1)S(1)}, bf16[16,1152]{1,0:T(8,128)(2,1)S(1)}, u32[]{:S(2)}, u32[]{:S(2)}) collective-permute-start(bf16[16,1152]{1,0:T(8,128)(2,1)S(1)} %collective-permute-done.5.before_c), channel_id=1, source_target_pairs={{0,3},{1,2},{2,5},{3,4},{4,7},{5,6},{6,9},{7,8},{8,11},{9,10},{10,... | collective-permute-start | bytes 110600 | tf_op jit(solution)/shard_map/ppermute | solution.py:229

commit v24 on v18

--- a/solution.py
+++ b/solution.py
@@ -10,6 +10,7 @@
 SHIFTS = 2
 AXES = ("dp", "group")
 STEP = 16
+CHUNKS = 4
 VMEM = pl.BlockSpec(memory_space=pltpu.VMEM)
 SMEM = pl.BlockSpec(memory_space=pltpu.SMEM)
 ANY = pl.BlockSpec(memory_space=pl.ANY)
@@ -42,8 +43,15 @@
     return coef.astype(jnp.bfloat16)
 
 
-def cast_kernel(text, out):
-    out[...] = text[...].astype(out.dtype)
+def cast_kernel(text, out, staged, sems):
+    step = text.shape[0] // CHUNKS
+    parts = [pl.ds(k * step, step) for k in range(CHUNKS)]
+    copies = [pltpu.make_async_copy(text.at[part], staged.at[part], sems.at[k]) for k, part in enumerate(parts)]
+    for k, copy in enumerate(copies):
+        copy.start(priority=k % 2)
+    for part, copy in zip(parts, copies):
+        copy.wait()
+        out[part, :] = staged[part, :].astype(out.dtype)
 
 
 def load_kernel(text, image, out_a, out_b, sems):
@@ -187,7 +195,16 @@
     def across(value):
         return lax.ppermute(value, AXES, swap)
 
-    (text,) = call(cast_kernel, "cast", [((rows, width), bf16)], (), text_emb)
+    text = pl.pallas_call(
+        cast_kernel,
+        out_shape=jax.ShapeDtypeStruct((rows, width), bf16),
+        in_specs=[HBM],
+        out_specs=VMEM,
+        scratch_shapes=[pltpu.VMEM((rows, width), f32), pltpu.SemaphoreType.DMA((CHUNKS,))],
+        compiler_params=pltpu.CompilerParams(vmem_limit_bytes=16 * 1024 * 1024),
+        cost_estimate=pl.CostEstimate(flops=0, bytes_accessed=0, transcendentals=0),
+        name="cast",
+    )(pltpu.with_memory_space_constraint(text_emb, pltpu.HBM))
     far = ahead(text)
 
     image_a, image_b = pl.pallas_call(

time: 35.4 us -> 35.4 us (level)
  Pallas kernels: 11 us -> 12.3 us
  local copies, waits for them, and re-layouts: 1.27 us -> 0.01 us
    pallas_call x0 -> x1, Pallas kernels: none -> 1.28 us  [body(): pl.pallas_call(cast_kernel, out_shape=jax.ShapeDtypeStruct((rows, width),...]
    unnamed x4 -> x2, local copies, waits for them, and re-layouts: 1.27 us -> 0.01 us
    pallas_call x5 -> x4, Pallas kernels: 4.37 us -> 4.31 us  [call(): pl.pallas_call(kernel, out_shape=[jax.ShapeDtypeStruct(s, d) for s, d in...]
where the time goes in v24:
time: 35.4 us; the launch traced here: 35.2 us
  waiting for transfers between devices  13.4 us (38%)
  Pallas kernels  12.3 us (35%)
  starting transfers between devices  7.34 us (21%)
  between operations  2.04 us (6%)
    ppermute x3, waiting for transfers between devices, ahead(): return lax.ppermute(value, AXES, skip)  13.3 us
    ppermute x3, starting transfers between devices, ahead(): return lax.ppermute(value, AXES, skip)  6.05 us
    pallas_call x4, Pallas kernels, call(): pl.pallas_call(kernel, out_shape=[jax.ShapeDtypeStruct(s, d) for s, d in...  4.31 us
    pallas_call x1, Pallas kernels, body(): pl.pallas_call(own_kernel, out_shape=[jax.ShapeDtypeStruct((cut, width),...  3.82 us
    pallas_call x2, Pallas kernels, add_part(): pl.pallas_call(functools.partial(add_kernel, start, chunks), out_shape=ja...  1.77 us
    ppermute x6, starting transfers between devices, across(): return lax.ppermute(value, AXES, swap)  1.29 us
    pallas_call x1, Pallas kernels, body(): pl.pallas_call(cast_kernel, out_shape=jax.ShapeDtypeStruct((rows, width),...  1.28 us
    pallas_call x1, Pallas kernels, body(): pl.pallas_call(load_kernel, out_shape=[jax.ShapeDtypeStruct((n, width), b...  1.07 us
  transfers between devices with their start and end apart: 10, of which 3 were waited for; matrix products, arithmetic and copies ran while one was open for 0% of the time, Pallas kernels for 29%

profile of v24, /device:TPU:0, one launch (start us, length us, event | category | flops | bytes accessed | tf_op | source)
XLA Modules:
  0.0 35.2 jit_solution(9262269294891210494)
XLA Ops:
  0.6 0.0 copy-start
  0.6 1.3 %cast.1.text = bf16[256,1152]{1,0:T(8,128)(2,1)S(1)} custom-call(f32[256,1152]{1,0:T(8,128)} %text.1), custom_call_target="tpu_custom_call" | custom-call | tf_op jit(solution)/shard_map/cast/pallas_call | solution.py:198
  1.9 3.0 %collective-permute-start.5 = (bf16[256,1152]{1,0:T(8,128)(2,1)S(1)}, bf16[256,1152]{1,0:T(8,128)(2,1)S(1)}, u32[]{:S(2)}, u32[]{:S(2)}) collective-permute-start(bf16[256,1152]{1,0:T(8,128)(2,1)S(1)} %cast.1.text), channel_id=1, source_target_pairs={{0,2},{1,3},{2,4},{3,5},{4,6},{5,7},{6,8},{7,9},{8,10},{9,11},{10,... | collective-permute-start | bytes 1769480 | tf_op jit(solution)/shard_map/ppermute | solution.py:193
  5.0 1.1 %load.1 = (bf16[128,1152]{1,0:T(8,128)(2,1)S(1)}, bf16[128,1152]{1,0:T(8,128)(2,1)S(1)}) custom-call(bf16[256,1152]{1,0:T(8,128)(2,1)S(1)} %cast.1.text, bf16[256,1152]{1,0:T(8,128)(2,1)} %image.1), custom_call_target="tpu_custom_call" | custom-call | tf_op jit(solution)/shard_map/load/pallas_call | solution.py:210
  6.0 0.1 collective-permute-start.1
  6.1 0.5 %collective-permute-start.2 = (bf16[128,1152]{1,0:T(8,128)(2,1)S(1)}, bf16[128,1152]{1,0:T(8,128)(2,1)S(1)}, u32[]{:S(2)}, u32[]{:S(2)}) collective-permute-start(bf16[128,1152]{1,0:T(8,128)(2,1)S(1)} %get-tuple-element.19.image_b), channel_id=1, source_target_pairs={{0,1},{1,0},{2,3},{3,2},{4,5},{5,4},{6,7},{7,6},{8,9},{9,8},{10,11... | collective-permute-start | bytes 884744 | tf_op jit(solution)/shard_map/ppermute | solution.py:196
  6.6 0.0 copy-done
  6.6 0.1 collective-permute-start
  8.0 0.1 collective-permute-done.mate_ids
  8.1 1.5 %collective-permute-start.3 = (s32[2,256]{1,0:T(2,128)S(1)}, s32[2,256]{1,0:T(2,128)S(1)}, u32[]{:S(2)}, u32[]{:S(2)}) collective-permute-start(s32[2,256]{1,0:T(2,128)S(1)} %pad_add_fusion), channel_id=1, source_target_pairs={{0,2},{1,3},{2,4},{3,5},{4,6},{5,7},{6,8},{7,9},{8,10},{9,11},{10,... | collective-permute-start | bytes 6152 | tf_op jit(solution)/shard_map/ppermute | solution.py:193
  9.6 0.1 pad_maximum_fusion.params
  9.6 0.0 collective-permute-done.1.mate_a
  9.6 0.0 collective-permute-done.2.mate_b
  9.6 3.8 %own.1 = (bf16[208,1152]{1,0:T(8,128)(2,1)S(1)}, bf16[48,1152]{1,0:T(8,128)(2,1)S(1)}, f32[256,1152]{1,0:T(8,128)S(1)}, f32[1,256]{1,0:T(1,128)S(1)}) custom-call(s32[1]{0:T(128)} %bitcast.flags, f32[2]{0:T(128)S(1)} %pad_maximum_fusion.params, s32[1,256]{1,0:T(1,128)S(1)} %bitcast.5, s32[1,256]{1,0:T(1,128)S(1)} %collective-permute-done.mate_ids, ...), custom_call_target="tpu_custom_call" | custom-call | tf_op jit(solution)/shard_map/own/pallas_call | solution.py:225
  13.5 0.1 collective-permute-start.4
  13.6 1.6 %collective-permute-start.9 = (bf16[208,1152]{1,0:T(8,128)(2,1)S(1)}, bf16[208,1152]{1,0:T(8,128)(2,1)S(1)}, u32[]{:S(2)}, u32[]{:S(2)}) collective-permute-start(bf16[208,1152]{1,0:T(8,128)(2,1)S(1)} %get-tuple-element.32), channel_id=1, source_target_pairs={{0,2},{1,3},{2,4},{3,5},{4,6},{5,7},{6,8},{7,9},{8,10},{9,11},{10,... | collective-permute-start | bytes 1437704 | tf_op jit(solution)/shard_map/ppermute | solution.py:193
  15.1 8.0 %collective-permute-done.3.both_ids = s32[2,256]{1,0:T(2,128)S(1)} collective-permute-done((s32[2,256]{1,0:T(2,128)S(1)}, s32[2,256]{1,0:T(2,128)S(1)}, u32[]{:S(2)}, u32[]{:S(2)}) %collective-permute-start.3) | collective-permute-done | bytes 2080 | tf_op jit(solution)/shard_map/ppermute | solution.py:193
  23.1 0.0 collective-permute-done.4.before
  23.1 0.0 collective-permute-done.5.far
  23.1 0.1 relay.1
  23.2 0.1 collective-permute-start.6
  23.3 0.5 %collective-permute-start.7 = (bf16[64,1152]{1,0:T(8,128)(2,1)S(1)}, bf16[64,1152]{1,0:T(8,128)(2,1)S(1)}, u32[]{:S(2)}, u32[]{:S(2)}) collective-permute-start(bf16[64,1152]{1,0:T(8,128)(2,1)S(1)} %get-tuple-element.23), channel_id=1, source_target_pairs={{0,1},{1,0},{2,3},{3,2},{4,5},{5,4},{6,7},{7,6},{8,9},{9,8},{10,11... | collective-permute-start | bytes 442376 | tf_op jit(solution)/shard_map/ppermute | solution.py:196
  23.8 0.0 collective-permute-start.8
  23.8 1.8 %far.1 = (f32[256,1152]{1,0:T(8,128)S(1)}, f32[256,1152]{1,0:T(8,128)S(1)}, f32[1,256]{1,0:T(1,128)S(1)}) custom-call(s32[1]{0:T(128)} %bitcast.flags, f32[2]{0:T(128)S(1)} %pad_maximum_fusion.params, s32[1,256]{1,0:T(1,128)S(1)} %bitcast.6, s32[1,256]{1,0:T(1,128)S(1)} %collective-permute-done.mate_ids, s32[2,256]{1,0:T(2,128)S(1)} %ids.1.token.both_ids, ...), custom_call_target="tpu_custom_call" | custom-call | tf_op jit(solution)/shard_map/far/pallas_call | solution.py:155
  25.6 0.0 collective-permute-done.7.near_b
  25.6 0.0 collective-permute-done.6.near_a
  25.6 2.4 %near.1 = (bf16[256,1152]{1,0:T(8,128)(2,1)}, f32[1,256]{1,0:T(1,128)}) custom-call(s32[1]{0:T(128)} %bitcast.flags, f32[2]{0:T(128)S(1)} %pad_maximum_fusion.params, s32[1,256]{1,0:T(1,128)S(1)} %bitcast.7, s32[1,256]{1,0:T(1,128)S(1)} %collective-permute-done.mate_ids, s32[2,256]{1,0:T(2,128)S(1)} %ids.1.token.both_ids, ...), custom_call_target="tpu_custom_call" | custom-call | tf_op jit(solution)/shard_map/near/pallas_call | solution.py:155
  28.1 5.3 %collective-permute-done.9.arrived = bf16[208,1152]{1,0:T(8,128)(2,1)S(1)} collective-permute-done((bf16[208,1152]{1,0:T(8,128)(2,1)S(1)}, bf16[208,1152]{1,0:T(8,128)(2,1)S(1)}, u32[]{:S(2)}, u32[]{:S(2)}) %collective-permute-start.9) | collective-permute-done | bytes 479264 | tf_op jit(solution)/shard_map/ppermute | solution.py:193
  33.4 1.1 %add_a.1.refs_0_ = f32[256,1152]{1,0:T(8,128)} custom-call(bf16[208,1152]{1,0:T(8,128)(2,1)S(1)} %collective-permute-done.9.arrived, f32[256,1152]{1,0:T(8,128)S(1)} %get-tuple-element.31.late), custom_call_target="tpu_custom_call" | custom-call | tf_op jit(solution)/shard_map/add_a/pallas_call | solution.py:167
  34.4 0.0 collective-permute-done.8.arrived
  34.5 0.7 %add_b.1 = f32[256,1152]{1,0:T(8,128)} custom-call(bf16[48,1152]{1,0:T(8,128)(2,1)S(1)} %collective-permute-done.8.arrived, f32[256,1152]{1,0:T(8,128)S(1)} %get-tuple-element.31.late, f32[256,1152]{1,0:T(8,128)} %add_a.1.refs_0_), custom_call_target="tpu_custom_call", output_to_operand_aliasing={{}: (2, {})} | custom-call | tf_op jit(solution)/shard_map/add_b/pallas_call | solution.py:167
  (2 shorter events, 0.0 us)
Async XLA Ops:
  0.6 6.0 %copy-start = (s32[256]{0:T(256)S(1)}, s32[256]{0:T(256)}, u32[]{:S(2)}) copy-start(s32[256]{0:T(256)} %param.9) | copy-start | bytes 3076
  1.9 21.2 %collective-permute-start.5 = (bf16[256,1152]{1,0:T(8,128)(2,1)S(1)}, bf16[256,1152]{1,0:T(8,128)(2,1)S(1)}, u32[]{:S(2)}, u32[]{:S(2)}) collective-permute-start(bf16[256,1152]{1,0:T(8,128)(2,1)S(1)} %cast.1.text), channel_id=1, source_target_pairs={{0,2},{1,3},{2,4},{3,5},{4,6},{5,7},{6,8},{7,9},{8,10},{9,11},{10,... | collective-permute-start | bytes 1769480 | tf_op jit(solution)/shard_map/ppermute | solution.py:193
  6.0 3.6 %collective-permute-start.1 = (bf16[128,1152]{1,0:T(8,128)(2,1)S(1)}, bf16[128,1152]{1,0:T(8,128)(2,1)S(1)}, u32[]{:S(2)}, u32[]{:S(2)}) collective-permute-start(bf16[128,1152]{1,0:T(8,128)(2,1)S(1)} %get-tuple-element.18.image_a), channel_id=1, source_target_pairs={{0,1},{1,0},{2,3},{3,2},{4,5},{5,4},{6,7},{7,6},{8,9},{9,8},{10,11... | collective-permute-start | bytes 884744 | tf_op jit(solution)/shard_map/ppermute | solution.py:196
  6.1 3.5 %collective-permute-start.2 = (bf16[128,1152]{1,0:T(8,128)(2,1)S(1)}, bf16[128,1152]{1,0:T(8,128)(2,1)S(1)}, u32[]{:S(2)}, u32[]{:S(2)}) collective-permute-start(bf16[128,1152]{1,0:T(8,128)(2,1)S(1)} %get-tuple-element.19.image_b), channel_id=1, source_target_pairs={{0,1},{1,0},{2,3},{3,2},{4,5},{5,4},{6,7},{7,6},{8,9},{9,8},{10,11... | collective-permute-start | bytes 884744 | tf_op jit(solution)/shard_map/ppermute | solution.py:196
  6.6 1.5 %collective-permute-start = (s32[1,256]{1,0:T(1,128)S(1)}, s32[1,256]{1,0:T(1,128)S(1)}, u32[]{:S(2)}, u32[]{:S(2)}) collective-permute-start(s32[1,256]{1,0:T(1,128)S(1)} %bitcast.3), channel_id=1, source_target_pairs={{0,1},{1,0},{2,3},{3,2},{4,5},{5,4},{6,7},{7,6},{8,9},{9,8},{10,11... | collective-permute-start | bytes 3080 | tf_op jit(solution)/shard_map/ppermute | solution.py:196
  8.1 15.0 %collective-permute-start.3 = (s32[2,256]{1,0:T(2,128)S(1)}, s32[2,256]{1,0:T(2,128)S(1)}, u32[]{:S(2)}, u32[]{:S(2)}) collective-permute-start(s32[2,256]{1,0:T(2,128)S(1)} %pad_add_fusion), channel_id=1, source_target_pairs={{0,2},{1,3},{2,4},{3,5},{4,6},{5,7},{6,8},{7,9},{8,10},{9,11},{10,... | collective-permute-start | bytes 6152 | tf_op jit(solution)/shard_map/ppermute | solution.py:193
  13.5 9.6 %collective-permute-start.4 = (bf16[48,1152]{1,0:T(8,128)(2,1)S(1)}, bf16[48,1152]{1,0:T(8,128)(2,1)S(1)}, u32[]{:S(2)}, u32[]{:S(2)}) collective-permute-start(bf16[48,1152]{1,0:T(8,128)(2,1)S(1)} %get-tuple-element.21), channel_id=1, source_target_pairs={{0,1},{1,0},{2,3},{3,2},{4,5},{5,4},{6,7},{7,6},{8,9},{9,8},{10,11... | collective-permute-start | bytes 331784 | tf_op jit(solution)/shard_map/ppermute | solution.py:196
  13.6 19.8 %collective-permute-start.9 = (bf16[208,1152]{1,0:T(8,128)(2,1)S(1)}, bf16[208,1152]{1,0:T(8,128)(2,1)S(1)}, u32[]{:S(2)}, u32[]{:S(2)}) collective-permute-start(bf16[208,1152]{1,0:T(8,128)(2,1)S(1)} %get-tuple-element.32), channel_id=1, source_target_pairs={{0,2},{1,3},{2,4},{3,5},{4,6},{5,7},{6,8},{7,9},{8,10},{9,11},{10,... | collective-permute-start | bytes 1437704 | tf_op jit(solution)/shard_map/ppermute | solution.py:193
  23.2 2.4 %collective-permute-start.6 = (bf16[192,1152]{1,0:T(8,128)(2,1)S(1)}, bf16[192,1152]{1,0:T(8,128)(2,1)S(1)}, u32[]{:S(2)}, u32[]{:S(2)}) collective-permute-start(bf16[192,1152]{1,0:T(8,128)(2,1)S(1)} %get-tuple-element.22), channel_id=1, source_target_pairs={{0,1},{1,0},{2,3},{3,2},{4,5},{5,4},{6,7},{7,6},{8,9},{9,8},{10,11... | collective-permute-start | bytes 1327112 | tf_op jit(solution)/shard_map/ppermute | solution.py:196
  23.3 2.3 %collective-permute-start.7 = (bf16[64,1152]{1,0:T(8,128)(2,1)S(1)}, bf16[64,1152]{1,0:T(8,128)(2,1)S(1)}, u32[]{:S(2)}, u32[]{:S(2)}) collective-permute-start(bf16[64,1152]{1,0:T(8,128)(2,1)S(1)} %get-tuple-element.23), channel_id=1, source_target_pairs={{0,1},{1,0},{2,3},{3,2},{4,5},{5,4},{6,7},{7,6},{8,9},{9,8},{10,11... | collective-permute-start | bytes 442376 | tf_op jit(solution)/shard_map/ppermute | solution.py:196
  23.8 10.7 %collective-permute-start.8 = (bf16[48,1152]{1,0:T(8,128)(2,1)S(1)}, bf16[48,1152]{1,0:T(8,128)(2,1)S(1)}, u32[]{:S(2)}, u32[]{:S(2)}) collective-permute-start(bf16[48,1152]{1,0:T(8,128)(2,1)S(1)} %collective-permute-done.4.before), channel_id=1, source_target_pairs={{0,3},{1,2},{2,5},{3,4},{4,7},{5,6},{6,9},{7,8},{8,11},{9,10},{10,... | collective-permute-start | bytes 331784 | tf_op jit(solution)/shard_map/ppermute | solution.py:244

commit v25 on v22

--- a/solution.py
+++ b/solution.py
@@ -9,7 +9,7 @@
 
 SHIFTS = 2
 AXES = ("dp", "group")
-STEP = 16
+STEP = 32
 VMEM = pl.BlockSpec(memory_space=pltpu.VMEM)
 SMEM = pl.BlockSpec(memory_space=pltpu.SMEM)
 ANY = pl.BlockSpec(memory_space=pl.ANY)

time: 35.3 us -> 35.3 us (level)
  no operation moved by 1% of the time
where the time goes in v25:
time: 35.3 us; the launch traced here: 34.9 us
  waiting for transfers between devices  13.2 us (37%)
  Pallas kernels  11 us (31%)
  starting transfers between devices  7.34 us (21%)
  between operations  2.03 us (6%)
  local copies, waits for them, and re-layouts  1.27 us (4%)
    ppermute x3, waiting for transfers between devices, ahead(): return lax.ppermute(value, AXES, skip)  12.5 us
    ppermute x3, starting transfers between devices, ahead(): return lax.ppermute(value, AXES, skip)  6.05 us
    pallas_call x5, Pallas kernels, call(): pl.pallas_call(kernel, out_shape=[jax.ShapeDtypeStruct(s, d) for s, d in...  4.37 us
    pallas_call x1, Pallas kernels, body(): pl.pallas_call(own_kernel, out_shape=[jax.ShapeDtypeStruct((cut, width),...  3.82 us
    pallas_call x2, Pallas kernels, add_part(): pl.pallas_call(functools.partial(add_kernel, start, chunks), out_shape=ja...  1.72 us
    ppermute x6, starting transfers between devices, across(): return lax.ppermute(value, AXES, swap)  1.29 us
    unnamed x4, local copies, waits for them, and re-layouts  1.27 us
    pallas_call x1, Pallas kernels, body(): pl.pallas_call(load_kernel, out_shape=[jax.ShapeDtypeStruct((n, width), b...  1.07 us
  transfers between devices with their start and end apart: 10, of which 4 were waited for; matrix products, arithmetic and copies ran while one was open for 0% of the time, Pallas kernels for 29%

profile of v25, /device:TPU:0, one launch (start us, length us, event | category | flops | bytes accessed | tf_op | source)
XLA Modules:
  0.0 34.9 jit_solution(4397832032479744017)
XLA Ops:
  0.6 0.0 copy-start
  0.6 1.3 %copy-done = f32[256,1152]{1,0:T(8,128)S(1)} copy-done((f32[256,1152]{1,0:T(8,128)S(1)}, f32[256,1152]{1,0:T(8,128)}, u32[]{:S(2)}) %copy-start) | copy-done | bytes 1179672
  1.9 0.0 copy-start.1
  1.9 0.1 cast.1.text
  2.0 3.0 %collective-permute-start.5 = (bf16[256,1152]{1,0:T(8,128)(2,1)S(1)}, bf16[256,1152]{1,0:T(8,128)(2,1)S(1)}, u32[]{:S(2)}, u32[]{:S(2)}) collective-permute-start(bf16[256,1152]{1,0:T(8,128)(2,1)S(1)} %cast.1.text), channel_id=1, source_target_pairs={{0,2},{1,3},{2,4},{3,5},{4,6},{5,7},{6,8},{7,9},{8,10},{9,11},{10,... | collective-permute-start | bytes 1769480 | tf_op jit(solution)/shard_map/ppermute | solution.py:185
  5.0 1.1 %load.1 = (bf16[128,1152]{1,0:T(8,128)(2,1)S(1)}, bf16[128,1152]{1,0:T(8,128)(2,1)S(1)}) custom-call(bf16[256,1152]{1,0:T(8,128)(2,1)S(1)} %cast.1.text, bf16[256,1152]{1,0:T(8,128)(2,1)} %image.1), custom_call_target="tpu_custom_call" | custom-call | tf_op jit(solution)/shard_map/load/pallas_call | solution.py:193
  6.1 0.1 collective-permute-start.1
  6.1 0.5 %collective-permute-start.2 = (bf16[128,1152]{1,0:T(8,128)(2,1)S(1)}, bf16[128,1152]{1,0:T(8,128)(2,1)S(1)}, u32[]{:S(2)}, u32[]{:S(2)}) collective-permute-start(bf16[128,1152]{1,0:T(8,128)(2,1)S(1)} %get-tuple-element.19.image_b), channel_id=1, source_target_pairs={{0,1},{1,0},{2,3},{3,2},{4,5},{5,4},{6,7},{7,6},{8,9},{9,8},{10,11... | collective-permute-start | bytes 884744 | tf_op jit(solution)/shard_map/ppermute | solution.py:188
  6.6 0.0 copy-done.1
  6.6 0.1 collective-permute-start
  8.0 0.1 collective-permute-done.mate_ids
  8.1 1.5 %collective-permute-start.3 = (s32[2,256]{1,0:T(2,128)S(1)}, s32[2,256]{1,0:T(2,128)S(1)}, u32[]{:S(2)}, u32[]{:S(2)}) collective-permute-start(s32[2,256]{1,0:T(2,128)S(1)} %pad_add_fusion), channel_id=1, source_target_pairs={{0,2},{1,3},{2,4},{3,5},{4,6},{5,7},{6,8},{7,9},{8,10},{9,11},{10,... | collective-permute-start | bytes 6152 | tf_op jit(solution)/shard_map/ppermute | solution.py:185
  9.6 0.1 pad_maximum_fusion.params
  9.7 0.0 collective-permute-done.1.mate_a
  9.7 0.0 collective-permute-done.2.mate_b
  9.7 3.8 %own.1 = (bf16[192,1152]{1,0:T(8,128)(2,1)S(1)}, bf16[64,1152]{1,0:T(8,128)(2,1)S(1)}, f32[256,1152]{1,0:T(8,128)S(1)}, f32[1,256]{1,0:T(1,128)S(1)}) custom-call(s32[1]{0:T(128)} %bitcast.flags, f32[2]{0:T(128)S(1)} %pad_maximum_fusion.params, s32[1,256]{1,0:T(1,128)S(1)} %bitcast.5, s32[1,256]{1,0:T(1,128)S(1)} %collective-permute-done.mate_ids, ...), custom_call_target="tpu_custom_call" | custom-call | tf_op jit(solution)/shard_map/own/pallas_call | solution.py:208
  13.5 0.1 collective-permute-start.4
  13.6 1.6 %collective-permute-start.9 = (bf16[192,1152]{1,0:T(8,128)(2,1)S(1)}, bf16[192,1152]{1,0:T(8,128)(2,1)S(1)}, u32[]{:S(2)}, u32[]{:S(2)}) collective-permute-start(bf16[192,1152]{1,0:T(8,128)(2,1)S(1)} %get-tuple-element.32), channel_id=1, source_target_pairs={{0,2},{1,3},{2,4},{3,5},{4,6},{5,7},{6,8},{7,9},{8,10},{9,11},{10,... | collective-permute-start | bytes 1327112 | tf_op jit(solution)/shard_map/ppermute | solution.py:185
  15.2 8.0 %collective-permute-done.3.both_ids = s32[2,256]{1,0:T(2,128)S(1)} collective-permute-done((s32[2,256]{1,0:T(2,128)S(1)}, s32[2,256]{1,0:T(2,128)S(1)}, u32[]{:S(2)}, u32[]{:S(2)}) %collective-permute-start.3) | collective-permute-done | bytes 2080 | tf_op jit(solution)/shard_map/ppermute | solution.py:185
  23.2 0.0 collective-permute-done.4.before
  23.2 0.0 collective-permute-done.5.far
  23.2 0.1 relay.1
  23.2 0.1 collective-permute-start.6
  23.3 0.5 %collective-permute-start.7 = (bf16[80,1152]{1,0:T(8,128)(2,1)S(1)}, bf16[80,1152]{1,0:T(8,128)(2,1)S(1)}, u32[]{:S(2)}, u32[]{:S(2)}) collective-permute-start(bf16[80,1152]{1,0:T(8,128)(2,1)S(1)} %get-tuple-element.23), channel_id=1, source_target_pairs={{0,1},{1,0},{2,3},{3,2},{4,5},{5,4},{6,7},{7,6},{8,9},{9,8},{10,11... | collective-permute-start | bytes 552968 | tf_op jit(solution)/shard_map/ppermute | solution.py:188
  23.8 0.0 collective-permute-start.8
  23.8 1.8 %far.1 = (f32[256,1152]{1,0:T(8,128)S(1)}, f32[256,1152]{1,0:T(8,128)S(1)}, f32[1,256]{1,0:T(1,128)S(1)}) custom-call(s32[1]{0:T(128)} %bitcast.flags, f32[2]{0:T(128)S(1)} %pad_maximum_fusion.params, s32[1,256]{1,0:T(1,128)S(1)} %bitcast.6, s32[1,256]{1,0:T(1,128)S(1)} %collective-permute-done.mate_ids, s32[2,256]{1,0:T(2,128)S(1)} %ids.1.token.both_ids, ...), custom_call_target="tpu_custom_call" | custom-call | tf_op jit(solution)/shard_map/far/pallas_call | solution.py:147
  25.6 0.0 collective-permute-done.7.near_b
  25.7 0.0 collective-permute-done.6.near_a
  25.7 2.4 %near.1 = (bf16[256,1152]{1,0:T(8,128)(2,1)}, f32[1,256]{1,0:T(1,128)}) custom-call(s32[1]{0:T(128)} %bitcast.flags, f32[2]{0:T(128)S(1)} %pad_maximum_fusion.params, s32[1,256]{1,0:T(1,128)S(1)} %bitcast.7, s32[1,256]{1,0:T(1,128)S(1)} %collective-permute-done.mate_ids, s32[2,256]{1,0:T(2,128)S(1)} %ids.1.token.both_ids, ...), custom_call_target="tpu_custom_call" | custom-call | tf_op jit(solution)/shard_map/near/pallas_call | solution.py:147
  28.1 4.5 %collective-permute-done.9.arrived = bf16[192,1152]{1,0:T(8,128)(2,1)S(1)} collective-permute-done((bf16[192,1152]{1,0:T(8,128)(2,1)S(1)}, bf16[192,1152]{1,0:T(8,128)(2,1)S(1)}, u32[]{:S(2)}, u32[]{:S(2)}) %collective-permute-start.9) | collective-permute-done | bytes 442400 | tf_op jit(solution)/shard_map/ppermute | solution.py:185
  32.6 1.0 %add_a.1.refs_0_ = f32[256,1152]{1,0:T(8,128)} custom-call(bf16[192,1152]{1,0:T(8,128)(2,1)S(1)} %collective-permute-done.9.arrived, f32[256,1152]{1,0:T(8,128)S(1)} %get-tuple-element.31.late), custom_call_target="tpu_custom_call" | custom-call | tf_op jit(solution)/shard_map/add_a/pallas_call | solution.py:159
  33.6 0.5 %collective-permute-done.8.arrived = bf16[64,1152]{1,0:T(8,128)(2,1)S(1)} collective-permute-done((bf16[64,1152]{1,0:T(8,128)(2,1)S(1)}, bf16[64,1152]{1,0:T(8,128)(2,1)S(1)}, u32[]{:S(2)}, u32[]{:S(2)}) %collective-permute-start.8) | collective-permute-done | bytes 147488 | tf_op jit(solution)/shard_map/ppermute | solution.py:227
  34.1 0.7 %add_b.1 = f32[256,1152]{1,0:T(8,128)} custom-call(bf16[64,1152]{1,0:T(8,128)(2,1)S(1)} %collective-permute-done.8.arrived, f32[256,1152]{1,0:T(8,128)S(1)} %get-tuple-element.31.late, f32[256,1152]{1,0:T(8,128)} %add_a.1.refs_0_), custom_call_target="tpu_custom_call", output_to_operand_aliasing={{}: (2, {})} | custom-call | tf_op jit(solution)/shard_map/add_b/pallas_call | solution.py:159
  (2 shorter events, 0.0 us)
Async XLA Ops:
  0.6 1.3 %copy-start = (f32[256,1152]{1,0:T(8,128)S(1)}, f32[256,1152]{1,0:T(8,128)}, u32[]{:S(2)}) copy-start(f32[256,1152]{1,0:T(8,128)} %text.1) | copy-start | bytes 3538948
  1.9 4.7 %copy-start.1 = (s32[256]{0:T(256)S(1)}, s32[256]{0:T(256)}, u32[]{:S(2)}) copy-start(s32[256]{0:T(256)} %param.9) | copy-start | bytes 3076
  2.0 21.2 %collective-permute-start.5 = (bf16[256,1152]{1,0:T(8,128)(2,1)S(1)}, bf16[256,1152]{1,0:T(8,128)(2,1)S(1)}, u32[]{:S(2)}, u32[]{:S(2)}) collective-permute-start(bf16[256,1152]{1,0:T(8,128)(2,1)S(1)} %cast.1.text), channel_id=1, source_target_pairs={{0,2},{1,3},{2,4},{3,5},{4,6},{5,7},{6,8},{7,9},{8,10},{9,11},{10,... | collective-permute-start | bytes 1769480 | tf_op jit(solution)/shard_map/ppermute | solution.py:185
  6.1 3.6 %collective-permute-start.1 = (bf16[128,1152]{1,0:T(8,128)(2,1)S(1)}, bf16[128,1152]{1,0:T(8,128)(2,1)S(1)}, u32[]{:S(2)}, u32[]{:S(2)}) collective-permute-start(bf16[128,1152]{1,0:T(8,128)(2,1)S(1)} %get-tuple-element.18.image_a), channel_id=1, source_target_pairs={{0,1},{1,0},{2,3},{3,2},{4,5},{5,4},{6,7},{7,6},{8,9},{9,8},{10,11... | collective-permute-start | bytes 884744 | tf_op jit(solution)/shard_map/ppermute | solution.py:188
  6.1 3.5 %collective-permute-start.2 = (bf16[128,1152]{1,0:T(8,128)(2,1)S(1)}, bf16[128,1152]{1,0:T(8,128)(2,1)S(1)}, u32[]{:S(2)}, u32[]{:S(2)}) collective-permute-start(bf16[128,1152]{1,0:T(8,128)(2,1)S(1)} %get-tuple-element.19.image_b), channel_id=1, source_target_pairs={{0,1},{1,0},{2,3},{3,2},{4,5},{5,4},{6,7},{7,6},{8,9},{9,8},{10,11... | collective-permute-start | bytes 884744 | tf_op jit(solution)/shard_map/ppermute | solution.py:188
  6.6 1.5 %collective-permute-start = (s32[1,256]{1,0:T(1,128)S(1)}, s32[1,256]{1,0:T(1,128)S(1)}, u32[]{:S(2)}, u32[]{:S(2)}) collective-permute-start(s32[1,256]{1,0:T(1,128)S(1)} %bitcast.3), channel_id=1, source_target_pairs={{0,1},{1,0},{2,3},{3,2},{4,5},{5,4},{6,7},{7,6},{8,9},{9,8},{10,11... | collective-permute-start | bytes 3080 | tf_op jit(solution)/shard_map/ppermute | solution.py:188
  8.1 15.0 %collective-permute-start.3 = (s32[2,256]{1,0:T(2,128)S(1)}, s32[2,256]{1,0:T(2,128)S(1)}, u32[]{:S(2)}, u32[]{:S(2)}) collective-permute-start(s32[2,256]{1,0:T(2,128)S(1)} %pad_add_fusion), channel_id=1, source_target_pairs={{0,2},{1,3},{2,4},{3,5},{4,6},{5,7},{6,8},{7,9},{8,10},{9,11},{10,... | collective-permute-start | bytes 6152 | tf_op jit(solution)/shard_map/ppermute | solution.py:185
  13.5 9.6 %collective-permute-start.4 = (bf16[64,1152]{1,0:T(8,128)(2,1)S(1)}, bf16[64,1152]{1,0:T(8,128)(2,1)S(1)}, u32[]{:S(2)}, u32[]{:S(2)}) collective-permute-start(bf16[64,1152]{1,0:T(8,128)(2,1)S(1)} %get-tuple-element.21), channel_id=1, source_target_pairs={{0,1},{1,0},{2,3},{3,2},{4,5},{5,4},{6,7},{7,6},{8,9},{9,8},{10,11... | collective-permute-start | bytes 442376 | tf_op jit(solution)/shard_map/ppermute | solution.py:188
  13.6 19.0 %collective-permute-start.9 = (bf16[192,1152]{1,0:T(8,128)(2,1)S(1)}, bf16[192,1152]{1,0:T(8,128)(2,1)S(1)}, u32[]{:S(2)}, u32[]{:S(2)}) collective-permute-start(bf16[192,1152]{1,0:T(8,128)(2,1)S(1)} %get-tuple-element.32), channel_id=1, source_target_pairs={{0,2},{1,3},{2,4},{3,5},{4,6},{5,7},{6,8},{7,9},{8,10},{9,11},{10,... | collective-permute-start | bytes 1327112 | tf_op jit(solution)/shard_map/ppermute | solution.py:185
  23.2 2.4 %collective-permute-start.6 = (bf16[176,1152]{1,0:T(8,128)(2,1)S(1)}, bf16[176,1152]{1,0:T(8,128)(2,1)S(1)}, u32[]{:S(2)}, u32[]{:S(2)}) collective-permute-start(bf16[176,1152]{1,0:T(8,128)(2,1)S(1)} %get-tuple-element.22), channel_id=1, source_target_pairs={{0,1},{1,0},{2,3},{3,2},{4,5},{5,4},{6,7},{7,6},{8,9},{9,8},{10,11... | collective-permute-start | bytes 1216520 | tf_op jit(solution)/shard_map/ppermute | solution.py:188
  23.3 2.3 %collective-permute-start.7 = (bf16[80,1152]{1,0:T(8,128)(2,1)S(1)}, bf16[80,1152]{1,0:T(8,128)(2,1)S(1)}, u32[]{:S(2)}, u32[]{:S(2)}) collective-permute-start(bf16[80,1152]{1,0:T(8,128)(2,1)S(1)} %get-tuple-element.23), channel_id=1, source_target_pairs={{0,1},{1,0},{2,3},{3,2},{4,5},{5,4},{6,7},{7,6},{8,9},{9,8},{10,11... | collective-permute-start | bytes 552968 | tf_op jit(solution)/shard_map/ppermute | solution.py:188
  23.8 10.3 %collective-permute-start.8 = (bf16[64,1152]{1,0:T(8,128)(2,1)S(1)}, bf16[64,1152]{1,0:T(8,128)(2,1)S(1)}, u32[]{:S(2)}, u32[]{:S(2)}) collective-permute-start(bf16[64,1152]{1,0:T(8,128)(2,1)S(1)} %collective-permute-done.4.before), channel_id=1, source_target_pairs={{0,3},{1,2},{2,5},{3,4},{4,7},{5,6},{6,9},{7,8},{8,11},{9,10},{10,... | collective-permute-start | bytes 442376 | tf_op jit(solution)/shard_map/ppermute | solution.py:227

commit v26 on v21

--- a/solution.py
+++ b/solution.py
@@ -203,7 +203,7 @@
     mate_ids = across(ids)
     both_ids = ahead(jnp.concatenate([ids, mate_ids]))
 
-    cut = rows - rows * 3 // 16
+    cut = rows - rows // 4
     out_a, out_b, image_sum, loss = pl.pallas_call(
         own_kernel,
         out_shape=[

time: 35.4 us -> 35.3 us (level)
    ppermute x3, waiting for transfers between devices: 14.2 us -> 13.4 us  [ahead(): return lax.ppermute(value, AXES, skip)]
    ppermute x1, waiting for transfers between devices: 0.01 us -> 0.47 us  [body(): arrived_b = lax.ppermute(mate_rows, AXES, crossed)]
  transfers between devices with their start and end apart: 10 -> 10, of which waited for: 3 -> 4; matrix products, arithmetic and copies ran while one was open for 0% -> 0% of each run, Pallas kernels for 27% -> 27%
where the time goes in v26:
time: 35.3 us; the launch traced here: 34.9 us
  waiting for transfers between devices  14 us (40%)
  Pallas kernels  10.2 us (29%)
  starting transfers between devices  7.34 us (21%)
  between operations  2.03 us (6%)
  local copies, waits for them, and re-layouts  1.27 us (4%)
    ppermute x3, waiting for transfers between devices, ahead(): return lax.ppermute(value, AXES, skip)  13.4 us
    ppermute x3, starting transfers between devices, ahead(): return lax.ppermute(value, AXES, skip)  6.05 us
    pallas_call x5, Pallas kernels, call(): pl.pallas_call(kernel, out_shape=[jax.ShapeDtypeStruct(s, d) for s, d in...  4.37 us
    pallas_call x1, Pallas kernels, body(): pl.pallas_call(own_kernel, out_shape=[jax.ShapeDtypeStruct((cut, width),...  2.96 us
    pallas_call x2, Pallas kernels, add_part(): pl.pallas_call(functools.partial(add_kernel, start, chunks), out_shape=ja...  1.77 us
    ppermute x6, starting transfers between devices, across(): return lax.ppermute(value, AXES, swap)  1.29 us
    unnamed x4, local copies, waits for them, and re-layouts  1.27 us
    pallas_call x1, Pallas kernels, body(): pl.pallas_call(load_kernel, out_shape=[jax.ShapeDtypeStruct((n, width), b...  1.07 us
  transfers between devices with their start and end apart: 10, of which 4 were waited for; matrix products, arithmetic and copies ran while one was open for 0% of the time, Pallas kernels for 27%

profile of v26, /device:TPU:0, one launch (start us, length us, event | category | flops | bytes accessed | tf_op | source)
XLA Modules:
  0.0 34.9 jit_solution(2116571002682742258)
XLA Ops:
  0.6 0.0 copy-start
  0.6 1.3 %copy-done = f32[256,1152]{1,0:T(8,128)S(1)} copy-done((f32[256,1152]{1,0:T(8,128)S(1)}, f32[256,1152]{1,0:T(8,128)}, u32[]{:S(2)}) %copy-start) | copy-done | bytes 1179672
  1.9 0.0 copy-start.1
  1.9 0.1 cast.1.text
  2.0 3.0 %collective-permute-start.5 = (bf16[256,1152]{1,0:T(8,128)(2,1)S(1)}, bf16[256,1152]{1,0:T(8,128)(2,1)S(1)}, u32[]{:S(2)}, u32[]{:S(2)}) collective-permute-start(bf16[256,1152]{1,0:T(8,128)(2,1)S(1)} %cast.1.text), channel_id=1, source_target_pairs={{0,2},{1,3},{2,4},{3,5},{4,6},{5,7},{6,8},{7,9},{8,10},{9,11},{10,... | collective-permute-start | bytes 1769480 | tf_op jit(solution)/shard_map/ppermute | solution.py:184
  5.0 1.1 %load.1 = (bf16[128,1152]{1,0:T(8,128)(2,1)S(1)}, bf16[128,1152]{1,0:T(8,128)(2,1)S(1)}) custom-call(bf16[256,1152]{1,0:T(8,128)(2,1)S(1)} %cast.1.text, bf16[256,1152]{1,0:T(8,128)(2,1)} %image.1), custom_call_target="tpu_custom_call" | custom-call | tf_op jit(solution)/shard_map/load/pallas_call | solution.py:192
  6.1 0.1 collective-permute-start.1
  6.1 0.5 %collective-permute-start.2 = (bf16[128,1152]{1,0:T(8,128)(2,1)S(1)}, bf16[128,1152]{1,0:T(8,128)(2,1)S(1)}, u32[]{:S(2)}, u32[]{:S(2)}) collective-permute-start(bf16[128,1152]{1,0:T(8,128)(2,1)S(1)} %get-tuple-element.19.image_b), channel_id=1, source_target_pairs={{0,1},{1,0},{2,3},{3,2},{4,5},{5,4},{6,7},{7,6},{8,9},{9,8},{10,11... | collective-permute-start | bytes 884744 | tf_op jit(solution)/shard_map/ppermute | solution.py:187
  6.6 0.0 copy-done.1
  6.6 0.1 collective-permute-start
  8.0 0.1 collective-permute-done.mate_ids
  8.1 1.5 %collective-permute-start.3 = (s32[2,256]{1,0:T(2,128)S(1)}, s32[2,256]{1,0:T(2,128)S(1)}, u32[]{:S(2)}, u32[]{:S(2)}) collective-permute-start(s32[2,256]{1,0:T(2,128)S(1)} %pad_add_fusion), channel_id=1, source_target_pairs={{0,2},{1,3},{2,4},{3,5},{4,6},{5,7},{6,8},{7,9},{8,10},{9,11},{10,... | collective-permute-start | bytes 6152 | tf_op jit(solution)/shard_map/ppermute | solution.py:184
  9.6 0.1 pad_maximum_fusion.params
  9.7 0.0 collective-permute-done.1.mate_a
  9.7 0.0 collective-permute-done.2.mate_b
  9.7 3.0 %own.1 = (bf16[192,1152]{1,0:T(8,128)(2,1)S(1)}, bf16[64,1152]{1,0:T(8,128)(2,1)S(1)}, f32[256,1152]{1,0:T(8,128)S(1)}, f32[1,256]{1,0:T(1,128)S(1)}) custom-call(s32[1]{0:T(128)} %bitcast.flags, f32[2]{0:T(128)S(1)} %pad_maximum_fusion.params, s32[1,256]{1,0:T(1,128)S(1)} %bitcast.5, s32[1,256]{1,0:T(1,128)S(1)} %collective-permute-done.mate_ids, ...), custom_call_target="tpu_custom_call" | custom-call | tf_op jit(solution)/shard_map/own/pallas_call | solution.py:207
  12.6 0.1 collective-permute-start.4
  12.7 1.6 %collective-permute-start.9 = (bf16[192,1152]{1,0:T(8,128)(2,1)S(1)}, bf16[192,1152]{1,0:T(8,128)(2,1)S(1)}, u32[]{:S(2)}, u32[]{:S(2)}) collective-permute-start(bf16[192,1152]{1,0:T(8,128)(2,1)S(1)} %get-tuple-element.32), channel_id=1, source_target_pairs={{0,2},{1,3},{2,4},{3,5},{4,6},{5,7},{6,8},{7,9},{8,10},{9,11},{10,... | collective-permute-start | bytes 1327112 | tf_op jit(solution)/shard_map/ppermute | solution.py:184
  14.3 8.9 %collective-permute-done.3.both_ids = s32[2,256]{1,0:T(2,128)S(1)} collective-permute-done((s32[2,256]{1,0:T(2,128)S(1)}, s32[2,256]{1,0:T(2,128)S(1)}, u32[]{:S(2)}, u32[]{:S(2)}) %collective-permute-start.3) | collective-permute-done | bytes 2080 | tf_op jit(solution)/shard_map/ppermute | solution.py:184
  23.2 0.0 collective-permute-done.4.before
  23.2 0.0 collective-permute-done.5.far
  23.2 0.1 relay.1
  23.2 0.1 collective-permute-start.6
  23.3 0.5 %collective-permute-start.7 = (bf16[80,1152]{1,0:T(8,128)(2,1)S(1)}, bf16[80,1152]{1,0:T(8,128)(2,1)S(1)}, u32[]{:S(2)}, u32[]{:S(2)}) collective-permute-start(bf16[80,1152]{1,0:T(8,128)(2,1)S(1)} %get-tuple-element.23), channel_id=1, source_target_pairs={{0,1},{1,0},{2,3},{3,2},{4,5},{5,4},{6,7},{7,6},{8,9},{9,8},{10,11... | collective-permute-start | bytes 552968 | tf_op jit(solution)/shard_map/ppermute | solution.py:187
  23.8 0.0 collective-permute-start.8
  23.8 1.8 %far.1 = (f32[256,1152]{1,0:T(8,128)S(1)}, f32[256,1152]{1,0:T(8,128)S(1)}, f32[1,256]{1,0:T(1,128)S(1)}) custom-call(s32[1]{0:T(128)} %bitcast.flags, f32[2]{0:T(128)S(1)} %pad_maximum_fusion.params, s32[1,256]{1,0:T(1,128)S(1)} %bitcast.6, s32[1,256]{1,0:T(1,128)S(1)} %collective-permute-done.mate_ids, s32[2,256]{1,0:T(2,128)S(1)} %ids.1.token.both_ids, ...), custom_call_target="tpu_custom_call" | custom-call | tf_op jit(solution)/shard_map/far/pallas_call | solution.py:146
  25.6 0.0 collective-permute-done.7.near_b
  25.7 0.0 collective-permute-done.6.near_a
  25.7 2.4 %near.1 = (bf16[256,1152]{1,0:T(8,128)(2,1)}, f32[1,256]{1,0:T(1,128)}) custom-call(s32[1]{0:T(128)} %bitcast.flags, f32[2]{0:T(128)S(1)} %pad_maximum_fusion.params, s32[1,256]{1,0:T(1,128)S(1)} %bitcast.7, s32[1,256]{1,0:T(1,128)S(1)} %collective-permute-done.mate_ids, s32[2,256]{1,0:T(2,128)S(1)} %ids.1.token.both_ids, ...), custom_call_target="tpu_custom_call" | custom-call | tf_op jit(solution)/shard_map/near/pallas_call | solution.py:146
  28.1 4.5 %collective-permute-done.9.arrived = bf16[192,1152]{1,0:T(8,128)(2,1)S(1)} collective-permute-done((bf16[192,1152]{1,0:T(8,128)(2,1)S(1)}, bf16[192,1152]{1,0:T(8,128)(2,1)S(1)}, u32[]{:S(2)}, u32[]{:S(2)}) %collective-permute-start.9) | collective-permute-done | bytes 442400 | tf_op jit(solution)/shard_map/ppermute | solution.py:184
  32.6 1.0 %add_a.1.refs_0_ = f32[256,1152]{1,0:T(8,128)} custom-call(bf16[192,1152]{1,0:T(8,128)(2,1)S(1)} %collective-permute-done.9.arrived, f32[256,1152]{1,0:T(8,128)S(1)} %get-tuple-element.31.late), custom_call_target="tpu_custom_call" | custom-call | tf_op jit(solution)/shard_map/add_a/pallas_call | solution.py:158
  33.7 0.5 %collective-permute-done.8.arrived = bf16[64,1152]{1,0:T(8,128)(2,1)S(1)} collective-permute-done((bf16[64,1152]{1,0:T(8,128)(2,1)S(1)}, bf16[64,1152]{1,0:T(8,128)(2,1)S(1)}, u32[]{:S(2)}, u32[]{:S(2)}) %collective-permute-start.8) | collective-permute-done | bytes 147488 | tf_op jit(solution)/shard_map/ppermute | solution.py:226
  34.1 0.7 %add_b.1 = f32[256,1152]{1,0:T(8,128)} custom-call(bf16[64,1152]{1,0:T(8,128)(2,1)S(1)} %collective-permute-done.8.arrived, f32[256,1152]{1,0:T(8,128)S(1)} %get-tuple-element.31.late, f32[256,1152]{1,0:T(8,128)} %add_a.1.refs_0_), custom_call_target="tpu_custom_call", output_to_operand_aliasing={{}: (2, {})} | custom-call | tf_op jit(solution)/shard_map/add_b/pallas_call | solution.py:158
  (2 shorter events, 0.0 us)
Async XLA Ops:
  0.6 1.3 %copy-start = (f32[256,1152]{1,0:T(8,128)S(1)}, f32[256,1152]{1,0:T(8,128)}, u32[]{:S(2)}) copy-start(f32[256,1152]{1,0:T(8,128)} %text.1) | copy-start | bytes 3538948
  1.9 4.7 %copy-start.1 = (s32[256]{0:T(256)S(1)}, s32[256]{0:T(256)}, u32[]{:S(2)}) copy-start(s32[256]{0:T(256)} %param.9) | copy-start | bytes 3076
  2.0 21.2 %collective-permute-start.5 = (bf16[256,1152]{1,0:T(8,128)(2,1)S(1)}, bf16[256,1152]{1,0:T(8,128)(2,1)S(1)}, u32[]{:S(2)}, u32[]{:S(2)}) collective-permute-start(bf16[256,1152]{1,0:T(8,128)(2,1)S(1)} %cast.1.text), channel_id=1, source_target_pairs={{0,2},{1,3},{2,4},{3,5},{4,6},{5,7},{6,8},{7,9},{8,10},{9,11},{10,... | collective-permute-start | bytes 1769480 | tf_op jit(solution)/shard_map/ppermute | solution.py:184
  6.1 3.6 %collective-permute-start.1 = (bf16[128,1152]{1,0:T(8,128)(2,1)S(1)}, bf16[128,1152]{1,0:T(8,128)(2,1)S(1)}, u32[]{:S(2)}, u32[]{:S(2)}) collective-permute-start(bf16[128,1152]{1,0:T(8,128)(2,1)S(1)} %get-tuple-element.18.image_a), channel_id=1, source_target_pairs={{0,1},{1,0},{2,3},{3,2},{4,5},{5,4},{6,7},{7,6},{8,9},{9,8},{10,11... | collective-permute-start | bytes 884744 | tf_op jit(solution)/shard_map/ppermute | solution.py:187
  6.1 3.5 %collective-permute-start.2 = (bf16[128,1152]{1,0:T(8,128)(2,1)S(1)}, bf16[128,1152]{1,0:T(8,128)(2,1)S(1)}, u32[]{:S(2)}, u32[]{:S(2)}) collective-permute-start(bf16[128,1152]{1,0:T(8,128)(2,1)S(1)} %get-tuple-element.19.image_b), channel_id=1, source_target_pairs={{0,1},{1,0},{2,3},{3,2},{4,5},{5,4},{6,7},{7,6},{8,9},{9,8},{10,11... | collective-permute-start | bytes 884744 | tf_op jit(solution)/shard_map/ppermute | solution.py:187
  6.6 1.5 %collective-permute-start = (s32[1,256]{1,0:T(1,128)S(1)}, s32[1,256]{1,0:T(1,128)S(1)}, u32[]{:S(2)}, u32[]{:S(2)}) collective-permute-start(s32[1,256]{1,0:T(1,128)S(1)} %bitcast.3), channel_id=1, source_target_pairs={{0,1},{1,0},{2,3},{3,2},{4,5},{5,4},{6,7},{7,6},{8,9},{9,8},{10,11... | collective-permute-start | bytes 3080 | tf_op jit(solution)/shard_map/ppermute | solution.py:187
  8.1 15.0 %collective-permute-start.3 = (s32[2,256]{1,0:T(2,128)S(1)}, s32[2,256]{1,0:T(2,128)S(1)}, u32[]{:S(2)}, u32[]{:S(2)}) collective-permute-start(s32[2,256]{1,0:T(2,128)S(1)} %pad_add_fusion), channel_id=1, source_target_pairs={{0,2},{1,3},{2,4},{3,5},{4,6},{5,7},{6,8},{7,9},{8,10},{9,11},{10,... | collective-permute-start | bytes 6152 | tf_op jit(solution)/shard_map/ppermute | solution.py:184
  12.6 10.5 %collective-permute-start.4 = (bf16[64,1152]{1,0:T(8,128)(2,1)S(1)}, bf16[64,1152]{1,0:T(8,128)(2,1)S(1)}, u32[]{:S(2)}, u32[]{:S(2)}) collective-permute-start(bf16[64,1152]{1,0:T(8,128)(2,1)S(1)} %get-tuple-element.21), channel_id=1, source_target_pairs={{0,1},{1,0},{2,3},{3,2},{4,5},{5,4},{6,7},{7,6},{8,9},{9,8},{10,11... | collective-permute-start | bytes 442376 | tf_op jit(solution)/shard_map/ppermute | solution.py:187
  12.7 19.9 %collective-permute-start.9 = (bf16[192,1152]{1,0:T(8,128)(2,1)S(1)}, bf16[192,1152]{1,0:T(8,128)(2,1)S(1)}, u32[]{:S(2)}, u32[]{:S(2)}) collective-permute-start(bf16[192,1152]{1,0:T(8,128)(2,1)S(1)} %get-tuple-element.32), channel_id=1, source_target_pairs={{0,2},{1,3},{2,4},{3,5},{4,6},{5,7},{6,8},{7,9},{8,10},{9,11},{10,... | collective-permute-start | bytes 1327112 | tf_op jit(solution)/shard_map/ppermute | solution.py:184
  23.2 2.4 %collective-permute-start.6 = (bf16[176,1152]{1,0:T(8,128)(2,1)S(1)}, bf16[176,1152]{1,0:T(8,128)(2,1)S(1)}, u32[]{:S(2)}, u32[]{:S(2)}) collective-permute-start(bf16[176,1152]{1,0:T(8,128)(2,1)S(1)} %get-tuple-element.22), channel_id=1, source_target_pairs={{0,1},{1,0},{2,3},{3,2},{4,5},{5,4},{6,7},{7,6},{8,9},{9,8},{10,11... | collective-permute-start | bytes 1216520 | tf_op jit(solution)/shard_map/ppermute | solution.py:187
  23.3 2.3 %collective-permute-start.7 = (bf16[80,1152]{1,0:T(8,128)(2,1)S(1)}, bf16[80,1152]{1,0:T(8,128)(2,1)S(1)}, u32[]{:S(2)}, u32[]{:S(2)}) collective-permute-start(bf16[80,1152]{1,0:T(8,128)(2,1)S(1)} %get-tuple-element.23), channel_id=1, source_target_pairs={{0,1},{1,0},{2,3},{3,2},{4,5},{5,4},{6,7},{7,6},{8,9},{9,8},{10,11... | collective-permute-start | bytes 552968 | tf_op jit(solution)/shard_map/ppermute | solution.py:187
  23.8 10.3 %collective-permute-start.8 = (bf16[64,1152]{1,0:T(8,128)(2,1)S(1)}, bf16[64,1152]{1,0:T(8,128)(2,1)S(1)}, u32[]{:S(2)}, u32[]{:S(2)}) collective-permute-start(bf16[64,1152]{1,0:T(8,128)(2,1)S(1)} %collective-permute-done.4.before), channel_id=1, source_target_pairs={{0,3},{1,2},{2,5},{3,4},{4,7},{5,6},{6,9},{7,8},{8,11},{9,10},{10,... | collective-permute-start | bytes 442376 | tf_op jit(solution)/shard_map/ppermute | solution.py:226
